TPU v7x, 32 devices: a whole 2x2x4 slice. The times are simulated.
32 devices in a mesh: replica: 2 (over y), branch: 4 (over z), tensor: 4 (over x, core).
Axes of the slice: x: 2, y: 2, z: 4, core: 2. Of those that a mesh axis runs over, the one named last changes fastest.
Arguments:
- prompt_ssm: float32 [8, 16, 4096], P(('replica', 'branch'), None, 'tensor'), parts along dimension 0, may hold values from -6 to 6
- prompt_conv: bfloat16 [8, 3, 4096], P(('replica', 'branch'), None, 'tensor'), parts along dimension 0, may hold values from -6 to 6
- prompt_of: int32 [128], P(('replica', 'branch')), parts along dimension 0, may hold values from 0 to 3
- step_in: bfloat16 [128, 4, 2, 4096], P(('replica', 'branch'), None, None, 'tensor'), parts along dimension 0, may hold values from -6 to 6
- conv_weight: float32 [4, 4096], P(None, 'tensor'), may hold values from -3 to 3
- conv_bias: float32 [4096], P('tensor'), may hold values from -3 to 3
- x_weight: bfloat16 [4096, 288], P('tensor'), may hold values from -0.09375 to 0.09375
- dt_weight: bfloat16 [256, 4096], P(None, 'tensor'), may hold values from -0.375 to 0.375
- dt_bias: float32 [4096], P('tensor'), may hold values from -4 to -1
- a_log: float32 [16, 4096], P(None, 'tensor'), may hold values from 0 to 2.77
- skip: float32 [4096], P('tensor'), may hold values from 0.5 to 1.5
- send_rows: int32 [8, 4, 1], P(('replica', 'branch')), parts along dimension 0, may hold values from -1 to 15, as said below
- child_slot: int32 [128], P(('replica', 'branch')), parts along dimension 0, may hold values from 0 to 3, as said below
Outputs:
- decoded: bfloat16 [128, 4, 4096], P(('replica', 'branch'), None, 'tensor'), parts along dimension 0
- child_ssm: float32 [128, 16, 4096], P(('replica', 'branch'), None, 'tensor'), parts along dimension 0
- child_conv: bfloat16 [128, 3, 4096], P(('replica', 'branch'), None, 'tensor'), parts along dimension 0
There are 2 independent parts, one for each index of `replica`. A program takes and returns all parts, laid end to end along the dimension named above; an argument that names none is the same for every part. Nothing has to cross between parts.
Inputs may be any that keep to these rules, and one draw needn't show every extreme that they name: send_rows[s, d, c] is a branch of owner s (its row among the 16 branches of s) carried in slot c to owner d, or -1 for an empty slot; in each block the full slots come first. child_slot[j] = s * 1 + c names a full slot that owner j // 16 receives from owner s; each full slot that an owner receives is named by at least one of its children.
All inputs are finite; a program needn't handle non-finite values.
Results may differ from a plain program's by a relative error of at most 0.0061.
Values may be sent and summed in bfloat16 or wider, within the bound.
No kernel may reach another device: no remote copies, remote signals or barrier semaphores. Data moves between devices by JAX's collectives and lax.ppermute only.
A program may use at most 64 MiB of HBM per device.

v0:
```python
import jax
import jax.numpy as jnp
from jax import lax
from jax.sharding import PartitionSpec as P


def select_prompts(prompt_ssm, prompt_wide, wanted):
    pieces = (
        lax.all_gather(prompt_ssm, "branch", axis=0, tiled=True),
        lax.all_gather(prompt_wide, "branch", axis=0, tiled=True),
    )
    piece_rows = pieces[0].shape[0]
    numbers = jnp.arange(piece_rows, dtype=jnp.int32)
    onehot = (wanted[:, None] == numbers[None, :]).astype(jnp.float32)
    ssm_add = jnp.einsum("rp,pne->rne", onehot, pieces[0], precision=lax.Precision.HIGHEST)
    conv_add = jnp.einsum("rp,pke->rke", onehot, pieces[1], precision=lax.Precision.HIGHEST)
    return (ssm_add, conv_add.astype(jnp.bfloat16))


def decode_rows(
    states, windows, x_all, z_all, conv_weight, conv_bias, x_weight, dt_weight, dt_bias, a_log, skip
):
    kernel_len = conv_weight.shape[0]
    rank_size = dt_weight.shape[0]
    state_size = a_log.shape[0]
    decay_rate = -jnp.exp(a_log)
    outputs = []
    for position in range(x_all.shape[1]):
        x_now = x_all[:, position]
        z_now = z_all[:, position]
        conv_sum = conv_weight[kernel_len - 1] * x_now.astype(jnp.float32) + conv_bias
        for offset in range(kernel_len - 1):
            conv_sum = conv_sum + conv_weight[offset] * windows[:, offset].astype(jnp.float32)
        activated = jax.nn.silu(conv_sum)
        partial_proj = jnp.dot(
            activated.astype(jnp.bfloat16), x_weight, preferred_element_type=jnp.float32
        )
        x_proj = lax.psum(partial_proj, "tensor")
        delta_in = x_proj[:, :rank_size].astype(jnp.bfloat16)
        b_proj = x_proj[:, rank_size : rank_size + state_size]
        c_proj = x_proj[:, rank_size + state_size :]
        delta = jax.nn.softplus(
            jnp.dot(delta_in, dt_weight, preferred_element_type=jnp.float32) + dt_bias
        )
        states = (
            jnp.exp(delta[:, None, :] * decay_rate[None]) * states
            + (delta * activated)[:, None, :] * b_proj[:, :, None]
        )
        output = jnp.sum(c_proj[:, :, None] * states, axis=1) + skip * activated
        outputs.append((output * jax.nn.silu(z_now.astype(jnp.float32))).astype(jnp.bfloat16))
        windows = jnp.concatenate([windows[:, 1:], x_now[:, None]], axis=1)
    return (states, windows, jnp.stack(outputs, axis=1))


def on_device(
    prompt_ssm,
    prompt_conv,
    prompt_of,
    step_in,
    conv_weight,
    conv_bias,
    x_weight,
    dt_weight,
    dt_bias,
    a_log,
    skip,
    send_rows,
    child_slot,
):
    owners = lax.axis_size("branch")
    capacity = send_rows.shape[2]
    x_own = step_in[:, :, 0]
    z_own = step_in[:, :, 1]
    slot_rows = send_rows[0]
    filled = slot_rows >= 0
    picked = jnp.maximum(slot_rows, 0)
    start_ssm, start_conv = select_prompts(prompt_ssm, prompt_conv.astype(jnp.float32), prompt_of)
    states, windows, decoded_all = decode_rows(
        start_ssm,
        start_conv,
        x_own,
        z_own,
        conv_weight,
        conv_bias,
        x_weight,
        dt_weight,
        dt_bias,
        a_log,
        skip,
    )
    out_ssm = jnp.where(filled[:, :, None, None], states[picked], 0.0)
    out_conv = jnp.where(filled[:, :, None, None], windows[picked].astype(jnp.float32), 0.0)
    got_ssm, got_conv = (
        lax.all_to_all(out_ssm, "branch", split_axis=0, concat_axis=0, tiled=True),
        lax.all_to_all(out_conv, "branch", split_axis=0, concat_axis=0, tiled=True),
    )
    flat_ssm = got_ssm.reshape((owners * capacity,) + states.shape[1:])
    flat_conv = got_conv.reshape((owners * capacity,) + windows.shape[1:])
    child_ssm = flat_ssm[child_slot]
    child_conv = flat_conv[child_slot].astype(jnp.bfloat16)
    return (decoded_all, child_ssm, child_conv)


def solution(mesh):
    placed = (
        P(("replica", "branch"), None, "tensor"),
        P(("replica", "branch"), None, "tensor"),
        P(("replica", "branch")),
        P(("replica", "branch"), None, None, "tensor"),
        P(None, "tensor"),
        P("tensor"),
        P("tensor", None),
        P(None, "tensor"),
        P("tensor"),
        P(None, "tensor"),
        P("tensor"),
        P(("replica", "branch"), None, None),
        P(("replica", "branch")),
    )
    return jax.shard_map(
        on_device,
        mesh=mesh,
        in_specs=placed,
        out_specs=(
            P(("replica", "branch"), None, "tensor"),
            P(("replica", "branch"), None, "tensor"),
            P(("replica", "branch"), None, "tensor"),
        ),
        check_vma=False,
    )
```

profile of v0, /device:TPU:0, one launch (start us, length us, event | category | flops | bytes accessed | tf_op | source)
XLA Modules:
  0.0 101.4 jit_solution(8026085475768798327)
XLA Ops:
  7.2 0.7 compare_bitcast_fusion
  7.9 0.7 maximum_bitcast_fusion
  8.6 14.9 %all_gather.6 = f32[4,3,1024]{2,1,0:T(4,128)S(1)} all-gather(f32[1,3,1024]{2,1,0:T(4,128)S(1)} %convert_element_type.152), channel_id=1, replica_groups=mesh['replica'=2,'branch'=4,'tensor'=4] {'branch'}, dimensions={0}, use_global_device_ids=true | all-gather | bytes 61440 | tf_op jit(solution)/shard_map/all_gather | solution.py:10
  23.5 1.0 convolution_convert_fusion
  25.3 0.8 slice-done
  27.5 0.8 reduce
  28.9 4.9 %all-to-all-start.1 = ((bf16[4,2,1536]{2,1,0:T(2,128)(2,1)}), bf16[4,2,1536]{2,1,0:T(2,128)(2,1)S(1)}, u32[]{:S(2)}, u32[]{:S(2)}) async-start(bf16[4,2,1536]{2,1,0:T(2,128)(2,1)} %reshape.276), calls=%async_computation.1 | async-start | bytes 49152 | tf_op jit(solution)/shard_map/all_to_all | solution.py:95
  33.9 0.7 copy-done.10
  34.5 0.9 fusion.75
  35.4 0.9 fusion.73
  36.3 0.9 fusion.79
  37.2 0.9 fusion.77
  38.2 0.8 copy-done.6
  38.9 14.4 %all_gather.7 = f32[4,16,1024]{2,1,0:T(8,128)S(1)} all-gather(f32[1,16,1024]{2,1,0:T(8,128)S(1)} %copy-done.5), channel_id=1, replica_groups=mesh['replica'=2,'branch'=4,'tensor'=4] {'branch'}, dimensions={0}, use_global_device_ids=true | all-gather | bytes 327680 | tf_op jit(solution)/shard_map/all_gather | solution.py:9
  53.5 17.8 %all-reduce.3.cloned.1.call-done = (f32[16,288]{1,0:T(8,128)}, f32[16,288]{1,0:T(8,128)}, f32[16,288]{1,0:T(8,128)}, f32[16,288]{1,0:T(8,128)}) async-done(((f32[16,288]{1,0:T(8,128)}, f32[16,288]{1,0:T(8,128)}, f32[16,288]{1,0:T(8,128)}, f32[16,288]{1,0:T(8,128)}), (f32[16,288]{1,0:T(8,128)}, f32[16,288]{1,0:T(8,128)}, f32[16,288]{1,0:T(8,128)}, f32[16,288]{1,0:T(8,128)})) %all-reduce.3.cloned.1.call-update) | async-done | bytes 73744 | tf_op jit(solution)/shard_map/psum | solution.py:38
  71.3 0.8 fusion.94
  76.5 1.9 %multiply_reduce_fusion.2 = (f32[16,1024]{1,0:T(8,128)S(1)}, f32[16,1024]{1,0:T(8,128)S(1)}, f32[16,1024]{1,0:T(8,128)S(1)}, f32[16,1024]{1,0:T(8,128)S(1)}, f32[16,16,1024]{2,0,1:T(8,128)S(1)}) fusion(f32[16,16]{0,1:T(8,128)S(1)} %copy.71, f32[16,1024]{1,0:T(8,128)S(1)} %get-tuple-element.34, f32[16,1024]{1,0:T(8,128)S(1)} %get-tuple-element.53, ...), kind=kOutput, calls=%fused_computation.15 | convolution fusion | flops 18808896 | bytes 2170944 | tf_op jit(solution)/shard_map/rp,pne->rne/dot_general | solution.py:15
  79.6 0.8 fusion.1
  80.4 4.6 %all-to-all-start = ((f32[4,1,16,1024]{3,2,1,0:T(8,128)}), f32[4,1,16,1024]{3,2,1,0:T(8,128)S(1)}, u32[]{:S(2)}, u32[]{:S(2)}) async-start(f32[4,1,16,1024]{3,2,1,0:T(8,128)} %fusion.1), calls=%async_computation | async-start | bytes 524288 | tf_op jit(solution)/shard_map/all_to_all | solution.py:94
  85.0 0.7 copy-done.11
  86.5 0.7 copy.83
  87.3 0.8 copy.82
  88.1 4.9 %all-to-all-done = f32[4,1,16,1024]{3,2,1,0:T(8,128)S(1)} async-done(((f32[4,1,16,1024]{3,2,1,0:T(8,128)}), f32[4,1,16,1024]{3,2,1,0:T(8,128)S(1)}, u32[]{:S(2)}, u32[]{:S(2)}) %all-to-all-start) | async-done | bytes 262176 | tf_op jit(solution)/shard_map/all_to_all | solution.py:94
  93.0 1.6 %gather_fusion.1 = f32[16,16,1024]{2,1,0:T(8,128)} fusion(f32[4,16,1024]{2,1,0:T(8,128)S(1)} %bitcast.284, s32[1024]{0:T(1024)S(1)} %pad_clamp_fusion), kind=kCustom, calls=%fused_computation.1 | custom fusion | bytes 2097216 | tf_op jit(solution)/shard_map/gather | solution.py:99
  (75 shorter events, 9.5 us)
Async XLA Ops:
  7.2 26.7 %copy-start = (bf16[1024,288]{0,1:T(8,128)(2,1)S(1)}, bf16[1024,288]{0,1:T(8,128)(2,1)}, u32[]{:S(2)}) copy-start(bf16[1024,288]{0,1:T(8,128)(2,1)} %param.19) | copy-start | bytes 1769476
  7.2 1.4 %copy-start.15 = (bf16[1,3,1024]{2,1,0:T(4,128)(2,1)S(1)}, bf16[1,3,1024]{2,1,0:T(4,128)(2,1)}, u32[]{:S(2)}) copy-start(bf16[1,3,1024]{2,1,0:T(4,128)(2,1)} %param.14) | copy-start | bytes 18436
  7.2 17.3 %copy-start.4 = (bf16[16,4,2,1024]{3,2,1,0:T(2,128)(2,1)S(1)}, bf16[16,4,2,1024]{3,2,1,0:T(2,128)(2,1)}, u32[]{:S(2)}) copy-start(bf16[16,4,2,1024]{3,2,1,0:T(2,128)(2,1)} %param.16) | copy-start | bytes 786436
  24.5 0.6 copy-start.2
  25.3 0.8 slice-start
  27.5 6.4 %copy-start.3 = (bf16[16,3,1024]{2,0,1:T(8,128)(2,1)S(1)}, bf16[16,3,1024]{2,0,1:T(8,128)(2,1)}, u32[]{:S(2)}) copy-start(bf16[16,3,1024]{2,0,1:T(8,128)(2,1)} %copy-done.2) | copy-start | bytes 294916
  28.9 4.9 %copy-start.12 = (f32[4,1024]{1,0:T(4,128)S(1)}, f32[4,1024]{1,0:T(4,128)}, u32[]{:S(2)}) copy-start(f32[4,1024]{1,0:T(4,128)} %param.17) | copy-start | bytes 49156
  28.9 51.4 %all-to-all-start.1 = ((bf16[4,2,1536]{2,1,0:T(2,128)(2,1)}), bf16[4,2,1536]{2,1,0:T(2,128)(2,1)S(1)}, u32[]{:S(2)}, u32[]{:S(2)}) async-start(bf16[4,2,1536]{2,1,0:T(2,128)(2,1)} %reshape.276), calls=%async_computation.1 | async-start | bytes 49152 | tf_op jit(solution)/shard_map/all_to_all | solution.py:95
  33.8 37.5 %all-reduce.3.cloned.1.call-start = ((), (), s32[]{:S(2)}) async-start(), calls=%async_computation.2 | async-start | bytes 196608 | tf_op jit(solution)/shard_map/psum | solution.py:38
  33.8 0.7 copy-start.10
  37.2 0.9 copy-start.17
  38.1 0.8 copy-start.6
  38.1 0.9 copy-start.5
  38.1 34.3 %copy-start.1 = (bf16[256,1024]{1,0:T(8,128)(2,1)S(1)}, bf16[256,1024]{1,0:T(8,128)(2,1)}, u32[]{:S(2)}) copy-start(bf16[256,1024]{1,0:T(8,128)(2,1)} %param.20) | copy-start | bytes 1572868
  72.2 0.7 copy-start.8
  72.3 0.7 copy-start.9
  73.0 0.7 copy-start.7
  73.8 0.7 copy-start.13
  74.6 0.7 copy-start.14
  75.8 0.7 copy-start.16
  80.4 12.6 %all-to-all-start = ((f32[4,1,16,1024]{3,2,1,0:T(8,128)}), f32[4,1,16,1024]{3,2,1,0:T(8,128)S(1)}, u32[]{:S(2)}, u32[]{:S(2)}) async-start(f32[4,1,16,1024]{3,2,1,0:T(8,128)} %fusion.1), calls=%async_computation | async-start | bytes 524288 | tf_op jit(solution)/shard_map/all_to_all | solution.py:94
  84.9 0.7 copy-start.11
Sparse Core Ops, SparseCore 0:
  38.2 33.0 all-reduce.2
where the time goes:
time: 102 us; the launch traced here: 101 us
  blocking collectives  29.3 us (29%)
  waiting for transfers between devices  22.7 us (22%)
  local copies, waits for them, and re-layouts  15 us (15%)
  between operations  14.3 us (14%)
  starting transfers between devices  9.47 us (9%)
  matrix products  7.21 us (7%)
  other arithmetic  3.41 us (3%)
    psum x1, waiting for transfers between devices, decode_rows(): x_proj = lax.psum(partial_proj, 'tensor')  17.8 us
    all_gather x1, blocking collectives, select_prompts(): lax.all_gather(prompt_wide, 'branch', axis=0, tiled=True)  14.9 us
    all_gather x1, blocking collectives, select_prompts(): lax.all_gather(prompt_ssm, 'branch', axis=0, tiled=True)  14.4 us
    unnamed x43, local copies, waits for them, and re-layouts  8 us
    all_to_all x1, waiting for transfers between devices, on_device(): lax.all_to_all(out_ssm, 'branch', split_axis=0, concat_axis=0, tiled=True)  4.89 us
    all_to_all x1, starting transfers between devices, on_device(): lax.all_to_all(out_conv, 'branch', split_axis=0, concat_axis=0, tiled=True)  4.87 us
    all_to_all x1, starting transfers between devices, on_device(): lax.all_to_all(out_ssm, 'branch', split_axis=0, concat_axis=0, tiled=True)  4.6 us
    dot_general x4, matrix products, decode_rows(): jnp.dot(activated.astype(jnp.bfloat16), x_weight, preferred_element_type=...  3.55 us
  transfers between devices with their start and end apart: 3, of which 2 were waited for; matrix products, arithmetic and copies ran while one was open for 12% of the time, Pallas kernels for 0%

commit v1 on v0

v1 whole, which is shorter than its diff:
```python
import functools
import math

import jax
import jax.numpy as jnp
from jax import lax
from jax.experimental import pallas as pl
from jax.experimental.pallas import tpu as pltpu
from jax.sharding import PartitionSpec as P

F32 = jnp.float32
BF16 = jnp.bfloat16
LANES = 128
VMEM_LIMIT = 48 * 2**20
DIRECT_MOST = 4


def vmem():
    return pl.BlockSpec(memory_space=pltpu.VMEM)


def smem():
    return pl.BlockSpec(memory_space=pltpu.SMEM)


def call(kernel, outs, in_specs, out_specs, scratch=(), flops=0, nbytes=0, trans=0):
    return pl.pallas_call(
        kernel,
        out_shape=outs,
        in_specs=in_specs,
        out_specs=out_specs,
        scratch_shapes=list(scratch),
        compiler_params=pltpu.CompilerParams(vmem_limit_bytes=VMEM_LIMIT),
        cost_estimate=pl.CostEstimate(flops=flops, bytes_accessed=nbytes, transcendentals=trans),
    )


def shift_exchange(parts, axis):
    size = lax.axis_size(axis)
    got = [parts[0]]
    for shift in range(1, size):
        pairs = [(i, (i + shift) % size) for i in range(size)]
        got.append(lax.ppermute(parts[shift], axis, pairs))
    return got


def read_rows(refs, row):
    rows = [
        ref[i, row : row + 1, :].astype(F32) for ref in refs for i in range(ref.shape[0])
    ]
    return rows[0] if len(rows) == 1 else jnp.concatenate(rows, axis=0)


def pack_kernel(kernel_len, capacity, me_ref, rows_ref, prompt_ref, step_hbm, conv_ref, *rest):
    outs, (held, sems) = rest[:-2], rest[-2:]
    owners = rows_ref.shape[0]
    channels = conv_ref.shape[2]
    me = me_ref[0]
    copies, rows = [], []
    for shift in range(owners):
        target = lax.rem(me + shift, owners)
        for c in range(capacity):
            row = jnp.maximum(rows_ref[target, c], 0)
            slot = shift * capacity + c
            copy = pltpu.make_async_copy(step_hbm.at[row], held.at[slot], sems.at[slot])
            copy.start()
            copies.append(copy)
            rows.append(row)
    conv = conv_ref[0].astype(F32)
    for shift in range(owners):
        pieces = [conv]
        for c in range(capacity):
            slot = shift * capacity + c
            copies[slot].wait()
            pieces.append(held[slot, :, 0, :].astype(F32))
        for c in range(capacity):
            number = prompt_ref[rows[shift * capacity + c]].astype(F32)
            pieces.append(jnp.full((1, channels), number, F32))
        message = jnp.concatenate(pieces, axis=0).astype(BF16)
        ref = outs[shift] if len(outs) > 1 else outs[0]
        ref[shift if len(outs) == 1 else 0] = message


def own_onehot(prompt_ref, me, owners):
    rows = prompt_ref.shape[0]
    row_of = lax.broadcasted_iota(jnp.int32, (rows, owners), 0)
    column = lax.broadcasted_iota(jnp.int32, (rows, owners), 1)
    wanted = jnp.zeros((rows, owners), jnp.int32)
    for b in range(rows):
        wanted = jnp.where(row_of == b, lax.rem(me - prompt_ref[b] + owners, owners), wanted)
    return (wanted == column).astype(F32)


def slot_onehot(numbers, me, owners):
    column = lax.broadcasted_iota(jnp.int32, (numbers.shape[0], owners), 1)
    held_by = lax.rem(me - column + owners, owners)
    return (numbers[:, :owners].astype(jnp.int32) == held_by).astype(F32)


def silu(v):
    return v / (1.0 + jnp.exp(-v))


def project_kernel(
    n_msgs, steps, me_ref, prompt_ref, x_ref, cw_ref, cb_ref, xw_ref, *rest
):
    msgs, (act_ref, part_ref) = rest[:n_msgs], rest[n_msgs:]
    owners = sum(m.shape[0] for m in msgs)
    taps = cw_ref.shape[0]
    me = me_ref[0]
    rb = x_ref.shape[1]
    windows = [read_rows(msgs, k) for k in range(taps - 1)]
    slot_x = [read_rows(msgs, taps - 1 + t) for t in range(steps)]
    numbers = read_rows(msgs, taps - 1 + steps)
    own_pick = own_onehot(prompt_ref, me, owners).astype(BF16)
    slot_pick = slot_onehot(numbers, me, owners).astype(BF16)

    def pick(onehot, table):
        return jnp.dot(onehot, table.astype(BF16), preferred_element_type=F32)

    row = 0
    for onehot, xs in (
        (own_pick, [x_ref[t].astype(F32) for t in range(steps)]),
        (slot_pick, slot_x),
    ):
        count = onehot.shape[0]
        line = [pick(onehot, w) for w in windows] + xs
        for t in range(steps):
            conv = cw_ref[taps - 1 : taps, :] * line[t + taps - 1] + cb_ref[...]
            for k in range(taps - 1):
                conv = conv + cw_ref[k : k + 1, :] * line[t + k]
            act_ref[row : row + count, :] = silu(conv)
            row += count
    part_ref[...] = jnp.dot(
        act_ref[...].astype(BF16), xw_ref[...], preferred_element_type=F32
    )


def windows_kernel(n_msgs, taps, steps, me_ref, child_ref, *rest):
    msgs, (out_ref, held) = rest[:n_msgs], rest[n_msgs:]
    owners = sum(m.shape[0] for m in msgs)
    me = me_ref[0]
    first = taps - 1 + steps - (taps - 1)
    slot = 0
    for ref in msgs:
        for i in range(ref.shape[0]):
            held[slot] = ref[i].astype(F32)[first : first + taps - 1, :]
            slot += 1
    for j in range(out_ref.shape[0]):
        at = lax.rem(me - child_ref[j] + owners, owners)
        out_ref[j] = held[at].astype(BF16)


def decode_kernel(
    n_parts,
    n_msgs,
    n_ssm,
    steps,
    taps,
    me_ref,
    prompt_ref,
    child_ref,
    act_ref,
    z_ref,
    dtw_ref,
    dtb_ref,
    alog_ref,
    skip_ref,
    *rest,
):
    parts, rest = rest[:n_parts], rest[n_parts:]
    msgs, rest = rest[:n_msgs], rest[n_msgs:]
    ssms, rest = rest[:n_ssm], rest[n_ssm:]
    dec_ref, child_ssm, delta_s, gain_s, rate_s, b_s, c_s, slots_s, sems = rest
    owners = sum(m.shape[0] for m in msgs)
    me = me_ref[0]
    rb = dec_ref.shape[0]
    rank = dtw_ref.shape[0]
    n_state, channels = alog_ref.shape
    own_rows = steps * rb
    chunks = channels // LANES

    proj = parts[0][...]
    for ref in parts[1:]:
        proj = proj + ref[...]
    delta_in = proj[:, :rank].astype(BF16)
    delta = jnp.dot(delta_in, dtw_ref[...], preferred_element_type=F32) + dtb_ref[...]
    delta = jnp.maximum(delta, 0.0) + jnp.log1p(jnp.exp(-jnp.abs(delta)))
    delta_s[...] = delta
    gain_s[...] = delta * act_ref[...]
    rate_s[...] = jnp.exp(alog_ref[...]) * (-math.log2(math.e))
    rows = proj.shape[0]
    for n in range(n_state):
        b_s[n] = jnp.broadcast_to(proj[:, rank + n : rank + n + 1], (rows, LANES))
        c_s[n] = jnp.broadcast_to(
            proj[:own_rows, rank + n_state + n : rank + n_state + n + 1], (own_rows, LANES)
        )
    own_pick = own_onehot(prompt_ref, me, owners)
    numbers = read_rows(msgs, taps - 1 + steps)
    slot_pick = slot_onehot(numbers, me, owners)
    n_slots = slot_pick.shape[0]

    def start(pick, n, columns):
        total, k = None, 0
        for ref in ssms:
            for i in range(ref.shape[0]):
                row = ref[i, n : n + 1, columns]
                term = pick[:, k : k + 1] * row
                total = term if total is None else total + term
                k += 1
        return total

    def slot_chunk(chunk, carry):
        columns = pl.ds(pl.multiple_of(chunk * LANES, LANES), LANES)
        for n in range(n_state):
            rate = rate_s[n : n + 1, columns]
            state = start(slot_pick, n, columns)
            for t in range(steps):
                at = pl.ds(own_rows + t * n_slots, n_slots)
                state = (
                    jnp.exp2(delta_s[at, columns] * rate) * state
                    + gain_s[at, columns] * b_s[n, at, :]
                )
            slots_s[:, n, columns] = state
        return carry

    lax.fori_loop(0, chunks, slot_chunk, 0)
    copies = []
    for j in range(rb):
        at = lax.rem(me - child_ref[j] + owners, owners)
        copy = pltpu.make_async_copy(slots_s.at[at], child_ssm.at[j], sems.at[j])
        copy.start()
        copies.append(copy)

    def own_chunk(chunk, carry):
        columns = pl.ds(pl.multiple_of(chunk * LANES, LANES), LANES)
        sums = [None] * steps
        for n in range(n_state):
            rate = rate_s[n : n + 1, columns]
            state = start(own_pick, n, columns)
            for t in range(steps):
                at = pl.ds(t * rb, rb)
                state = (
                    jnp.exp2(delta_s[at, columns] * rate) * state
                    + gain_s[at, columns] * b_s[n, at, :]
                )
                term = c_s[n, at, :] * state
                sums[t] = term if sums[t] is None else sums[t] + term
        for t in range(steps):
            at = pl.ds(t * rb, rb)
            out = sums[t] + skip_ref[:, columns] * act_ref[at, columns]
            out = out * silu(z_ref[t, :, columns].astype(F32))
            dec_ref[:, t, columns] = out.astype(BF16)
        return carry

    lax.fori_loop(0, chunks, own_chunk, 0)
    for copy in copies:
        copy.wait()


def on_device(
    prompt_ssm,
    prompt_conv,
    prompt_of,
    step_in,
    conv_weight,
    conv_bias,
    x_weight,
    dt_weight,
    dt_bias,
    a_log,
    skip,
    send_rows,
    child_slot,
):
    owners = lax.axis_size("branch")
    capacity = send_rows.shape[2]
    assert prompt_ssm.shape[0] == 1 and capacity == 1
    rb, steps, _, channels = step_in.shape
    taps = conv_weight.shape[0]
    width = x_weight.shape[1]
    n_state = a_log.shape[0]
    n_slots = owners * capacity
    rows = steps * (rb + n_slots)
    depth = taps - 1 + capacity * (steps + 1)
    direct = owners <= DIRECT_MOST
    me = lax.axis_index("branch").astype(jnp.int32).reshape(1)

    if direct:
        msg_shapes = [jax.ShapeDtypeStruct((1, depth, channels), BF16)] * owners
    else:
        msg_shapes = [jax.ShapeDtypeStruct((owners, depth, channels), BF16)]
    msgs = call(
        functools.partial(pack_kernel, taps, capacity),
        msg_shapes,
        [smem(), smem(), smem(), pl.BlockSpec(memory_space=pl.ANY), vmem()],
        [vmem()] * len(msg_shapes),
        [
            pltpu.VMEM((n_slots,) + step_in.shape[1:], BF16),
            pltpu.SemaphoreType.DMA((n_slots,)),
        ],
        nbytes=n_slots * steps * channels * 4,
    )(me, send_rows[0], prompt_of, step_in, prompt_conv)
    x_own = jnp.transpose(step_in[:, :, 0], (1, 0, 2))
    z_own = jnp.transpose(step_in[:, :, 1], (1, 0, 2))

    if direct:
        msgs = shift_exchange(msgs, "branch")
        (prompt_later, msgs) = lax.optimization_barrier((prompt_ssm, msgs))
        ssms = shift_exchange([prompt_later] * owners, "branch")
    else:
        by_owner = jnp.roll(msgs[0], me[0], axis=0)
        came = lax.all_to_all(by_owner, "branch", split_axis=0, concat_axis=0, tiled=True)
        msgs = [jnp.roll(came[::-1], me[0] + 1, axis=0)]
        every = lax.all_gather(prompt_ssm, "branch", axis=0, tiled=True)
        ssms = [jnp.roll(every[::-1], me[0] + 1, axis=0)]

    n_msgs = len(msgs)
    act, part = call(
        functools.partial(project_kernel, n_msgs, steps),
        [
            jax.ShapeDtypeStruct((rows, channels), F32),
            jax.ShapeDtypeStruct((rows, width), F32),
        ],
        [smem(), smem()] + [vmem()] * (4 + n_msgs),
        [vmem()] * 2,
        flops=2 * rows * channels * width,
        nbytes=channels * width * 2 + rows * (channels + width) * 4,
        trans=rows * channels,
    )(me, prompt_of, x_own, conv_weight, conv_bias[None], x_weight, *msgs)
    parts = shift_exchange([part] * lax.axis_size("tensor"), "tensor")

    child_conv = call(
        functools.partial(windows_kernel, n_msgs, taps, steps),
        jax.ShapeDtypeStruct((rb, taps - 1, channels), BF16),
        [smem(), smem()] + [vmem()] * n_msgs,
        vmem(),
        [pltpu.VMEM((n_slots, taps - 1, channels), F32)],
        nbytes=rb * taps * channels * 2,
    )(me, child_slot, *msgs)

    decoded, child_ssm = call(
        functools.partial(decode_kernel, len(parts), n_msgs, len(ssms), steps, taps),
        [
            jax.ShapeDtypeStruct((rb, steps, channels), BF16),
            jax.ShapeDtypeStruct((rb, n_state, channels), F32),
        ],
        [smem()] * 3 + [vmem()] * (6 + len(parts) + n_msgs + len(ssms)),
        [vmem(), pl.BlockSpec(memory_space=pl.ANY)],
        [
            pltpu.VMEM((rows, channels), F32),
            pltpu.VMEM((rows, channels), F32),
            pltpu.VMEM((n_state, channels), F32),
            pltpu.VMEM((n_state, rows, LANES), F32),
            pltpu.VMEM((n_state, steps * rb, LANES), F32),
            pltpu.VMEM((n_slots, n_state, channels), F32),
            pltpu.SemaphoreType.DMA((rb,)),
        ],
        flops=8 * rows * n_state * channels,
        nbytes=(rb + owners) * n_state * channels * 4,
        trans=rows * n_state * channels,
    )(
        me,
        prompt_of,
        child_slot,
        act,
        z_own,
        dt_weight,
        dt_bias[None],
        a_log,
        skip[None],
        *parts,
        *msgs,
        *ssms,
    )
    return (decoded, child_ssm, child_conv)


def solution(mesh):
    placed = (
        P(("replica", "branch"), None, "tensor"),
        P(("replica", "branch"), None, "tensor"),
        P(("replica", "branch")),
        P(("replica", "branch"), None, None, "tensor"),
        P(None, "tensor"),
        P("tensor"),
        P("tensor", None),
        P(None, "tensor"),
        P("tensor"),
        P(None, "tensor"),
        P("tensor"),
        P(("replica", "branch"), None, None),
        P(("replica", "branch")),
    )
    return jax.shard_map(
        on_device,
        mesh=mesh,
        in_specs=placed,
        out_specs=(
            P(("replica", "branch"), None, "tensor"),
            P(("replica", "branch"), None, "tensor"),
            P(("replica", "branch"), None, "tensor"),
        ),
        check_vma=False,
    )
```

time: 102 us -> 32.4 us (0.32)
  blocking collectives: 29.3 us -> 0 us
  waiting for transfers between devices: 22.7 us -> 4.63 us
  between operations: 14.3 us -> 0.77 us
  local copies, waits for them, and re-layouts: 15 us -> 5.39 us
  Pallas kernels: 0 us -> 7.8 us
  matrix products: 7.21 us -> 0 us
  starting transfers between devices: 9.47 us -> 13.5 us
  other arithmetic: 3.41 us -> 0 us
    all_gather x2 -> x0, blocking collectives: 29.3 us -> none  [the longest x1 14.9 us: select_prompts(): lax.all_gather(prompt_wide, 'branch', axis=0, tiled=True)]
    psum x1 -> x0, waiting for transfers between devices: 17.8 us -> none  [decode_rows(): x_proj = lax.psum(partial_proj, 'tensor')]
    ppermute x0 -> x9, starting transfers between devices: none -> 13.5 us  [shift_exchange(): got.append(lax.ppermute(parts[shift], axis, pairs))]
    all_to_all x2 -> x0, starting transfers between devices: 9.47 us -> none  [the longest x1 4.87 us: on_device(): lax.all_to_all(out_conv, 'branch', split_axis=0, concat_axis=0, tiled=True)]
    pallas_call x0 -> x4, Pallas kernels: none -> 7.8 us  [the longest x1 5.29 us: on_device(): call(functools.partial(decode_kernel, len(parts), n_msgs, len(ssms), step...]
    dot_general x10 -> x0, matrix products: 7.21 us -> none  [the longest x4 3.55 us: decode_rows(): jnp.dot(activated.astype(jnp.bfloat16), x_weight, preferred_element_type=...]
    all_to_all x2 -> x0, waiting for transfers between devices: 4.89 us -> none  [the longest x1 4.89 us: on_device(): lax.all_to_all(out_ssm, 'branch', split_axis=0, concat_axis=0, tiled=True)]
    ppermute x0 -> x9, waiting for transfers between devices: none -> 4.63 us  [shift_exchange(): got.append(lax.ppermute(parts[shift], axis, pairs))]
  transfers between devices with their start and end apart: 3 -> 9, of which waited for: 2 -> 4; matrix products, arithmetic and copies ran while one was open for 12% -> 5% of each run, Pallas kernels for 0% -> 5%
where the time goes in v1:
time: 32.4 us; the launch traced here: 32 us
  starting transfers between devices  13.5 us (42%)
  Pallas kernels  7.8 us (24%)
  local copies, waits for them, and re-layouts  5.39 us (17%)
  waiting for transfers between devices  4.63 us (14%)
  between operations  0.77 us (2%)
    ppermute x9, starting transfers between devices, shift_exchange(): got.append(lax.ppermute(parts[shift], axis, pairs))  13.5 us
    pallas_call x1, Pallas kernels, on_device(): call(functools.partial(decode_kernel, len(parts), n_msgs, len(ssms), step...  5.29 us
    unnamed x30, local copies, waits for them, and re-layouts  4.93 us
    ppermute x9, waiting for transfers between devices, shift_exchange(): got.append(lax.ppermute(parts[shift], axis, pairs))  4.63 us
    pallas_call x1, Pallas kernels, on_device(): call(functools.partial(project_kernel, n_msgs, steps), [jax.ShapeDtypeStr...  1.13 us
    pallas_call x1, Pallas kernels, on_device(): call(functools.partial(pack_kernel, taps, capacity), msg_shapes, [smem(),...  0.78 us
  transfers between devices with their start and end apart: 9, of which 4 were waited for; matrix products, arithmetic and copies ran while one was open for 5% of the time, Pallas kernels for 5%

profile of v1, /device:TPU:0, one launch (start us, length us, event | category | flops | bytes accessed | tf_op | source)
XLA Modules:
  0.0 32.0 jit_solution(11093375357249107688)
XLA Ops:
  0.7 0.6 %copy-done.12 = s32[1,4,1]{1,2,0:T(1,128)S(1)} copy-done((s32[1,4,1]{1,2,0:T(1,128)S(1)}, s32[1,4,1]{1,2,0:T(1,128)}, u32[]{:S(2)}) %copy-start.12) | copy-done | bytes 40
  1.4 0.7 %copy-done.4 = s32[16]{0:T(128)S(1)} copy-done((s32[16]{0:T(128)S(1)}, s32[16]{0:T(128)}, u32[]{:S(2)}) %copy-start.4) | copy-done | bytes 88
  2.1 0.9 %copy-done = bf16[16,4,2,1024]{3,2,1,0:T(2,128)(2,1)S(1)} copy-done((bf16[16,4,2,1024]{3,2,1,0:T(2,128)(2,1)S(1)}, bf16[16,4,2,1024]{3,2,1,0:T(2,128)(2,1)}, u32[]{:S(2)}) %copy-start) | copy-done | bytes 262168
  3.0 0.8 %shard_map.148 = (bf16[1,8,1024]{2,1,0:T(8,128)(2,1)S(1)}, bf16[1,8,1024]{2,1,0:T(8,128)(2,1)S(1)}, bf16[1,8,1024]{2,1,0:T(8,128)(2,1)S(1)}, bf16[1,8,1024]{2,1,0:T(8,128)(2,1)S(1)}) custom-call(s32[1]{0:T(128)} %bitcast.me_ref, s32[4,1]{1,0:T(4,128)S(1)} %copy.17.rows_ref, s32[16]{0:T(128)S(1)} %copy-done.4, bf16[16,4,2,1024]{3,2,1,0:T(2,128)(2,1)S(1)} %copy-done, ...), custom_call_target="tpu_custom_call" | custom-call | bytes 65536 | tf_op jit(solution)/shard_map/pallas_call | solution.py:293
  3.8 3.1 %collective-permute-start = (bf16[1,8,1024]{2,1,0:T(8,128)(2,1)S(1)}, bf16[1,8,1024]{2,1,0:T(8,128)(2,1)S(1)}, u32[]{:S(2)}, u32[]{:S(2)}) collective-permute-start(bf16[1,8,1024]{2,1,0:T(8,128)(2,1)S(1)} %get-tuple-element.17), channel_id=1, source_target_pairs={{0,4},{4,8},{8,12},{12,0},{1,5},{5,9},{9,13},{13,1},{2,6},{6,10},{... | collective-permute-start | bytes 49160 | tf_op jit(solution)/shard_map/ppermute | solution.py:43
  6.9 2.6 %collective-permute-start.1 = (bf16[1,8,1024]{2,1,0:T(8,128)(2,1)S(1)}, bf16[1,8,1024]{2,1,0:T(8,128)(2,1)S(1)}, u32[]{:S(2)}, u32[]{:S(2)}) collective-permute-start(bf16[1,8,1024]{2,1,0:T(8,128)(2,1)S(1)} %get-tuple-element.18), channel_id=1, source_target_pairs={{0,8},{4,12},{8,0},{12,4},{1,9},{5,13},{9,1},{13,5},{2,10},{6,14},... | collective-permute-start | bytes 49160 | tf_op jit(solution)/shard_map/ppermute | solution.py:43
  9.5 1.3 %collective-permute-start.2 = (bf16[1,8,1024]{2,1,0:T(8,128)(2,1)S(1)}, bf16[1,8,1024]{2,1,0:T(8,128)(2,1)S(1)}, u32[]{:S(2)}, u32[]{:S(2)}) collective-permute-start(bf16[1,8,1024]{2,1,0:T(8,128)(2,1)S(1)} %get-tuple-element.19), channel_id=1, source_target_pairs={{0,12},{4,0},{8,4},{12,8},{1,13},{5,1},{9,5},{13,9},{2,14},{6,2},{... | collective-permute-start | bytes 49160 | tf_op jit(solution)/shard_map/ppermute | solution.py:43
  10.8 0.8 %collective-permute-done.1.rest_2_.rest_6_ = bf16[1,8,1024]{2,1,0:T(8,128)(2,1)S(1)} collective-permute-done((bf16[1,8,1024]{2,1,0:T(8,128)(2,1)S(1)}, bf16[1,8,1024]{2,1,0:T(8,128)(2,1)S(1)}, u32[]{:S(2)}, u32[]{:S(2)}) %collective-permute-start.1) | collective-permute-done | bytes 16416 | tf_op jit(solution)/shard_map/ppermute | solution.py:43
  11.6 1.6 %collective-permute-done.2.rest_3_.rest_7_ = bf16[1,8,1024]{2,1,0:T(8,128)(2,1)S(1)} collective-permute-done((bf16[1,8,1024]{2,1,0:T(8,128)(2,1)S(1)}, bf16[1,8,1024]{2,1,0:T(8,128)(2,1)S(1)}, u32[]{:S(2)}, u32[]{:S(2)}) %collective-permute-start.2) | collective-permute-done | bytes 16416 | tf_op jit(solution)/shard_map/ppermute | solution.py:43
  13.3 0.4 %fusion = (bf16[16,4,1,1024]{3,2,1,0:T(2,128)(2,1)S(1)}, bf16[16,4,1,1024]{3,2,1,0:T(2,128)(2,1)S(1)}) fusion(bf16[16,4,2,1024]{3,2,1,0:T(2,128)(2,1)S(1)} %copy-done), kind=kLoop, calls=%fused_computation.2 | loop fusion | bytes 524288 | tf_op jit(solution)/shard_map/slice | solution.py:305
  13.6 0.1 copy.26
  13.8 0.5 %copy-done.11 = bf16[1024,288]{0,1:T(8,128)(2,1)S(1)} copy-done((bf16[1024,288]{0,1:T(8,128)(2,1)S(1)}, bf16[1024,288]{0,1:T(8,128)(2,1)}, u32[]{:S(2)}) %copy-start.11) | copy-done | bytes 589848
  14.3 0.4 %copy.18.xw_ref = bf16[1024,288]{1,0:T(8,128)(2,1)S(1)} copy(bf16[1024,288]{0,1:T(8,128)(2,1)S(1)} %copy-done.11) | data formatting | bytes 1179648 | tf_op args[6]
  14.6 0.4 %copy-done.1 = f32[4,1024]{1,0:T(4,128)S(1)} copy-done((f32[4,1024]{1,0:T(4,128)S(1)}, f32[4,1024]{1,0:T(4,128)}, u32[]{:S(2)}) %copy-start.1) | copy-done | bytes 16408
  15.0 1.1 %shard_map.149 = (f32[80,1024]{1,0:T(8,128)S(1)}, f32[80,288]{1,0:T(8,128)S(1)}) custom-call(s32[1]{0:T(128)} %bitcast.me_ref, s32[16]{0:T(128)S(1)} %copy-done.4, bf16[4,16,1024]{2,1,0:T(8,128)(2,1)S(1)} %bitcast.15, f32[4,1024]{1,0:T(4,128)S(1)} %copy-done.1, f32[1,1024]{1,0:T(1,128)S(1)} %bitcast.17, bf16[1024,288]{1,0:T(8,128)(2,1)S(1)} %copy.18.xw_ref, ...), custom_call_target="tpu_custom_call" | custom-call | flops 47185920 | bytes 1009664 | tf_op jit(solution)/shard_map/pallas_call | solution.py:319
  16.2 1.6 %collective-permute-start.4 = (f32[80,288]{1,0:T(8,128)S(1)}, f32[80,288]{1,0:T(8,128)S(1)}, u32[]{:S(2)}, u32[]{:S(2)}) collective-permute-start(f32[80,288]{1,0:T(8,128)S(1)} %get-tuple-element.25.rest_0_), channel_id=1, source_target_pairs={{0,2},{1,3},{2,0},{3,1},{4,6},{5,7},{6,4},{7,5},{8,10},{9,11},{10,... | collective-permute-start | bytes 276488 | tf_op jit(solution)/shard_map/ppermute | solution.py:43
  17.7 1.4 %collective-permute-start.5 = (f32[80,288]{1,0:T(8,128)S(1)}, f32[80,288]{1,0:T(8,128)S(1)}, u32[]{:S(2)}, u32[]{:S(2)}) collective-permute-start(f32[80,288]{1,0:T(8,128)S(1)} %get-tuple-element.25.rest_0_), channel_id=1, source_target_pairs={{0,3},{1,0},{2,1},{3,2},{4,7},{5,4},{6,5},{7,6},{8,11},{9,8},{10,9... | collective-permute-start | bytes 276488 | tf_op jit(solution)/shard_map/ppermute | solution.py:43
  19.1 3.3 %collective-permute-start.7 = (f32[1,16,1024]{2,1,0:T(8,128)S(1)}, f32[1,16,1024]{2,1,0:T(8,128)S(1)}, u32[]{:S(2)}, u32[]{:S(2)}) collective-permute-start(f32[1,16,1024]{2,1,0:T(8,128)S(1)} %copy-done.8), channel_id=1, source_target_pairs={{0,8},{4,12},{8,0},{12,4},{1,9},{5,13},{9,1},{13,5},{2,10},{6,14},... | collective-permute-start | bytes 196616 | tf_op jit(solution)/shard_map/ppermute | solution.py:43
  22.6 0.5 %copy-done.5 = s32[16]{0:T(128)S(1)} copy-done((s32[16]{0:T(128)S(1)}, s32[16]{0:T(128)}, u32[]{:S(2)}) %copy-start.5) | copy-done | bytes 88
  23.1 0.6 %shard_map.151 = bf16[16,3,1024]{2,1,0:T(4,128)(2,1)S(1)} custom-call(s32[1]{0:T(128)} %bitcast.me_ref, s32[16]{0:T(128)S(1)} %copy-done.5, bf16[1,8,1024]{2,1,0:T(8,128)(2,1)S(1)} %get-tuple-element.20.rest_0_.rest_4_, bf16[1,8,1024]{2,1,0:T(8,128)(2,1)S(1)} %collective-permute-done.rest_1_.rest_5_, ...), custom_call_target="tpu_custom_call" | custom-call | bytes 131072 | tf_op jit(solution)/shard_map/pallas_call | solution.py:333
  23.8 0.7 %copy.20 = bf16[16,3,1024]{2,0,1:T(8,128)(2,1)} copy(bf16[16,3,1024]{2,1,0:T(4,128)(2,1)S(1)} %shard_map.151) | data formatting | bytes 196608
  24.5 1.5 %collective-permute-done.7.rest_10_ = f32[1,16,1024]{2,1,0:T(8,128)S(1)} collective-permute-done((f32[1,16,1024]{2,1,0:T(8,128)S(1)}, f32[1,16,1024]{2,1,0:T(8,128)S(1)}, u32[]{:S(2)}, u32[]{:S(2)}) %collective-permute-start.7) | collective-permute-done | bytes 65568 | tf_op jit(solution)/shard_map/ppermute | solution.py:43
  26.0 0.7 %collective-permute-done.8.rest_11_ = f32[1,16,1024]{2,1,0:T(8,128)S(1)} collective-permute-done((f32[1,16,1024]{2,1,0:T(8,128)S(1)}, f32[1,16,1024]{2,1,0:T(8,128)S(1)}, u32[]{:S(2)}, u32[]{:S(2)}) %collective-permute-start.8) | collective-permute-done | bytes 65568 | tf_op jit(solution)/shard_map/ppermute | solution.py:43
  26.7 5.3 %shard_map.150 = (bf16[16,4,1024]{2,1,0:T(4,128)(2,1)}, f32[16,16,1024]{2,1,0:T(8,128)}) custom-call(s32[1]{0:T(128)} %bitcast.me_ref, s32[16]{0:T(128)S(1)} %copy-done.4, s32[16]{0:T(128)S(1)} %copy-done.5, f32[80,1024]{1,0:T(8,128)S(1)} %get-tuple-element.24.act_ref, bf16[4,16,1024]{2,1,0:T(8,128)(2,1)S(1)} %bitcast.16, bf16[256,1024]{1,0:T(8,128)(2,1)S(1)} %copy-done.6, ...), custom_call_target="tpu_custom_call" | custom-call | flops 10485760 | bytes 1310720 | tf_op jit(solution)/shard_map/pallas_call | solution.py:342
  (30 shorter events, 0.5 us)
Async XLA Ops:
  0.6 0.8 %copy-start.2 = (bf16[1,3,1024]{2,1,0:T(4,128)(2,1)S(1)}, bf16[1,3,1024]{2,1,0:T(4,128)(2,1)}, u32[]{:S(2)}) copy-start(bf16[1,3,1024]{2,1,0:T(4,128)(2,1)} %conv_ref.1) | copy-start | bytes 18436
  0.6 0.7 %copy-start.12 = (s32[1,4,1]{1,2,0:T(1,128)S(1)}, s32[1,4,1]{1,2,0:T(1,128)}, u32[]{:S(2)}) copy-start(s32[1,4,1]{1,2,0:T(1,128)} %param.24) | copy-start | bytes 52
  1.4 0.7 %copy-start.4 = (s32[16]{0:T(128)S(1)}, s32[16]{0:T(128)}, u32[]{:S(2)}) copy-start(s32[16]{0:T(128)} %prompt_ref.5) | copy-start | bytes 196
  2.1 0.9 %copy-start = (bf16[16,4,2,1024]{3,2,1,0:T(2,128)(2,1)S(1)}, bf16[16,4,2,1024]{3,2,1,0:T(2,128)(2,1)}, u32[]{:S(2)}) copy-start(bf16[16,4,2,1024]{3,2,1,0:T(2,128)(2,1)} %step_hbm.1) | copy-start | bytes 786436
  3.0 10.2 %copy-start.8 = (f32[1,16,1024]{2,1,0:T(8,128)S(1)}, f32[1,16,1024]{2,1,0:T(8,128)}, u32[]{:S(2)}) copy-start(f32[1,16,1024]{2,1,0:T(8,128)} %rest_8_) | copy-start | bytes 196612
  3.8 7.0 %collective-permute-start = (bf16[1,8,1024]{2,1,0:T(8,128)(2,1)S(1)}, bf16[1,8,1024]{2,1,0:T(8,128)(2,1)S(1)}, u32[]{:S(2)}, u32[]{:S(2)}) collective-permute-start(bf16[1,8,1024]{2,1,0:T(8,128)(2,1)S(1)} %get-tuple-element.17), channel_id=1, source_target_pairs={{0,4},{4,8},{8,12},{12,0},{1,5},{5,9},{9,13},{13,1},{2,6},{6,10},{... | collective-permute-start | bytes 49160 | tf_op jit(solution)/shard_map/ppermute | solution.py:43
  6.9 4.7 %collective-permute-start.1 = (bf16[1,8,1024]{2,1,0:T(8,128)(2,1)S(1)}, bf16[1,8,1024]{2,1,0:T(8,128)(2,1)S(1)}, u32[]{:S(2)}, u32[]{:S(2)}) collective-permute-start(bf16[1,8,1024]{2,1,0:T(8,128)(2,1)S(1)} %get-tuple-element.18), channel_id=1, source_target_pairs={{0,8},{4,12},{8,0},{12,4},{1,9},{5,13},{9,1},{13,5},{2,10},{6,14},... | collective-permute-start | bytes 49160 | tf_op jit(solution)/shard_map/ppermute | solution.py:43
  9.5 3.7 %collective-permute-start.2 = (bf16[1,8,1024]{2,1,0:T(8,128)(2,1)S(1)}, bf16[1,8,1024]{2,1,0:T(8,128)(2,1)S(1)}, u32[]{:S(2)}, u32[]{:S(2)}) collective-permute-start(bf16[1,8,1024]{2,1,0:T(8,128)(2,1)S(1)} %get-tuple-element.19), channel_id=1, source_target_pairs={{0,12},{4,0},{8,4},{12,8},{1,13},{5,1},{9,5},{13,9},{2,14},{6,2},{... | collective-permute-start | bytes 49160 | tf_op jit(solution)/shard_map/ppermute | solution.py:43
  13.2 1.1 %copy-start.11 = (bf16[1024,288]{0,1:T(8,128)(2,1)S(1)}, bf16[1024,288]{0,1:T(8,128)(2,1)}, u32[]{:S(2)}) copy-start(bf16[1024,288]{0,1:T(8,128)(2,1)} %param.19) | copy-start | bytes 1769476
  13.2 9.2 %collective-permute-start.6 = (f32[1,16,1024]{2,1,0:T(8,128)S(1)}, f32[1,16,1024]{2,1,0:T(8,128)S(1)}, u32[]{:S(2)}, u32[]{:S(2)}) collective-permute-start(f32[1,16,1024]{2,1,0:T(8,128)S(1)} %copy-done.8), channel_id=1, source_target_pairs={{0,4},{4,8},{8,12},{12,0},{1,5},{5,9},{9,13},{13,1},{2,6},{6,10},{... | collective-permute-start | bytes 196616 | tf_op jit(solution)/shard_map/ppermute | solution.py:43
  14.3 0.7 %copy-start.1 = (f32[4,1024]{1,0:T(4,128)S(1)}, f32[4,1024]{1,0:T(4,128)}, u32[]{:S(2)}) copy-start(f32[4,1024]{1,0:T(4,128)} %cw_ref.1) | copy-start | bytes 49156
  14.3 0.7 %copy-start.3 = (f32[1024]{0:T(1024)S(1)}, f32[1024]{0:T(1024)}, u32[]{:S(2)}) copy-start(f32[1024]{0:T(1024)} %param.18) | copy-start | bytes 12292
  15.0 11.7 %copy-start.6 = (bf16[256,1024]{1,0:T(8,128)(2,1)S(1)}, bf16[256,1024]{1,0:T(8,128)(2,1)}, u32[]{:S(2)}) copy-start(bf16[256,1024]{1,0:T(8,128)(2,1)} %dtw_ref.1) | copy-start | bytes 1572868
  16.1 10.6 %collective-permute-start.3 = (f32[80,288]{1,0:T(8,128)S(1)}, f32[80,288]{1,0:T(8,128)S(1)}, u32[]{:S(2)}, u32[]{:S(2)}) collective-permute-start(f32[80,288]{1,0:T(8,128)S(1)} %get-tuple-element.25.rest_0_), channel_id=1, source_target_pairs={{0,1},{1,2},{2,3},{3,0},{4,5},{5,6},{6,7},{7,4},{8,9},{9,10},{10,1... | collective-permute-start | bytes 276488 | tf_op jit(solution)/shard_map/ppermute | solution.py:43
  16.2 10.5 %collective-permute-start.4 = (f32[80,288]{1,0:T(8,128)S(1)}, f32[80,288]{1,0:T(8,128)S(1)}, u32[]{:S(2)}, u32[]{:S(2)}) collective-permute-start(f32[80,288]{1,0:T(8,128)S(1)} %get-tuple-element.25.rest_0_), channel_id=1, source_target_pairs={{0,2},{1,3},{2,0},{3,1},{4,6},{5,7},{6,4},{7,5},{8,10},{9,11},{10,... | collective-permute-start | bytes 276488 | tf_op jit(solution)/shard_map/ppermute | solution.py:43
  17.7 9.0 %collective-permute-start.5 = (f32[80,288]{1,0:T(8,128)S(1)}, f32[80,288]{1,0:T(8,128)S(1)}, u32[]{:S(2)}, u32[]{:S(2)}) collective-permute-start(f32[80,288]{1,0:T(8,128)S(1)} %get-tuple-element.25.rest_0_), channel_id=1, source_target_pairs={{0,3},{1,0},{2,1},{3,2},{4,7},{5,4},{6,5},{7,6},{8,11},{9,8},{10,9... | collective-permute-start | bytes 276488 | tf_op jit(solution)/shard_map/ppermute | solution.py:43
  19.1 6.8 %collective-permute-start.7 = (f32[1,16,1024]{2,1,0:T(8,128)S(1)}, f32[1,16,1024]{2,1,0:T(8,128)S(1)}, u32[]{:S(2)}, u32[]{:S(2)}) collective-permute-start(f32[1,16,1024]{2,1,0:T(8,128)S(1)} %copy-done.8), channel_id=1, source_target_pairs={{0,8},{4,12},{8,0},{12,4},{1,9},{5,13},{9,1},{13,5},{2,10},{6,14},... | collective-permute-start | bytes 196616 | tf_op jit(solution)/shard_map/ppermute | solution.py:43
  22.4 4.3 %collective-permute-start.8 = (f32[1,16,1024]{2,1,0:T(8,128)S(1)}, f32[1,16,1024]{2,1,0:T(8,128)S(1)}, u32[]{:S(2)}, u32[]{:S(2)}) collective-permute-start(f32[1,16,1024]{2,1,0:T(8,128)S(1)} %copy-done.8), channel_id=1, source_target_pairs={{0,12},{4,0},{8,4},{12,8},{1,13},{5,1},{9,5},{13,9},{2,14},{6,2},{... | collective-permute-start | bytes 196616 | tf_op jit(solution)/shard_map/ppermute | solution.py:43
  22.5 0.7 %copy-start.5 = (s32[16]{0:T(128)S(1)}, s32[16]{0:T(128)}, u32[]{:S(2)}) copy-start(s32[16]{0:T(128)} %child_ref.3) | copy-start | bytes 196
  23.8 3.0 %copy-start.7 = (f32[16,1024]{1,0:T(8,128)S(1)}, f32[16,1024]{1,0:T(8,128)}, u32[]{:S(2)}) copy-start(f32[16,1024]{1,0:T(8,128)} %alog_ref.1) | copy-start | bytes 196612
  23.8 3.0 %copy-start.10 = (f32[1024]{0:T(1024)S(1)}, f32[1024]{0:T(1024)}, u32[]{:S(2)}) copy-start(f32[1024]{0:T(1024)} %param.23) | copy-start | bytes 12292
  24.5 2.3 %copy-start.9 = (f32[1024]{0:T(1024)S(1)}, f32[1024]{0:T(1024)}, u32[]{:S(2)}) copy-start(f32[1024]{0:T(1024)} %param.21) | copy-start | bytes 12292

commit v2 on v0

v2 whole, which is shorter than its diff:
```python
import functools
import math

import jax
import jax.numpy as jnp
from jax import lax
from jax.experimental import pallas as pl
from jax.experimental.pallas import tpu as pltpu
from jax.sharding import PartitionSpec as P

F32 = jnp.float32
BF16 = jnp.bfloat16
LANES = 128
VMEM_LIMIT = 48 * 2**20
DIRECT_MOST = 4


def vmem():
    return pl.BlockSpec(memory_space=pltpu.VMEM)


def smem():
    return pl.BlockSpec(memory_space=pltpu.SMEM)


def hbm():
    return pl.BlockSpec(memory_space=pltpu.HBM)


def anywhere():
    return pl.BlockSpec(memory_space=pl.ANY)


def shaped(shape, dtype):
    return jax.ShapeDtypeStruct(shape, dtype)


def call(kernel, outs, in_specs, out_specs, scratch=(), flops=0, nbytes=0, trans=0):
    return pl.pallas_call(
        kernel,
        out_shape=outs,
        in_specs=in_specs,
        out_specs=out_specs,
        scratch_shapes=list(scratch),
        compiler_params=pltpu.CompilerParams(vmem_limit_bytes=VMEM_LIMIT),
        cost_estimate=pl.CostEstimate(flops=flops, bytes_accessed=nbytes, transcendentals=trans),
    )


def swap(value, axis, distance):
    size = lax.axis_size(axis)
    return lax.ppermute(value, axis, [(i, i ^ distance) for i in range(size)])


def blocks(refs):
    return [(ref, i) for ref in refs for i in range(ref.shape[0])]


def read_rows(refs, row):
    return jnp.concatenate(
        [ref[i, row : row + 1, :].astype(F32) for ref, i in blocks(refs)], axis=0
    )


def pick_rows(pick, rows):
    if len(rows) > DIRECT_MOST:
        table = jnp.concatenate(rows, axis=0).astype(BF16)
        return jnp.dot(pick.astype(BF16), table, preferred_element_type=F32)
    total = pick[:, 0:1] * rows[0]
    for k in range(1, len(rows)):
        total = total + pick[:, k : k + 1] * rows[k]
    return total


def pack_kernel(key_ref, rows_hbm, prompt_hbm, step_hbm, conv_hbm, ssm_hbm, *rest):
    outs, (rows_s, prompt_s, held, conv, ssm, sems, row_sems) = rest[:-7], rest[-7:]
    owners = rows_hbm.shape[0]
    channels = conv_hbm.shape[2]
    first = pltpu.make_async_copy(rows_hbm, rows_s, sems.at[0])
    others = [
        pltpu.make_async_copy(prompt_hbm, prompt_s, sems.at[1]),
        pltpu.make_async_copy(conv_hbm, conv, sems.at[2]),
        pltpu.make_async_copy(ssm_hbm, ssm, sems.at[3]),
    ]
    first.start()
    for copy in others:
        copy.start()
    first.wait()
    key = key_ref[0]
    copies, rows = [], []
    for k in range(owners):
        row = jnp.maximum(rows_s[jnp.bitwise_xor(key, k)], 0)
        copy = pltpu.make_async_copy(step_hbm.at[row], held.at[k], row_sems.at[k])
        copy.start()
        copies.append(copy)
        rows.append(row)
    for copy in others:
        copy.wait()
    fixed = [ssm[0], conv[0].astype(F32)]
    for k, (ref, i) in enumerate(blocks(outs)):
        copies[k].wait()
        xs = held[k, :, 0, :].astype(F32)
        number = jnp.full((1, channels), prompt_s[rows[k]].astype(F32), F32)
        ref[i] = jnp.concatenate(fixed + [xs, number], axis=0).astype(BF16)


def own_onehot(prompt_ref, key, owners):
    shape = (prompt_ref.shape[0], owners)
    row_of = lax.broadcasted_iota(jnp.int32, shape, 0)
    wanted = jnp.zeros(shape, jnp.int32)
    for b in range(shape[0]):
        wanted = jnp.where(row_of == b, jnp.bitwise_xor(prompt_ref[b], key), wanted)
    return (wanted == lax.broadcasted_iota(jnp.int32, shape, 1)).astype(F32)


def slot_onehot(numbers, key, owners):
    column = lax.broadcasted_iota(jnp.int32, (numbers.shape[0], owners), 1)
    held_by = jnp.bitwise_xor(column, key)
    return (numbers[:, :owners].astype(jnp.int32) == held_by).astype(F32)


def silu(v):
    return v / (1.0 + jnp.exp(-v))


def prepare_kernel(step_ref, cw_ref, cb_ref, after_ref, base_ref, gate_ref):
    del after_ref
    steps = step_ref.shape[1]
    taps = cw_ref.shape[0]
    xs = [step_ref[:, t, 0, :].astype(F32) for t in range(steps)]
    for t in range(steps):
        total = cw_ref[taps - 1 : taps, :] * xs[t] + cb_ref[...]
        for k in range(max(0, taps - 1 - t), taps - 1):
            total = total + cw_ref[k : k + 1, :] * xs[t + k - taps + 1]
        base_ref[t] = total
        gate_ref[t] = silu(step_ref[:, t, 1, :].astype(F32))


def project_kernel(n_msgs, n_state, key_ref, prompt_ref, base_ref, cw_ref, cb_ref, xwt_ref, *rest):
    msgs, (act_ref, part_ref, short_ref) = rest[:n_msgs], rest[n_msgs:]
    owners = sum(m.shape[0] for m in msgs)
    taps = cw_ref.shape[0]
    steps, rb, _ = base_ref.shape
    key = key_ref[0]
    past = taps - 1
    at_x = n_state + past
    windows = [
        [ref[i, n_state + k : n_state + k + 1, :].astype(F32) for ref, i in blocks(msgs)]
        for k in range(past)
    ]
    numbers = read_rows(msgs, at_x + steps)
    own = own_onehot(prompt_ref, key, owners)
    own_windows = [pick_rows(own, w) for w in windows]
    for t in range(steps):
        conv = base_ref[t]
        for k in range(past - t):
            conv = conv + cw_ref[k : k + 1, :] * own_windows[t + k]
        act_ref[t * rb : (t + 1) * rb, :] = silu(conv)
    slot = slot_onehot(numbers, key, owners)
    line = [pick_rows(slot, w) for w in windows]
    line += [read_rows(msgs, at_x + t) for t in range(steps)]
    row = steps * rb
    for t in range(steps):
        conv = cw_ref[past:taps, :] * line[t + past] + cb_ref[...]
        for k in range(past):
            conv = conv + cw_ref[k : k + 1, :] * line[t + k]
        act_ref[row : row + owners, :] = silu(conv)
        row += owners
    part = lax.dot_general(
        act_ref[...].astype(BF16),
        xwt_ref[...],
        (((1,), (1,)), ((), ())),
        preferred_element_type=F32,
    )
    part_ref[...] = part
    short_ref[...] = part.astype(BF16)


def start_kernel(
    n_msgs, taps, steps, key_ref, prompt_ref, child_ref, alog_ref, after_ref, *rest
):
    del after_ref
    msgs, (own_ref, slot_ref, rate_ref, conv_ref, held) = rest[:n_msgs], rest[n_msgs:]
    owners = sum(m.shape[0] for m in msgs)
    key = key_ref[0]
    n_state = own_ref.shape[0]
    past = taps - 1
    rate_ref[...] = jnp.exp(alog_ref[...]) * (-math.log2(math.e))
    own = own_onehot(prompt_ref, key, owners)
    slot = slot_onehot(read_rows(msgs, n_state + past + steps), key, owners)
    for n in range(n_state):
        rows = [ref[i, n : n + 1, :].astype(F32) for ref, i in blocks(msgs)]
        own_ref[n] = pick_rows(own, rows)
        slot_ref[n] = pick_rows(slot, rows)
    first = n_state + past + steps - past
    for k, (ref, i) in enumerate(blocks(msgs)):
        held[k] = ref[i].astype(F32)[first : first + past, :]
    for j in range(child_ref.shape[0]):
        window = held[jnp.bitwise_xor(child_ref[j], key)].astype(BF16)
        for k in range(past):
            conv_ref[k, j : j + 1, :] = window[k : k + 1, :]


def decode_kernel(
    n_parts,
    key_ref,
    child_ref,
    act_ref,
    gate_ref,
    own_ref,
    slot_ref,
    rate_ref,
    dtw_ref,
    dtb_ref,
    skip_ref,
    *rest,
):
    parts, rest = rest[:n_parts], rest[n_parts:]
    dec_ref, child_ssm, delta_s, gain_s, b_s, c_s, slots_s, line_s, sems = rest
    key = key_ref[0]
    rb, steps, channels = dec_ref.shape
    rank = dtw_ref.shape[0]
    n_state, n_slots, _ = slot_ref.shape
    own_rows = steps * rb
    chunks = channels // LANES

    proj = parts[0][...]
    for ref in parts[1:]:
        proj = proj + ref[...].astype(F32)
    delta_in = proj[:, :rank].astype(BF16)
    delta = jnp.dot(delta_in, dtw_ref[...], preferred_element_type=F32) + dtb_ref[...]
    delta = jnp.maximum(delta, 0.0) + jnp.log1p(jnp.exp(-jnp.abs(delta)))
    delta_s[...] = delta
    gain_s[...] = delta * act_ref[...]
    rows = proj.shape[0]
    for n in range(n_state):
        b_s[n] = jnp.broadcast_to(proj[:, rank + n : rank + n + 1], (rows, LANES))
        c_s[n] = jnp.broadcast_to(
            proj[:own_rows, rank + n_state + n : rank + n_state + n + 1], (own_rows, LANES)
        )

    def step(state, rate, n, at, columns):
        decay = jnp.exp2(delta_s[at, columns] * rate)
        return decay * state + gain_s[at, columns] * b_s[n, at, :]

    def slot_chunk(chunk, carry):
        columns = pl.ds(pl.multiple_of(chunk * LANES, LANES), LANES)
        for n in range(n_state):
            rate = rate_ref[n : n + 1, columns]
            state = slot_ref[n, :, columns]
            for t in range(steps):
                state = step(state, rate, n, pl.ds(own_rows + t * n_slots, n_slots), columns)
            slots_s[:, n, columns] = state
        return carry

    lax.fori_loop(0, chunks, slot_chunk, 0)
    copies = []
    for j in range(rb):
        at = jnp.bitwise_xor(child_ref[j], key)
        copy = pltpu.make_async_copy(slots_s.at[at], child_ssm.at[j], sems.at[j])
        copy.start()
        copies.append(copy)

    def own_chunk(chunk, carry):
        columns = pl.ds(pl.multiple_of(chunk * LANES, LANES), LANES)
        sums = [None] * steps
        for n in range(n_state):
            rate = rate_ref[n : n + 1, columns]
            state = own_ref[n, :, columns]
            for t in range(steps):
                at = pl.ds(t * rb, rb)
                state = step(state, rate, n, at, columns)
                term = c_s[n, at, :] * state
                sums[t] = term if sums[t] is None else sums[t] + term
        for t in range(steps):
            out = sums[t] + skip_ref[:, columns] * act_ref[pl.ds(t * rb, rb), columns]
            line_s[pl.ds(t, rb, stride=steps), :] = out * gate_ref[t, :, columns]
        dec_ref[:, :, columns] = line_s[...].reshape(rb, steps, LANES).astype(BF16)
        return carry

    lax.fori_loop(0, chunks, own_chunk, 0)
    for copy in copies:
        copy.wait()


def on_device(
    prompt_ssm,
    prompt_conv,
    prompt_of,
    step_in,
    conv_weight,
    conv_bias,
    x_weight,
    dt_weight,
    dt_bias,
    a_log,
    skip,
    send_rows,
    child_slot,
):
    owners = lax.axis_size("branch")
    tensors = lax.axis_size("tensor")
    assert owners & (owners - 1) == 0 and tensors & (tensors - 1) == 0
    assert prompt_ssm.shape[0] == 1 and send_rows.shape[2] == 1
    rb, steps, _, channels = step_in.shape
    taps = conv_weight.shape[0]
    width = x_weight.shape[1]
    n_state = a_log.shape[0]
    rows = steps * (rb + owners)
    depth = n_state + taps - 1 + steps + 1
    direct = owners <= DIRECT_MOST
    me = lax.axis_index("branch").astype(jnp.int32).reshape(1)
    key = me if direct else jnp.zeros((1,), jnp.int32)
    conv_bias, dt_bias, skip = conv_bias[None], dt_bias[None], skip[None]

    msg_shapes = [(1, depth, channels)] * owners if direct else [(owners, depth, channels)]
    msgs = call(
        pack_kernel,
        [shaped(s, BF16) for s in msg_shapes],
        [smem()] + [hbm()] * 5,
        [vmem()] * len(msg_shapes),
        [
            pltpu.SMEM((owners,), jnp.int32),
            pltpu.SMEM((rb,), jnp.int32),
            pltpu.VMEM((owners,) + step_in.shape[1:], BF16),
            pltpu.VMEM(prompt_conv.shape, BF16),
            pltpu.VMEM(prompt_ssm.shape, F32),
            pltpu.SemaphoreType.DMA((4,)),
            pltpu.SemaphoreType.DMA((owners,)),
        ],
        nbytes=owners * depth * channels * 2,
    )(key, send_rows.reshape(owners), prompt_of, step_in, prompt_conv, prompt_ssm)
    base, gate = call(
        prepare_kernel,
        [shaped((steps, rb, channels), F32)] * 2,
        [vmem()] * 3 + [anywhere()],
        [vmem()] * 2,
        flops=10 * steps * rb * channels,
        nbytes=12 * steps * rb * channels,
        trans=steps * rb * channels,
    )(step_in, conv_weight, conv_bias, msgs[0])
    if direct:
        msgs = [msgs[0]] + [swap(msgs[k], "branch", k) for k in range(1, owners)]
    else:
        msgs = [lax.all_to_all(msgs[0], "branch", split_axis=0, concat_axis=0, tiled=True)]

    n_msgs = len(msgs)
    act, part, short = call(
        functools.partial(project_kernel, n_msgs, n_state),
        [
            shaped((rows, channels), F32),
            shaped((rows, width), F32),
            shaped((rows, width), BF16),
        ],
        [smem(), smem()] + [vmem()] * (4 + n_msgs),
        [vmem()] * 3,
        flops=2 * rows * channels * width,
        nbytes=channels * width * 2 + rows * (channels + width) * 4,
        trans=rows * channels,
    )(key, prompt_of, base, conv_weight, conv_bias, x_weight.T, *msgs)
    parts = [part, swap(part, "tensor", 1)]
    parts += [swap(short, "tensor", k) for k in range(2, tensors)]

    own_start, slot_start, rate, child_conv = call(
        functools.partial(start_kernel, n_msgs, taps, steps),
        [
            shaped((n_state, rb, channels), F32),
            shaped((n_state, owners, channels), F32),
            shaped((n_state, channels), F32),
            shaped((taps - 1, rb, channels), BF16),
        ],
        [smem()] * 3 + [vmem(), anywhere()] + [vmem()] * n_msgs,
        [vmem()] * 4,
        [pltpu.VMEM((owners, taps - 1, channels), F32)],
        flops=6 * n_state * (rb + owners) * channels,
        nbytes=4 * n_state * (rb + owners) * channels,
    )(key, prompt_of, child_slot, a_log, act, *msgs)

    decoded, child_ssm = call(
        functools.partial(decode_kernel, len(parts)),
        [
            shaped((rb, steps, channels), BF16),
            shaped((rb, n_state, channels), F32),
        ],
        [smem()] * 2 + [vmem()] * (8 + len(parts)),
        [vmem(), anywhere()],
        [
            pltpu.VMEM((rows, channels), F32),
            pltpu.VMEM((rows, channels), F32),
            pltpu.VMEM((n_state, rows, LANES), F32),
            pltpu.VMEM((n_state, steps * rb, LANES), F32),
            pltpu.VMEM((owners, n_state, channels), F32),
            pltpu.VMEM((steps * rb, LANES), F32),
            pltpu.SemaphoreType.DMA((rb,)),
        ],
        flops=8 * rows * n_state * channels,
        nbytes=(rb + owners) * n_state * channels * 4,
        trans=rows * n_state * channels,
    )(
        key,
        child_slot,
        act,
        gate,
        own_start,
        slot_start,
        rate,
        dt_weight,
        dt_bias,
        skip,
        *parts,
    )
    return (decoded, child_ssm, jnp.transpose(child_conv, (1, 0, 2)))


def solution(mesh):
    placed = (
        P(("replica", "branch"), None, "tensor"),
        P(("replica", "branch"), None, "tensor"),
        P(("replica", "branch")),
        P(("replica", "branch"), None, None, "tensor"),
        P(None, "tensor"),
        P("tensor"),
        P("tensor", None),
        P(None, "tensor"),
        P("tensor"),
        P(None, "tensor"),
        P("tensor"),
        P(("replica", "branch"), None, None),
        P(("replica", "branch")),
    )
    return jax.shard_map(
        on_device,
        mesh=mesh,
        in_specs=placed,
        out_specs=(
            P(("replica", "branch"), None, "tensor"),
            P(("replica", "branch"), None, "tensor"),
            P(("replica", "branch"), None, "tensor"),
        ),
        check_vma=False,
    )
```

time: 102 us -> 28.3 us (0.28)
  blocking collectives: 29.3 us -> 0 us
  waiting for transfers between devices: 22.7 us -> 7.6 us
  between operations: 14.3 us -> 0.74 us
  local copies, waits for them, and re-layouts: 15 us -> 4.25 us
  Pallas kernels: 0 us -> 7.53 us
  matrix products: 7.21 us -> 0 us
  other arithmetic: 3.41 us -> 0 us
  starting transfers between devices: 9.47 us -> 7.89 us
    all_gather x2 -> x0, blocking collectives: 29.3 us -> none  [the longest x1 14.9 us: select_prompts(): lax.all_gather(prompt_wide, 'branch', axis=0, tiled=True)]
    psum x1 -> x0, waiting for transfers between devices: 17.8 us -> none  [decode_rows(): x_proj = lax.psum(partial_proj, 'tensor')]
    all_to_all x2 -> x0, starting transfers between devices: 9.47 us -> none  [the longest x1 4.87 us: on_device(): lax.all_to_all(out_conv, 'branch', split_axis=0, concat_axis=0, tiled=True)]
    ppermute x0 -> x6, starting transfers between devices: none -> 7.89 us  [swap(): return lax.ppermute(value, axis, [(i, i ^ distance) for i in range(size)])]
    ppermute x0 -> x6, waiting for transfers between devices: none -> 7.6 us  [swap(): return lax.ppermute(value, axis, [(i, i ^ distance) for i in range(size)])]
    pallas_call x0 -> x5, Pallas kernels: none -> 7.53 us  [the longest x1 3.73 us: on_device(): call(functools.partial(decode_kernel, len(parts)), [shaped((rb, steps, ch...]
    dot_general x10 -> x0, matrix products: 7.21 us -> none  [the longest x4 3.55 us: decode_rows(): jnp.dot(activated.astype(jnp.bfloat16), x_weight, preferred_element_type=...]
    all_to_all x2 -> x0, waiting for transfers between devices: 4.89 us -> none  [the longest x1 4.89 us: on_device(): lax.all_to_all(out_ssm, 'branch', split_axis=0, concat_axis=0, tiled=True)]
  transfers between devices with their start and end apart: 3 -> 6, of which waited for: 2 -> 4; matrix products, arithmetic and copies ran while one was open for 12% -> 0% of each run, Pallas kernels for 0% -> 7%
where the time goes in v2:
time: 28.3 us; the launch traced here: 28 us
  starting transfers between devices  7.89 us (28%)
  waiting for transfers between devices  7.6 us (27%)
  Pallas kernels  7.53 us (27%)
  local copies, waits for them, and re-layouts  4.25 us (15%)
  between operations  0.74 us (3%)
    ppermute x6, starting transfers between devices, swap(): return lax.ppermute(value, axis, [(i, i ^ distance) for i in range(size)])  7.89 us
    ppermute x6, waiting for transfers between devices, swap(): return lax.ppermute(value, axis, [(i, i ^ distance) for i in range(size)])  7.6 us
    unnamed x28, local copies, waits for them, and re-layouts  4.25 us
    pallas_call x1, Pallas kernels, on_device(): call(functools.partial(decode_kernel, len(parts)), [shaped((rb, steps, ch...  3.73 us
    pallas_call x1, Pallas kernels, on_device(): call(functools.partial(start_kernel, n_msgs, taps, steps), [shaped((n_sta...  1.62 us
    pallas_call x1, Pallas kernels, on_device(): call(functools.partial(project_kernel, n_msgs, n_state), [shaped((rows, c...  1.07 us
    pallas_call x1, Pallas kernels, on_device(): call(pack_kernel, [shaped(s, BF16) for s in msg_shapes], [smem()] + [hbm(...  0.79 us
  transfers between devices with their start and end apart: 6, of which 4 were waited for; matrix products, arithmetic and copies ran while one was open for 0% of the time, Pallas kernels for 7%

profile of v2, /device:TPU:0, one launch (start us, length us, event | category | flops | bytes accessed | tf_op | source)
XLA Modules:
  0.0 28.0 jit_solution(17110208919370881855)
XLA Ops:
  0.7 0.7 %copy-done.8 = bf16[1,3,1024]{2,1,0:T(4,128)(2,1)S(1)} copy-done((bf16[1,3,1024]{2,1,0:T(4,128)(2,1)S(1)}, bf16[1,3,1024]{2,1,0:T(4,128)(2,1)}, u32[]{:S(2)}) %copy-start.8) | copy-done | bytes 6168
  1.3 0.9 %copy-done = bf16[16,4,2,1024]{3,2,1,0:T(2,128)(2,1)S(1)} copy-done((bf16[16,4,2,1024]{3,2,1,0:T(2,128)(2,1)S(1)}, bf16[16,4,2,1024]{3,2,1,0:T(2,128)(2,1)}, u32[]{:S(2)}) %copy-start) | copy-done | bytes 262168
  2.3 0.8 %copy-done.5 = f32[1,16,1024]{2,1,0:T(8,128)S(1)} copy-done((f32[1,16,1024]{2,1,0:T(8,128)S(1)}, f32[1,16,1024]{2,1,0:T(8,128)}, u32[]{:S(2)}) %copy-start.5) | copy-done | bytes 65560
  3.1 0.8 %shard_map.148 = (bf16[1,24,1024]{2,1,0:T(8,128)(2,1)S(1)}, bf16[1,24,1024]{2,1,0:T(8,128)(2,1)S(1)}, bf16[1,24,1024]{2,1,0:T(8,128)(2,1)S(1)}, bf16[1,24,1024]{2,1,0:T(8,128)(2,1)S(1)}) custom-call(s32[1]{0:T(128)} %bitcast.key_ref, s32[4]{0:T(128)S(1)} %bitcast.12, s32[16]{0:T(128)S(1)} %copy-done.9, bf16[16,4,2,1024]{3,2,1,0:T(2,128)(2,1)S(1)} %copy-done, ...), custom_call_target="tpu_custom_call" | custom-call | bytes 196608 | tf_op jit(solution)/shard_map/pallas_call | solution.py:317
  3.9 0.0 copy-start.7
  3.9 3.1 %collective-permute-start = (bf16[1,24,1024]{2,1,0:T(8,128)(2,1)S(1)}, bf16[1,24,1024]{2,1,0:T(8,128)(2,1)S(1)}, u32[]{:S(2)}, u32[]{:S(2)}) collective-permute-start(bf16[1,24,1024]{2,1,0:T(8,128)(2,1)S(1)} %get-tuple-element.20), channel_id=1, source_target_pairs={{0,4},{4,0},{8,12},{12,8},{1,5},{5,1},{9,13},{13,9},{2,6},{6,2},{1... | collective-permute-start | bytes 147464 | tf_op jit(solution)/shard_map/ppermute | solution.py:52
  7.0 2.6 %collective-permute-start.1 = (bf16[1,24,1024]{2,1,0:T(8,128)(2,1)S(1)}, bf16[1,24,1024]{2,1,0:T(8,128)(2,1)S(1)}, u32[]{:S(2)}, u32[]{:S(2)}) collective-permute-start(bf16[1,24,1024]{2,1,0:T(8,128)(2,1)S(1)} %get-tuple-element.21), channel_id=1, source_target_pairs={{0,8},{4,12},{8,0},{12,4},{1,9},{5,13},{9,1},{13,5},{2,10},{6,14},... | collective-permute-start | bytes 147464 | tf_op jit(solution)/shard_map/ppermute | solution.py:52
  9.6 0.0 collective-permute-start.2
  9.6 0.3 %shard_map.149 = (f32[4,16,1024]{2,1,0:T(8,128)S(1)}, f32[4,16,1024]{2,1,0:T(8,128)S(1)}) custom-call(bf16[16,4,2,1024]{3,2,1,0:T(2,128)(2,1)S(1)} %copy-done.1, f32[4,1024]{1,0:T(4,128)S(1)} %copy-done.4, f32[1,1024]{1,0:T(1,128)S(1)} %bitcast.8, bf16[1,24,1024]{2,1,0:T(8,128)(2,1)S(1)} %get-tuple-element.18.after_ref.rest_0_), custom_call_target="tpu_custom_call" | custom-call | flops 655360 | bytes 786432 | tf_op jit(solution)/shard_map/pallas_call | solution.py:333
  10.0 0.0 collective-permute-done.rest_1_
  10.0 3.0 %collective-permute-done.1.rest_2_ = bf16[1,24,1024]{2,1,0:T(8,128)(2,1)S(1)} collective-permute-done((bf16[1,24,1024]{2,1,0:T(8,128)(2,1)S(1)}, bf16[1,24,1024]{2,1,0:T(8,128)(2,1)S(1)}, u32[]{:S(2)}, u32[]{:S(2)}) %collective-permute-start.1) | collective-permute-done | bytes 49184 | tf_op jit(solution)/shard_map/ppermute | solution.py:52
  13.0 2.6 %collective-permute-done.2.rest_3_ = bf16[1,24,1024]{2,1,0:T(8,128)(2,1)S(1)} collective-permute-done((bf16[1,24,1024]{2,1,0:T(8,128)(2,1)S(1)}, bf16[1,24,1024]{2,1,0:T(8,128)(2,1)S(1)}, u32[]{:S(2)}, u32[]{:S(2)}) %collective-permute-start.2) | collective-permute-done | bytes 49184 | tf_op jit(solution)/shard_map/ppermute | solution.py:52
  15.5 1.1 %copy-done.2 = bf16[1024,288]{0,1:T(8,128)(2,1)S(1)} copy-done((bf16[1024,288]{0,1:T(8,128)(2,1)S(1)}, bf16[1024,288]{0,1:T(8,128)(2,1)}, u32[]{:S(2)}) %copy-start.2) | copy-done | bytes 589848
  16.6 1.1 %shard_map.150 = (f32[80,1024]{1,0:T(8,128)S(1)}, f32[80,288]{1,0:T(8,128)S(1)}, bf16[80,288]{1,0:T(8,128)(2,1)S(1)}) custom-call(s32[1]{0:T(128)} %bitcast.key_ref, s32[16]{0:T(128)S(1)} %copy-done.9, f32[4,16,1024]{2,1,0:T(8,128)S(1)} %get-tuple-element.19.base_ref, f32[4,1024]{1,0:T(4,128)S(1)} %copy-done.4, f32[1,1024]{1,0:T(1,128)S(1)} %bitcast.9, ...), custom_call_target="tpu_custom_call" | custom-call | flops 47185920 | bytes 1009664 | tf_op jit(solution)/shard_map/pallas_call | solution.py:348
  17.7 0.0 copy-start.3
  17.7 0.1 collective-permute-start.3
  17.7 1.6 %collective-permute-start.5 = (bf16[80,288]{1,0:T(8,128)(2,1)S(1)}, bf16[80,288]{1,0:T(8,128)(2,1)S(1)}, u32[]{:S(2)}, u32[]{:S(2)}) collective-permute-start(bf16[80,288]{1,0:T(8,128)(2,1)S(1)} %get-tuple-element.29), channel_id=1, source_target_pairs={{0,3},{1,2},{2,1},{3,0},{4,7},{5,6},{6,5},{7,4},{8,11},{9,10},{10,... | collective-permute-start | bytes 138248 | tf_op jit(solution)/shard_map/ppermute | solution.py:52
  19.4 0.5 %collective-permute-start.4 = (bf16[80,288]{1,0:T(8,128)(2,1)S(1)}, bf16[80,288]{1,0:T(8,128)(2,1)S(1)}, u32[]{:S(2)}, u32[]{:S(2)}) collective-permute-start(bf16[80,288]{1,0:T(8,128)(2,1)S(1)} %get-tuple-element.29), channel_id=1, source_target_pairs={{0,2},{1,3},{2,0},{3,1},{4,6},{5,7},{6,4},{7,5},{8,10},{9,11},{10,... | collective-permute-start | bytes 138248 | tf_op jit(solution)/shard_map/ppermute | solution.py:52
  19.9 1.6 %shard_map.151 = (f32[16,16,1024]{2,1,0:T(8,128)S(1)}, f32[16,4,1024]{2,1,0:T(4,128)S(1)}, f32[16,1024]{1,0:T(8,128)S(1)}, bf16[3,16,1024]{2,1,0:T(8,128)(2,1)}) custom-call(s32[1]{0:T(128)} %bitcast.key_ref, s32[16]{0:T(128)S(1)} %copy-done.9, s32[16]{0:T(128)S(1)} %copy-done.12, f32[16,1024]{1,0:T(8,128)S(1)} %copy-done.6, ...), custom_call_target="tpu_custom_call" | custom-call | flops 1966080 | bytes 1310720 | tf_op jit(solution)/shard_map/pallas_call | solution.py:364
  21.5 0.2 collective-permute-done.5.rest_3_
  21.7 1.9 %collective-permute-done.4.rest_2_ = bf16[80,288]{1,0:T(8,128)(2,1)S(1)} collective-permute-done((bf16[80,288]{1,0:T(8,128)(2,1)S(1)}, bf16[80,288]{1,0:T(8,128)(2,1)S(1)}, u32[]{:S(2)}, u32[]{:S(2)}) %collective-permute-start.4) | collective-permute-done | bytes 46112 | tf_op jit(solution)/shard_map/ppermute | solution.py:52
  23.6 0.7 %copy-done.11 = f32[1024]{0:T(1024)S(1)} copy-done((f32[1024]{0:T(1024)S(1)}, f32[1024]{0:T(1024)}, u32[]{:S(2)}) %copy-start.11) | copy-done | bytes 4120
  24.3 0.0 copy-done.10
  24.3 3.7 %shard_map.152 = (bf16[16,4,1024]{2,1,0:T(4,128)(2,1)}, f32[16,16,1024]{2,1,0:T(8,128)}) custom-call(s32[1]{0:T(128)} %bitcast.key_ref, s32[16]{0:T(128)S(1)} %copy-done.12, f32[80,1024]{1,0:T(8,128)S(1)} %get-tuple-element.23.after_ref.act_ref, f32[4,16,1024]{2,1,0:T(8,128)S(1)} %get-tuple-element.24.gate_ref, ...), custom_call_target="tpu_custom_call" | custom-call | flops 10485760 | bytes 1310720 | tf_op jit(solution)/shard_map/pallas_call | solution.py:379
  (21 shorter events, 0.0 us)
Async XLA Ops:
  0.6 0.7 %copy-start.8 = (bf16[1,3,1024]{2,1,0:T(4,128)(2,1)S(1)}, bf16[1,3,1024]{2,1,0:T(4,128)(2,1)}, u32[]{:S(2)}) copy-start(bf16[1,3,1024]{2,1,0:T(4,128)(2,1)} %conv_hbm.1) | copy-start | bytes 18436
  0.6 0.7 %copy-start.9 = (s32[16]{0:T(128)S(1)}, s32[16]{0:T(128)}, u32[]{:S(2)}) copy-start(s32[16]{0:T(128)} %prompt_ref.3) | copy-start | bytes 196
  0.7 0.7 %copy-start.13 = (s32[1,4,1]{1,2,0:T(1,128)S(1)}, s32[1,4,1]{1,2,0:T(1,128)}, u32[]{:S(2)}) copy-start(s32[1,4,1]{1,2,0:T(1,128)} %param.24) | copy-start | bytes 52
  1.3 1.0 %copy-start = (bf16[16,4,2,1024]{3,2,1,0:T(2,128)(2,1)S(1)}, bf16[16,4,2,1024]{3,2,1,0:T(2,128)(2,1)}, u32[]{:S(2)}) copy-start(bf16[16,4,2,1024]{3,2,1,0:T(2,128)(2,1)} %step_ref.1) | copy-start | bytes 786436
  2.3 0.8 %copy-start.5 = (f32[1,16,1024]{2,1,0:T(8,128)S(1)}, f32[1,16,1024]{2,1,0:T(8,128)}, u32[]{:S(2)}) copy-start(f32[1,16,1024]{2,1,0:T(8,128)} %ssm_hbm.1) | copy-start | bytes 196612
  3.1 6.5 %copy-start.1 = (bf16[16,4,2,1024]{3,2,1,0:T(2,128)(2,1)S(1)}, bf16[16,4,2,1024]{3,2,1,0:T(2,128)(2,1)}, u32[]{:S(2)}) copy-start(bf16[16,4,2,1024]{3,2,1,0:T(2,128)(2,1)} %step_ref.1) | copy-start | bytes 786436
  3.1 6.5 %copy-start.4 = (f32[4,1024]{1,0:T(4,128)S(1)}, f32[4,1024]{1,0:T(4,128)}, u32[]{:S(2)}) copy-start(f32[4,1024]{1,0:T(4,128)} %cw_ref.3) | copy-start | bytes 49156
  3.9 5.7 %copy-start.7 = (f32[1024]{0:T(1024)S(1)}, f32[1024]{0:T(1024)}, u32[]{:S(2)}) copy-start(f32[1024]{0:T(1024)} %param.18) | copy-start | bytes 12292
  3.9 6.0 %collective-permute-start = (bf16[1,24,1024]{2,1,0:T(8,128)(2,1)S(1)}, bf16[1,24,1024]{2,1,0:T(8,128)(2,1)S(1)}, u32[]{:S(2)}, u32[]{:S(2)}) collective-permute-start(bf16[1,24,1024]{2,1,0:T(8,128)(2,1)S(1)} %get-tuple-element.20), channel_id=1, source_target_pairs={{0,4},{4,0},{8,12},{12,8},{1,5},{5,1},{9,13},{13,9},{2,6},{6,2},{1... | collective-permute-start | bytes 147464 | tf_op jit(solution)/shard_map/ppermute | solution.py:52
  7.0 5.9 %collective-permute-start.1 = (bf16[1,24,1024]{2,1,0:T(8,128)(2,1)S(1)}, bf16[1,24,1024]{2,1,0:T(8,128)(2,1)S(1)}, u32[]{:S(2)}, u32[]{:S(2)}) collective-permute-start(bf16[1,24,1024]{2,1,0:T(8,128)(2,1)S(1)} %get-tuple-element.21), channel_id=1, source_target_pairs={{0,8},{4,12},{8,0},{12,4},{1,9},{5,13},{9,1},{13,5},{2,10},{6,14},... | collective-permute-start | bytes 147464 | tf_op jit(solution)/shard_map/ppermute | solution.py:52
  9.6 5.9 %collective-permute-start.2 = (bf16[1,24,1024]{2,1,0:T(8,128)(2,1)S(1)}, bf16[1,24,1024]{2,1,0:T(8,128)(2,1)S(1)}, u32[]{:S(2)}, u32[]{:S(2)}) collective-permute-start(bf16[1,24,1024]{2,1,0:T(8,128)(2,1)S(1)} %get-tuple-element.22), channel_id=1, source_target_pairs={{0,12},{4,8},{8,4},{12,0},{1,13},{5,9},{9,5},{13,1},{2,14},{6,10},... | collective-permute-start | bytes 147464 | tf_op jit(solution)/shard_map/ppermute | solution.py:52
  15.5 1.1 %copy-start.2 = (bf16[1024,288]{0,1:T(8,128)(2,1)S(1)}, bf16[1024,288]{0,1:T(8,128)(2,1)}, u32[]{:S(2)}) copy-start(bf16[1024,288]{0,1:T(8,128)(2,1)} %param.19) | copy-start | bytes 1769476
  16.6 3.3 %copy-start.6 = (f32[16,1024]{1,0:T(8,128)S(1)}, f32[16,1024]{1,0:T(8,128)}, u32[]{:S(2)}) copy-start(f32[16,1024]{1,0:T(8,128)} %alog_ref.1) | copy-start | bytes 196612
  16.6 3.3 %copy-start.12 = (s32[16]{0:T(128)S(1)}, s32[16]{0:T(128)}, u32[]{:S(2)}) copy-start(s32[16]{0:T(128)} %child_ref.3) | copy-start | bytes 196
  17.7 5.9 %copy-start.3 = (bf16[256,1024]{1,0:T(8,128)(2,1)S(1)}, bf16[256,1024]{1,0:T(8,128)(2,1)}, u32[]{:S(2)}) copy-start(bf16[256,1024]{1,0:T(8,128)(2,1)} %dtw_ref.1) | copy-start | bytes 1572868
  17.7 5.9 %collective-permute-start.3 = (f32[80,288]{1,0:T(8,128)S(1)}, f32[80,288]{1,0:T(8,128)S(1)}, u32[]{:S(2)}, u32[]{:S(2)}) collective-permute-start(f32[80,288]{1,0:T(8,128)S(1)} %get-tuple-element.28.rest_0_), channel_id=1, source_target_pairs={{0,1},{1,0},{2,3},{3,2},{4,5},{5,4},{6,7},{7,6},{8,9},{9,8},{10,11... | collective-permute-start | bytes 276488 | tf_op jit(solution)/shard_map/ppermute | solution.py:52
  17.7 3.9 %collective-permute-start.5 = (bf16[80,288]{1,0:T(8,128)(2,1)S(1)}, bf16[80,288]{1,0:T(8,128)(2,1)S(1)}, u32[]{:S(2)}, u32[]{:S(2)}) collective-permute-start(bf16[80,288]{1,0:T(8,128)(2,1)S(1)} %get-tuple-element.29), channel_id=1, source_target_pairs={{0,3},{1,2},{2,1},{3,0},{4,7},{5,6},{6,5},{7,4},{8,11},{9,10},{10,... | collective-permute-start | bytes 138248 | tf_op jit(solution)/shard_map/ppermute | solution.py:52
  19.4 4.2 %collective-permute-start.4 = (bf16[80,288]{1,0:T(8,128)(2,1)S(1)}, bf16[80,288]{1,0:T(8,128)(2,1)S(1)}, u32[]{:S(2)}, u32[]{:S(2)}) collective-permute-start(bf16[80,288]{1,0:T(8,128)(2,1)S(1)} %get-tuple-element.29), channel_id=1, source_target_pairs={{0,2},{1,3},{2,0},{3,1},{4,6},{5,7},{6,4},{7,5},{8,10},{9,11},{10,... | collective-permute-start | bytes 138248 | tf_op jit(solution)/shard_map/ppermute | solution.py:52
  23.6 0.7 %copy-start.11 = (f32[1024]{0:T(1024)S(1)}, f32[1024]{0:T(1024)}, u32[]{:S(2)}) copy-start(f32[1024]{0:T(1024)} %param.23) | copy-start | bytes 12292
  23.6 0.7 %copy-start.10 = (f32[1024]{0:T(1024)S(1)}, f32[1024]{0:T(1024)}, u32[]{:S(2)}) copy-start(f32[1024]{0:T(1024)} %param.21) | copy-start | bytes 12292

commit v3 on v2

v3 whole, which is shorter than its diff:
```python
import functools
import math

import jax
import jax.numpy as jnp
from jax import lax
from jax.experimental import pallas as pl
from jax.experimental.pallas import tpu as pltpu
from jax.sharding import PartitionSpec as P

F32 = jnp.float32
BF16 = jnp.bfloat16
LANES = 128
VMEM_LIMIT = 48 * 2**20
DIRECT = 4


def vmem():
    return pl.BlockSpec(memory_space=pltpu.VMEM)


def smem():
    return pl.BlockSpec(memory_space=pltpu.SMEM)


def hbm():
    return pl.BlockSpec(memory_space=pltpu.HBM)


def anywhere():
    return pl.BlockSpec(memory_space=pl.ANY)


def pinned(array):
    return pltpu.with_memory_space_constraint(array, pltpu.HBM)


def shaped(shape, dtype):
    return jax.ShapeDtypeStruct(shape, dtype)


def call(kernel, outs, in_specs, out_specs, scratch=(), flops=0, nbytes=0, trans=0):
    return pl.pallas_call(
        kernel,
        out_shape=outs,
        in_specs=in_specs,
        out_specs=out_specs,
        scratch_shapes=list(scratch),
        compiler_params=pltpu.CompilerParams(vmem_limit_bytes=VMEM_LIMIT),
        cost_estimate=pl.CostEstimate(flops=flops, bytes_accessed=nbytes, transcendentals=trans),
    )


def swap(value, axis, distance):
    size = lax.axis_size(axis)
    return lax.ppermute(value, axis, [(i, i ^ distance) for i in range(size)])


def all_of(copies):
    for copy in copies:
        copy.start()
    for copy in copies:
        copy.wait()


def blocks(refs):
    return [(ref, i) for ref in refs for i in range(ref.shape[0])]


def pick_rows(pick, rows):
    total = pick[:, 0:1] * rows[0]
    for k in range(1, len(rows)):
        total = total + pick[:, k : k + 1] * rows[k]
    return total


def pack_kernel(direct, key_ref, rows_hbm, prompt_hbm, step_hbm, conv_hbm, ssm_hbm, *rest):
    outs, (rows_s, prompt_s, step, conv, ssm, sems) = rest[:-6], rest[-6:]
    owners = rows_hbm.shape[0]
    rb, _, _, channels = step_hbm.shape
    part = rb // 4
    copies = [
        pltpu.make_async_copy(rows_hbm, rows_s, sems.at[0]),
        pltpu.make_async_copy(prompt_hbm, prompt_s, sems.at[1]),
        pltpu.make_async_copy(conv_hbm, conv, sems.at[2]),
        pltpu.make_async_copy(ssm_hbm, ssm, sems.at[3]),
    ]
    for i in range(4):
        some = pl.ds(i * part, part)
        copies.append(pltpu.make_async_copy(step_hbm.at[some], step.at[some], sems.at[4 + i]))
    all_of(copies)
    key = key_ref[0]
    window = conv[0].astype(F32)
    for k, (ref, i) in enumerate(blocks(outs)):
        target = jnp.bitwise_xor(key, k)
        row = jnp.maximum(rows_s[target], 0)
        xs = step[row, :, 0, :].astype(F32)
        told = jnp.bitwise_xor(prompt_s[row], target) if direct else prompt_s[row]
        pieces = [window, xs, jnp.full((1, channels), told.astype(F32), F32)]
        if ref.shape[1] > sum(p.shape[0] for p in pieces):
            pieces.append(ssm[0])
        ref[i] = jnp.concatenate(pieces, axis=0).astype(BF16)


def silu(v):
    return v / (1.0 + jnp.exp(-v))


def prepare_kernel(
    key_ref, prompt_ref, step_ref, cw_hbm, cb_hbm, xwt_hbm, after_ref, *rest
):
    del after_ref
    base_ref, gate_ref, pick_ref, cw_ref, cb_ref, xwt_ref, sems = rest
    copies = [
        pltpu.make_async_copy(cw_hbm, cw_ref, sems.at[0]),
        pltpu.make_async_copy(cb_hbm, cb_ref, sems.at[1]),
        pltpu.make_async_copy(xwt_hbm, xwt_ref, sems.at[2]),
    ]
    for copy in copies:
        copy.start()
    steps = step_ref.shape[1]
    taps = cw_hbm.shape[0]
    shape = pick_ref.shape
    row_of = lax.broadcasted_iota(jnp.int32, shape, 0)
    wanted = jnp.zeros(shape, jnp.int32)
    for b in range(shape[0]):
        wanted = jnp.where(row_of == b, jnp.bitwise_xor(prompt_ref[b], key_ref[0]), wanted)
    pick_ref[...] = (wanted == lax.broadcasted_iota(jnp.int32, shape, 1)).astype(F32)
    xs = [step_ref[:, t, 0, :].astype(F32) for t in range(steps)]
    for t in range(steps):
        gate_ref[t] = silu(step_ref[:, t, 1, :].astype(F32))
    copies[0].wait()
    copies[1].wait()
    for t in range(steps):
        total = cw_ref[taps - 1 : taps, :] * xs[t] + cb_ref[...]
        for k in range(max(0, taps - 1 - t), taps - 1):
            total = total + cw_ref[k : k + 1, :] * xs[t + k - taps + 1]
        base_ref[t] = total
    copies[2].wait()


def slot_onehot(numbers, owners):
    column = lax.broadcasted_iota(jnp.int32, (numbers.shape[0], owners), 1)
    return (numbers[:, :owners].astype(jnp.int32) == column).astype(F32)


def project_kernel(n_msgs, pick_ref, base_ref, cw_ref, cb_ref, xwt_ref, *rest):
    msgs, outs = rest[:n_msgs], rest[n_msgs:]
    act_ref, part_ref = outs[:2]
    taps = cw_ref.shape[0]
    steps, rb, _ = base_ref.shape
    past = taps - 1
    text = past + steps + 1
    held = [ref[i].astype(F32) for ref, i in blocks(msgs)]
    owners = len(held)
    windows = [[h[k : k + 1, :] for h in held] for k in range(past)]
    own = pick_ref[...]
    own_windows = [pick_rows(own, w) for w in windows]
    for t in range(steps):
        conv = base_ref[t]
        for k in range(past - t):
            conv = conv + cw_ref[k : k + 1, :] * own_windows[t + k]
        act_ref[t * rb : (t + 1) * rb, :] = silu(conv)

    def line_of(row):
        return jnp.concatenate([h[row : row + 1, :] for h in held], axis=0)

    slot = slot_onehot(line_of(past + steps), owners)
    line = [pick_rows(slot, w) for w in windows]
    line += [line_of(past + t) for t in range(steps)]
    row = steps * rb
    for t in range(steps):
        conv = cw_ref[past:taps, :] * line[t + past] + cb_ref[...]
        for k in range(past):
            conv = conv + cw_ref[k : k + 1, :] * line[t + k]
        act_ref[row : row + owners, :] = silu(conv)
        row += owners
    part_ref[...] = lax.dot_general(
        act_ref[...].astype(BF16),
        xwt_ref[...],
        (((1,), (1,)), ((), ())),
        preferred_element_type=F32,
    )
    for pair_ref in outs[2:]:
        states = [held[0][text:, :], held[1][text:, :]]
        pair_ref[0] = jnp.concatenate(states, axis=0).astype(BF16)


def add_kernel(a_ref, b_ref, sum_ref, short_ref):
    total = a_ref[...] + b_ref[...].astype(F32)
    sum_ref[...] = total
    short_ref[...] = total.astype(BF16)


def late_kernel(
    n_msgs, taps, key_ref, child_ref, alog_ref, dtw_hbm, dtb_hbm, skip_hbm, after_ref, *rest
):
    del after_ref
    msgs, rest = rest[:n_msgs], rest[n_msgs:]
    rate_ref, conv_ref, dtw_ref, dtb_ref, skip_ref, held, sems = rest
    copies = [
        pltpu.make_async_copy(dtw_hbm, dtw_ref, sems.at[0]),
        pltpu.make_async_copy(dtb_hbm, dtb_ref, sems.at[1]),
        pltpu.make_async_copy(skip_hbm, skip_ref, sems.at[2]),
    ]
    for copy in copies:
        copy.start()
    rate_ref[...] = jnp.exp(alog_ref[...]) * (-math.log2(math.e))
    past, rb, _ = conv_ref.shape
    steps = held.shape[1]
    for k, (ref, i) in enumerate(blocks(msgs)):
        held[k] = ref[i].astype(F32)[past : past + steps, :]
    for j in range(rb):
        window = held[jnp.bitwise_xor(child_ref[j], key_ref[0])].astype(BF16)
        for k in range(past):
            at = steps - past + k
            conv_ref[k, j : j + 1, :] = window[at : at + 1, :]
    for copy in copies:
        copy.wait()


def decode_kernel(
    n_msgs,
    pair,
    taps,
    key_ref,
    child_ref,
    pick_ref,
    act_ref,
    gate_ref,
    rate_ref,
    dtw_ref,
    dtb_ref,
    skip_ref,
    part_ref,
    other_ref,
    *rest,
):
    msgs, rest = rest[:n_msgs], rest[n_msgs:]
    pairs, rest = rest[:pair], rest[pair:]
    dec_ref, child_ssm, delta_s, gain_s, b_s, c_s, start_s, slots_s, line_s, sems = rest
    key = key_ref[0]
    rb, steps, channels = dec_ref.shape
    rank = dtw_ref.shape[0]
    n_state = rate_ref.shape[0]
    n_slots = slots_s.shape[0]
    own_rows = steps * rb
    rows = own_rows + steps * n_slots
    chunks = channels // LANES
    past = taps - 1
    text = past + steps + 1

    proj = part_ref[...] + other_ref[...].astype(F32)
    delta_in = proj[:, :rank].astype(BF16)
    delta = jnp.dot(delta_in, dtw_ref[...], preferred_element_type=F32) + dtb_ref[...]
    delta = jnp.maximum(delta, 0.0) + jnp.log1p(jnp.exp(-jnp.abs(delta)))
    delta_s[...] = delta
    gain_s[...] = delta * act_ref[...]
    for n in range(n_state):
        b_s[n] = jnp.broadcast_to(proj[:, rank + n : rank + n + 1], (rows, LANES))
        c_s[n] = jnp.broadcast_to(
            proj[:own_rows, rank + n_state + n : rank + n_state + n + 1], (own_rows, LANES)
        )

    held = [ref[i].astype(F32) for ref, i in blocks(msgs)]
    numbers = jnp.concatenate([h[text - 1 : text, :] for h in held], axis=0)
    states = [h[text:, :] for h in held if h.shape[0] > text]
    for ref in pairs:
        both = ref[0].astype(F32)
        states += [both[:n_state, :], both[n_state:, :]]
    for k, state in enumerate(states):
        start_s[k] = state

    def masks(pick):
        wide = (pick.shape[0], LANES)
        return [jnp.broadcast_to(pick[:, k : k + 1], wide) for k in range(n_slots)]

    own_masks = masks(pick_ref[...])
    slot_masks = masks(slot_onehot(numbers, n_slots))

    def start(mask, n, columns):
        total = mask[0] * start_s[0, n : n + 1, columns]
        for k in range(1, n_slots):
            total = total + mask[k] * start_s[k, n : n + 1, columns]
        return total

    def slot_chunk(chunk, carry):
        columns = pl.ds(pl.multiple_of(chunk * LANES, LANES), LANES)
        at = [pl.ds(own_rows + t * n_slots, n_slots) for t in range(steps)]
        delta = [delta_s[a, columns] for a in at]
        gain = [gain_s[a, columns] for a in at]
        for n in range(n_state):
            rate = rate_ref[n : n + 1, columns]
            state = start(slot_masks, n, columns)
            for t in range(steps):
                state = jnp.exp2(delta[t] * rate) * state + gain[t] * b_s[n, at[t], :]
            slots_s[:, n, columns] = state
        return carry

    lax.fori_loop(0, chunks, slot_chunk, 0)
    copies = []
    for j in range(rb):
        at = jnp.bitwise_xor(child_ref[j], key)
        copy = pltpu.make_async_copy(slots_s.at[at], child_ssm.at[j], sems.at[j])
        copy.start()
        copies.append(copy)

    def own_chunk(chunk, carry):
        columns = pl.ds(pl.multiple_of(chunk * LANES, LANES), LANES)
        at = [pl.ds(t * rb, rb) for t in range(steps)]
        delta = [delta_s[a, columns] for a in at]
        gain = [gain_s[a, columns] for a in at]
        sums = [skip_ref[:, columns] * act_ref[a, columns] for a in at]
        for n in range(n_state):
            rate = rate_ref[n : n + 1, columns]
            state = start(own_masks, n, columns)
            for t in range(steps):
                state = jnp.exp2(delta[t] * rate) * state + gain[t] * b_s[n, at[t], :]
                sums[t] = sums[t] + c_s[n, at[t], :] * state
        for t in range(steps):
            line_s[pl.ds(t, rb, stride=steps), :] = sums[t] * gate_ref[t, :, columns]
        dec_ref[:, :, columns] = line_s[...].reshape(rb, steps, LANES).astype(BF16)
        return carry

    lax.fori_loop(0, chunks, own_chunk, 0)
    for copy in copies:
        copy.wait()


def on_device(
    prompt_ssm,
    prompt_conv,
    prompt_of,
    step_in,
    conv_weight,
    conv_bias,
    x_weight,
    dt_weight,
    dt_bias,
    a_log,
    skip,
    send_rows,
    child_slot,
):
    owners = lax.axis_size("branch")
    tensors = lax.axis_size("tensor")
    assert owners & (owners - 1) == 0 and tensors & (tensors - 1) == 0
    assert prompt_ssm.shape[0] == 1 and send_rows.shape[2] == 1
    rb, steps, _, channels = step_in.shape
    taps = conv_weight.shape[0]
    width = x_weight.shape[1]
    n_state = a_log.shape[0]
    rows = steps * (rb + owners)
    short = taps - 1 + steps + 1
    depth = short + n_state
    direct = owners == DIRECT
    me = lax.axis_index("branch").astype(jnp.int32).reshape(1)
    key = me if direct else jnp.zeros((1,), jnp.int32)

    if direct:
        msg_shapes = [(1, d, channels) for d in (depth, depth, short, short)]
    else:
        msg_shapes = [(owners, depth, channels)]
    msgs = call(
        functools.partial(pack_kernel, direct),
        [shaped(s, BF16) for s in msg_shapes],
        [smem()] + [hbm()] * 5,
        [vmem()] * len(msg_shapes),
        [
            pltpu.SMEM((owners,), jnp.int32),
            pltpu.SMEM((rb,), jnp.int32),
            pltpu.VMEM(step_in.shape, BF16),
            pltpu.VMEM(prompt_conv.shape, BF16),
            pltpu.VMEM(prompt_ssm.shape, F32),
            pltpu.SemaphoreType.DMA((8,)),
        ],
        nbytes=owners * depth * channels * 2,
    )(
        key,
        pinned(send_rows.reshape(owners)),
        pinned(prompt_of),
        pinned(step_in),
        pinned(prompt_conv),
        pinned(prompt_ssm),
    )
    base, gate, pick, taps_near, bias_near, weight_near = call(
        prepare_kernel,
        [
            shaped((steps, rb, channels), F32),
            shaped((steps, rb, channels), F32),
            shaped((rb, owners), F32),
            shaped((taps, channels), F32),
            shaped((1, channels), F32),
            shaped((width, channels), BF16),
        ],
        [smem(), smem(), vmem(), hbm(), hbm(), hbm(), anywhere()],
        [vmem()] * 6,
        [pltpu.SemaphoreType.DMA((3,))],
        flops=10 * steps * rb * channels,
        nbytes=12 * steps * rb * channels,
        trans=steps * rb * channels,
    )(
        key,
        prompt_of,
        step_in,
        pinned(conv_weight),
        pinned(conv_bias[None]),
        pinned(x_weight.T),
        msgs[0],
    )
    if direct:
        msgs = [msgs[0]] + [swap(msgs[k], "branch", k) for k in range(1, owners)]
    else:
        msgs = [lax.all_to_all(msgs[0], "branch", split_axis=0, concat_axis=0, tiled=True)]

    n_msgs = len(msgs)
    pair_shapes = [(1, 2 * n_state, channels)] if direct else []
    act, part, *pairs = call(
        functools.partial(project_kernel, n_msgs),
        [
            shaped((rows, channels), F32),
            shaped((rows, width), F32),
        ]
        + [shaped(s, BF16) for s in pair_shapes],
        [vmem()] * (5 + n_msgs),
        [vmem()] * (2 + len(pair_shapes)),
        flops=2 * rows * channels * width,
        nbytes=channels * width * 2 + rows * (channels + width) * 4,
        trans=rows * channels,
    )(pick, base, taps_near, bias_near, weight_near, *msgs)
    other = swap(part, "tensor", 1)
    pairs = [swap(p, "branch", 2) for p in pairs]
    distance = 2
    while distance < tensors:
        part, brief = call(
            add_kernel,
            [shaped((rows, width), F32), shaped((rows, width), BF16)],
            [vmem()] * 2,
            [vmem()] * 2,
            flops=rows * width,
            nbytes=rows * width * 14,
        )(part, other)
        other = swap(brief, "tensor", distance)
        distance *= 2

    rate, child_conv, dtw_near, dtb_near, skip_near = call(
        functools.partial(late_kernel, n_msgs, taps),
        [
            shaped((n_state, channels), F32),
            shaped((taps - 1, rb, channels), BF16),
            shaped(dt_weight.shape, BF16),
            shaped((1, channels), F32),
            shaped((1, channels), F32),
        ],
        [smem()] * 2 + [vmem()] + [hbm()] * 3 + [anywhere()] + [vmem()] * n_msgs,
        [vmem()] * 5,
        [
            pltpu.VMEM((owners, steps, channels), F32),
            pltpu.SemaphoreType.DMA((3,)),
        ],
        flops=4 * n_state * channels,
        nbytes=4 * n_state * (rb + owners) * channels,
    )(
        key,
        child_slot,
        a_log,
        pinned(dt_weight),
        pinned(dt_bias[None]),
        pinned(skip[None]),
        part,
        *msgs,
    )

    decoded, child_ssm = call(
        functools.partial(decode_kernel, n_msgs, len(pairs), taps),
        [
            shaped((rb, steps, channels), BF16),
            shaped((rb, n_state, channels), F32),
        ],
        [smem()] * 2 + [vmem()] * (9 + n_msgs + len(pairs)),
        [vmem(), anywhere()],
        [
            pltpu.VMEM((rows, channels), F32),
            pltpu.VMEM((rows, channels), F32),
            pltpu.VMEM((n_state, rows, LANES), F32),
            pltpu.VMEM((n_state, steps * rb, LANES), F32),
            pltpu.VMEM((owners, n_state, channels), F32),
            pltpu.VMEM((owners, n_state, channels), F32),
            pltpu.VMEM((steps * rb, LANES), F32),
            pltpu.SemaphoreType.DMA((rb,)),
        ],
        flops=8 * rows * n_state * channels,
        nbytes=(rb + owners) * n_state * channels * 4,
        trans=rows * n_state * channels,
    )(
        key,
        child_slot,
        pick,
        act,
        gate,
        rate,
        dtw_near,
        dtb_near,
        skip_near,
        part,
        other,
        *msgs,
        *pairs,
    )
    return (decoded, child_ssm, jnp.transpose(child_conv, (1, 0, 2)))


def solution(mesh):
    placed = (
        P(("replica", "branch"), None, "tensor"),
        P(("replica", "branch"), None, "tensor"),
        P(("replica", "branch")),
        P(("replica", "branch"), None, None, "tensor"),
        P(None, "tensor"),
        P("tensor"),
        P("tensor", None),
        P(None, "tensor"),
        P("tensor"),
        P(None, "tensor"),
        P("tensor"),
        P(("replica", "branch"), None, None),
        P(("replica", "branch")),
    )
    return jax.shard_map(
        on_device,
        mesh=mesh,
        in_specs=placed,
        out_specs=(
            P(("replica", "branch"), None, "tensor"),
            P(("replica", "branch"), None, "tensor"),
            P(("replica", "branch"), None, "tensor"),
        ),
        check_vma=False,
    )
```

time: 28.3 us -> 23.9 us (0.84)
  waiting for transfers between devices: 7.6 us -> 4.44 us
  local copies, waits for them, and re-layouts: 4.25 us -> 1.32 us
  Pallas kernels: 7.53 us -> 9.76 us
  starting transfers between devices: 7.89 us -> 7.38 us
    ppermute x6, waiting for transfers between devices: 7.6 us -> 4.44 us  [swap(): return lax.ppermute(value, axis, [(i, i ^ distance) for i in range(size)])]
    unnamed x28 -> x8, local copies, waits for them, and re-layouts: 4.25 us -> 1.32 us
    pallas_call x5 -> x6, Pallas kernels: 7.53 us -> 9.76 us  [the longest x1 4.18 us: on_device(): call(functools.partial(decode_kernel, n_msgs, len(pairs), taps), [shaped(...]
    ppermute x6, starting transfers between devices: 7.89 us -> 7.38 us  [swap(): return lax.ppermute(value, axis, [(i, i ^ distance) for i in range(size)])]
  transfers between devices with their start and end apart: 6 -> 6, of which waited for: 4 -> 2; matrix products, arithmetic and copies ran while one was open for 0% -> 0% of each run, Pallas kernels for 7% -> 17%
where the time goes in v3:
time: 23.9 us; the launch traced here: 23.6 us
  Pallas kernels  9.76 us (41%)
  starting transfers between devices  7.38 us (31%)
  waiting for transfers between devices  4.44 us (19%)
  local copies, waits for them, and re-layouts  1.32 us (6%)
  between operations  0.73 us (3%)
    ppermute x6, starting transfers between devices, swap(): return lax.ppermute(value, axis, [(i, i ^ distance) for i in range(size)])  7.38 us
    ppermute x6, waiting for transfers between devices, swap(): return lax.ppermute(value, axis, [(i, i ^ distance) for i in range(size)])  4.44 us
    pallas_call x1, Pallas kernels, on_device(): call(functools.partial(decode_kernel, n_msgs, len(pairs), taps), [shaped(...  4.18 us
    pallas_call x1, Pallas kernels, on_device(): call(functools.partial(late_kernel, n_msgs, taps), [shaped((n_state, chan...  2.25 us
    pallas_call x1, Pallas kernels, on_device(): call(prepare_kernel, [shaped((steps, rb, channels), F32), shaped((steps,...  1.66 us
    unnamed x8, local copies, waits for them, and re-layouts  1.32 us
    pallas_call x1, Pallas kernels, on_device(): call(functools.partial(pack_kernel, direct), [shaped(s, BF16) for s in ms...  1.14 us
    pallas_call x1, Pallas kernels, on_device(): call(functools.partial(project_kernel, n_msgs), [shaped((rows, channels),...  0.51 us
  transfers between devices with their start and end apart: 6, of which 2 were waited for; matrix products, arithmetic and copies ran while one was open for 0% of the time, Pallas kernels for 17%

profile of v3, /device:TPU:0, one launch (start us, length us, event | category | flops | bytes accessed | tf_op | source)
XLA Modules:
  0.0 23.6 jit_solution(8964670668336741390)
XLA Ops:
  0.6 0.0 copy-start
  0.6 1.1 %shard_map.148 = (bf16[1,24,1024]{2,1,0:T(8,128)(2,1)S(1)}, bf16[1,24,1024]{2,1,0:T(8,128)(2,1)S(1)}, bf16[1,8,1024]{2,1,0:T(8,128)(2,1)S(1)}, bf16[1,8,1024]{2,1,0:T(8,128)(2,1)S(1)}) custom-call(s32[1]{0:T(128)} %bitcast.key_ref, s32[4]{0:T(128)} %bitcast.11, s32[16]{0:T(128)} %prompt_ref.1, bf16[16,4,2,1024]{3,2,1,0:T(2,128)(2,1)} %step_ref.1, ...), custom_call_target="tpu_custom_call" | custom-call | bytes 196608 | tf_op jit(solution)/shard_map/pallas_call | solution.py:364
  1.8 3.1 %collective-permute-start = (bf16[1,24,1024]{2,1,0:T(8,128)(2,1)S(1)}, bf16[1,24,1024]{2,1,0:T(8,128)(2,1)S(1)}, u32[]{:S(2)}, u32[]{:S(2)}) collective-permute-start(bf16[1,24,1024]{2,1,0:T(8,128)(2,1)S(1)} %get-tuple-element.31), channel_id=1, source_target_pairs={{0,4},{4,0},{8,12},{12,8},{1,5},{5,1},{9,13},{13,9},{2,6},{6,2},{1... | collective-permute-start | bytes 147464 | tf_op jit(solution)/shard_map/ppermute | solution.py:56
  4.9 2.6 %collective-permute-start.1 = (bf16[1,8,1024]{2,1,0:T(8,128)(2,1)S(1)}, bf16[1,8,1024]{2,1,0:T(8,128)(2,1)S(1)}, u32[]{:S(2)}, u32[]{:S(2)}) collective-permute-start(bf16[1,8,1024]{2,1,0:T(8,128)(2,1)S(1)} %get-tuple-element.32), channel_id=1, source_target_pairs={{0,8},{4,12},{8,0},{12,4},{1,9},{5,13},{9,1},{13,5},{2,10},{6,14},... | collective-permute-start | bytes 49160 | tf_op jit(solution)/shard_map/ppermute | solution.py:56
  7.5 0.0 collective-permute-start.2
  7.5 0.0 copy-start.2
  7.5 0.0 copy-done
  7.5 0.7 %copy-done.2 = s32[16]{0:T(128)S(1)} copy-done((s32[16]{0:T(128)S(1)}, s32[16]{0:T(128)}, u32[]{:S(2)}) %copy-start.2) | copy-done | bytes 88
  8.1 1.7 %shard_map.149 = (f32[4,16,1024]{2,1,0:T(8,128)S(1)}, f32[4,16,1024]{2,1,0:T(8,128)S(1)}, f32[16,4]{1,0:T(8,128)S(1)}, f32[4,1024]{1,0:T(4,128)S(1)}, f32[1,1024...) custom-call(s32[1]{0:T(128)} %bitcast.key_ref, s32[16]{0:T(128)S(1)} %copy-done.2, bf16[16,4,2,1024]{3,2,1,0:T(2,128)(2,1)S(1)} %copy-done, ...), custom_call_target="tpu_custom_call" | custom-call | flops 655360 | bytes 786432 | tf_op jit(solution)/shard_map/pallas_call | solution.py:386
  9.8 0.0 collective-permute-done.1.rest_2_
  9.8 3.2 %collective-permute-done.2.rest_3_ = bf16[1,8,1024]{2,1,0:T(8,128)(2,1)S(1)} collective-permute-done((bf16[1,8,1024]{2,1,0:T(8,128)(2,1)S(1)}, bf16[1,8,1024]{2,1,0:T(8,128)(2,1)S(1)}, u32[]{:S(2)}, u32[]{:S(2)}) %collective-permute-start.2) | collective-permute-done | bytes 16416 | tf_op jit(solution)/shard_map/ppermute | solution.py:56
  13.0 0.0 collective-permute-done.rest_1_
  13.0 0.5 %shard_map.150 = (f32[80,1024]{1,0:T(8,128)S(1)}, f32[80,288]{1,0:T(8,128)S(1)}, bf16[1,32,1024]{2,1,0:T(8,128)(2,1)S(1)}) custom-call(f32[16,4]{1,0:T(8,128)S(1)} %get-tuple-element.26.pick_ref, f32[4,16,1024]{2,1,0:T(8,128)S(1)} %get-tuple-element.27.base_ref, f32[4,1024]{1,0:T(4,128)S(1)} %get-tuple-element.28.cw_ref, ...), custom_call_target="tpu_custom_call" | custom-call | flops 47185920 | bytes 1009664 | tf_op jit(solution)/shard_map/pallas_call | solution.py:418
  13.5 0.1 collective-permute-start.3
  13.6 0.0 copy-start.1
  13.6 0.1 collective-permute-start.5
  13.7 1.2 %collective-permute-done.3.b_ref = f32[80,288]{1,0:T(8,128)S(1)} collective-permute-done((f32[80,288]{1,0:T(8,128)S(1)}, f32[80,288]{1,0:T(8,128)S(1)}, u32[]{:S(2)}, u32[]{:S(2)}) %collective-permute-start.3) | collective-permute-done | bytes 92192 | tf_op jit(solution)/shard_map/ppermute | solution.py:56
  15.0 1.6 %collective-permute-start.4 = (bf16[80,288]{1,0:T(8,128)(2,1)S(1)}, bf16[80,288]{1,0:T(8,128)(2,1)S(1)}, u32[]{:S(2)}, u32[]{:S(2)}) collective-permute-start(bf16[80,288]{1,0:T(8,128)(2,1)S(1)} %get-tuple-element.42), channel_id=1, source_target_pairs={{0,2},{1,3},{2,0},{3,1},{4,6},{5,7},{6,4},{7,5},{8,10},{9,11},{10,... | collective-permute-start | bytes 138248 | tf_op jit(solution)/shard_map/ppermute | solution.py:56
  16.5 0.0 copy-done.1
  16.5 0.7 %copy-done.3 = s32[16]{0:T(128)S(1)} copy-done((s32[16]{0:T(128)S(1)}, s32[16]{0:T(128)}, u32[]{:S(2)}) %copy-start.3) | copy-done | bytes 88
  17.2 2.2 %shard_map.152 = (f32[16,1024]{1,0:T(8,128)S(1)}, bf16[3,16,1024]{2,1,0:T(8,128)(2,1)}, bf16[256,1024]{1,0:T(8,128)(2,1)S(1)}, f32[1,1024]{1,0:T(1,128)S(1)}, f32[1,1024]{1,0:T(1,128)S(1)}) custom-call(s32[1]{0:T(128)} %bitcast.key_ref, s32[16]{0:T(128)S(1)} %copy-done.3, f32[16,1024]{1,0:T(8,128)S(1)} %copy-done.1, bf16[256,1024]{1,0:T(8,128)(2,1)} %dtw_hbm.1, ...), custom_call_target="tpu_custom_call" | custom-call | flops 65536 | bytes 1310720 | tf_op jit(solution)/shard_map/pallas_call | solution.py:446
  19.4 0.0 collective-permute-done.5.rest_4_
  19.4 0.0 collective-permute-done.4.other_ref
  19.4 4.2 %shard_map.153 = (bf16[16,4,1024]{2,1,0:T(4,128)(2,1)}, f32[16,16,1024]{2,1,0:T(8,128)}) custom-call(s32[1]{0:T(128)} %bitcast.key_ref, s32[16]{0:T(128)S(1)} %copy-done.3, f32[16,4]{1,0:T(8,128)S(1)} %get-tuple-element.26.pick_ref, f32[80,1024]{1,0:T(8,128)S(1)} %get-tuple-element.34.act_ref, f32[4,16,1024]{2,1,0:T(8,128)S(1)} %get-tuple-element.35.gate_ref, ...), custom_call_target="tpu_custom_call" | custom-call | flops 10485760 | bytes 1310720 | tf_op jit(solution)/shard_map/pallas_call | solution.py:474
  (2 shorter events, 0.0 us)
Async XLA Ops:
  0.6 6.8 %copy-start = (bf16[16,4,2,1024]{3,2,1,0:T(2,128)(2,1)S(1)}, bf16[16,4,2,1024]{3,2,1,0:T(2,128)(2,1)}, u32[]{:S(2)}) copy-start(bf16[16,4,2,1024]{3,2,1,0:T(2,128)(2,1)} %step_ref.1) | copy-start | bytes 786436
  1.8 11.2 %collective-permute-start = (bf16[1,24,1024]{2,1,0:T(8,128)(2,1)S(1)}, bf16[1,24,1024]{2,1,0:T(8,128)(2,1)S(1)}, u32[]{:S(2)}, u32[]{:S(2)}) collective-permute-start(bf16[1,24,1024]{2,1,0:T(8,128)(2,1)S(1)} %get-tuple-element.31), channel_id=1, source_target_pairs={{0,4},{4,0},{8,12},{12,8},{1,5},{5,1},{9,13},{13,9},{2,6},{6,2},{1... | collective-permute-start | bytes 147464 | tf_op jit(solution)/shard_map/ppermute | solution.py:56
  4.9 4.9 %collective-permute-start.1 = (bf16[1,8,1024]{2,1,0:T(8,128)(2,1)S(1)}, bf16[1,8,1024]{2,1,0:T(8,128)(2,1)S(1)}, u32[]{:S(2)}, u32[]{:S(2)}) collective-permute-start(bf16[1,8,1024]{2,1,0:T(8,128)(2,1)S(1)} %get-tuple-element.32), channel_id=1, source_target_pairs={{0,8},{4,12},{8,0},{12,4},{1,9},{5,13},{9,1},{13,5},{2,10},{6,14},... | collective-permute-start | bytes 49160 | tf_op jit(solution)/shard_map/ppermute | solution.py:56
  7.5 5.5 %collective-permute-start.2 = (bf16[1,8,1024]{2,1,0:T(8,128)(2,1)S(1)}, bf16[1,8,1024]{2,1,0:T(8,128)(2,1)S(1)}, u32[]{:S(2)}, u32[]{:S(2)}) collective-permute-start(bf16[1,8,1024]{2,1,0:T(8,128)(2,1)S(1)} %get-tuple-element.33), channel_id=1, source_target_pairs={{0,12},{4,8},{8,4},{12,0},{1,13},{5,9},{9,5},{13,1},{2,14},{6,10},... | collective-permute-start | bytes 49160 | tf_op jit(solution)/shard_map/ppermute | solution.py:56
  7.5 0.7 %copy-start.2 = (s32[16]{0:T(128)S(1)}, s32[16]{0:T(128)}, u32[]{:S(2)}) copy-start(s32[16]{0:T(128)} %prompt_ref.1) | copy-start | bytes 196
  13.5 1.4 %collective-permute-start.3 = (f32[80,288]{1,0:T(8,128)S(1)}, f32[80,288]{1,0:T(8,128)S(1)}, u32[]{:S(2)}, u32[]{:S(2)}) collective-permute-start(f32[80,288]{1,0:T(8,128)S(1)} %get-tuple-element.36.a_ref), channel_id=1, source_target_pairs={{0,1},{1,0},{2,3},{3,2},{4,5},{5,4},{6,7},{7,6},{8,9},{9,8},{10,11... | collective-permute-start | bytes 276488 | tf_op jit(solution)/shard_map/ppermute | solution.py:56
  13.6 2.9 %copy-start.1 = (f32[16,1024]{1,0:T(8,128)S(1)}, f32[16,1024]{1,0:T(8,128)}, u32[]{:S(2)}) copy-start(f32[16,1024]{1,0:T(8,128)} %alog_ref.1) | copy-start | bytes 196612
  13.6 5.8 %collective-permute-start.5 = (bf16[1,32,1024]{2,1,0:T(8,128)(2,1)S(1)}, bf16[1,32,1024]{2,1,0:T(8,128)(2,1)S(1)}, u32[]{:S(2)}, u32[]{:S(2)}) collective-permute-start(bf16[1,32,1024]{2,1,0:T(8,128)(2,1)S(1)} %get-tuple-element.43), channel_id=1, source_target_pairs={{0,8},{4,12},{8,0},{12,4},{1,9},{5,13},{9,1},{13,5},{2,10},{6,14},... | collective-permute-start | bytes 196616 | tf_op jit(solution)/shard_map/ppermute | solution.py:56
  15.0 4.5 %collective-permute-start.4 = (bf16[80,288]{1,0:T(8,128)(2,1)S(1)}, bf16[80,288]{1,0:T(8,128)(2,1)S(1)}, u32[]{:S(2)}, u32[]{:S(2)}) collective-permute-start(bf16[80,288]{1,0:T(8,128)(2,1)S(1)} %get-tuple-element.42), channel_id=1, source_target_pairs={{0,2},{1,3},{2,0},{3,1},{4,6},{5,7},{6,4},{7,5},{8,10},{9,11},{10,... | collective-permute-start | bytes 138248 | tf_op jit(solution)/shard_map/ppermute | solution.py:56
  16.5 0.7 %copy-start.3 = (s32[16]{0:T(128)S(1)}, s32[16]{0:T(128)}, u32[]{:S(2)}) copy-start(s32[16]{0:T(128)} %child_ref.3) | copy-start | bytes 196

commit v4 on v3

v4 whole, which is shorter than its diff:
```python
import functools
import math

import jax
import jax.numpy as jnp
from jax import lax
from jax.experimental import pallas as pl
from jax.experimental.pallas import tpu as pltpu
from jax.sharding import PartitionSpec as P

F32 = jnp.float32
BF16 = jnp.bfloat16
LANES = 128
VMEM_LIMIT = 48 * 2**20
WEIGHT_PARTS = 6
DT_PARTS = 4
DIRECT = 4


def vmem():
    return pl.BlockSpec(memory_space=pltpu.VMEM)


def hbm():
    return pl.BlockSpec(memory_space=pltpu.HBM)


def anywhere():
    return pl.BlockSpec(memory_space=pl.ANY)


def pinned(array):
    return pltpu.with_memory_space_constraint(array, pltpu.HBM)


def shaped(shape, dtype):
    return jax.ShapeDtypeStruct(shape, dtype)


def call(kernel, outs, in_specs, out_specs, scratch=(), flops=0, nbytes=0, trans=0):
    return pl.pallas_call(
        kernel,
        out_shape=outs,
        in_specs=in_specs,
        out_specs=out_specs,
        scratch_shapes=list(scratch),
        compiler_params=pltpu.CompilerParams(vmem_limit_bytes=VMEM_LIMIT),
        cost_estimate=pl.CostEstimate(flops=flops, bytes_accessed=nbytes, transcendentals=trans),
    )


def swap(value, axis, distance):
    size = lax.axis_size(axis)
    return lax.ppermute(value, axis, [(i, i ^ distance) for i in range(size)])


def all_of(copies):
    for copy in copies:
        copy.start()
    for copy in copies:
        copy.wait()


def blocks(refs):
    return [(ref, i) for ref in refs for i in range(ref.shape[0])]


def in_parts(source, target, sems, first, count):
    rows = source.shape[0] // count
    at = [pl.ds(i * rows, rows) for i in range(count)]
    return [
        pltpu.make_async_copy(source.at[a], target.at[a], sems.at[first + i])
        for i, a in enumerate(at)
    ]


def scalar_onehot(numbers_s, key, shape):
    row_of = lax.broadcasted_iota(jnp.int32, shape, 0)
    wanted = jnp.zeros(shape, jnp.int32)
    for b in range(shape[0]):
        wanted = jnp.where(row_of == b, jnp.bitwise_xor(numbers_s[b], key), wanted)
    return (wanted == lax.broadcasted_iota(jnp.int32, shape, 1)).astype(F32)


def pick_rows(pick, rows):
    total = pick[:, 0:1] * rows[0]
    for k in range(1, len(rows)):
        total = total + pick[:, k : k + 1] * rows[k]
    return total


def pack_kernel(direct, key_hbm, rows_hbm, prompt_hbm, step_hbm, conv_hbm, ssm_hbm, *rest):
    outs, (key_s, rows_s, prompt_s, step, conv, ssm, sems) = rest[:-7], rest[-7:]
    owners = rows_hbm.shape[0]
    channels = step_hbm.shape[3]
    copies = [
        pltpu.make_async_copy(key_hbm, key_s, sems.at[4]),
        pltpu.make_async_copy(rows_hbm, rows_s, sems.at[0]),
        pltpu.make_async_copy(prompt_hbm, prompt_s, sems.at[1]),
        pltpu.make_async_copy(conv_hbm, conv, sems.at[2]),
        pltpu.make_async_copy(ssm_hbm, ssm, sems.at[3]),
    ]
    all_of(copies + in_parts(step_hbm, step, sems, 5, 4))
    key = key_s[0]
    window = conv[0].astype(F32)
    for k, (ref, i) in enumerate(blocks(outs)):
        target = jnp.bitwise_xor(key, k)
        row = jnp.maximum(rows_s[target], 0)
        xs = step[row, :, 0, :].astype(F32)
        told = jnp.bitwise_xor(prompt_s[row], target) if direct else prompt_s[row]
        pieces = [window, xs, jnp.full((1, channels), told.astype(F32), F32)]
        if ref.shape[1] > sum(p.shape[0] for p in pieces):
            pieces.append(ssm[0])
        ref[i] = jnp.concatenate(pieces, axis=0).astype(BF16)


def silu(v):
    return v / (1.0 + jnp.exp(-v))


def pair_kernel(text, own_ref, other_ref, pair_ref):
    states = [ref[0].astype(F32)[text:, :] for ref in (own_ref, other_ref)]
    pair_ref[0] = jnp.concatenate(states, axis=0).astype(BF16)


def prepare_kernel(
    key_hbm, prompt_hbm, step_ref, cw_hbm, cb_hbm, xwt_hbm, after_ref, *rest
):
    del after_ref
    base_ref, gate_ref, pick_ref, cw_ref, cb_ref, xwt_ref, key_s, prompt_s, sems = rest
    small = [
        pltpu.make_async_copy(cw_hbm, cw_ref, sems.at[0]),
        pltpu.make_async_copy(cb_hbm, cb_ref, sems.at[1]),
        pltpu.make_async_copy(key_hbm, key_s, sems.at[2]),
        pltpu.make_async_copy(prompt_hbm, prompt_s, sems.at[3]),
    ]
    large = in_parts(xwt_hbm, xwt_ref, sems, 4, WEIGHT_PARTS)
    for copy in small + large:
        copy.start()
    steps = step_ref.shape[1]
    taps = cw_hbm.shape[0]
    xs = [step_ref[:, t, 0, :].astype(F32) for t in range(steps)]
    for t in range(steps):
        gate_ref[t] = silu(step_ref[:, t, 1, :].astype(F32))
    for copy in small:
        copy.wait()
    for t in range(steps):
        total = cw_ref[taps - 1 : taps, :] * xs[t] + cb_ref[...]
        for k in range(max(0, taps - 1 - t), taps - 1):
            total = total + cw_ref[k : k + 1, :] * xs[t + k - taps + 1]
        base_ref[t] = total
    pick_ref[...] = scalar_onehot(prompt_s, key_s[0], pick_ref.shape)
    for copy in large:
        copy.wait()


def slot_onehot(numbers, owners):
    column = lax.broadcasted_iota(jnp.int32, (numbers.shape[0], owners), 1)
    return (numbers[:, :owners].astype(jnp.int32) == column).astype(F32)


def project_kernel(n_msgs, pick_ref, base_ref, cw_ref, cb_ref, xwt_ref, *rest):
    msgs, (act_ref, part_ref) = rest[:n_msgs], rest[n_msgs:]
    taps = cw_ref.shape[0]
    steps, rb, _ = base_ref.shape
    past = taps - 1
    held = [ref[i].astype(F32) for ref, i in blocks(msgs)]
    owners = len(held)
    windows = [[h[k : k + 1, :] for h in held] for k in range(past)]
    own = pick_ref[...]
    own_windows = [pick_rows(own, w) for w in windows]
    for t in range(steps):
        conv = base_ref[t]
        for k in range(past - t):
            conv = conv + cw_ref[k : k + 1, :] * own_windows[t + k]
        act_ref[t * rb : (t + 1) * rb, :] = silu(conv)

    def line_of(row):
        return jnp.concatenate([h[row : row + 1, :] for h in held], axis=0)

    slot = slot_onehot(line_of(past + steps), owners)
    line = [pick_rows(slot, w) for w in windows]
    line += [line_of(past + t) for t in range(steps)]
    row = steps * rb
    for t in range(steps):
        conv = cw_ref[past:taps, :] * line[t + past] + cb_ref[...]
        for k in range(past):
            conv = conv + cw_ref[k : k + 1, :] * line[t + k]
        act_ref[row : row + owners, :] = silu(conv)
        row += owners
    part_ref[...] = lax.dot_general(
        act_ref[...].astype(BF16),
        xwt_ref[...],
        (((1,), (1,)), ((), ())),
        preferred_element_type=F32,
    )


def fetch_kernel(
    n_msgs, steps, key_hbm, child_hbm, alog_hbm, dtw_hbm, dtb_hbm, skip_hbm, after_ref, *rest
):
    del after_ref
    msgs, rest = rest[:n_msgs], rest[n_msgs:]
    rate_ref, twin_ref, conv_ref, dtw_ref, dtb_ref, skip_ref, key_s, child_s, alog, sems = rest
    small = [
        pltpu.make_async_copy(key_hbm, key_s, sems.at[0]),
        pltpu.make_async_copy(child_hbm, child_s, sems.at[1]),
        pltpu.make_async_copy(alog_hbm, alog, sems.at[2]),
        pltpu.make_async_copy(dtb_hbm, dtb_ref, sems.at[3]),
        pltpu.make_async_copy(skip_hbm, skip_ref, sems.at[4]),
    ]
    large = in_parts(dtw_hbm, dtw_ref, sems, 5, DT_PARTS)
    for copy in small + large:
        copy.start()
    past, rb, channels = conv_ref.shape
    held = [ref[i].astype(F32) for ref, i in blocks(msgs)]
    for copy in small:
        copy.wait()
    owners = len(held)
    rate = jnp.exp(alog[...]) * (-math.log2(math.e))
    rate_ref[...] = rate
    half = (owners, channels)
    for m in range(rate.shape[0] // 2):
        two = [jnp.broadcast_to(rate[n : n + 1, :], half) for n in (2 * m, 2 * m + 1)]
        twin_ref[m] = jnp.concatenate(two, axis=0)
    pick = scalar_onehot(child_s, key_s[0], (rb, owners))
    first = past + steps - past
    for k in range(past):
        conv_ref[k] = pick_rows(pick, [h[first + k : first + k + 1, :] for h in held]).astype(BF16)
    for copy in large:
        copy.wait()


def add_kernel(a_ref, b_ref, sum_ref, short_ref):
    total = a_ref[...] + b_ref[...].astype(F32)
    sum_ref[...] = total
    short_ref[...] = total.astype(BF16)


def start_kernel(n_msgs, n_pairs, text, pick_ref, after_ref, *rest):
    del after_ref
    msgs, rest = rest[:n_msgs], rest[n_msgs:]
    pairs, (own_ref, slot_ref, state_s) = rest[:n_pairs], rest[n_pairs:]
    n_state = own_ref.shape[0]
    held = [ref[i].astype(F32) for ref, i in blocks(msgs)]
    owners = len(held)
    numbers = jnp.concatenate([h[text - 1 : text, :] for h in held], axis=0)
    states = [h[text:, :] for h in held]
    for ref in pairs:
        both = ref[0].astype(F32)
        states[1], states[3] = both[:n_state, :], both[n_state:, :]
    for k, state in enumerate(states):
        state_s[k] = state
    own = pick_ref[...]
    slot = slot_onehot(numbers, owners)

    def two(m, carry):
        picked = []
        for n in (2 * m, 2 * m + 1):
            rows = [state_s[k, pl.ds(n, 1), :] for k in range(owners)]
            own_ref[n] = pick_rows(own, rows)
            picked.append(pick_rows(slot, rows))
        slot_ref[m] = jnp.concatenate(picked, axis=0)
        return carry

    lax.fori_loop(0, n_state // 2, two, 0)


def decode_kernel(
    key_hbm,
    child_hbm,
    act_ref,
    gate_ref,
    own_ref,
    slot_ref,
    rate_ref,
    twin_ref,
    dtw_ref,
    dtb_ref,
    skip_ref,
    part_ref,
    other_ref,
    dec_ref,
    child_ssm,
    key_s,
    child_s,
    delta_s,
    gain_s,
    slot_delta_s,
    slot_gain_s,
    b_s,
    c_s,
    twin_b_s,
    slots_s,
    line_s,
    sems,
):
    scalars = [
        pltpu.make_async_copy(key_hbm, key_s, sems.at[0]),
        pltpu.make_async_copy(child_hbm, child_s, sems.at[1]),
    ]
    for copy in scalars:
        copy.start()
    rb, steps, channels = dec_ref.shape
    rank = dtw_ref.shape[0]
    n_state = rate_ref.shape[0]
    n_slots = slots_s.shape[0]
    own_rows = steps * rb
    chunks = channels // LANES

    proj = part_ref[...] + other_ref[...].astype(F32)
    delta_in = proj[:, :rank].astype(BF16)
    delta = jnp.dot(delta_in, dtw_ref[...], preferred_element_type=F32) + dtb_ref[...]
    delta = jnp.maximum(delta, 0.0) + jnp.log(1.0 + jnp.exp(-jnp.abs(delta)))
    gain = delta * act_ref[...]
    delta_s[...] = delta[:own_rows, :]
    gain_s[...] = gain[:own_rows, :]

    def column(at, n, rows):
        return jnp.broadcast_to(at[:, n : n + 1], (rows, LANES))

    for t in range(steps):
        at = slice(own_rows + t * n_slots, own_rows + (t + 1) * n_slots)
        slot_delta_s[t] = jnp.concatenate([delta[at, :]] * 2, axis=0)
        slot_gain_s[t] = jnp.concatenate([gain[at, :]] * 2, axis=0)
        twice = jnp.concatenate([proj[at, rank:]] * 2, axis=0)
        upper = lax.broadcasted_iota(jnp.int32, (2 * n_slots, LANES), 0) < n_slots
        for m in range(n_state // 2):
            twin_b_s[m, t] = jnp.where(
                upper, column(twice, 2 * m, 2 * n_slots), column(twice, 2 * m + 1, 2 * n_slots)
            )
    for n in range(n_state):
        b_s[n] = column(proj[:own_rows, rank:], n, own_rows)
        c_s[n] = column(proj[:own_rows, rank:], n_state + n, own_rows)

    def slot_chunk(chunk, carry):
        columns = pl.ds(pl.multiple_of(chunk * LANES, LANES), LANES)
        delta = [slot_delta_s[t, :, columns] for t in range(steps)]
        gain = [slot_gain_s[t, :, columns] for t in range(steps)]
        for m in range(n_state // 2):
            rate = twin_ref[m, :, columns]
            state = slot_ref[m, :, columns]
            for t in range(steps):
                state = jnp.exp2(delta[t] * rate) * state + gain[t] * twin_b_s[m, t]
            slots_s[:, 2 * m, columns] = state[:n_slots, :]
            slots_s[:, 2 * m + 1, columns] = state[n_slots:, :]
        return carry

    lax.fori_loop(0, chunks, slot_chunk, 0)
    for copy in scalars:
        copy.wait()
    copies = []
    for j in range(rb):
        at = jnp.bitwise_xor(child_s[j], key_s[0])
        copy = pltpu.make_async_copy(slots_s.at[at], child_ssm.at[j], sems.at[2 + j])
        copy.start()
        copies.append(copy)

    def own_chunk(chunk, carry):
        columns = pl.ds(pl.multiple_of(chunk * LANES, LANES), LANES)
        at = [pl.ds(t * rb, rb) for t in range(steps)]
        delta = [delta_s[a, columns] for a in at]
        gain = [gain_s[a, columns] for a in at]
        sums = [skip_ref[:, columns] * act_ref[a, columns] for a in at]
        for n in range(n_state):
            rate = rate_ref[n : n + 1, columns]
            state = own_ref[n, :, columns]
            for t in range(steps):
                state = jnp.exp2(delta[t] * rate) * state + gain[t] * b_s[n, at[t], :]
                sums[t] = sums[t] + c_s[n, at[t], :] * state
        for t in range(steps):
            line_s[pl.ds(t, rb, stride=steps), :] = sums[t] * gate_ref[t, :, columns]
        dec_ref[:, :, columns] = line_s[...].reshape(rb, steps, LANES).astype(BF16)
        return carry

    lax.fori_loop(0, chunks, own_chunk, 0)
    for copy in copies:
        copy.wait()


def on_device(
    prompt_ssm,
    prompt_conv,
    prompt_of,
    step_in,
    conv_weight,
    conv_bias,
    x_weight,
    dt_weight,
    dt_bias,
    a_log,
    skip,
    send_rows,
    child_slot,
):
    owners = lax.axis_size("branch")
    tensors = lax.axis_size("tensor")
    assert owners & (owners - 1) == 0 and tensors & (tensors - 1) == 0
    assert prompt_ssm.shape[0] == 1 and send_rows.shape[2] == 1
    rb, steps, _, channels = step_in.shape
    taps = conv_weight.shape[0]
    width = x_weight.shape[1]
    n_state = a_log.shape[0]
    rows = steps * (rb + owners)
    short = taps - 1 + steps + 1
    depth = short + n_state
    direct = owners == DIRECT
    me = lax.axis_index("branch").astype(jnp.int32).reshape(1)
    key = pinned(me if direct else jnp.zeros((1,), jnp.int32))

    if direct:
        msg_shapes = [(1, d, channels) for d in (depth, short, depth, short)]
    else:
        msg_shapes = [(owners, depth, channels)]
    msgs = call(
        functools.partial(pack_kernel, direct),
        [shaped(s, BF16) for s in msg_shapes],
        [hbm()] * 6,
        [vmem()] * len(msg_shapes),
        [
            pltpu.SMEM((1,), jnp.int32),
            pltpu.SMEM((owners,), jnp.int32),
            pltpu.SMEM((rb,), jnp.int32),
            pltpu.VMEM(step_in.shape, BF16),
            pltpu.VMEM(prompt_conv.shape, BF16),
            pltpu.VMEM(prompt_ssm.shape, F32),
            pltpu.SemaphoreType.DMA((9,)),
        ],
        nbytes=owners * depth * channels * 2,
    )(
        key,
        pinned(send_rows.reshape(owners)),
        pinned(prompt_of),
        pinned(step_in),
        pinned(prompt_conv),
        pinned(prompt_ssm),
    )
    if direct:
        own = msgs[0]
        came = {k: swap(msgs[k], "branch", k) for k in (2, 3, 1)}
        msgs = [own] + [came[k] for k in range(1, owners)]
        pair = call(
            functools.partial(pair_kernel, short),
            shaped((1, 2 * n_state, channels), BF16),
            [vmem()] * 2,
            vmem(),
            nbytes=8 * n_state * channels,
        )(msgs[0], msgs[2])
        pairs, after = [swap(pair, "branch", 1)], own
    else:
        msgs = [lax.all_to_all(msgs[0], "branch", split_axis=0, concat_axis=0, tiled=True)]
        pairs, after = [], msgs[0]
    n_msgs = len(msgs)
    base, gate, pick, taps_near, bias_near, weight_near = call(
        prepare_kernel,
        [
            shaped((steps, rb, channels), F32),
            shaped((steps, rb, channels), F32),
            shaped((rb, owners), F32),
            shaped((taps, channels), F32),
            shaped((1, channels), F32),
            shaped((width, channels), BF16),
        ],
        [hbm(), hbm(), vmem(), hbm(), hbm(), hbm(), anywhere()],
        [vmem()] * 6,
        [
            pltpu.SMEM((1,), jnp.int32),
            pltpu.SMEM((rb,), jnp.int32),
            pltpu.SemaphoreType.DMA((4 + WEIGHT_PARTS,)),
        ],
        flops=10 * steps * rb * channels,
        nbytes=12 * steps * rb * channels,
        trans=steps * rb * channels,
    )(
        key,
        pinned(prompt_of),
        step_in,
        pinned(conv_weight),
        pinned(conv_bias[None]),
        pinned(x_weight.T),
        after,
    )
    act, part = call(
        functools.partial(project_kernel, n_msgs),
        [
            shaped((rows, channels), F32),
            shaped((rows, width), F32),
        ],
        [vmem()] * (5 + n_msgs),
        [vmem()] * 2,
        flops=2 * rows * channels * width,
        nbytes=channels * width * 2 + rows * (channels + width) * 4,
        trans=rows * channels,
    )(pick, base, taps_near, bias_near, weight_near, *msgs)
    other = swap(part, "tensor", 1)
    distance = 2
    while distance < tensors:
        part, brief = call(
            add_kernel,
            [shaped((rows, width), F32), shaped((rows, width), BF16)],
            [vmem()] * 2,
            [vmem()] * 2,
            flops=rows * width,
            nbytes=rows * width * 14,
        )(part, other)
        other = swap(brief, "tensor", distance)
        distance *= 2

    rate, twin, child_conv, dtw_near, dtb_near, skip_near = call(
        functools.partial(fetch_kernel, n_msgs, steps),
        [
            shaped((n_state, channels), F32),
            shaped((n_state // 2, 2 * owners, channels), F32),
            shaped((taps - 1, rb, channels), BF16),
            shaped(dt_weight.shape, BF16),
            shaped((1, channels), F32),
            shaped((1, channels), F32),
        ],
        [hbm()] * 6 + [anywhere()] + [vmem()] * n_msgs,
        [vmem()] * 6,
        [
            pltpu.SMEM((1,), jnp.int32),
            pltpu.SMEM((rb,), jnp.int32),
            pltpu.VMEM((n_state, channels), F32),
            pltpu.SemaphoreType.DMA((5 + DT_PARTS,)),
        ],
        flops=4 * n_state * channels,
        nbytes=4 * n_state * (rb + owners) * channels,
    )(
        key,
        pinned(child_slot),
        pinned(a_log),
        pinned(dt_weight),
        pinned(dt_bias[None]),
        pinned(skip[None]),
        part,
        *msgs,
    )
    own_start, slot_start = call(
        functools.partial(start_kernel, n_msgs, len(pairs), short),
        [
            shaped((n_state, rb, channels), F32),
            shaped((n_state // 2, 2 * owners, channels), F32),
        ],
        [vmem(), anywhere()] + [vmem()] * (n_msgs + len(pairs)),
        [vmem()] * 2,
        [pltpu.VMEM((owners, n_state, channels), F32)],
        flops=2 * owners * n_state * (rb + owners) * channels,
        nbytes=4 * n_state * (rb + owners) * channels,
    )(pick, part, *msgs, *pairs)

    decoded, child_ssm = call(
        decode_kernel,
        [
            shaped((rb, steps, channels), BF16),
            shaped((rb, n_state, channels), F32),
        ],
        [hbm()] * 2 + [vmem()] * 11,
        [vmem(), anywhere()],
        [
            pltpu.SMEM((1,), jnp.int32),
            pltpu.SMEM((rb,), jnp.int32),
            pltpu.VMEM((steps * rb, channels), F32),
            pltpu.VMEM((steps * rb, channels), F32),
            pltpu.VMEM((steps, 2 * owners, channels), F32),
            pltpu.VMEM((steps, 2 * owners, channels), F32),
            pltpu.VMEM((n_state, steps * rb, LANES), F32),
            pltpu.VMEM((n_state, steps * rb, LANES), F32),
            pltpu.VMEM((n_state // 2, steps, 2 * owners, LANES), F32),
            pltpu.VMEM((owners, n_state, channels), F32),
            pltpu.VMEM((steps * rb, LANES), F32),
            pltpu.SemaphoreType.DMA((2 + rb,)),
        ],
        flops=8 * rows * n_state * channels,
        nbytes=(rb + owners) * n_state * channels * 4,
        trans=rows * n_state * channels,
    )(
        key,
        pinned(child_slot),
        act,
        gate,
        own_start,
        slot_start,
        rate,
        twin,
        dtw_near,
        dtb_near,
        skip_near,
        part,
        other,
    )
    return (decoded, child_ssm, jnp.transpose(child_conv, (1, 0, 2)))


def solution(mesh):
    placed = (
        P(("replica", "branch"), None, "tensor"),
        P(("replica", "branch"), None, "tensor"),
        P(("replica", "branch")),
        P(("replica", "branch"), None, None, "tensor"),
        P(None, "tensor"),
        P("tensor"),
        P("tensor", None),
        P(None, "tensor"),
        P("tensor"),
        P(None, "tensor"),
        P("tensor"),
        P(("replica", "branch"), None, None),
        P(("replica", "branch")),
    )
    return jax.shard_map(
        on_device,
        mesh=mesh,
        in_specs=placed,
        out_specs=(
            P(("replica", "branch"), None, "tensor"),
            P(("replica", "branch"), None, "tensor"),
            P(("replica", "branch"), None, "tensor"),
        ),
        check_vma=False,
    )
```

time: 23.9 us -> 22.7 us (0.950)
  local copies, waits for them, and re-layouts: 1.32 us -> 0.01 us
  waiting for transfers between devices: 4.44 us -> 5.51 us
  Pallas kernels: 9.76 us -> 8.86 us
    unnamed x8 -> x2, local copies, waits for them, and re-layouts: 1.32 us -> 0.01 us
    ppermute x6, waiting for transfers between devices: 4.44 us -> 5.51 us  [swap(): return lax.ppermute(value, axis, [(i, i ^ distance) for i in range(size)])]
    pallas_call x2 -> x4, Pallas kernels: 6.43 us -> 5.95 us  [the longest x1 3.08 us: on_device(): call(decode_kernel, [shaped((rb, steps, channels), BF16), shaped((rb, n_s...]
    pallas_call x1, Pallas kernels: 1.66 us -> 1.25 us  [on_device(): call(prepare_kernel, [shaped((steps, rb, channels), F32), shaped((steps,...]
  transfers between devices with their start and end apart: 6 -> 6, of which waited for: 2 -> 3; matrix products, arithmetic and copies ran while one was open for 0% -> 0% of each run, Pallas kernels for 17% -> 18%
where the time goes in v4:
time: 22.7 us; the launch traced here: 22.5 us
  Pallas kernels  8.86 us (39%)
  starting transfers between devices  7.38 us (33%)
  waiting for transfers between devices  5.51 us (24%)
  between operations  0.73 us (3%)
    ppermute x6, starting transfers between devices, swap(): return lax.ppermute(value, axis, [(i, i ^ distance) for i in range(size)])  7.38 us
    ppermute x6, waiting for transfers between devices, swap(): return lax.ppermute(value, axis, [(i, i ^ distance) for i in range(size)])  5.51 us
    pallas_call x1, Pallas kernels, on_device(): call(decode_kernel, [shaped((rb, steps, channels), BF16), shaped((rb, n_s...  3.08 us
    pallas_call x1, Pallas kernels, on_device(): call(functools.partial(fetch_kernel, n_msgs, steps), [shaped((n_state, ch...  1.89 us
    pallas_call x1, Pallas kernels, on_device(): call(prepare_kernel, [shaped((steps, rb, channels), F32), shaped((steps,...  1.25 us
    pallas_call x1, Pallas kernels, on_device(): call(functools.partial(pack_kernel, direct), [shaped(s, BF16) for s in ms...  1.15 us
    pallas_call x1, Pallas kernels, on_device(): call(functools.partial(start_kernel, n_msgs, len(pairs), short), [shaped(...  0.97 us
    pallas_call x1, Pallas kernels, on_device(): call(functools.partial(project_kernel, n_msgs), [shaped((rows, channels),...  0.5 us
  transfers between devices with their start and end apart: 6, of which 3 were waited for; matrix products, arithmetic and copies ran while one was open for 0% of the time, Pallas kernels for 18%

profile of v4, /device:TPU:0, one launch (start us, length us, event | category | flops | bytes accessed | tf_op | source)
XLA Modules:
  0.0 22.5 jit_solution(12452322488651760405)
XLA Ops:
  0.6 0.0 copy-start
  0.6 1.1 %shard_map.148 = (bf16[1,24,1024]{2,1,0:T(8,128)(2,1)S(1)}, bf16[1,8,1024]{2,1,0:T(8,128)(2,1)S(1)}, bf16[1,24,1024]{2,1,0:T(8,128)(2,1)S(1)}, bf16[1,8,1024]{2,1,0:T(8,128)(2,1)S(1)}) custom-call(s32[1]{0:T(128)} %bitcast.key_hbm, s32[4]{0:T(128)} %bitcast.11, s32[16]{0:T(128)} %prompt_hbm.3, bf16[16,4,2,1024]{3,2,1,0:T(2,128)(2,1)} %step_ref.1, ...), custom_call_target="tpu_custom_call" | custom-call | bytes 196608 | tf_op jit(solution)/shard_map/pallas_call | solution.py:415
  1.8 4.1 %collective-permute-start.1 = (bf16[1,24,1024]{2,1,0:T(8,128)(2,1)S(1)}, bf16[1,24,1024]{2,1,0:T(8,128)(2,1)S(1)}, u32[]{:S(2)}, u32[]{:S(2)}) collective-permute-start(bf16[1,24,1024]{2,1,0:T(8,128)(2,1)S(1)} %get-tuple-element.34), channel_id=1, source_target_pairs={{0,8},{4,12},{8,0},{12,4},{1,9},{5,13},{9,1},{13,5},{2,10},{6,14},... | collective-permute-start | bytes 147464 | tf_op jit(solution)/shard_map/ppermute | solution.py:54
  5.9 1.6 %collective-permute-start = (bf16[1,8,1024]{2,1,0:T(8,128)(2,1)S(1)}, bf16[1,8,1024]{2,1,0:T(8,128)(2,1)S(1)}, u32[]{:S(2)}, u32[]{:S(2)}) collective-permute-start(bf16[1,8,1024]{2,1,0:T(8,128)(2,1)S(1)} %get-tuple-element.33), channel_id=1, source_target_pairs={{0,4},{4,0},{8,12},{12,8},{1,5},{5,1},{9,13},{13,9},{2,6},{6,2},{1... | collective-permute-start | bytes 49160 | tf_op jit(solution)/shard_map/ppermute | solution.py:54
  7.5 0.0 collective-permute-start.2
  7.5 0.0 copy-done
  7.5 1.2 %shard_map.149 = (f32[4,16,1024]{2,1,0:T(8,128)S(1)}, f32[4,16,1024]{2,1,0:T(8,128)S(1)}, f32[16,4]{1,0:T(8,128)S(1)}, f32[4,1024]{1,0:T(4,128)S(1)}, f32[1,1024...) custom-call(s32[1]{0:T(128)} %bitcast.key_hbm, s32[16]{0:T(128)} %prompt_hbm.3, bf16[16,4,2,1024]{3,2,1,0:T(2,128)(2,1)S(1)} %copy-done, ...), custom_call_target="tpu_custom_call" | custom-call | flops 655360 | bytes 786432 | tf_op jit(solution)/shard_map/pallas_call | solution.py:454
  8.7 0.9 %collective-permute-done.rest_1_ = bf16[1,8,1024]{2,1,0:T(8,128)(2,1)S(1)} collective-permute-done((bf16[1,8,1024]{2,1,0:T(8,128)(2,1)S(1)}, bf16[1,8,1024]{2,1,0:T(8,128)(2,1)S(1)}, u32[]{:S(2)}, u32[]{:S(2)}) %collective-permute-start) | collective-permute-done | bytes 16416 | tf_op jit(solution)/shard_map/ppermute | solution.py:54
  9.6 3.4 %collective-permute-done.2.rest_3_ = bf16[1,8,1024]{2,1,0:T(8,128)(2,1)S(1)} collective-permute-done((bf16[1,8,1024]{2,1,0:T(8,128)(2,1)S(1)}, bf16[1,8,1024]{2,1,0:T(8,128)(2,1)S(1)}, u32[]{:S(2)}, u32[]{:S(2)}) %collective-permute-start.2) | collective-permute-done | bytes 16416 | tf_op jit(solution)/shard_map/ppermute | solution.py:54
  13.0 0.0 collective-permute-done.1.rest_2_.other_ref
  13.0 0.5 %shard_map.150 = (f32[80,1024]{1,0:T(8,128)S(1)}, f32[80,288]{1,0:T(8,128)S(1)}) custom-call(f32[16,4]{1,0:T(8,128)S(1)} %get-tuple-element.28.pick_ref, f32[4,16,1024]{2,1,0:T(8,128)S(1)} %get-tuple-element.29.base_ref, f32[4,1024]{1,0:T(4,128)S(1)} %get-tuple-element.30.cw_ref, f32[1,1024]{1,0:T(1,128)S(1)} %get-tuple-element.31.cb_ref, ...), custom_call_target="tpu_custom_call" | custom-call | flops 47185920 | bytes 1009664 | tf_op jit(solution)/shard_map/pallas_call | solution.py:483
  13.5 0.1 collective-permute-start.3
  13.6 0.1 collective-permute-start.4
  13.7 1.2 %collective-permute-done.3.b_ref = f32[80,288]{1,0:T(8,128)S(1)} collective-permute-done((f32[80,288]{1,0:T(8,128)S(1)}, f32[80,288]{1,0:T(8,128)S(1)}, u32[]{:S(2)}, u32[]{:S(2)}) %collective-permute-start.3) | collective-permute-done | bytes 92192 | tf_op jit(solution)/shard_map/ppermute | solution.py:54
  14.9 1.6 %collective-permute-start.5 = (bf16[80,288]{1,0:T(8,128)(2,1)S(1)}, bf16[80,288]{1,0:T(8,128)(2,1)S(1)}, u32[]{:S(2)}, u32[]{:S(2)}) collective-permute-start(bf16[80,288]{1,0:T(8,128)(2,1)S(1)} %get-tuple-element.47), channel_id=1, source_target_pairs={{0,2},{1,3},{2,0},{3,1},{4,6},{5,7},{6,4},{7,5},{8,10},{9,11},{10,... | collective-permute-start | bytes 138248 | tf_op jit(solution)/shard_map/ppermute | solution.py:54
  16.5 1.9 %shard_map.154 = (f32[16,1024]{1,0:T(8,128)S(1)}, f32[8,8,1024]{2,1,0:T(8,128)S(1)}, bf16[3,16,1024]{2,1,0:T(8,128)(2,1)}, bf16[256,1024]{1,0:T(8,128)(2,1)S(1)}...) custom-call(s32[1]{0:T(128)} %bitcast.key_hbm, s32[16]{0:T(128)} %child_hbm.3, f32[16,1024]{1,0:T(8,128)} %alog_hbm.1, ...), custom_call_target="tpu_custom_call" | custom-call | flops 65536 | bytes 1310720 | tf_op jit(solution)/shard_map/pallas_call | solution.py:509
  18.4 0.0 collective-permute-done.4.rest_4_
  18.4 1.0 %shard_map.153 = (f32[16,16,1024]{2,1,0:T(8,128)S(1)}, f32[8,8,1024]{2,1,0:T(8,128)S(1)}) custom-call(f32[16,4]{1,0:T(8,128)S(1)} %get-tuple-element.28.pick_ref, f32[80,288]{1,0:T(8,128)S(1)} %get-tuple-element.39.after_ref.part_ref, bf16[1,24,1024]{2,1,0:T(8,128)(2,1)S(1)} %get-tuple-element.27.after_ref.rest_0_.own_ref, ...), custom_call_target="tpu_custom_call" | custom-call | flops 2621440 | bytes 1310720 | tf_op jit(solution)/shard_map/pallas_call | solution.py:539
  19.4 0.0 collective-permute-done.5.other_ref
  19.4 3.1 %shard_map.155 = (bf16[16,4,1024]{2,1,0:T(4,128)(2,1)}, f32[16,16,1024]{2,1,0:T(8,128)}) custom-call(s32[1]{0:T(128)} %bitcast.key_hbm, s32[16]{0:T(128)} %child_hbm.3, f32[80,1024]{1,0:T(8,128)S(1)} %get-tuple-element.36.act_ref, f32[4,16,1024]{2,1,0:T(8,128)S(1)} %get-tuple-element.37.gate_ref, f32[16,16,1024]{2,1,0:T(8,128)S(1)} %get-tuple-element.40.own_ref, ...), custom_call_target="tpu_custom_call" | custom-call | flops 10485760 | bytes 1310720 | tf_op jit(solution)/shard_map/pallas_call | solution.py:552
  (2 shorter events, 0.0 us)
Async XLA Ops:
  0.6 6.9 %copy-start = (bf16[16,4,2,1024]{3,2,1,0:T(2,128)(2,1)S(1)}, bf16[16,4,2,1024]{3,2,1,0:T(2,128)(2,1)}, u32[]{:S(2)}) copy-start(bf16[16,4,2,1024]{3,2,1,0:T(2,128)(2,1)} %step_ref.1) | copy-start | bytes 786436
  1.8 11.2 %collective-permute-start.1 = (bf16[1,24,1024]{2,1,0:T(8,128)(2,1)S(1)}, bf16[1,24,1024]{2,1,0:T(8,128)(2,1)S(1)}, u32[]{:S(2)}, u32[]{:S(2)}) collective-permute-start(bf16[1,24,1024]{2,1,0:T(8,128)(2,1)S(1)} %get-tuple-element.34), channel_id=1, source_target_pairs={{0,8},{4,12},{8,0},{12,4},{1,9},{5,13},{9,1},{13,5},{2,10},{6,14},... | collective-permute-start | bytes 147464 | tf_op jit(solution)/shard_map/ppermute | solution.py:54
  5.9 3.7 %collective-permute-start = (bf16[1,8,1024]{2,1,0:T(8,128)(2,1)S(1)}, bf16[1,8,1024]{2,1,0:T(8,128)(2,1)S(1)}, u32[]{:S(2)}, u32[]{:S(2)}) collective-permute-start(bf16[1,8,1024]{2,1,0:T(8,128)(2,1)S(1)} %get-tuple-element.33), channel_id=1, source_target_pairs={{0,4},{4,0},{8,12},{12,8},{1,5},{5,1},{9,13},{13,9},{2,6},{6,2},{1... | collective-permute-start | bytes 49160 | tf_op jit(solution)/shard_map/ppermute | solution.py:54
  7.5 5.5 %collective-permute-start.2 = (bf16[1,8,1024]{2,1,0:T(8,128)(2,1)S(1)}, bf16[1,8,1024]{2,1,0:T(8,128)(2,1)S(1)}, u32[]{:S(2)}, u32[]{:S(2)}) collective-permute-start(bf16[1,8,1024]{2,1,0:T(8,128)(2,1)S(1)} %get-tuple-element.35), channel_id=1, source_target_pairs={{0,12},{4,8},{8,4},{12,0},{1,13},{5,9},{9,5},{13,1},{2,14},{6,10},... | collective-permute-start | bytes 49160 | tf_op jit(solution)/shard_map/ppermute | solution.py:54
  13.5 1.4 %collective-permute-start.3 = (f32[80,288]{1,0:T(8,128)S(1)}, f32[80,288]{1,0:T(8,128)S(1)}, u32[]{:S(2)}, u32[]{:S(2)}) collective-permute-start(f32[80,288]{1,0:T(8,128)S(1)} %get-tuple-element.38.a_ref), channel_id=1, source_target_pairs={{0,1},{1,0},{2,3},{3,2},{4,5},{5,4},{6,7},{7,6},{8,9},{9,8},{10,11... | collective-permute-start | bytes 276488 | tf_op jit(solution)/shard_map/ppermute | solution.py:54
  13.6 4.8 %collective-permute-start.4 = (bf16[1,32,1024]{2,1,0:T(8,128)(2,1)S(1)}, bf16[1,32,1024]{2,1,0:T(8,128)(2,1)S(1)}, u32[]{:S(2)}, u32[]{:S(2)}) collective-permute-start(bf16[1,32,1024]{2,1,0:T(8,128)(2,1)S(1)} %shard_map.152), channel_id=1, source_target_pairs={{0,4},{4,0},{8,12},{12,8},{1,5},{5,1},{9,13},{13,9},{2,6},{6,2},{1... | collective-permute-start | bytes 196616 | tf_op jit(solution)/shard_map/ppermute | solution.py:54
  14.9 4.4 %collective-permute-start.5 = (bf16[80,288]{1,0:T(8,128)(2,1)S(1)}, bf16[80,288]{1,0:T(8,128)(2,1)S(1)}, u32[]{:S(2)}, u32[]{:S(2)}) collective-permute-start(bf16[80,288]{1,0:T(8,128)(2,1)S(1)} %get-tuple-element.47), channel_id=1, source_target_pairs={{0,2},{1,3},{2,0},{3,1},{4,6},{5,7},{6,4},{7,5},{8,10},{9,11},{10,... | collective-permute-start | bytes 138248 | tf_op jit(solution)/shard_map/ppermute | solution.py:54

commit v5 on v4

--- a/solution.py
+++ b/solution.py
@@ -15,6 +15,7 @@
 WEIGHT_PARTS = 6
 DT_PARTS = 4
 DIRECT = 4
+ORDER = (0, 2, 3, 1)
 
 
 def vmem():
@@ -62,6 +63,8 @@
 
 
 def blocks(refs):
+    if len(refs) == DIRECT:
+        refs = [refs[ORDER.index(k)] for k in range(DIRECT)]
     return [(ref, i) for ref in refs for i in range(ref.shape[0])]
 
 
@@ -409,7 +412,7 @@
     key = pinned(me if direct else jnp.zeros((1,), jnp.int32))
 
     if direct:
-        msg_shapes = [(1, d, channels) for d in (depth, short, depth, short)]
+        msg_shapes = [(1, depth if k in (0, 2) else short, channels) for k in ORDER]
     else:
         msg_shapes = [(owners, depth, channels)]
     msgs = call(
@@ -437,15 +440,14 @@
     )
     if direct:
         own = msgs[0]
-        came = {k: swap(msgs[k], "branch", k) for k in (2, 3, 1)}
-        msgs = [own] + [came[k] for k in range(1, owners)]
+        msgs = [own] + [swap(msgs[i], "branch", ORDER[i]) for i in range(1, owners)]
         pair = call(
             functools.partial(pair_kernel, short),
             shaped((1, 2 * n_state, channels), BF16),
             [vmem()] * 2,
             vmem(),
             nbytes=8 * n_state * channels,
-        )(msgs[0], msgs[2])
+        )(own, msgs[ORDER.index(2)])
         pairs, after = [swap(pair, "branch", 1)], own
     else:
         msgs = [lax.all_to_all(msgs[0], "branch", split_axis=0, concat_axis=0, tiled=True)]

time: 22.7 us -> 21.2 us (0.934)
  waiting for transfers between devices: 5.51 us -> 3.94 us
    ppermute x6, waiting for transfers between devices: 5.51 us -> 3.94 us  [swap(): return lax.ppermute(value, axis, [(i, i ^ distance) for i in range(size)])]
  transfers between devices with their start and end apart: 6 -> 6, of which waited for: 3 -> 2; matrix products, arithmetic and copies ran while one was open for 0% -> 0% of each run, Pallas kernels for 18% -> 20%
where the time goes in v5:
time: 21.2 us; the launch traced here: 20.9 us
  Pallas kernels  8.87 us (42%)
  starting transfers between devices  7.38 us (35%)
  waiting for transfers between devices  3.94 us (19%)
  between operations  0.73 us (3%)
    ppermute x6, starting transfers between devices, swap(): return lax.ppermute(value, axis, [(i, i ^ distance) for i in range(size)])  7.38 us
    ppermute x6, waiting for transfers between devices, swap(): return lax.ppermute(value, axis, [(i, i ^ distance) for i in range(size)])  3.94 us
    pallas_call x1, Pallas kernels, on_device(): call(decode_kernel, [shaped((rb, steps, channels), BF16), shaped((rb, n_s...  3.09 us
    pallas_call x1, Pallas kernels, on_device(): call(functools.partial(fetch_kernel, n_msgs, steps), [shaped((n_state, ch...  1.89 us
    pallas_call x1, Pallas kernels, on_device(): call(prepare_kernel, [shaped((steps, rb, channels), F32), shaped((steps,...  1.25 us
    pallas_call x1, Pallas kernels, on_device(): call(functools.partial(pack_kernel, direct), [shaped(s, BF16) for s in ms...  1.15 us
    pallas_call x1, Pallas kernels, on_device(): call(functools.partial(start_kernel, n_msgs, len(pairs), short), [shaped(...  0.97 us
    pallas_call x1, Pallas kernels, on_device(): call(functools.partial(project_kernel, n_msgs), [shaped((rows, channels),...  0.5 us
  transfers between devices with their start and end apart: 6, of which 2 were waited for; matrix products, arithmetic and copies ran while one was open for 0% of the time, Pallas kernels for 20%

profile of v5, /device:TPU:0, one launch (start us, length us, event | category | flops | bytes accessed | tf_op | source)
XLA Modules:
  0.0 20.9 jit_solution(3100599098736108376)
XLA Ops:
  0.6 0.0 copy-start
  0.6 1.1 %shard_map.148 = (bf16[1,24,1024]{2,1,0:T(8,128)(2,1)S(1)}, bf16[1,24,1024]{2,1,0:T(8,128)(2,1)S(1)}, bf16[1,8,1024]{2,1,0:T(8,128)(2,1)S(1)}, bf16[1,8,1024]{2,1,0:T(8,128)(2,1)S(1)}) custom-call(s32[1]{0:T(128)} %bitcast.key_hbm, s32[4]{0:T(128)} %bitcast.11, s32[16]{0:T(128)} %prompt_hbm.3, bf16[16,4,2,1024]{3,2,1,0:T(2,128)(2,1)} %step_ref.1, ...), custom_call_target="tpu_custom_call" | custom-call | bytes 196608 | tf_op jit(solution)/shard_map/pallas_call | solution.py:418
  1.8 4.1 %collective-permute-start = (bf16[1,24,1024]{2,1,0:T(8,128)(2,1)S(1)}, bf16[1,24,1024]{2,1,0:T(8,128)(2,1)S(1)}, u32[]{:S(2)}, u32[]{:S(2)}) collective-permute-start(bf16[1,24,1024]{2,1,0:T(8,128)(2,1)S(1)} %get-tuple-element.33), channel_id=1, source_target_pairs={{0,8},{4,12},{8,0},{12,4},{1,9},{5,13},{9,1},{13,5},{2,10},{6,14},... | collective-permute-start | bytes 147464 | tf_op jit(solution)/shard_map/ppermute | solution.py:55
  5.9 1.3 %collective-permute-start.1 = (bf16[1,8,1024]{2,1,0:T(8,128)(2,1)S(1)}, bf16[1,8,1024]{2,1,0:T(8,128)(2,1)S(1)}, u32[]{:S(2)}, u32[]{:S(2)}) collective-permute-start(bf16[1,8,1024]{2,1,0:T(8,128)(2,1)S(1)} %get-tuple-element.34), channel_id=1, source_target_pairs={{0,12},{4,8},{8,4},{12,0},{1,13},{5,9},{9,5},{13,1},{2,14},{6,10},... | collective-permute-start | bytes 49160 | tf_op jit(solution)/shard_map/ppermute | solution.py:55
  7.3 0.2 %collective-permute-start.2 = (bf16[1,8,1024]{2,1,0:T(8,128)(2,1)S(1)}, bf16[1,8,1024]{2,1,0:T(8,128)(2,1)S(1)}, u32[]{:S(2)}, u32[]{:S(2)}) collective-permute-start(bf16[1,8,1024]{2,1,0:T(8,128)(2,1)S(1)} %get-tuple-element.35), channel_id=1, source_target_pairs={{0,4},{4,0},{8,12},{12,8},{1,5},{5,1},{9,13},{13,9},{2,6},{6,2},{1... | collective-permute-start | bytes 49160 | tf_op jit(solution)/shard_map/ppermute | solution.py:55
  7.5 0.0 copy-done
  7.5 1.2 %shard_map.149 = (f32[4,16,1024]{2,1,0:T(8,128)S(1)}, f32[4,16,1024]{2,1,0:T(8,128)S(1)}, f32[16,4]{1,0:T(8,128)S(1)}, f32[4,1024]{1,0:T(4,128)S(1)}, f32[1,1024...) custom-call(s32[1]{0:T(128)} %bitcast.key_hbm, s32[16]{0:T(128)} %prompt_hbm.3, bf16[16,4,2,1024]{3,2,1,0:T(2,128)(2,1)S(1)} %copy-done, ...), custom_call_target="tpu_custom_call" | custom-call | flops 655360 | bytes 786432 | tf_op jit(solution)/shard_map/pallas_call | solution.py:456
  8.7 2.7 %collective-permute-done.1.rest_2_ = bf16[1,8,1024]{2,1,0:T(8,128)(2,1)S(1)} collective-permute-done((bf16[1,8,1024]{2,1,0:T(8,128)(2,1)S(1)}, bf16[1,8,1024]{2,1,0:T(8,128)(2,1)S(1)}, u32[]{:S(2)}, u32[]{:S(2)}) %collective-permute-start.1) | collective-permute-done | bytes 16416 | tf_op jit(solution)/shard_map/ppermute | solution.py:55
  11.4 0.0 collective-permute-done.2.rest_3_
  11.4 0.0 collective-permute-done.rest_1_.other_ref
  11.4 0.5 %shard_map.150 = (f32[80,1024]{1,0:T(8,128)S(1)}, f32[80,288]{1,0:T(8,128)S(1)}) custom-call(f32[16,4]{1,0:T(8,128)S(1)} %get-tuple-element.28.pick_ref, f32[4,16,1024]{2,1,0:T(8,128)S(1)} %get-tuple-element.29.base_ref, f32[4,1024]{1,0:T(4,128)S(1)} %get-tuple-element.30.cw_ref, f32[1,1024]{1,0:T(1,128)S(1)} %get-tuple-element.31.cb_ref, ...), custom_call_target="tpu_custom_call" | custom-call | flops 47185920 | bytes 1009664 | tf_op jit(solution)/shard_map/pallas_call | solution.py:485
  12.0 0.1 collective-permute-start.3
  12.0 0.1 collective-permute-start.4
  12.1 1.2 %collective-permute-done.3.b_ref = f32[80,288]{1,0:T(8,128)S(1)} collective-permute-done((f32[80,288]{1,0:T(8,128)S(1)}, f32[80,288]{1,0:T(8,128)S(1)}, u32[]{:S(2)}, u32[]{:S(2)}) %collective-permute-start.3) | collective-permute-done | bytes 92192 | tf_op jit(solution)/shard_map/ppermute | solution.py:55
  13.4 1.6 %collective-permute-start.5 = (bf16[80,288]{1,0:T(8,128)(2,1)S(1)}, bf16[80,288]{1,0:T(8,128)(2,1)S(1)}, u32[]{:S(2)}, u32[]{:S(2)}) collective-permute-start(bf16[80,288]{1,0:T(8,128)(2,1)S(1)} %get-tuple-element.47), channel_id=1, source_target_pairs={{0,2},{1,3},{2,0},{3,1},{4,6},{5,7},{6,4},{7,5},{8,10},{9,11},{10,... | collective-permute-start | bytes 138248 | tf_op jit(solution)/shard_map/ppermute | solution.py:55
  14.9 1.9 %shard_map.154 = (f32[16,1024]{1,0:T(8,128)S(1)}, f32[8,8,1024]{2,1,0:T(8,128)S(1)}, bf16[3,16,1024]{2,1,0:T(8,128)(2,1)}, bf16[256,1024]{1,0:T(8,128)(2,1)S(1)}...) custom-call(s32[1]{0:T(128)} %bitcast.key_hbm, s32[16]{0:T(128)} %child_hbm.3, f32[16,1024]{1,0:T(8,128)} %alog_hbm.1, ...), custom_call_target="tpu_custom_call" | custom-call | flops 65536 | bytes 1310720 | tf_op jit(solution)/shard_map/pallas_call | solution.py:511
  16.8 0.0 collective-permute-done.4.rest_4_
  16.8 1.0 %shard_map.153 = (f32[16,16,1024]{2,1,0:T(8,128)S(1)}, f32[8,8,1024]{2,1,0:T(8,128)S(1)}) custom-call(f32[16,4]{1,0:T(8,128)S(1)} %get-tuple-element.28.pick_ref, f32[80,288]{1,0:T(8,128)S(1)} %get-tuple-element.39.after_ref.part_ref, bf16[1,24,1024]{2,1,0:T(8,128)(2,1)S(1)} %get-tuple-element.27.after_ref.rest_0_.own_ref, ...), custom_call_target="tpu_custom_call" | custom-call | flops 2621440 | bytes 1310720 | tf_op jit(solution)/shard_map/pallas_call | solution.py:541
  17.8 0.0 collective-permute-done.5.other_ref
  17.8 3.1 %shard_map.155 = (bf16[16,4,1024]{2,1,0:T(4,128)(2,1)}, f32[16,16,1024]{2,1,0:T(8,128)}) custom-call(s32[1]{0:T(128)} %bitcast.key_hbm, s32[16]{0:T(128)} %child_hbm.3, f32[80,1024]{1,0:T(8,128)S(1)} %get-tuple-element.36.act_ref, f32[4,16,1024]{2,1,0:T(8,128)S(1)} %get-tuple-element.37.gate_ref, f32[16,16,1024]{2,1,0:T(8,128)S(1)} %get-tuple-element.40.own_ref, ...), custom_call_target="tpu_custom_call" | custom-call | flops 10485760 | bytes 1310720 | tf_op jit(solution)/shard_map/pallas_call | solution.py:554
  (2 shorter events, 0.0 us)
Async XLA Ops:
  0.6 6.9 %copy-start = (bf16[16,4,2,1024]{3,2,1,0:T(2,128)(2,1)S(1)}, bf16[16,4,2,1024]{3,2,1,0:T(2,128)(2,1)}, u32[]{:S(2)}) copy-start(bf16[16,4,2,1024]{3,2,1,0:T(2,128)(2,1)} %step_ref.1) | copy-start | bytes 786436
  1.8 9.6 %collective-permute-start = (bf16[1,24,1024]{2,1,0:T(8,128)(2,1)S(1)}, bf16[1,24,1024]{2,1,0:T(8,128)(2,1)S(1)}, u32[]{:S(2)}, u32[]{:S(2)}) collective-permute-start(bf16[1,24,1024]{2,1,0:T(8,128)(2,1)S(1)} %get-tuple-element.33), channel_id=1, source_target_pairs={{0,8},{4,12},{8,0},{12,4},{1,9},{5,13},{9,1},{13,5},{2,10},{6,14},... | collective-permute-start | bytes 147464 | tf_op jit(solution)/shard_map/ppermute | solution.py:55
  5.9 5.5 %collective-permute-start.1 = (bf16[1,8,1024]{2,1,0:T(8,128)(2,1)S(1)}, bf16[1,8,1024]{2,1,0:T(8,128)(2,1)S(1)}, u32[]{:S(2)}, u32[]{:S(2)}) collective-permute-start(bf16[1,8,1024]{2,1,0:T(8,128)(2,1)S(1)} %get-tuple-element.34), channel_id=1, source_target_pairs={{0,12},{4,8},{8,4},{12,0},{1,13},{5,9},{9,5},{13,1},{2,14},{6,10},... | collective-permute-start | bytes 49160 | tf_op jit(solution)/shard_map/ppermute | solution.py:55
  7.3 4.2 %collective-permute-start.2 = (bf16[1,8,1024]{2,1,0:T(8,128)(2,1)S(1)}, bf16[1,8,1024]{2,1,0:T(8,128)(2,1)S(1)}, u32[]{:S(2)}, u32[]{:S(2)}) collective-permute-start(bf16[1,8,1024]{2,1,0:T(8,128)(2,1)S(1)} %get-tuple-element.35), channel_id=1, source_target_pairs={{0,4},{4,0},{8,12},{12,8},{1,5},{5,1},{9,13},{13,9},{2,6},{6,2},{1... | collective-permute-start | bytes 49160 | tf_op jit(solution)/shard_map/ppermute | solution.py:55
  12.0 1.4 %collective-permute-start.3 = (f32[80,288]{1,0:T(8,128)S(1)}, f32[80,288]{1,0:T(8,128)S(1)}, u32[]{:S(2)}, u32[]{:S(2)}) collective-permute-start(f32[80,288]{1,0:T(8,128)S(1)} %get-tuple-element.38.a_ref), channel_id=1, source_target_pairs={{0,1},{1,0},{2,3},{3,2},{4,5},{5,4},{6,7},{7,6},{8,9},{9,8},{10,11... | collective-permute-start | bytes 276488 | tf_op jit(solution)/shard_map/ppermute | solution.py:55
  12.0 4.8 %collective-permute-start.4 = (bf16[1,32,1024]{2,1,0:T(8,128)(2,1)S(1)}, bf16[1,32,1024]{2,1,0:T(8,128)(2,1)S(1)}, u32[]{:S(2)}, u32[]{:S(2)}) collective-permute-start(bf16[1,32,1024]{2,1,0:T(8,128)(2,1)S(1)} %shard_map.152), channel_id=1, source_target_pairs={{0,4},{4,0},{8,12},{12,8},{1,5},{5,1},{9,13},{13,9},{2,6},{6,2},{1... | collective-permute-start | bytes 196616 | tf_op jit(solution)/shard_map/ppermute | solution.py:55
  13.4 4.4 %collective-permute-start.5 = (bf16[80,288]{1,0:T(8,128)(2,1)S(1)}, bf16[80,288]{1,0:T(8,128)(2,1)S(1)}, u32[]{:S(2)}, u32[]{:S(2)}) collective-permute-start(bf16[80,288]{1,0:T(8,128)(2,1)S(1)} %get-tuple-element.47), channel_id=1, source_target_pairs={{0,2},{1,3},{2,0},{3,1},{4,6},{5,7},{6,4},{7,5},{8,10},{9,11},{10,... | collective-permute-start | bytes 138248 | tf_op jit(solution)/shard_map/ppermute | solution.py:55

commit v6 on v5

--- a/solution.py
+++ b/solution.py
@@ -111,7 +111,7 @@
         row = jnp.maximum(rows_s[target], 0)
         xs = step[row, :, 0, :].astype(F32)
         told = jnp.bitwise_xor(prompt_s[row], target) if direct else prompt_s[row]
-        pieces = [window, xs, jnp.full((1, channels), told.astype(F32), F32)]
+        pieces = [xs, window, jnp.full((1, channels), told.astype(F32), F32)]
         if ref.shape[1] > sum(p.shape[0] for p in pieces):
             pieces.append(ssm[0])
         ref[i] = jnp.concatenate(pieces, axis=0).astype(BF16)
@@ -127,17 +127,50 @@
 
 
 def prepare_kernel(
-    key_hbm, prompt_hbm, step_ref, cw_hbm, cb_hbm, xwt_hbm, after_ref, *rest
+    key_hbm,
+    prompt_hbm,
+    step_ref,
+    cw_hbm,
+    cb_hbm,
+    xwt_hbm,
+    alog_hbm,
+    dtw_hbm,
+    dtb_hbm,
+    skip_hbm,
+    after_ref,
+    base_ref,
+    gate_ref,
+    pick_ref,
+    cw_ref,
+    cb_ref,
+    xwt_ref,
+    rate_ref,
+    twin_ref,
+    dtw_ref,
+    dtb_ref,
+    skip_ref,
+    key_s,
+    prompt_s,
+    alog,
+    sems,
 ):
     del after_ref
-    base_ref, gate_ref, pick_ref, cw_ref, cb_ref, xwt_ref, key_s, prompt_s, sems = rest
     small = [
-        pltpu.make_async_copy(cw_hbm, cw_ref, sems.at[0]),
-        pltpu.make_async_copy(cb_hbm, cb_ref, sems.at[1]),
-        pltpu.make_async_copy(key_hbm, key_s, sems.at[2]),
-        pltpu.make_async_copy(prompt_hbm, prompt_s, sems.at[3]),
+        pltpu.make_async_copy(source, target, sems.at[i])
+        for i, (source, target) in enumerate(
+            (
+                (cw_hbm, cw_ref),
+                (cb_hbm, cb_ref),
+                (key_hbm, key_s),
+                (prompt_hbm, prompt_s),
+                (alog_hbm, alog),
+                (dtb_hbm, dtb_ref),
+                (skip_hbm, skip_ref),
+            )
+        )
     ]
-    large = in_parts(xwt_hbm, xwt_ref, sems, 4, WEIGHT_PARTS)
+    large = in_parts(xwt_hbm, xwt_ref, sems, len(small), WEIGHT_PARTS)
+    large += in_parts(dtw_hbm, dtw_ref, sems, len(small) + WEIGHT_PARTS, DT_PARTS)
     for copy in small + large:
         copy.start()
     steps = step_ref.shape[1]
@@ -153,6 +186,12 @@
             total = total + cw_ref[k : k + 1, :] * xs[t + k - taps + 1]
         base_ref[t] = total
     pick_ref[...] = scalar_onehot(prompt_s, key_s[0], pick_ref.shape)
+    rate = jnp.exp(alog[...]) * (-math.log2(math.e))
+    rate_ref[...] = rate
+    half = (twin_ref.shape[1] // 2, rate.shape[1])
+    for m in range(rate.shape[0] // 2):
+        two = [jnp.broadcast_to(rate[n : n + 1, :], half) for n in (2 * m, 2 * m + 1)]
+        twin_ref[m] = jnp.concatenate(two, axis=0)
     for copy in large:
         copy.wait()
 
@@ -169,7 +208,7 @@
     past = taps - 1
     held = [ref[i].astype(F32) for ref, i in blocks(msgs)]
     owners = len(held)
-    windows = [[h[k : k + 1, :] for h in held] for k in range(past)]
+    windows = [[h[steps + k : steps + k + 1, :] for h in held] for k in range(past)]
     own = pick_ref[...]
     own_windows = [pick_rows(own, w) for w in windows]
     for t in range(steps):
@@ -183,7 +222,7 @@
 
     slot = slot_onehot(line_of(past + steps), owners)
     line = [pick_rows(slot, w) for w in windows]
-    line += [line_of(past + t) for t in range(steps)]
+    line += [line_of(t) for t in range(steps)]
     row = steps * rb
     for t in range(steps):
         conv = cw_ref[past:taps, :] * line[t + past] + cb_ref[...]
@@ -199,52 +238,25 @@
     )
 
 
-def fetch_kernel(
-    n_msgs, steps, key_hbm, child_hbm, alog_hbm, dtw_hbm, dtb_hbm, skip_hbm, after_ref, *rest
-):
-    del after_ref
-    msgs, rest = rest[:n_msgs], rest[n_msgs:]
-    rate_ref, twin_ref, conv_ref, dtw_ref, dtb_ref, skip_ref, key_s, child_s, alog, sems = rest
-    small = [
-        pltpu.make_async_copy(key_hbm, key_s, sems.at[0]),
-        pltpu.make_async_copy(child_hbm, child_s, sems.at[1]),
-        pltpu.make_async_copy(alog_hbm, alog, sems.at[2]),
-        pltpu.make_async_copy(dtb_hbm, dtb_ref, sems.at[3]),
-        pltpu.make_async_copy(skip_hbm, skip_ref, sems.at[4]),
-    ]
-    large = in_parts(dtw_hbm, dtw_ref, sems, 5, DT_PARTS)
-    for copy in small + large:
-        copy.start()
-    past, rb, channels = conv_ref.shape
-    held = [ref[i].astype(F32) for ref, i in blocks(msgs)]
-    for copy in small:
-        copy.wait()
-    owners = len(held)
-    rate = jnp.exp(alog[...]) * (-math.log2(math.e))
-    rate_ref[...] = rate
-    half = (owners, channels)
-    for m in range(rate.shape[0] // 2):
-        two = [jnp.broadcast_to(rate[n : n + 1, :], half) for n in (2 * m, 2 * m + 1)]
-        twin_ref[m] = jnp.concatenate(two, axis=0)
-    pick = scalar_onehot(child_s, key_s[0], (rb, owners))
-    first = past + steps - past
-    for k in range(past):
-        conv_ref[k] = pick_rows(pick, [h[first + k : first + k + 1, :] for h in held]).astype(BF16)
-    for copy in large:
-        copy.wait()
-
-
 def add_kernel(a_ref, b_ref, sum_ref, short_ref):
     total = a_ref[...] + b_ref[...].astype(F32)
     sum_ref[...] = total
     short_ref[...] = total.astype(BF16)
 
 
-def start_kernel(n_msgs, n_pairs, text, pick_ref, after_ref, *rest):
+def start_kernel(n_msgs, n_pairs, steps, text, key_hbm, child_hbm, pick_ref, after_ref, *rest):
     del after_ref
     msgs, rest = rest[:n_msgs], rest[n_msgs:]
-    pairs, (own_ref, slot_ref, state_s) = rest[:n_pairs], rest[n_pairs:]
+    pairs, rest = rest[:n_pairs], rest[n_pairs:]
+    own_ref, slot_ref, conv_hbm, state_s, conv_s, key_s, child_s, sems = rest
+    copies = [
+        pltpu.make_async_copy(key_hbm, key_s, sems.at[0]),
+        pltpu.make_async_copy(child_hbm, child_s, sems.at[1]),
+    ]
+    for copy in copies:
+        copy.start()
     n_state = own_ref.shape[0]
+    past, rb, _ = conv_s.shape
     held = [ref[i].astype(F32) for ref, i in blocks(msgs)]
     owners = len(held)
     numbers = jnp.concatenate([h[text - 1 : text, :] for h in held], axis=0)
@@ -266,7 +278,16 @@
         slot_ref[m] = jnp.concatenate(picked, axis=0)
         return carry
 
+    for copy in copies:
+        copy.wait()
+    child = scalar_onehot(child_s, key_s[0], (rb, owners))
+    for k in range(past):
+        at = steps - past + k
+        conv_s[k] = pick_rows(child, [h[at : at + 1, :] for h in held]).astype(BF16)
+    out = pltpu.make_async_copy(conv_s, conv_hbm, sems.at[2])
+    out.start()
     lax.fori_loop(0, n_state // 2, two, 0)
+    out.wait()
 
 
 def decode_kernel(
@@ -283,7 +304,7 @@
     skip_ref,
     part_ref,
     other_ref,
-    dec_ref,
+    dec_hbm,
     child_ssm,
     key_s,
     child_s,
@@ -296,6 +317,7 @@
     twin_b_s,
     slots_s,
     line_s,
+    dec_ref,
     sems,
 ):
     scalars = [
@@ -374,11 +396,20 @@
         for t in range(steps):
             line_s[pl.ds(t, rb, stride=steps), :] = sums[t] * gate_ref[t, :, columns]
         dec_ref[:, :, columns] = line_s[...].reshape(rb, steps, LANES).astype(BF16)
+        leave(chunk).start()
         return carry
+
+    def leave(chunk):
+        columns = pl.ds(pl.multiple_of(chunk * LANES, LANES), LANES)
+        return pltpu.make_async_copy(
+            dec_ref.at[:, :, columns], dec_hbm.at[:, :, columns], sems.at[2 + rb + chunk]
+        )
 
     lax.fori_loop(0, chunks, own_chunk, 0)
     for copy in copies:
         copy.wait()
+    for chunk in range(chunks):
+        leave(chunk).wait()
 
 
 def on_device(
@@ -453,7 +484,7 @@
         msgs = [lax.all_to_all(msgs[0], "branch", split_axis=0, concat_axis=0, tiled=True)]
         pairs, after = [], msgs[0]
     n_msgs = len(msgs)
-    base, gate, pick, taps_near, bias_near, weight_near = call(
+    near = call(
         prepare_kernel,
         [
             shaped((steps, rb, channels), F32),
@@ -462,13 +493,19 @@
             shaped((taps, channels), F32),
             shaped((1, channels), F32),
             shaped((width, channels), BF16),
-        ],
-        [hbm(), hbm(), vmem(), hbm(), hbm(), hbm(), anywhere()],
-        [vmem()] * 6,
+            shaped((n_state, channels), F32),
+            shaped((n_state // 2, 2 * owners, channels), F32),
+            shaped(dt_weight.shape, BF16),
+            shaped((1, channels), F32),
+            shaped((1, channels), F32),
+        ],
+        [hbm(), hbm(), vmem()] + [hbm()] * 7 + [anywhere()],
+        [vmem()] * 11,
         [
             pltpu.SMEM((1,), jnp.int32),
             pltpu.SMEM((rb,), jnp.int32),
-            pltpu.SemaphoreType.DMA((4 + WEIGHT_PARTS,)),
+            pltpu.VMEM((n_state, channels), F32),
+            pltpu.SemaphoreType.DMA((7 + WEIGHT_PARTS + DT_PARTS,)),
         ],
         flops=10 * steps * rb * channels,
         nbytes=12 * steps * rb * channels,
@@ -480,8 +517,14 @@
         pinned(conv_weight),
         pinned(conv_bias[None]),
         pinned(x_weight.T),
+        pinned(a_log),
+        pinned(dt_weight),
+        pinned(dt_bias[None]),
+        pinned(skip[None]),
         after,
     )
+    base, gate, pick, taps_near, bias_near, weight_near = near[:6]
+    rate, twin, dtw_near, dtb_near, skip_near = near[6:]
     act, part = call(
         functools.partial(project_kernel, n_msgs),
         [
@@ -508,48 +551,25 @@
         other = swap(brief, "tensor", distance)
         distance *= 2
 
-    rate, twin, child_conv, dtw_near, dtb_near, skip_near = call(
-        functools.partial(fetch_kernel, n_msgs, steps),
-        [
-            shaped((n_state, channels), F32),
+    own_start, slot_start, child_conv = call(
+        functools.partial(start_kernel, n_msgs, len(pairs), steps, short),
+        [
+            shaped((n_state, rb, channels), F32),
             shaped((n_state // 2, 2 * owners, channels), F32),
             shaped((taps - 1, rb, channels), BF16),
-            shaped(dt_weight.shape, BF16),
-            shaped((1, channels), F32),
-            shaped((1, channels), F32),
-        ],
-        [hbm()] * 6 + [anywhere()] + [vmem()] * n_msgs,
-        [vmem()] * 6,
-        [
+        ],
+        [hbm()] * 2 + [vmem(), anywhere()] + [vmem()] * (n_msgs + len(pairs)),
+        [vmem()] * 2 + [anywhere()],
+        [
+            pltpu.VMEM((owners, n_state, channels), F32),
+            pltpu.VMEM((taps - 1, rb, channels), BF16),
             pltpu.SMEM((1,), jnp.int32),
             pltpu.SMEM((rb,), jnp.int32),
-            pltpu.VMEM((n_state, channels), F32),
-            pltpu.SemaphoreType.DMA((5 + DT_PARTS,)),
-        ],
-        flops=4 * n_state * channels,
-        nbytes=4 * n_state * (rb + owners) * channels,
-    )(
-        key,
-        pinned(child_slot),
-        pinned(a_log),
-        pinned(dt_weight),
-        pinned(dt_bias[None]),
-        pinned(skip[None]),
-        part,
-        *msgs,
-    )
-    own_start, slot_start = call(
-        functools.partial(start_kernel, n_msgs, len(pairs), short),
-        [
-            shaped((n_state, rb, channels), F32),
-            shaped((n_state // 2, 2 * owners, channels), F32),
-        ],
-        [vmem(), anywhere()] + [vmem()] * (n_msgs + len(pairs)),
-        [vmem()] * 2,
-        [pltpu.VMEM((owners, n_state, channels), F32)],
+            pltpu.SemaphoreType.DMA((3,)),
+        ],
         flops=2 * owners * n_state * (rb + owners) * channels,
         nbytes=4 * n_state * (rb + owners) * channels,
-    )(pick, part, *msgs, *pairs)
+    )(key, pinned(child_slot), pick, part, *msgs, *pairs)
 
     decoded, child_ssm = call(
         decode_kernel,
@@ -558,7 +578,7 @@
             shaped((rb, n_state, channels), F32),
         ],
         [hbm()] * 2 + [vmem()] * 11,
-        [vmem(), anywhere()],
+        [anywhere()] * 2,
         [
             pltpu.SMEM((1,), jnp.int32),
             pltpu.SMEM((rb,), jnp.int32),
@@ -571,7 +591,8 @@
             pltpu.VMEM((n_state // 2, steps, 2 * owners, LANES), F32),
             pltpu.VMEM((owners, n_state, channels), F32),
             pltpu.VMEM((steps * rb, LANES), F32),
-            pltpu.SemaphoreType.DMA((2 + rb,)),
+            pltpu.VMEM((rb, steps, channels), BF16),
+            pltpu.SemaphoreType.DMA((2 + rb + channels // LANES,)),
         ],
         flops=8 * rows * n_state * channels,
         nbytes=(rb + owners) * n_state * channels * 4,

time: 21.2 us -> 21.9 us (1.033)
  waiting for transfers between devices: 3.94 us -> 5.25 us
  Pallas kernels: 8.87 us -> 8.31 us
    ppermute x6, waiting for transfers between devices: 3.94 us -> 5.25 us  [swap(): return lax.ppermute(value, axis, [(i, i ^ distance) for i in range(size)])]
    pallas_call x2 -> x1, Pallas kernels: 2.86 us -> 1.8 us  [on_device(): call(functools.partial(start_kernel, n_msgs, len(pairs), steps, short), [...]
    pallas_call x1, Pallas kernels: 1.25 us -> 1.54 us  [on_device(): call(prepare_kernel, [shaped((steps, rb, channels), F32), shaped((steps,...]
  transfers between devices with their start and end apart: 6 -> 6, of which waited for: 2 -> 3; matrix products, arithmetic and copies ran while one was open for 0% -> 0% of each run, Pallas kernels for 20% -> 16%
where the time goes in v6:
time: 21.9 us; the launch traced here: 21.7 us
  Pallas kernels  8.31 us (38%)
  starting transfers between devices  7.38 us (34%)
  waiting for transfers between devices  5.25 us (24%)
  between operations  0.71 us (3%)
    ppermute x6, starting transfers between devices, swap(): return lax.ppermute(value, axis, [(i, i ^ distance) for i in range(size)])  7.38 us
    ppermute x6, waiting for transfers between devices, swap(): return lax.ppermute(value, axis, [(i, i ^ distance) for i in range(size)])  5.25 us
    pallas_call x1, Pallas kernels, on_device(): call(decode_kernel, [shaped((rb, steps, channels), BF16), shaped((rb, n_s...  3.3 us
    pallas_call x1, Pallas kernels, on_device(): call(functools.partial(start_kernel, n_msgs, len(pairs), steps, short), [...  1.8 us
    pallas_call x1, Pallas kernels, on_device(): call(prepare_kernel, [shaped((steps, rb, channels), F32), shaped((steps,...  1.54 us
    pallas_call x1, Pallas kernels, on_device(): call(functools.partial(pack_kernel, direct), [shaped(s, BF16) for s in ms...  1.15 us
    pallas_call x1, Pallas kernels, on_device(): call(functools.partial(project_kernel, n_msgs), [shaped((rows, channels),...  0.5 us
  transfers between devices with their start and end apart: 6, of which 3 were waited for; matrix products, arithmetic and copies ran while one was open for 0% of the time, Pallas kernels for 16%

profile of v6, /device:TPU:0, one launch (start us, length us, event | category | flops | bytes accessed | tf_op | source)
XLA Modules:
  0.0 21.7 jit_solution(12351979239222555458)
XLA Ops:
  0.6 0.0 copy-start
  0.6 1.1 %shard_map.148 = (bf16[1,24,1024]{2,1,0:T(8,128)(2,1)S(1)}, bf16[1,24,1024]{2,1,0:T(8,128)(2,1)S(1)}, bf16[1,8,1024]{2,1,0:T(8,128)(2,1)S(1)}, bf16[1,8,1024]{2,1,0:T(8,128)(2,1)S(1)}) custom-call(s32[1]{0:T(128)} %bitcast.key_hbm, s32[4]{0:T(128)} %bitcast.11, s32[16]{0:T(128)} %prompt_hbm.3, bf16[16,4,2,1024]{3,2,1,0:T(2,128)(2,1)} %step_ref.1, ...), custom_call_target="tpu_custom_call" | custom-call | bytes 196608 | tf_op jit(solution)/shard_map/pallas_call | solution.py:449
  1.8 4.1 %collective-permute-start = (bf16[1,24,1024]{2,1,0:T(8,128)(2,1)S(1)}, bf16[1,24,1024]{2,1,0:T(8,128)(2,1)S(1)}, u32[]{:S(2)}, u32[]{:S(2)}) collective-permute-start(bf16[1,24,1024]{2,1,0:T(8,128)(2,1)S(1)} %get-tuple-element.33), channel_id=1, source_target_pairs={{0,8},{4,12},{8,0},{12,4},{1,9},{5,13},{9,1},{13,5},{2,10},{6,14},... | collective-permute-start | bytes 147464 | tf_op jit(solution)/shard_map/ppermute | solution.py:55
  5.9 1.3 %collective-permute-start.1 = (bf16[1,8,1024]{2,1,0:T(8,128)(2,1)S(1)}, bf16[1,8,1024]{2,1,0:T(8,128)(2,1)S(1)}, u32[]{:S(2)}, u32[]{:S(2)}) collective-permute-start(bf16[1,8,1024]{2,1,0:T(8,128)(2,1)S(1)} %get-tuple-element.34), channel_id=1, source_target_pairs={{0,12},{4,8},{8,4},{12,0},{1,13},{5,9},{9,5},{13,1},{2,14},{6,10},... | collective-permute-start | bytes 49160 | tf_op jit(solution)/shard_map/ppermute | solution.py:55
  7.3 0.2 %collective-permute-start.2 = (bf16[1,8,1024]{2,1,0:T(8,128)(2,1)S(1)}, bf16[1,8,1024]{2,1,0:T(8,128)(2,1)S(1)}, u32[]{:S(2)}, u32[]{:S(2)}) collective-permute-start(bf16[1,8,1024]{2,1,0:T(8,128)(2,1)S(1)} %get-tuple-element.35), channel_id=1, source_target_pairs={{0,4},{4,0},{8,12},{12,8},{1,5},{5,1},{9,13},{13,9},{2,6},{6,2},{1... | collective-permute-start | bytes 49160 | tf_op jit(solution)/shard_map/ppermute | solution.py:55
  7.5 0.0 copy-done
  7.5 1.5 %shard_map.149 = (f32[4,16,1024]{2,1,0:T(8,128)S(1)}, f32[4,16,1024]{2,1,0:T(8,128)S(1)}, f32[16,4]{1,0:T(8,128)S(1)}, f32[4,1024]{1,0:T(4,128)S(1)}, f32[1,1024...) custom-call(s32[1]{0:T(128)} %bitcast.key_hbm, ...), custom_call_target="tpu_custom_call" | custom-call | flops 655360 | bytes 786432 | tf_op jit(solution)/shard_map/pallas_call | solution.py:487
  9.0 2.4 %collective-permute-done.1.rest_2_ = bf16[1,8,1024]{2,1,0:T(8,128)(2,1)S(1)} collective-permute-done((bf16[1,8,1024]{2,1,0:T(8,128)(2,1)S(1)}, bf16[1,8,1024]{2,1,0:T(8,128)(2,1)S(1)}, u32[]{:S(2)}, u32[]{:S(2)}) %collective-permute-start.1) | collective-permute-done | bytes 16416 | tf_op jit(solution)/shard_map/ppermute | solution.py:55
  11.4 0.0 collective-permute-done.2.rest_3_
  11.4 0.0 collective-permute-done.rest_1_.other_ref
  11.4 0.5 %shard_map.150 = (f32[80,1024]{1,0:T(8,128)S(1)}, f32[80,288]{1,0:T(8,128)S(1)}) custom-call(f32[16,4]{1,0:T(8,128)S(1)} %get-tuple-element.28.pick_ref, f32[4,16,1024]{2,1,0:T(8,128)S(1)} %get-tuple-element.29.base_ref, f32[4,1024]{1,0:T(4,128)S(1)} %get-tuple-element.30.cw_ref, f32[1,1024]{1,0:T(1,128)S(1)} %get-tuple-element.31.cb_ref, ...), custom_call_target="tpu_custom_call" | custom-call | flops 47185920 | bytes 1009664 | tf_op jit(solution)/shard_map/pallas_call | solution.py:528
  11.9 0.1 collective-permute-start.3
  12.0 0.1 collective-permute-start.4
  12.1 1.2 %collective-permute-done.3.b_ref = f32[80,288]{1,0:T(8,128)S(1)} collective-permute-done((f32[80,288]{1,0:T(8,128)S(1)}, f32[80,288]{1,0:T(8,128)S(1)}, u32[]{:S(2)}, u32[]{:S(2)}) %collective-permute-start.3) | collective-permute-done | bytes 92192 | tf_op jit(solution)/shard_map/ppermute | solution.py:55
  13.4 1.6 %collective-permute-start.5 = (bf16[80,288]{1,0:T(8,128)(2,1)S(1)}, bf16[80,288]{1,0:T(8,128)(2,1)S(1)}, u32[]{:S(2)}, u32[]{:S(2)}) collective-permute-start(bf16[80,288]{1,0:T(8,128)(2,1)S(1)} %get-tuple-element.47), channel_id=1, source_target_pairs={{0,2},{1,3},{2,0},{3,1},{4,6},{5,7},{6,4},{7,5},{8,10},{9,11},{10,... | collective-permute-start | bytes 138248 | tf_op jit(solution)/shard_map/ppermute | solution.py:55
  14.9 1.6 %collective-permute-done.4.rest_4_ = bf16[1,32,1024]{2,1,0:T(8,128)(2,1)S(1)} collective-permute-done((bf16[1,32,1024]{2,1,0:T(8,128)(2,1)S(1)}, bf16[1,32,1024]{2,1,0:T(8,128)(2,1)S(1)}, u32[]{:S(2)}, u32[]{:S(2)}) %collective-permute-start.4) | collective-permute-done | bytes 65568 | tf_op jit(solution)/shard_map/ppermute | solution.py:55
  16.5 1.8 %shard_map.153 = (f32[16,16,1024]{2,1,0:T(8,128)S(1)}, f32[8,8,1024]{2,1,0:T(8,128)S(1)}, bf16[3,16,1024]{2,1,0:T(8,128)(2,1)}) custom-call(s32[1]{0:T(128)} %bitcast.key_hbm, s32[16]{0:T(128)} %child_hbm.3, f32[16,4]{1,0:T(8,128)S(1)} %get-tuple-element.28.pick_ref, f32[80,288]{1,0:T(8,128)S(1)} %get-tuple-element.39.after_ref.part_ref, ...), custom_call_target="tpu_custom_call" | custom-call | flops 2621440 | bytes 1310720 | tf_op jit(solution)/shard_map/pallas_call | solution.py:554
  18.4 0.0 collective-permute-done.5.other_ref
  18.4 3.3 %shard_map.154 = (bf16[16,4,1024]{2,1,0:T(4,128)(2,1)}, f32[16,16,1024]{2,1,0:T(8,128)}) custom-call(s32[1]{0:T(128)} %bitcast.key_hbm, s32[16]{0:T(128)} %child_hbm.3, f32[80,1024]{1,0:T(8,128)S(1)} %get-tuple-element.36.act_ref, f32[4,16,1024]{2,1,0:T(8,128)S(1)} %get-tuple-element.37.gate_ref, f32[16,16,1024]{2,1,0:T(8,128)S(1)} %get-tuple-element.40.own_ref, ...), custom_call_target="tpu_custom_call" | custom-call | flops 10485760 | bytes 1310720 | tf_op jit(solution)/shard_map/pallas_call | solution.py:574
  (2 shorter events, 0.0 us)
Async XLA Ops:
  0.6 6.9 %copy-start = (bf16[16,4,2,1024]{3,2,1,0:T(2,128)(2,1)S(1)}, bf16[16,4,2,1024]{3,2,1,0:T(2,128)(2,1)}, u32[]{:S(2)}) copy-start(bf16[16,4,2,1024]{3,2,1,0:T(2,128)(2,1)} %step_ref.1) | copy-start | bytes 786436
  1.8 9.6 %collective-permute-start = (bf16[1,24,1024]{2,1,0:T(8,128)(2,1)S(1)}, bf16[1,24,1024]{2,1,0:T(8,128)(2,1)S(1)}, u32[]{:S(2)}, u32[]{:S(2)}) collective-permute-start(bf16[1,24,1024]{2,1,0:T(8,128)(2,1)S(1)} %get-tuple-element.33), channel_id=1, source_target_pairs={{0,8},{4,12},{8,0},{12,4},{1,9},{5,13},{9,1},{13,5},{2,10},{6,14},... | collective-permute-start | bytes 147464 | tf_op jit(solution)/shard_map/ppermute | solution.py:55
  5.9 5.5 %collective-permute-start.1 = (bf16[1,8,1024]{2,1,0:T(8,128)(2,1)S(1)}, bf16[1,8,1024]{2,1,0:T(8,128)(2,1)S(1)}, u32[]{:S(2)}, u32[]{:S(2)}) collective-permute-start(bf16[1,8,1024]{2,1,0:T(8,128)(2,1)S(1)} %get-tuple-element.34), channel_id=1, source_target_pairs={{0,12},{4,8},{8,4},{12,0},{1,13},{5,9},{9,5},{13,1},{2,14},{6,10},... | collective-permute-start | bytes 49160 | tf_op jit(solution)/shard_map/ppermute | solution.py:55
  7.3 4.2 %collective-permute-start.2 = (bf16[1,8,1024]{2,1,0:T(8,128)(2,1)S(1)}, bf16[1,8,1024]{2,1,0:T(8,128)(2,1)S(1)}, u32[]{:S(2)}, u32[]{:S(2)}) collective-permute-start(bf16[1,8,1024]{2,1,0:T(8,128)(2,1)S(1)} %get-tuple-element.35), channel_id=1, source_target_pairs={{0,4},{4,0},{8,12},{12,8},{1,5},{5,1},{9,13},{13,9},{2,6},{6,2},{1... | collective-permute-start | bytes 49160 | tf_op jit(solution)/shard_map/ppermute | solution.py:55
  11.9 1.4 %collective-permute-start.3 = (f32[80,288]{1,0:T(8,128)S(1)}, f32[80,288]{1,0:T(8,128)S(1)}, u32[]{:S(2)}, u32[]{:S(2)}) collective-permute-start(f32[80,288]{1,0:T(8,128)S(1)} %get-tuple-element.38.a_ref), channel_id=1, source_target_pairs={{0,1},{1,0},{2,3},{3,2},{4,5},{5,4},{6,7},{7,6},{8,9},{9,8},{10,11... | collective-permute-start | bytes 276488 | tf_op jit(solution)/shard_map/ppermute | solution.py:55
  12.0 4.5 %collective-permute-start.4 = (bf16[1,32,1024]{2,1,0:T(8,128)(2,1)S(1)}, bf16[1,32,1024]{2,1,0:T(8,128)(2,1)S(1)}, u32[]{:S(2)}, u32[]{:S(2)}) collective-permute-start(bf16[1,32,1024]{2,1,0:T(8,128)(2,1)S(1)} %shard_map.152), channel_id=1, source_target_pairs={{0,4},{4,0},{8,12},{12,8},{1,5},{5,1},{9,13},{13,9},{2,6},{6,2},{1... | collective-permute-start | bytes 196616 | tf_op jit(solution)/shard_map/ppermute | solution.py:55
  13.4 5.0 %collective-permute-start.5 = (bf16[80,288]{1,0:T(8,128)(2,1)S(1)}, bf16[80,288]{1,0:T(8,128)(2,1)S(1)}, u32[]{:S(2)}, u32[]{:S(2)}) collective-permute-start(bf16[80,288]{1,0:T(8,128)(2,1)S(1)} %get-tuple-element.47), channel_id=1, source_target_pairs={{0,2},{1,3},{2,0},{3,1},{4,6},{5,7},{6,4},{7,5},{8,10},{9,11},{10,... | collective-permute-start | bytes 138248 | tf_op jit(solution)/shard_map/ppermute | solution.py:55

commit v7 on v6

--- a/solution.py
+++ b/solution.py
@@ -15,7 +15,7 @@
 WEIGHT_PARTS = 6
 DT_PARTS = 4
 DIRECT = 4
-ORDER = (0, 2, 3, 1)
+ROUNDS = ((3, (2, 3)), (2, (2, 3)), (1, (0, 1, 2, 3)), (2, (0, 1)), (3, (0, 1)))
 
 
 def vmem():
@@ -50,9 +50,9 @@
     )
 
 
-def swap(value, axis, distance):
-    size = lax.axis_size(axis)
-    return lax.ppermute(value, axis, [(i, i ^ distance) for i in range(size)])
+def swap(value, axis, distance, senders=None):
+    senders = range(lax.axis_size(axis)) if senders is None else senders
+    return lax.ppermute(value, axis, [(i, i ^ distance) for i in senders])
 
 
 def all_of(copies):
@@ -62,10 +62,14 @@
         copy.wait()
 
 
-def blocks(refs):
-    if len(refs) == DIRECT:
-        refs = [refs[ORDER.index(k)] for k in range(DIRECT)]
-    return [(ref, i) for ref in refs for i in range(ref.shape[0])]
+def read_messages(refs):
+    if len(refs) == 1:
+        return [refs[0][i].astype(F32) for i in range(refs[0].shape[0])]
+    held = [refs[0][0].astype(F32)] + [None] * (DIRECT - 1)
+    for ref, (k, _) in zip(refs[1:], ROUNDS):
+        came = ref[0].astype(F32)
+        held[k] = came if held[k] is None else held[k] + came
+    return held
 
 
 def in_parts(source, target, sems, first, count):
@@ -106,24 +110,24 @@
     all_of(copies + in_parts(step_hbm, step, sems, 5, 4))
     key = key_s[0]
     window = conv[0].astype(F32)
-    for k, (ref, i) in enumerate(blocks(outs)):
+    for k in range(owners):
         target = jnp.bitwise_xor(key, k)
         row = jnp.maximum(rows_s[target], 0)
         xs = step[row, :, 0, :].astype(F32)
         told = jnp.bitwise_xor(prompt_s[row], target) if direct else prompt_s[row]
         pieces = [xs, window, jnp.full((1, channels), told.astype(F32), F32)]
-        if ref.shape[1] > sum(p.shape[0] for p in pieces):
-            pieces.append(ssm[0])
-        ref[i] = jnp.concatenate(pieces, axis=0).astype(BF16)
+        message = jnp.concatenate(pieces + [ssm[0]], axis=0).astype(BF16)
+        if direct:
+            into = [outs[0].at[0]] if k == 0 else []
+            into += [ref.at[0] for ref, (d, _) in zip(outs[1:], ROUNDS) if d == k]
+        else:
+            into = [outs[0].at[k]]
+        for ref in into:
+            ref[...] = message
 
 
 def silu(v):
     return v / (1.0 + jnp.exp(-v))
-
-
-def pair_kernel(text, own_ref, other_ref, pair_ref):
-    states = [ref[0].astype(F32)[text:, :] for ref in (own_ref, other_ref)]
-    pair_ref[0] = jnp.concatenate(states, axis=0).astype(BF16)
 
 
 def prepare_kernel(
@@ -206,7 +210,7 @@
     taps = cw_ref.shape[0]
     steps, rb, _ = base_ref.shape
     past = taps - 1
-    held = [ref[i].astype(F32) for ref, i in blocks(msgs)]
+    held = read_messages(msgs)
     owners = len(held)
     windows = [[h[steps + k : steps + k + 1, :] for h in held] for k in range(past)]
     own = pick_ref[...]
@@ -244,28 +248,32 @@
     short_ref[...] = total.astype(BF16)
 
 
-def start_kernel(n_msgs, n_pairs, steps, text, key_hbm, child_hbm, pick_ref, after_ref, *rest):
+def windows_kernel(n_msgs, steps, key_hbm, child_hbm, after_ref, *rest):
     del after_ref
-    msgs, rest = rest[:n_msgs], rest[n_msgs:]
-    pairs, rest = rest[:n_pairs], rest[n_pairs:]
-    own_ref, slot_ref, conv_hbm, state_s, conv_s, key_s, child_s, sems = rest
-    copies = [
-        pltpu.make_async_copy(key_hbm, key_s, sems.at[0]),
-        pltpu.make_async_copy(child_hbm, child_s, sems.at[1]),
-    ]
-    for copy in copies:
-        copy.start()
+    msgs, (conv_ref, key_s, child_s, sems) = rest[:n_msgs], rest[n_msgs:]
+    all_of(
+        [
+            pltpu.make_async_copy(key_hbm, key_s, sems.at[0]),
+            pltpu.make_async_copy(child_hbm, child_s, sems.at[1]),
+        ]
+    )
+    past, rb, _ = conv_ref.shape
+    held = read_messages(msgs)
+    child = scalar_onehot(child_s, key_s[0], (rb, len(held)))
+    for k in range(past):
+        at = steps - past + k
+        conv_ref[k] = pick_rows(child, [h[at : at + 1, :] for h in held]).astype(BF16)
+
+
+def start_kernel(n_msgs, text, pick_ref, after_ref, *rest):
+    del after_ref
+    msgs, (own_ref, slot_ref, state_s) = rest[:n_msgs], rest[n_msgs:]
     n_state = own_ref.shape[0]
-    past, rb, _ = conv_s.shape
-    held = [ref[i].astype(F32) for ref, i in blocks(msgs)]
+    held = read_messages(msgs)
     owners = len(held)
     numbers = jnp.concatenate([h[text - 1 : text, :] for h in held], axis=0)
-    states = [h[text:, :] for h in held]
-    for ref in pairs:
-        both = ref[0].astype(F32)
-        states[1], states[3] = both[:n_state, :], both[n_state:, :]
-    for k, state in enumerate(states):
-        state_s[k] = state
+    for k, h in enumerate(held):
+        state_s[k] = h[text:, :]
     own = pick_ref[...]
     slot = slot_onehot(numbers, owners)
 
@@ -278,16 +286,7 @@
         slot_ref[m] = jnp.concatenate(picked, axis=0)
         return carry
 
-    for copy in copies:
-        copy.wait()
-    child = scalar_onehot(child_s, key_s[0], (rb, owners))
-    for k in range(past):
-        at = steps - past + k
-        conv_s[k] = pick_rows(child, [h[at : at + 1, :] for h in held]).astype(BF16)
-    out = pltpu.make_async_copy(conv_s, conv_hbm, sems.at[2])
-    out.start()
-    lax.fori_loop(0, n_state // 2, two, 0)
-    out.wait()
+    lax.fori_loop(0, n_state // 2, two, 0, unroll=owners <= DIRECT)
 
 
 def decode_kernel(
@@ -304,7 +303,7 @@
     skip_ref,
     part_ref,
     other_ref,
-    dec_hbm,
+    dec_ref,
     child_ssm,
     key_s,
     child_s,
@@ -317,7 +316,6 @@
     twin_b_s,
     slots_s,
     line_s,
-    dec_ref,
     sems,
 ):
     scalars = [
@@ -396,20 +394,11 @@
         for t in range(steps):
             line_s[pl.ds(t, rb, stride=steps), :] = sums[t] * gate_ref[t, :, columns]
         dec_ref[:, :, columns] = line_s[...].reshape(rb, steps, LANES).astype(BF16)
-        leave(chunk).start()
         return carry
-
-    def leave(chunk):
-        columns = pl.ds(pl.multiple_of(chunk * LANES, LANES), LANES)
-        return pltpu.make_async_copy(
-            dec_ref.at[:, :, columns], dec_hbm.at[:, :, columns], sems.at[2 + rb + chunk]
-        )
 
     lax.fori_loop(0, chunks, own_chunk, 0)
     for copy in copies:
         copy.wait()
-    for chunk in range(chunks):
-        leave(chunk).wait()
 
 
 def on_device(
@@ -443,7 +432,7 @@
     key = pinned(me if direct else jnp.zeros((1,), jnp.int32))
 
     if direct:
-        msg_shapes = [(1, depth if k in (0, 2) else short, channels) for k in ORDER]
+        msg_shapes = [(1, depth, channels)] * (1 + len(ROUNDS))
     else:
         msg_shapes = [(owners, depth, channels)]
     msgs = call(
@@ -471,18 +460,11 @@
     )
     if direct:
         own = msgs[0]
-        msgs = [own] + [swap(msgs[i], "branch", ORDER[i]) for i in range(1, owners)]
-        pair = call(
-            functools.partial(pair_kernel, short),
-            shaped((1, 2 * n_state, channels), BF16),
-            [vmem()] * 2,
-            vmem(),
-            nbytes=8 * n_state * channels,
-        )(own, msgs[ORDER.index(2)])
-        pairs, after = [swap(pair, "branch", 1)], own
+        msgs = [own] + [swap(m, "branch", k, who) for m, (k, who) in zip(msgs[1:], ROUNDS)]
+        after = own
     else:
         msgs = [lax.all_to_all(msgs[0], "branch", split_axis=0, concat_axis=0, tiled=True)]
-        pairs, after = [], msgs[0]
+        after = msgs[0]
     n_msgs = len(msgs)
     near = call(
         prepare_kernel,
@@ -551,25 +533,31 @@
         other = swap(brief, "tensor", distance)
         distance *= 2
 
-    own_start, slot_start, child_conv = call(
-        functools.partial(start_kernel, n_msgs, len(pairs), steps, short),
+    child_conv = call(
+        functools.partial(windows_kernel, n_msgs, steps),
+        shaped((taps - 1, rb, channels), BF16),
+        [hbm()] * 2 + [anywhere()] + [vmem()] * n_msgs,
+        vmem(),
+        [
+            pltpu.SMEM((1,), jnp.int32),
+            pltpu.SMEM((rb,), jnp.int32),
+            pltpu.SemaphoreType.DMA((2,)),
+        ],
+        flops=2 * owners * taps * rb * channels,
+        nbytes=4 * taps * rb * channels,
+    )(key, pinned(child_slot), part, *msgs)
+    own_start, slot_start = call(
+        functools.partial(start_kernel, n_msgs, short),
         [
             shaped((n_state, rb, channels), F32),
             shaped((n_state // 2, 2 * owners, channels), F32),
-            shaped((taps - 1, rb, channels), BF16),
-        ],
-        [hbm()] * 2 + [vmem(), anywhere()] + [vmem()] * (n_msgs + len(pairs)),
-        [vmem()] * 2 + [anywhere()],
-        [
-            pltpu.VMEM((owners, n_state, channels), F32),
-            pltpu.VMEM((taps - 1, rb, channels), BF16),
-            pltpu.SMEM((1,), jnp.int32),
-            pltpu.SMEM((rb,), jnp.int32),
-            pltpu.SemaphoreType.DMA((3,)),
-        ],
+        ],
+        [vmem(), anywhere()] + [vmem()] * n_msgs,
+        [vmem()] * 2,
+        [pltpu.VMEM((owners, n_state, channels), F32)],
         flops=2 * owners * n_state * (rb + owners) * channels,
         nbytes=4 * n_state * (rb + owners) * channels,
-    )(key, pinned(child_slot), pick, part, *msgs, *pairs)
+    )(pick, part, *msgs)
 
     decoded, child_ssm = call(
         decode_kernel,
@@ -578,7 +566,7 @@
             shaped((rb, n_state, channels), F32),
         ],
         [hbm()] * 2 + [vmem()] * 11,
-        [anywhere()] * 2,
+        [vmem(), anywhere()],
         [
             pltpu.SMEM((1,), jnp.int32),
             pltpu.SMEM((rb,), jnp.int32),
@@ -591,8 +579,7 @@
             pltpu.VMEM((n_state // 2, steps, 2 * owners, LANES), F32),
             pltpu.VMEM((owners, n_state, channels), F32),
             pltpu.VMEM((steps * rb, LANES), F32),
-            pltpu.VMEM((rb, steps, channels), BF16),
-            pltpu.SemaphoreType.DMA((2 + rb + channels // LANES,)),
+            pltpu.SemaphoreType.DMA((2 + rb,)),
         ],
         flops=8 * rows * n_state * channels,
         nbytes=(rb + owners) * n_state * channels * 4,

time: 21.9 us -> 25.6 us (1.17)
  starting transfers between devices: 7.38 us -> 14 us
  waiting for transfers between devices: 5.25 us -> 2.15 us
    ppermute x6 -> x7, starting transfers between devices: 7.38 us -> 14 us  [swap(): return lax.ppermute(value, axis, [(i, i ^ distance) for i in senders])]
    ppermute x6 -> x7, waiting for transfers between devices: 5.25 us -> 2.15 us  [swap(): return lax.ppermute(value, axis, [(i, i ^ distance) for i in senders])]
  transfers between devices with their start and end apart: 6 -> 7, of which waited for: 3 -> 3; matrix products, arithmetic and copies ran while one was open for 0% -> 0% of each run, Pallas kernels for 16% -> 14%
where the time goes in v7:
time: 25.6 us; the launch traced here: 25.3 us
  starting transfers between devices  14 us (55%)
  Pallas kernels  8.32 us (32%)
  waiting for transfers between devices  2.15 us (8%)
  between operations  0.76 us (3%)
    ppermute x7, starting transfers between devices, swap(): return lax.ppermute(value, axis, [(i, i ^ distance) for i in senders])  14 us
    pallas_call x1, Pallas kernels, on_device(): call(decode_kernel, [shaped((rb, steps, channels), BF16), shaped((rb, n_s...  3.08 us
    ppermute x7, waiting for transfers between devices, swap(): return lax.ppermute(value, axis, [(i, i ^ distance) for i in senders])  2.15 us
    pallas_call x1, Pallas kernels, on_device(): call(prepare_kernel, [shaped((steps, rb, channels), F32), shaped((steps,...  1.55 us
    pallas_call x1, Pallas kernels, on_device(): call(functools.partial(windows_kernel, n_msgs, steps), shaped((taps - 1,...  1.48 us
    pallas_call x1, Pallas kernels, on_device(): call(functools.partial(pack_kernel, direct), [shaped(s, BF16) for s in ms...  1.15 us
    pallas_call x1, Pallas kernels, on_device(): call(functools.partial(start_kernel, n_msgs, short), [shaped((n_state, rb...  0.53 us
  transfers between devices with their start and end apart: 7, of which 3 were waited for; matrix products, arithmetic and copies ran while one was open for 0% of the time, Pallas kernels for 14%

profile of v7, /device:TPU:0, one launch (start us, length us, event | category | flops | bytes accessed | tf_op | source)
XLA Modules:
  0.0 25.3 jit_solution(6185543266479548429)
XLA Ops:
  0.6 0.0 copy-start
  0.6 1.2 %shard_map.148 = (bf16[1,24,1024]{2,1,0:T(8,128)(2,1)S(1)}, bf16[1,24,1024]{2,1,0:T(8,128)(2,1)S(1)}, bf16[1,24,1024]{2,1,0:T(8,128)(2,1)S(1)}, bf16[1,24,1024]{...) custom-call(s32[1]{0:T(128)} %bitcast.key_hbm, s32[4]{0:T(128)} %bitcast.12, ...), custom_call_target="tpu_custom_call" | custom-call | bytes 196608 | tf_op jit(solution)/shard_map/pallas_call | solution.py:438
  1.8 1.3 %collective-permute-start = (bf16[1,24,1024]{2,1,0:T(8,128)(2,1)S(1)}, bf16[1,24,1024]{2,1,0:T(8,128)(2,1)S(1)}, u32[]{:S(2)}, u32[]{:S(2)}) collective-permute-start(bf16[1,24,1024]{2,1,0:T(8,128)(2,1)S(1)} %get-tuple-element.34), channel_id=1, source_target_pairs={{8,4},{12,0},{9,5},{13,1},{10,6},{14,2},{11,7},{15,3},{24,20},{28,... | collective-permute-start | bytes 147464 | tf_op jit(solution)/shard_map/ppermute | solution.py:55
  3.1 1.3 %collective-permute-start.1 = (bf16[1,24,1024]{2,1,0:T(8,128)(2,1)S(1)}, bf16[1,24,1024]{2,1,0:T(8,128)(2,1)S(1)}, u32[]{:S(2)}, u32[]{:S(2)}) collective-permute-start(bf16[1,24,1024]{2,1,0:T(8,128)(2,1)S(1)} %get-tuple-element.35), channel_id=1, source_target_pairs={{8,0},{12,4},{9,1},{13,5},{10,2},{14,6},{11,3},{15,7},{24,16},{28,... | collective-permute-start | bytes 147464 | tf_op jit(solution)/shard_map/ppermute | solution.py:55
  4.4 3.1 %collective-permute-start.2 = (bf16[1,24,1024]{2,1,0:T(8,128)(2,1)S(1)}, bf16[1,24,1024]{2,1,0:T(8,128)(2,1)S(1)}, u32[]{:S(2)}, u32[]{:S(2)}) collective-permute-start(bf16[1,24,1024]{2,1,0:T(8,128)(2,1)S(1)} %get-tuple-element.36), channel_id=1, source_target_pairs={{0,4},{4,0},{8,12},{12,8},{1,5},{5,1},{9,13},{13,9},{2,6},{6,2},{1... | collective-permute-start | bytes 147464 | tf_op jit(solution)/shard_map/ppermute | solution.py:55
  7.5 5.4 %collective-permute-start.3 = (bf16[1,24,1024]{2,1,0:T(8,128)(2,1)S(1)}, bf16[1,24,1024]{2,1,0:T(8,128)(2,1)S(1)}, u32[]{:S(2)}, u32[]{:S(2)}) collective-permute-start(bf16[1,24,1024]{2,1,0:T(8,128)(2,1)S(1)} %get-tuple-element.37), channel_id=1, source_target_pairs={{0,8},{4,12},{1,9},{5,13},{2,10},{6,14},{3,11},{7,15},{16,24},{20,... | collective-permute-start | bytes 147464 | tf_op jit(solution)/shard_map/ppermute | solution.py:55
  12.9 1.3 %collective-permute-start.4 = (bf16[1,24,1024]{2,1,0:T(8,128)(2,1)S(1)}, bf16[1,24,1024]{2,1,0:T(8,128)(2,1)S(1)}, u32[]{:S(2)}, u32[]{:S(2)}) collective-permute-start(bf16[1,24,1024]{2,1,0:T(8,128)(2,1)S(1)} %get-tuple-element.38), channel_id=1, source_target_pairs={{0,12},{4,8},{1,13},{5,9},{2,14},{6,10},{3,15},{7,11},{16,28},{20,... | collective-permute-start | bytes 147464 | tf_op jit(solution)/shard_map/ppermute | solution.py:55
  14.2 0.0 copy-done
  14.2 1.6 %shard_map.149 = (f32[4,16,1024]{2,1,0:T(8,128)S(1)}, f32[4,16,1024]{2,1,0:T(8,128)S(1)}, f32[16,4]{1,0:T(8,128)S(1)}, f32[4,1024]{1,0:T(4,128)S(1)}, f32[1,1024...) custom-call(s32[1]{0:T(128)} %bitcast.key_hbm, ...), custom_call_target="tpu_custom_call" | custom-call | flops 655360 | bytes 786432 | tf_op jit(solution)/shard_map/pallas_call | solution.py:469
  15.8 0.0 collective-permute-done.rest_1_
  15.8 0.0 collective-permute-done.1.rest_2_
  15.8 0.0 collective-permute-done.2.rest_3_
  15.8 0.0 collective-permute-done.3.rest_4_
  15.8 0.1 collective-permute-done.4.rest_5_
  16.0 0.5 %shard_map.150 = (f32[80,1024]{1,0:T(8,128)S(1)}, f32[80,288]{1,0:T(8,128)S(1)}) custom-call(f32[16,4]{1,0:T(8,128)S(1)} %get-tuple-element.29.pick_ref, f32[4,16,1024]{2,1,0:T(8,128)S(1)} %get-tuple-element.30.base_ref, f32[4,1024]{1,0:T(4,128)S(1)} %get-tuple-element.31.cw_ref, f32[1,1024]{1,0:T(1,128)S(1)} %get-tuple-element.32.cb_ref, ...), custom_call_target="tpu_custom_call" | custom-call | flops 47185920 | bytes 1009664 | tf_op jit(solution)/shard_map/pallas_call | solution.py:510
  16.5 0.1 collective-permute-start.5
  16.6 1.3 %collective-permute-done.5.b_ref = f32[80,288]{1,0:T(8,128)S(1)} collective-permute-done((f32[80,288]{1,0:T(8,128)S(1)}, f32[80,288]{1,0:T(8,128)S(1)}, u32[]{:S(2)}, u32[]{:S(2)}) %collective-permute-start.5) | collective-permute-done | bytes 92192 | tf_op jit(solution)/shard_map/ppermute | solution.py:55
  17.9 1.6 %collective-permute-start.6 = (bf16[80,288]{1,0:T(8,128)(2,1)S(1)}, bf16[80,288]{1,0:T(8,128)(2,1)S(1)}, u32[]{:S(2)}, u32[]{:S(2)}) collective-permute-start(bf16[80,288]{1,0:T(8,128)(2,1)S(1)} %get-tuple-element.50), channel_id=1, source_target_pairs={{0,2},{1,3},{2,0},{3,1},{4,6},{5,7},{6,4},{7,5},{8,10},{9,11},{10,... | collective-permute-start | bytes 138248 | tf_op jit(solution)/shard_map/ppermute | solution.py:55
  19.5 1.5 %shard_map.154 = bf16[3,16,1024]{2,1,0:T(8,128)(2,1)} custom-call(s32[1]{0:T(128)} %bitcast.key_hbm, s32[16]{0:T(128)} %child_hbm.3, f32[80,288]{1,0:T(8,128)S(1)} %get-tuple-element.42.after_ref.part_ref, bf16[1,24,1024]{2,1,0:T(8,128)(2,1)S(1)} %get-tuple-element.28.after_ref.rest_0_, bf16[1,24,1024]{2,1,0:T(8,128)(2,1)S(1)} %collective-permute-done.rest_1_, ...), custom_call_target="tpu_custom_call" | custom-call | flops 524288 | bytes 262144 | tf_op jit(solution)/shard_map/pallas_call | solution.py:536
  20.9 0.5 %shard_map.152 = (f32[16,16,1024]{2,1,0:T(8,128)S(1)}, f32[8,8,1024]{2,1,0:T(8,128)S(1)}) custom-call(f32[16,4]{1,0:T(8,128)S(1)} %get-tuple-element.29.pick_ref, f32[80,288]{1,0:T(8,128)S(1)} %get-tuple-element.42.after_ref.part_ref, bf16[1,24,1024]{2,1,0:T(8,128)(2,1)S(1)} %get-tuple-element.28.after_ref.rest_0_, ...), custom_call_target="tpu_custom_call" | custom-call | flops 2621440 | bytes 1310720 | tf_op jit(solution)/shard_map/pallas_call | solution.py:549
  21.5 0.7 %collective-permute-done.6.other_ref = bf16[80,288]{1,0:T(8,128)(2,1)S(1)} collective-permute-done((bf16[80,288]{1,0:T(8,128)(2,1)S(1)}, bf16[80,288]{1,0:T(8,128)(2,1)S(1)}, u32[]{:S(2)}, u32[]{:S(2)}) %collective-permute-start.6) | collective-permute-done | bytes 46112 | tf_op jit(solution)/shard_map/ppermute | solution.py:55
  22.2 3.1 %shard_map.153 = (bf16[16,4,1024]{2,1,0:T(4,128)(2,1)}, f32[16,16,1024]{2,1,0:T(8,128)}) custom-call(s32[1]{0:T(128)} %bitcast.key_hbm, s32[16]{0:T(128)} %child_hbm.3, f32[80,1024]{1,0:T(8,128)S(1)} %get-tuple-element.39.act_ref, f32[4,16,1024]{2,1,0:T(8,128)S(1)} %get-tuple-element.40.gate_ref, f32[16,16,1024]{2,1,0:T(8,128)S(1)} %get-tuple-element.43.own_ref, ...), custom_call_target="tpu_custom_call" | custom-call | flops 10485760 | bytes 1310720 | tf_op jit(solution)/shard_map/pallas_call | solution.py:562
  (1 shorter events, 0.0 us)
Async XLA Ops:
  0.6 13.6 %copy-start = (bf16[16,4,2,1024]{3,2,1,0:T(2,128)(2,1)S(1)}, bf16[16,4,2,1024]{3,2,1,0:T(2,128)(2,1)}, u32[]{:S(2)}) copy-start(bf16[16,4,2,1024]{3,2,1,0:T(2,128)(2,1)} %step_ref.1) | copy-start | bytes 786436
  1.8 14.0 %collective-permute-start = (bf16[1,24,1024]{2,1,0:T(8,128)(2,1)S(1)}, bf16[1,24,1024]{2,1,0:T(8,128)(2,1)S(1)}, u32[]{:S(2)}, u32[]{:S(2)}) collective-permute-start(bf16[1,24,1024]{2,1,0:T(8,128)(2,1)S(1)} %get-tuple-element.34), channel_id=1, source_target_pairs={{8,4},{12,0},{9,5},{13,1},{10,6},{14,2},{11,7},{15,3},{24,20},{28,... | collective-permute-start | bytes 147464 | tf_op jit(solution)/shard_map/ppermute | solution.py:55
  3.1 12.7 %collective-permute-start.1 = (bf16[1,24,1024]{2,1,0:T(8,128)(2,1)S(1)}, bf16[1,24,1024]{2,1,0:T(8,128)(2,1)S(1)}, u32[]{:S(2)}, u32[]{:S(2)}) collective-permute-start(bf16[1,24,1024]{2,1,0:T(8,128)(2,1)S(1)} %get-tuple-element.35), channel_id=1, source_target_pairs={{8,0},{12,4},{9,1},{13,5},{10,2},{14,6},{11,3},{15,7},{24,16},{28,... | collective-permute-start | bytes 147464 | tf_op jit(solution)/shard_map/ppermute | solution.py:55
  4.4 11.4 %collective-permute-start.2 = (bf16[1,24,1024]{2,1,0:T(8,128)(2,1)S(1)}, bf16[1,24,1024]{2,1,0:T(8,128)(2,1)S(1)}, u32[]{:S(2)}, u32[]{:S(2)}) collective-permute-start(bf16[1,24,1024]{2,1,0:T(8,128)(2,1)S(1)} %get-tuple-element.36), channel_id=1, source_target_pairs={{0,4},{4,0},{8,12},{12,8},{1,5},{5,1},{9,13},{13,9},{2,6},{6,2},{1... | collective-permute-start | bytes 147464 | tf_op jit(solution)/shard_map/ppermute | solution.py:55
  7.5 8.3 %collective-permute-start.3 = (bf16[1,24,1024]{2,1,0:T(8,128)(2,1)S(1)}, bf16[1,24,1024]{2,1,0:T(8,128)(2,1)S(1)}, u32[]{:S(2)}, u32[]{:S(2)}) collective-permute-start(bf16[1,24,1024]{2,1,0:T(8,128)(2,1)S(1)} %get-tuple-element.37), channel_id=1, source_target_pairs={{0,8},{4,12},{1,9},{5,13},{2,10},{6,14},{3,11},{7,15},{16,24},{20,... | collective-permute-start | bytes 147464 | tf_op jit(solution)/shard_map/ppermute | solution.py:55
  12.9 3.0 %collective-permute-start.4 = (bf16[1,24,1024]{2,1,0:T(8,128)(2,1)S(1)}, bf16[1,24,1024]{2,1,0:T(8,128)(2,1)S(1)}, u32[]{:S(2)}, u32[]{:S(2)}) collective-permute-start(bf16[1,24,1024]{2,1,0:T(8,128)(2,1)S(1)} %get-tuple-element.38), channel_id=1, source_target_pairs={{0,12},{4,8},{1,13},{5,9},{2,14},{6,10},{3,15},{7,11},{16,28},{20,... | collective-permute-start | bytes 147464 | tf_op jit(solution)/shard_map/ppermute | solution.py:55
  16.5 1.4 %collective-permute-start.5 = (f32[80,288]{1,0:T(8,128)S(1)}, f32[80,288]{1,0:T(8,128)S(1)}, u32[]{:S(2)}, u32[]{:S(2)}) collective-permute-start(f32[80,288]{1,0:T(8,128)S(1)} %get-tuple-element.41.a_ref), channel_id=1, source_target_pairs={{0,1},{1,0},{2,3},{3,2},{4,5},{5,4},{6,7},{7,6},{8,9},{9,8},{10,11... | collective-permute-start | bytes 276488 | tf_op jit(solution)/shard_map/ppermute | solution.py:55
  17.9 4.3 %collective-permute-start.6 = (bf16[80,288]{1,0:T(8,128)(2,1)S(1)}, bf16[80,288]{1,0:T(8,128)(2,1)S(1)}, u32[]{:S(2)}, u32[]{:S(2)}) collective-permute-start(bf16[80,288]{1,0:T(8,128)(2,1)S(1)} %get-tuple-element.50), channel_id=1, source_target_pairs={{0,2},{1,3},{2,0},{3,1},{4,6},{5,7},{6,4},{7,5},{8,10},{9,11},{10,... | collective-permute-start | bytes 138248 | tf_op jit(solution)/shard_map/ppermute | solution.py:55

commit v8 on v7

--- a/solution.py
+++ b/solution.py
@@ -15,7 +15,7 @@
 WEIGHT_PARTS = 6
 DT_PARTS = 4
 DIRECT = 4
-ROUNDS = ((3, (2, 3)), (2, (2, 3)), (1, (0, 1, 2, 3)), (2, (0, 1)), (3, (0, 1)))
+SENDS = ((2, 3, 1, 0), (3, 2, 0, 1), (1, 0, 3, 2))
 
 
 def vmem():
@@ -50,9 +50,27 @@
     )
 
 
-def swap(value, axis, distance, senders=None):
-    senders = range(lax.axis_size(axis)) if senders is None else senders
-    return lax.ppermute(value, axis, [(i, i ^ distance) for i in senders])
+def swap(value, axis, distance):
+    size = lax.axis_size(axis)
+    return lax.ppermute(value, axis, [(i, i ^ distance) for i in range(size)])
+
+
+def chosen(number, values):
+    total = values[0]
+    for i in range(1, len(values)):
+        total = jnp.where(number == i, values[i], total)
+    return total
+
+
+def block_of(sender, owner, direct):
+    if not direct:
+        return sender
+    table = [
+        [0 if s == r else 1 + [to[s] for to in SENDS].index(r) for s in range(DIRECT)]
+        for r in range(DIRECT)
+    ]
+    places = [chosen(owner, [row[s] for row in table]) for s in range(DIRECT)]
+    return chosen(sender, places)
 
 
 def all_of(copies):
@@ -63,13 +81,7 @@
 
 
 def read_messages(refs):
-    if len(refs) == 1:
-        return [refs[0][i].astype(F32) for i in range(refs[0].shape[0])]
-    held = [refs[0][0].astype(F32)] + [None] * (DIRECT - 1)
-    for ref, (k, _) in zip(refs[1:], ROUNDS):
-        came = ref[0].astype(F32)
-        held[k] = came if held[k] is None else held[k] + came
-    return held
+    return [ref[i].astype(F32) for ref in refs for i in range(ref.shape[0])]
 
 
 def in_parts(source, target, sems, first, count):
@@ -81,11 +93,12 @@
     ]
 
 
-def scalar_onehot(numbers_s, key, shape):
+def scalar_onehot(senders_s, owner, shape, direct):
     row_of = lax.broadcasted_iota(jnp.int32, shape, 0)
     wanted = jnp.zeros(shape, jnp.int32)
     for b in range(shape[0]):
-        wanted = jnp.where(row_of == b, jnp.bitwise_xor(numbers_s[b], key), wanted)
+        wanted = jnp.where(row_of == b, senders_s[b], wanted)
+    wanted = block_of(wanted, owner, direct)
     return (wanted == lax.broadcasted_iota(jnp.int32, shape, 1)).astype(F32)
 
 
@@ -96,34 +109,42 @@
     return total
 
 
-def pack_kernel(direct, key_hbm, rows_hbm, prompt_hbm, step_hbm, conv_hbm, ssm_hbm, *rest):
-    outs, (key_s, rows_s, prompt_s, step, conv, ssm, sems) = rest[:-7], rest[-7:]
+def pack_kernel(direct, owner_hbm, rows_hbm, prompt_hbm, step_hbm, conv_hbm, ssm_hbm, *rest):
+    outs, (owner_s, rows_s, prompt_s, step, conv, ssm, sems) = rest[:-7], rest[-7:]
     owners = rows_hbm.shape[0]
     channels = step_hbm.shape[3]
     copies = [
-        pltpu.make_async_copy(key_hbm, key_s, sems.at[4]),
+        pltpu.make_async_copy(owner_hbm, owner_s, sems.at[4]),
         pltpu.make_async_copy(rows_hbm, rows_s, sems.at[0]),
         pltpu.make_async_copy(prompt_hbm, prompt_s, sems.at[1]),
         pltpu.make_async_copy(conv_hbm, conv, sems.at[2]),
         pltpu.make_async_copy(ssm_hbm, ssm, sems.at[3]),
     ]
     all_of(copies + in_parts(step_hbm, step, sems, 5, 4))
-    key = key_s[0]
+    owner = owner_s[0]
     window = conv[0].astype(F32)
-    for k in range(owners):
-        target = jnp.bitwise_xor(key, k)
+
+    def write(ref, target):
         row = jnp.maximum(rows_s[target], 0)
         xs = step[row, :, 0, :].astype(F32)
-        told = jnp.bitwise_xor(prompt_s[row], target) if direct else prompt_s[row]
+        told = block_of(prompt_s[row], target, direct)
         pieces = [xs, window, jnp.full((1, channels), told.astype(F32), F32)]
-        message = jnp.concatenate(pieces + [ssm[0]], axis=0).astype(BF16)
-        if direct:
-            into = [outs[0].at[0]] if k == 0 else []
-            into += [ref.at[0] for ref, (d, _) in zip(outs[1:], ROUNDS) if d == k]
-        else:
-            into = [outs[0].at[k]]
-        for ref in into:
-            ref[...] = message
+        if ref.shape[0] > sum(p.shape[0] for p in pieces):
+            pieces.append(ssm[0])
+        ref[...] = jnp.concatenate(pieces, axis=0).astype(BF16)
+
+    if direct:
+        write(outs[0].at[0], owner)
+        for ref, to in zip(outs[1:], SENDS):
+            write(ref.at[0], chosen(owner, to))
+    else:
+        for target in range(owners):
+            write(outs[0].at[target], target)
+
+
+def pair_kernel(text, own_ref, other_ref, pair_ref):
+    states = [ref[0].astype(F32)[text:, :] for ref in (own_ref, other_ref)]
+    pair_ref[0] = jnp.concatenate(states, axis=0).astype(BF16)
 
 
 def silu(v):
@@ -131,8 +152,10 @@
 
 
 def prepare_kernel(
-    key_hbm,
+    direct,
+    owner_hbm,
     prompt_hbm,
+    child_hbm,
     step_ref,
     cw_hbm,
     cb_hbm,
@@ -145,6 +168,7 @@
     base_ref,
     gate_ref,
     pick_ref,
+    child_ref,
     cw_ref,
     cb_ref,
     xwt_ref,
@@ -153,8 +177,9 @@
     dtw_ref,
     dtb_ref,
     skip_ref,
-    key_s,
+    owner_s,
     prompt_s,
+    child_s,
     alog,
     sems,
 ):
@@ -165,8 +190,9 @@
             (
                 (cw_hbm, cw_ref),
                 (cb_hbm, cb_ref),
-                (key_hbm, key_s),
+                (owner_hbm, owner_s),
                 (prompt_hbm, prompt_s),
+                (child_hbm, child_s),
                 (alog_hbm, alog),
                 (dtb_hbm, dtb_ref),
                 (skip_hbm, skip_ref),
@@ -189,7 +215,8 @@
         for k in range(max(0, taps - 1 - t), taps - 1):
             total = total + cw_ref[k : k + 1, :] * xs[t + k - taps + 1]
         base_ref[t] = total
-    pick_ref[...] = scalar_onehot(prompt_s, key_s[0], pick_ref.shape)
+    pick_ref[...] = scalar_onehot(prompt_s, owner_s[0], pick_ref.shape, direct)
+    child_ref[...] = scalar_onehot(child_s, owner_s[0], child_ref.shape, direct)
     rate = jnp.exp(alog[...]) * (-math.log2(math.e))
     rate_ref[...] = rate
     half = (twin_ref.shape[1] // 2, rate.shape[1])
@@ -248,32 +275,31 @@
     short_ref[...] = total.astype(BF16)
 
 
-def windows_kernel(n_msgs, steps, key_hbm, child_hbm, after_ref, *rest):
+def windows_kernel(n_msgs, steps, child_ref, after_ref, *rest):
     del after_ref
-    msgs, (conv_ref, key_s, child_s, sems) = rest[:n_msgs], rest[n_msgs:]
-    all_of(
-        [
-            pltpu.make_async_copy(key_hbm, key_s, sems.at[0]),
-            pltpu.make_async_copy(child_hbm, child_s, sems.at[1]),
-        ]
-    )
-    past, rb, _ = conv_ref.shape
+    msgs, (conv_ref,) = rest[:n_msgs], rest[n_msgs:]
     held = read_messages(msgs)
-    child = scalar_onehot(child_s, key_s[0], (rb, len(held)))
+    past = conv_ref.shape[0]
     for k in range(past):
         at = steps - past + k
-        conv_ref[k] = pick_rows(child, [h[at : at + 1, :] for h in held]).astype(BF16)
-
-
-def start_kernel(n_msgs, text, pick_ref, after_ref, *rest):
+        rows = [h[at : at + 1, :] for h in held]
+        conv_ref[k] = pick_rows(child_ref[...], rows).astype(BF16)
+
+
+def start_kernel(n_msgs, n_pairs, text, pick_ref, after_ref, *rest):
     del after_ref
-    msgs, (own_ref, slot_ref, state_s) = rest[:n_msgs], rest[n_msgs:]
+    msgs, rest = rest[:n_msgs], rest[n_msgs:]
+    pairs, (own_ref, slot_ref, state_s) = rest[:n_pairs], rest[n_pairs:]
     n_state = own_ref.shape[0]
     held = read_messages(msgs)
     owners = len(held)
     numbers = jnp.concatenate([h[text - 1 : text, :] for h in held], axis=0)
-    for k, h in enumerate(held):
-        state_s[k] = h[text:, :]
+    states = [h[text:, :] for h in held]
+    for ref in pairs:
+        both = ref[0].astype(F32)
+        states[3], states[2] = both[:n_state, :], both[n_state:, :]
+    for k, state in enumerate(states):
+        state_s[k] = state
     own = pick_ref[...]
     slot = slot_onehot(numbers, owners)
 
@@ -290,7 +316,8 @@
 
 
 def decode_kernel(
-    key_hbm,
+    direct,
+    owner_hbm,
     child_hbm,
     act_ref,
     gate_ref,
@@ -305,7 +332,7 @@
     other_ref,
     dec_ref,
     child_ssm,
-    key_s,
+    owner_s,
     child_s,
     delta_s,
     gain_s,
@@ -319,7 +346,7 @@
     sems,
 ):
     scalars = [
-        pltpu.make_async_copy(key_hbm, key_s, sems.at[0]),
+        pltpu.make_async_copy(owner_hbm, owner_s, sems.at[0]),
         pltpu.make_async_copy(child_hbm, child_s, sems.at[1]),
     ]
     for copy in scalars:
@@ -374,7 +401,7 @@
         copy.wait()
     copies = []
     for j in range(rb):
-        at = jnp.bitwise_xor(child_s[j], key_s[0])
+        at = block_of(child_s[j], owner_s[0], direct)
         copy = pltpu.make_async_copy(slots_s.at[at], child_ssm.at[j], sems.at[2 + j])
         copy.start()
         copies.append(copy)
@@ -428,11 +455,10 @@
     short = taps - 1 + steps + 1
     depth = short + n_state
     direct = owners == DIRECT
-    me = lax.axis_index("branch").astype(jnp.int32).reshape(1)
-    key = pinned(me if direct else jnp.zeros((1,), jnp.int32))
+    owner = pinned(lax.axis_index("branch").astype(jnp.int32).reshape(1))
 
     if direct:
-        msg_shapes = [(1, depth, channels)] * (1 + len(ROUNDS))
+        msg_shapes = [(1, d, channels) for d in (depth, depth, short, short)]
     else:
         msg_shapes = [(owners, depth, channels)]
     msgs = call(
@@ -451,7 +477,7 @@
         ],
         nbytes=owners * depth * channels * 2,
     )(
-        key,
+        owner,
         pinned(send_rows.reshape(owners)),
         pinned(prompt_of),
         pinned(step_in),
@@ -460,17 +486,27 @@
     )
     if direct:
         own = msgs[0]
-        msgs = [own] + [swap(m, "branch", k, who) for m, (k, who) in zip(msgs[1:], ROUNDS)]
-        after = own
+        msgs = [own] + [
+            lax.ppermute(m, "branch", list(enumerate(to))) for m, to in zip(msgs[1:], SENDS)
+        ]
+        pair = call(
+            functools.partial(pair_kernel, short),
+            shaped((1, 2 * n_state, channels), BF16),
+            [vmem()] * 2,
+            vmem(),
+            nbytes=8 * n_state * channels,
+        )(own, msgs[1])
+        pairs, after = [swap(pair, "branch", 1)], own
     else:
         msgs = [lax.all_to_all(msgs[0], "branch", split_axis=0, concat_axis=0, tiled=True)]
-        after = msgs[0]
+        pairs, after = [], msgs[0]
     n_msgs = len(msgs)
     near = call(
-        prepare_kernel,
+        functools.partial(prepare_kernel, direct),
         [
             shaped((steps, rb, channels), F32),
             shaped((steps, rb, channels), F32),
+            shaped((rb, owners), F32),
             shaped((rb, owners), F32),
             shaped((taps, channels), F32),
             shaped((1, channels), F32),
@@ -481,20 +517,22 @@
             shaped((1, channels), F32),
             shaped((1, channels), F32),
         ],
-        [hbm(), hbm(), vmem()] + [hbm()] * 7 + [anywhere()],
-        [vmem()] * 11,
+        [hbm()] * 3 + [vmem()] + [hbm()] * 7 + [anywhere()],
+        [vmem()] * 12,
         [
             pltpu.SMEM((1,), jnp.int32),
             pltpu.SMEM((rb,), jnp.int32),
+            pltpu.SMEM((rb,), jnp.int32),
             pltpu.VMEM((n_state, channels), F32),
-            pltpu.SemaphoreType.DMA((7 + WEIGHT_PARTS + DT_PARTS,)),
+            pltpu.SemaphoreType.DMA((8 + WEIGHT_PARTS + DT_PARTS,)),
         ],
         flops=10 * steps * rb * channels,
         nbytes=12 * steps * rb * channels,
         trans=steps * rb * channels,
     )(
-        key,
+        owner,
         pinned(prompt_of),
+        pinned(child_slot),
         step_in,
         pinned(conv_weight),
         pinned(conv_bias[None]),
@@ -505,8 +543,8 @@
         pinned(skip[None]),
         after,
     )
-    base, gate, pick, taps_near, bias_near, weight_near = near[:6]
-    rate, twin, dtw_near, dtb_near, skip_near = near[6:]
+    base, gate, pick, child_pick, taps_near, bias_near, weight_near = near[:7]
+    rate, twin, dtw_near, dtb_near, skip_near = near[7:]
     act, part = call(
         functools.partial(project_kernel, n_msgs),
         [
@@ -536,31 +574,26 @@
     child_conv = call(
         functools.partial(windows_kernel, n_msgs, steps),
         shaped((taps - 1, rb, channels), BF16),
-        [hbm()] * 2 + [anywhere()] + [vmem()] * n_msgs,
+        [vmem(), anywhere()] + [vmem()] * n_msgs,
         vmem(),
-        [
-            pltpu.SMEM((1,), jnp.int32),
-            pltpu.SMEM((rb,), jnp.int32),
-            pltpu.SemaphoreType.DMA((2,)),
-        ],
         flops=2 * owners * taps * rb * channels,
         nbytes=4 * taps * rb * channels,
-    )(key, pinned(child_slot), part, *msgs)
+    )(child_pick, part, *msgs)
     own_start, slot_start = call(
-        functools.partial(start_kernel, n_msgs, short),
+        functools.partial(start_kernel, n_msgs, len(pairs), short),
         [
             shaped((n_state, rb, channels), F32),
             shaped((n_state // 2, 2 * owners, channels), F32),
         ],
-        [vmem(), anywhere()] + [vmem()] * n_msgs,
+        [vmem(), anywhere()] + [vmem()] * (n_msgs + len(pairs)),
         [vmem()] * 2,
         [pltpu.VMEM((owners, n_state, channels), F32)],
         flops=2 * owners * n_state * (rb + owners) * channels,
         nbytes=4 * n_state * (rb + owners) * channels,
-    )(pick, part, *msgs)
+    )(pick, part, *msgs, *pairs)
 
     decoded, child_ssm = call(
-        decode_kernel,
+        functools.partial(decode_kernel, direct),
         [
             shaped((rb, steps, channels), BF16),
             shaped((rb, n_state, channels), F32),
@@ -585,7 +618,7 @@
         nbytes=(rb + owners) * n_state * channels * 4,
         trans=rows * n_state * channels,
     )(
-        key,
+        owner,
         pinned(child_slot),
         act,
         gate,

time: 25.6 us -> 20.5 us (0.80)
  starting transfers between devices: 14 us -> 8.76 us
  waiting for transfers between devices: 2.15 us -> 3.09 us
  Pallas kernels: 8.32 us -> 7.67 us
    ppermute x7 -> x6, starting transfers between devices: 14 us -> 8.76 us  [the longest x3 5.67 us: on_device(): lax.ppermute(m, 'branch', list(enumerate(to)))]
    ppermute x7 -> x6, waiting for transfers between devices: 2.15 us -> 3.09 us  [the longest x3 1.67 us: on_device(): lax.ppermute(m, 'branch', list(enumerate(to)))]
    pallas_call x1, Pallas kernels: 1.48 us -> 0.78 us  [on_device(): call(functools.partial(windows_kernel, n_msgs, steps), shaped((taps - 1,...]
    pallas_call x3 -> x4, Pallas kernels: 5.17 us -> 5.21 us  [the longest x1 3.12 us: on_device(): call(functools.partial(decode_kernel, direct), [shaped((rb, steps, channe...]
  transfers between devices with their start and end apart: 7 -> 6, of which waited for: 3 -> 4; matrix products, arithmetic and copies ran while one was open for 0% -> 0% of each run, Pallas kernels for 14% -> 14%
where the time goes in v8:
time: 20.5 us; the launch traced here: 20.2 us
  starting transfers between devices  8.76 us (43%)
  Pallas kernels  7.67 us (37%)
  waiting for transfers between devices  3.09 us (15%)
  between operations  0.7 us (3%)
    ppermute x3, starting transfers between devices, on_device(): lax.ppermute(m, 'branch', list(enumerate(to)))  5.67 us
    pallas_call x1, Pallas kernels, on_device(): call(functools.partial(decode_kernel, direct), [shaped((rb, steps, channe...  3.12 us
    ppermute x3, starting transfers between devices, swap(): return lax.ppermute(value, axis, [(i, i ^ distance) for i in range(size)])  3.09 us
    ppermute x3, waiting for transfers between devices, on_device(): lax.ppermute(m, 'branch', list(enumerate(to)))  1.67 us
    pallas_call x1, Pallas kernels, on_device(): call(functools.partial(prepare_kernel, direct), [shaped((steps, rb, chann...  1.55 us
    ppermute x3, waiting for transfers between devices, swap(): return lax.ppermute(value, axis, [(i, i ^ distance) for i in range(size)])  1.41 us
    pallas_call x1, Pallas kernels, on_device(): call(functools.partial(pack_kernel, direct), [shaped(s, BF16) for s in ms...  1.16 us
    pallas_call x1, Pallas kernels, on_device(): call(functools.partial(windows_kernel, n_msgs, steps), shaped((taps - 1,...  0.78 us
  transfers between devices with their start and end apart: 6, of which 4 were waited for; matrix products, arithmetic and copies ran while one was open for 0% of the time, Pallas kernels for 14%

profile of v8, /device:TPU:0, one launch (start us, length us, event | category | flops | bytes accessed | tf_op | source)
XLA Modules:
  0.0 20.2 jit_solution(12511216458253727237)
XLA Ops:
  0.6 0.0 copy-start
  0.6 1.2 %shard_map.148 = (bf16[1,24,1024]{2,1,0:T(8,128)(2,1)S(1)}, bf16[1,24,1024]{2,1,0:T(8,128)(2,1)S(1)}, bf16[1,8,1024]{2,1,0:T(8,128)(2,1)S(1)}, bf16[1,8,1024]{2,1,0:T(8,128)(2,1)S(1)}) custom-call(s32[1]{0:T(128)} %bitcast.owner_hbm, s32[4]{0:T(128)} %bitcast.12, s32[16]{0:T(128)} %prompt_hbm.3, bf16[16,4,2,1024]{3,2,1,0:T(2,128)(2,1)} %step_ref.1, ...), custom_call_target="tpu_custom_call" | custom-call | bytes 196608 | tf_op jit(solution)/shard_map/pallas_call | solution.py:464
  1.8 4.1 %collective-permute-start = (bf16[1,24,1024]{2,1,0:T(8,128)(2,1)S(1)}, bf16[1,24,1024]{2,1,0:T(8,128)(2,1)S(1)}, u32[]{:S(2)}, u32[]{:S(2)}) collective-permute-start(bf16[1,24,1024]{2,1,0:T(8,128)(2,1)S(1)} %get-tuple-element.33), channel_id=1, source_target_pairs={{0,8},{4,12},{8,4},{12,0},{1,9},{5,13},{9,5},{13,1},{2,10},{6,14},... | collective-permute-start | bytes 147464 | tf_op jit(solution)/shard_map/ppermute | solution.py:490
  5.9 1.1 %collective-permute-start.1 = (bf16[1,8,1024]{2,1,0:T(8,128)(2,1)S(1)}, bf16[1,8,1024]{2,1,0:T(8,128)(2,1)S(1)}, u32[]{:S(2)}, u32[]{:S(2)}) collective-permute-start(bf16[1,8,1024]{2,1,0:T(8,128)(2,1)S(1)} %get-tuple-element.34), channel_id=1, source_target_pairs={{0,12},{4,8},{8,0},{12,4},{1,13},{5,9},{9,1},{13,5},{2,14},{6,10},... | collective-permute-start | bytes 49160 | tf_op jit(solution)/shard_map/ppermute | solution.py:490
  7.0 0.5 %collective-permute-start.2 = (bf16[1,8,1024]{2,1,0:T(8,128)(2,1)S(1)}, bf16[1,8,1024]{2,1,0:T(8,128)(2,1)S(1)}, u32[]{:S(2)}, u32[]{:S(2)}) collective-permute-start(bf16[1,8,1024]{2,1,0:T(8,128)(2,1)S(1)} %get-tuple-element.35), channel_id=1, source_target_pairs={{0,4},{4,0},{8,12},{12,8},{1,5},{5,1},{9,13},{13,9},{2,6},{6,2},{1... | collective-permute-start | bytes 49160 | tf_op jit(solution)/shard_map/ppermute | solution.py:490
  7.5 0.0 copy-done
  7.5 1.6 %shard_map.149 = (f32[4,16,1024]{2,1,0:T(8,128)S(1)}, f32[4,16,1024]{2,1,0:T(8,128)S(1)}, f32[16,4]{1,0:T(8,128)S(1)}, f32[16,4]{1,0:T(8,128)S(1)}, f32[4,1024]{...) custom-call(s32[1]{0:T(128)} %bitcast.owner_hbm, ...), custom_call_target="tpu_custom_call" | custom-call | flops 655360 | bytes 786432 | tf_op jit(solution)/shard_map/pallas_call | solution.py:504
  9.0 1.5 %collective-permute-done.1.rest_2_ = bf16[1,8,1024]{2,1,0:T(8,128)(2,1)S(1)} collective-permute-done((bf16[1,8,1024]{2,1,0:T(8,128)(2,1)S(1)}, bf16[1,8,1024]{2,1,0:T(8,128)(2,1)S(1)}, u32[]{:S(2)}, u32[]{:S(2)}) %collective-permute-start.1) | collective-permute-done | bytes 16416 | tf_op jit(solution)/shard_map/ppermute | solution.py:490
  10.5 0.2 collective-permute-done.2.rest_3_
  10.7 0.0 collective-permute-done.rest_1_.other_ref
  10.7 0.5 %shard_map.150 = (f32[80,1024]{1,0:T(8,128)S(1)}, f32[80,288]{1,0:T(8,128)S(1)}) custom-call(f32[16,4]{1,0:T(8,128)S(1)} %get-tuple-element.28.pick_ref, f32[4,16,1024]{2,1,0:T(8,128)S(1)} %get-tuple-element.29.base_ref, f32[4,1024]{1,0:T(4,128)S(1)} %get-tuple-element.30.cw_ref, f32[1,1024]{1,0:T(1,128)S(1)} %get-tuple-element.31.cb_ref, ...), custom_call_target="tpu_custom_call" | custom-call | flops 47185920 | bytes 1009664 | tf_op jit(solution)/shard_map/pallas_call | solution.py:548
  11.2 0.1 collective-permute-start.3
  11.3 1.5 %collective-permute-start.4 = (bf16[1,32,1024]{2,1,0:T(8,128)(2,1)S(1)}, bf16[1,32,1024]{2,1,0:T(8,128)(2,1)S(1)}, u32[]{:S(2)}, u32[]{:S(2)}) collective-permute-start(bf16[1,32,1024]{2,1,0:T(8,128)(2,1)S(1)} %shard_map.152), channel_id=1, source_target_pairs={{0,4},{4,0},{8,12},{12,8},{1,5},{5,1},{9,13},{13,9},{2,6},{6,2},{1... | collective-permute-start | bytes 196616 | tf_op jit(solution)/shard_map/ppermute | solution.py:55
  12.8 0.0 collective-permute-done.3.b_ref
  12.8 1.6 %collective-permute-start.5 = (bf16[80,288]{1,0:T(8,128)(2,1)S(1)}, bf16[80,288]{1,0:T(8,128)(2,1)S(1)}, u32[]{:S(2)}, u32[]{:S(2)}) collective-permute-start(bf16[80,288]{1,0:T(8,128)(2,1)S(1)} %get-tuple-element.47), channel_id=1, source_target_pairs={{0,2},{1,3},{2,0},{3,1},{4,6},{5,7},{6,4},{7,5},{8,10},{9,11},{10,... | collective-permute-start | bytes 138248 | tf_op jit(solution)/shard_map/ppermute | solution.py:55
  14.4 0.8 %shard_map.155 = bf16[3,16,1024]{2,1,0:T(8,128)(2,1)} custom-call(f32[16,4]{1,0:T(8,128)S(1)} %get-tuple-element.50.child_ref, f32[80,288]{1,0:T(8,128)S(1)} %get-tuple-element.39.after_ref.part_ref, bf16[1,24,1024]{2,1,0:T(8,128)(2,1)S(1)} %get-tuple-element.27.after_ref.rest_0_.own_ref, bf16[1,24,1024]{2,1,0:T(8,128)(2,1)S(1)} %collective-permute-done.rest_1_.other_ref, ...), custom_call_target="tpu_custom_call" | custom-call | flops 524288 | bytes 262144 | tf_op jit(solution)/shard_map/pallas_call | solution.py:574
  15.2 0.7 %collective-permute-done.4.rest_4_ = bf16[1,32,1024]{2,1,0:T(8,128)(2,1)S(1)} collective-permute-done((bf16[1,32,1024]{2,1,0:T(8,128)(2,1)S(1)}, bf16[1,32,1024]{2,1,0:T(8,128)(2,1)S(1)}, u32[]{:S(2)}, u32[]{:S(2)}) %collective-permute-start.4) | collective-permute-done | bytes 65568 | tf_op jit(solution)/shard_map/ppermute | solution.py:55
  15.8 0.5 %shard_map.153 = (f32[16,16,1024]{2,1,0:T(8,128)S(1)}, f32[8,8,1024]{2,1,0:T(8,128)S(1)}) custom-call(f32[16,4]{1,0:T(8,128)S(1)} %get-tuple-element.28.pick_ref, f32[80,288]{1,0:T(8,128)S(1)} %get-tuple-element.39.after_ref.part_ref, bf16[1,24,1024]{2,1,0:T(8,128)(2,1)S(1)} %get-tuple-element.27.after_ref.rest_0_.own_ref, ...), custom_call_target="tpu_custom_call" | custom-call | flops 2621440 | bytes 1310720 | tf_op jit(solution)/shard_map/pallas_call | solution.py:582
  16.4 0.7 %collective-permute-done.5.other_ref = bf16[80,288]{1,0:T(8,128)(2,1)S(1)} collective-permute-done((bf16[80,288]{1,0:T(8,128)(2,1)S(1)}, bf16[80,288]{1,0:T(8,128)(2,1)S(1)}, u32[]{:S(2)}, u32[]{:S(2)}) %collective-permute-start.5) | collective-permute-done | bytes 46112 | tf_op jit(solution)/shard_map/ppermute | solution.py:55
  17.1 3.1 %shard_map.154 = (bf16[16,4,1024]{2,1,0:T(4,128)(2,1)}, f32[16,16,1024]{2,1,0:T(8,128)}) custom-call(s32[1]{0:T(128)} %bitcast.owner_hbm, s32[16]{0:T(128)} %child_hbm.3, f32[80,1024]{1,0:T(8,128)S(1)} %get-tuple-element.36.act_ref, f32[4,16,1024]{2,1,0:T(8,128)S(1)} %get-tuple-element.37.gate_ref, f32[16,16,1024]{2,1,0:T(8,128)S(1)} %get-tuple-element.40.own_ref, ...), custom_call_target="tpu_custom_call" | custom-call | flops 10485760 | bytes 1310720 | tf_op jit(solution)/shard_map/pallas_call | solution.py:595
  (2 shorter events, 0.0 us)
Async XLA Ops:
  0.6 6.9 %copy-start = (bf16[16,4,2,1024]{3,2,1,0:T(2,128)(2,1)S(1)}, bf16[16,4,2,1024]{3,2,1,0:T(2,128)(2,1)}, u32[]{:S(2)}) copy-start(bf16[16,4,2,1024]{3,2,1,0:T(2,128)(2,1)} %step_ref.1) | copy-start | bytes 786436
  1.8 8.9 %collective-permute-start = (bf16[1,24,1024]{2,1,0:T(8,128)(2,1)S(1)}, bf16[1,24,1024]{2,1,0:T(8,128)(2,1)S(1)}, u32[]{:S(2)}, u32[]{:S(2)}) collective-permute-start(bf16[1,24,1024]{2,1,0:T(8,128)(2,1)S(1)} %get-tuple-element.33), channel_id=1, source_target_pairs={{0,8},{4,12},{8,4},{12,0},{1,9},{5,13},{9,5},{13,1},{2,10},{6,14},... | collective-permute-start | bytes 147464 | tf_op jit(solution)/shard_map/ppermute | solution.py:490
  5.9 4.6 %collective-permute-start.1 = (bf16[1,8,1024]{2,1,0:T(8,128)(2,1)S(1)}, bf16[1,8,1024]{2,1,0:T(8,128)(2,1)S(1)}, u32[]{:S(2)}, u32[]{:S(2)}) collective-permute-start(bf16[1,8,1024]{2,1,0:T(8,128)(2,1)S(1)} %get-tuple-element.34), channel_id=1, source_target_pairs={{0,12},{4,8},{8,0},{12,4},{1,13},{5,9},{9,1},{13,5},{2,14},{6,10},... | collective-permute-start | bytes 49160 | tf_op jit(solution)/shard_map/ppermute | solution.py:490
  7.0 3.7 %collective-permute-start.2 = (bf16[1,8,1024]{2,1,0:T(8,128)(2,1)S(1)}, bf16[1,8,1024]{2,1,0:T(8,128)(2,1)S(1)}, u32[]{:S(2)}, u32[]{:S(2)}) collective-permute-start(bf16[1,8,1024]{2,1,0:T(8,128)(2,1)S(1)} %get-tuple-element.35), channel_id=1, source_target_pairs={{0,4},{4,0},{8,12},{12,8},{1,5},{5,1},{9,13},{13,9},{2,6},{6,2},{1... | collective-permute-start | bytes 49160 | tf_op jit(solution)/shard_map/ppermute | solution.py:490
  11.2 1.6 %collective-permute-start.3 = (f32[80,288]{1,0:T(8,128)S(1)}, f32[80,288]{1,0:T(8,128)S(1)}, u32[]{:S(2)}, u32[]{:S(2)}) collective-permute-start(f32[80,288]{1,0:T(8,128)S(1)} %get-tuple-element.38.a_ref), channel_id=1, source_target_pairs={{0,1},{1,0},{2,3},{3,2},{4,5},{5,4},{6,7},{7,6},{8,9},{9,8},{10,11... | collective-permute-start | bytes 276488 | tf_op jit(solution)/shard_map/ppermute | solution.py:55
  11.3 4.5 %collective-permute-start.4 = (bf16[1,32,1024]{2,1,0:T(8,128)(2,1)S(1)}, bf16[1,32,1024]{2,1,0:T(8,128)(2,1)S(1)}, u32[]{:S(2)}, u32[]{:S(2)}) collective-permute-start(bf16[1,32,1024]{2,1,0:T(8,128)(2,1)S(1)} %shard_map.152), channel_id=1, source_target_pairs={{0,4},{4,0},{8,12},{12,8},{1,5},{5,1},{9,13},{13,9},{2,6},{6,2},{1... | collective-permute-start | bytes 196616 | tf_op jit(solution)/shard_map/ppermute | solution.py:55
  12.8 4.3 %collective-permute-start.5 = (bf16[80,288]{1,0:T(8,128)(2,1)S(1)}, bf16[80,288]{1,0:T(8,128)(2,1)S(1)}, u32[]{:S(2)}, u32[]{:S(2)}) collective-permute-start(bf16[80,288]{1,0:T(8,128)(2,1)S(1)} %get-tuple-element.47), channel_id=1, source_target_pairs={{0,2},{1,3},{2,0},{3,1},{4,6},{5,7},{6,4},{7,5},{8,10},{9,11},{10,... | collective-permute-start | bytes 138248 | tf_op jit(solution)/shard_map/ppermute | solution.py:55

commit v9 on v8

--- a/solution.py
+++ b/solution.py
@@ -70,7 +70,7 @@
         for r in range(DIRECT)
     ]
     places = [chosen(owner, [row[s] for row in table]) for s in range(DIRECT)]
-    return chosen(sender, places)
+    return places[sender] if isinstance(sender, int) else chosen(sender, places)
 
 
 def all_of(copies):
@@ -127,8 +127,8 @@
     def write(ref, target):
         row = jnp.maximum(rows_s[target], 0)
         xs = step[row, :, 0, :].astype(F32)
-        told = block_of(prompt_s[row], target, direct)
-        pieces = [xs, window, jnp.full((1, channels), told.astype(F32), F32)]
+        number = prompt_s[row].astype(F32)
+        pieces = [xs, window, jnp.full((1, channels), number, F32)]
         if ref.shape[0] > sum(p.shape[0] for p in pieces):
             pieces.append(ssm[0])
         ref[...] = jnp.concatenate(pieces, axis=0).astype(BF16)
@@ -169,6 +169,7 @@
     gate_ref,
     pick_ref,
     child_ref,
+    sender_ref,
     cw_ref,
     cb_ref,
     xwt_ref,
@@ -217,6 +218,11 @@
         base_ref[t] = total
     pick_ref[...] = scalar_onehot(prompt_s, owner_s[0], pick_ref.shape, direct)
     child_ref[...] = scalar_onehot(child_s, owner_s[0], child_ref.shape, direct)
+    column = lax.broadcasted_iota(jnp.int32, sender_ref.shape, 1)
+    sender = column
+    for sent in range(sender_ref.shape[1] if direct else 0):
+        sender = jnp.where(column == block_of(sent, owner_s[0], direct), sent, sender)
+    sender_ref[...] = sender.astype(F32)
     rate = jnp.exp(alog[...]) * (-math.log2(math.e))
     rate_ref[...] = rate
     half = (twin_ref.shape[1] // 2, rate.shape[1])
@@ -227,13 +233,13 @@
         copy.wait()
 
 
-def slot_onehot(numbers, owners):
-    column = lax.broadcasted_iota(jnp.int32, (numbers.shape[0], owners), 1)
-    return (numbers[:, :owners].astype(jnp.int32) == column).astype(F32)
-
-
-def project_kernel(n_msgs, pick_ref, base_ref, cw_ref, cb_ref, xwt_ref, *rest):
-    msgs, (act_ref, part_ref) = rest[:n_msgs], rest[n_msgs:]
+def slot_onehot(numbers, sender_ref):
+    owners = sender_ref.shape[1]
+    return (numbers[:, :owners] == sender_ref[...]).astype(F32)
+
+
+def project_kernel(n_msgs, pick_ref, sender_ref, base_ref, cw_ref, cb_ref, xwt_ref, *rest):
+    msgs, (act_ref, part_ref, short_ref) = rest[:n_msgs], rest[n_msgs:]
     taps = cw_ref.shape[0]
     steps, rb, _ = base_ref.shape
     past = taps - 1
@@ -251,7 +257,7 @@
     def line_of(row):
         return jnp.concatenate([h[row : row + 1, :] for h in held], axis=0)
 
-    slot = slot_onehot(line_of(past + steps), owners)
+    slot = slot_onehot(line_of(past + steps), sender_ref)
     line = [pick_rows(slot, w) for w in windows]
     line += [line_of(t) for t in range(steps)]
     row = steps * rb
@@ -261,12 +267,14 @@
             conv = conv + cw_ref[k : k + 1, :] * line[t + k]
         act_ref[row : row + owners, :] = silu(conv)
         row += owners
-    part_ref[...] = lax.dot_general(
+    part = lax.dot_general(
         act_ref[...].astype(BF16),
         xwt_ref[...],
         (((1,), (1,)), ((), ())),
         preferred_element_type=F32,
     )
+    part_ref[...] = part
+    short_ref[...] = part.astype(BF16)
 
 
 def add_kernel(a_ref, b_ref, sum_ref, short_ref):
@@ -286,7 +294,7 @@
         conv_ref[k] = pick_rows(child_ref[...], rows).astype(BF16)
 
 
-def start_kernel(n_msgs, n_pairs, text, pick_ref, after_ref, *rest):
+def start_kernel(n_msgs, n_pairs, text, pick_ref, sender_ref, after_ref, *rest):
     del after_ref
     msgs, rest = rest[:n_msgs], rest[n_msgs:]
     pairs, (own_ref, slot_ref, state_s) = rest[:n_pairs], rest[n_pairs:]
@@ -301,7 +309,7 @@
     for k, state in enumerate(states):
         state_s[k] = state
     own = pick_ref[...]
-    slot = slot_onehot(numbers, owners)
+    slot = slot_onehot(numbers, sender_ref)
 
     def two(m, carry):
         picked = []
@@ -508,6 +516,7 @@
             shaped((steps, rb, channels), F32),
             shaped((rb, owners), F32),
             shaped((rb, owners), F32),
+            shaped((1, owners), F32),
             shaped((taps, channels), F32),
             shaped((1, channels), F32),
             shaped((width, channels), BF16),
@@ -518,7 +527,7 @@
             shaped((1, channels), F32),
         ],
         [hbm()] * 3 + [vmem()] + [hbm()] * 7 + [anywhere()],
-        [vmem()] * 12,
+        [vmem()] * 13,
         [
             pltpu.SMEM((1,), jnp.int32),
             pltpu.SMEM((rb,), jnp.int32),
@@ -543,21 +552,22 @@
         pinned(skip[None]),
         after,
     )
-    base, gate, pick, child_pick, taps_near, bias_near, weight_near = near[:7]
-    rate, twin, dtw_near, dtb_near, skip_near = near[7:]
-    act, part = call(
+    base, gate, pick, child_pick, sender, taps_near, bias_near, weight_near = near[:8]
+    rate, twin, dtw_near, dtb_near, skip_near = near[8:]
+    act, part, brief = call(
         functools.partial(project_kernel, n_msgs),
         [
             shaped((rows, channels), F32),
             shaped((rows, width), F32),
+            shaped((rows, width), BF16),
         ],
-        [vmem()] * (5 + n_msgs),
-        [vmem()] * 2,
+        [vmem()] * (6 + n_msgs),
+        [vmem()] * 3,
         flops=2 * rows * channels * width,
         nbytes=channels * width * 2 + rows * (channels + width) * 4,
         trans=rows * channels,
-    )(pick, base, taps_near, bias_near, weight_near, *msgs)
-    other = swap(part, "tensor", 1)
+    )(pick, sender, base, taps_near, bias_near, weight_near, *msgs)
+    other = swap(brief, "tensor", 1)
     distance = 2
     while distance < tensors:
         part, brief = call(
@@ -568,7 +578,7 @@
             flops=rows * width,
             nbytes=rows * width * 14,
         )(part, other)
-        other = swap(brief, "tensor", distance)
+        other = swap(brief, "tensor", 2 * distance - 1)
         distance *= 2
 
     child_conv = call(
@@ -585,12 +595,12 @@
             shaped((n_state, rb, channels), F32),
             shaped((n_state // 2, 2 * owners, channels), F32),
         ],
-        [vmem(), anywhere()] + [vmem()] * (n_msgs + len(pairs)),
+        [vmem()] * 2 + [anywhere()] + [vmem()] * (n_msgs + len(pairs)),
         [vmem()] * 2,
         [pltpu.VMEM((owners, n_state, channels), F32)],
         flops=2 * owners * n_state * (rb + owners) * channels,
         nbytes=4 * n_state * (rb + owners) * channels,
-    )(pick, part, *msgs, *pairs)
+    )(pick, sender, part, *msgs, *pairs)
 
     decoded, child_ssm = call(
         functools.partial(decode_kernel, direct),

time: 20.5 us -> 20.2 us (0.985)
  starting transfers between devices: 8.76 us -> 8.52 us
    ppermute x3, starting transfers between devices: 3.09 us -> 2.86 us  [swap(): return lax.ppermute(value, axis, [(i, i ^ distance) for i in range(size)])]
  transfers between devices with their start and end apart: 6 -> 6, of which waited for: 4 -> 4; matrix products, arithmetic and copies ran while one was open for 0% -> 0% of each run, Pallas kernels for 14% -> 15%
where the time goes in v9:
time: 20.2 us; the launch traced here: 19.9 us
  starting transfers between devices  8.52 us (42%)
  Pallas kernels  7.66 us (38%)
  waiting for transfers between devices  3.07 us (15%)
  between operations  0.7 us (3%)
    ppermute x3, starting transfers between devices, on_device(): lax.ppermute(m, 'branch', list(enumerate(to)))  5.67 us
    pallas_call x1, Pallas kernels, on_device(): call(functools.partial(decode_kernel, direct), [shaped((rb, steps, channe...  3.12 us
    ppermute x3, starting transfers between devices, swap(): return lax.ppermute(value, axis, [(i, i ^ distance) for i in range(size)])  2.86 us
    ppermute x3, waiting for transfers between devices, on_device(): lax.ppermute(m, 'branch', list(enumerate(to)))  1.67 us
    pallas_call x1, Pallas kernels, on_device(): call(functools.partial(prepare_kernel, direct), [shaped((steps, rb, chann...  1.56 us
    ppermute x3, waiting for transfers between devices, swap(): return lax.ppermute(value, axis, [(i, i ^ distance) for i in range(size)])  1.4 us
    pallas_call x1, Pallas kernels, on_device(): call(functools.partial(pack_kernel, direct), [shaped(s, BF16) for s in ms...  1.15 us
    pallas_call x1, Pallas kernels, on_device(): call(functools.partial(windows_kernel, n_msgs, steps), shaped((taps - 1,...  0.78 us
  transfers between devices with their start and end apart: 6, of which 4 were waited for; matrix products, arithmetic and copies ran while one was open for 0% of the time, Pallas kernels for 15%

profile of v9, /device:TPU:0, one launch (start us, length us, event | category | flops | bytes accessed | tf_op | source)
XLA Modules:
  0.0 19.9 jit_solution(10134754114378191012)
XLA Ops:
  0.6 0.0 copy-start
  0.6 1.1 %shard_map.148 = (bf16[1,24,1024]{2,1,0:T(8,128)(2,1)S(1)}, bf16[1,24,1024]{2,1,0:T(8,128)(2,1)S(1)}, bf16[1,8,1024]{2,1,0:T(8,128)(2,1)S(1)}, bf16[1,8,1024]{2,1,0:T(8,128)(2,1)S(1)}) custom-call(s32[1]{0:T(128)} %bitcast.owner_hbm, s32[4]{0:T(128)} %bitcast.12, s32[16]{0:T(128)} %prompt_hbm.3, bf16[16,4,2,1024]{3,2,1,0:T(2,128)(2,1)} %step_ref.1, ...), custom_call_target="tpu_custom_call" | custom-call | bytes 196608 | tf_op jit(solution)/shard_map/pallas_call | solution.py:472
  1.8 4.1 %collective-permute-start = (bf16[1,24,1024]{2,1,0:T(8,128)(2,1)S(1)}, bf16[1,24,1024]{2,1,0:T(8,128)(2,1)S(1)}, u32[]{:S(2)}, u32[]{:S(2)}) collective-permute-start(bf16[1,24,1024]{2,1,0:T(8,128)(2,1)S(1)} %get-tuple-element.36), channel_id=1, source_target_pairs={{0,8},{4,12},{8,4},{12,0},{1,9},{5,13},{9,5},{13,1},{2,10},{6,14},... | collective-permute-start | bytes 147464 | tf_op jit(solution)/shard_map/ppermute | solution.py:498
  5.9 1.1 %collective-permute-start.1 = (bf16[1,8,1024]{2,1,0:T(8,128)(2,1)S(1)}, bf16[1,8,1024]{2,1,0:T(8,128)(2,1)S(1)}, u32[]{:S(2)}, u32[]{:S(2)}) collective-permute-start(bf16[1,8,1024]{2,1,0:T(8,128)(2,1)S(1)} %get-tuple-element.37), channel_id=1, source_target_pairs={{0,12},{4,8},{8,0},{12,4},{1,13},{5,9},{9,1},{13,5},{2,14},{6,10},... | collective-permute-start | bytes 49160 | tf_op jit(solution)/shard_map/ppermute | solution.py:498
  7.0 0.5 %collective-permute-start.2 = (bf16[1,8,1024]{2,1,0:T(8,128)(2,1)S(1)}, bf16[1,8,1024]{2,1,0:T(8,128)(2,1)S(1)}, u32[]{:S(2)}, u32[]{:S(2)}) collective-permute-start(bf16[1,8,1024]{2,1,0:T(8,128)(2,1)S(1)} %get-tuple-element.38), channel_id=1, source_target_pairs={{0,4},{4,0},{8,12},{12,8},{1,5},{5,1},{9,13},{13,9},{2,6},{6,2},{1... | collective-permute-start | bytes 49160 | tf_op jit(solution)/shard_map/ppermute | solution.py:498
  7.5 0.0 copy-done
  7.5 1.6 %shard_map.149 = (f32[4,16,1024]{2,1,0:T(8,128)S(1)}, f32[4,16,1024]{2,1,0:T(8,128)S(1)}, f32[16,4]{1,0:T(8,128)S(1)}, f32[16,4]{1,0:T(8,128)S(1)}, f32[1,4]{1,0...) custom-call(s32[1]{0:T(128)} %bitcast.owner_hbm, ...), custom_call_target="tpu_custom_call" | custom-call | flops 655360 | bytes 786432 | tf_op jit(solution)/shard_map/pallas_call | solution.py:512
  9.0 1.5 %collective-permute-done.1.rest_2_ = bf16[1,8,1024]{2,1,0:T(8,128)(2,1)S(1)} collective-permute-done((bf16[1,8,1024]{2,1,0:T(8,128)(2,1)S(1)}, bf16[1,8,1024]{2,1,0:T(8,128)(2,1)S(1)}, u32[]{:S(2)}, u32[]{:S(2)}) %collective-permute-start.1) | collective-permute-done | bytes 16416 | tf_op jit(solution)/shard_map/ppermute | solution.py:498
  10.5 0.2 collective-permute-done.2.rest_3_
  10.7 0.0 collective-permute-done.rest_1_.other_ref
  10.7 0.5 %shard_map.150 = (f32[80,1024]{1,0:T(8,128)S(1)}, f32[80,288]{1,0:T(8,128)S(1)}, bf16[80,288]{1,0:T(8,128)(2,1)S(1)}) custom-call(f32[16,4]{1,0:T(8,128)S(1)} %get-tuple-element.30.pick_ref, f32[1,4]{1,0:T(1,128)S(1)} %get-tuple-element.31.sender_ref, f32[4,16,1024]{2,1,0:T(8,128)S(1)} %get-tuple-element.32.base_ref, ...), custom_call_target="tpu_custom_call" | custom-call | flops 47185920 | bytes 1009664 | tf_op jit(solution)/shard_map/pallas_call | solution.py:557
  11.2 0.1 collective-permute-start.3
  11.3 1.5 %collective-permute-start.4 = (bf16[1,32,1024]{2,1,0:T(8,128)(2,1)S(1)}, bf16[1,32,1024]{2,1,0:T(8,128)(2,1)S(1)}, u32[]{:S(2)}, u32[]{:S(2)}) collective-permute-start(bf16[1,32,1024]{2,1,0:T(8,128)(2,1)S(1)} %shard_map.152), channel_id=1, source_target_pairs={{0,4},{4,0},{8,12},{12,8},{1,5},{5,1},{9,13},{13,9},{2,6},{6,2},{1... | collective-permute-start | bytes 196616 | tf_op jit(solution)/shard_map/ppermute | solution.py:55
  12.8 0.0 collective-permute-done.3.b_ref
  12.8 1.3 %collective-permute-start.5 = (bf16[80,288]{1,0:T(8,128)(2,1)S(1)}, bf16[80,288]{1,0:T(8,128)(2,1)S(1)}, u32[]{:S(2)}, u32[]{:S(2)}) collective-permute-start(bf16[80,288]{1,0:T(8,128)(2,1)S(1)} %get-tuple-element.51), channel_id=1, source_target_pairs={{0,3},{1,2},{2,1},{3,0},{4,7},{5,6},{6,5},{7,4},{8,11},{9,10},{10,... | collective-permute-start | bytes 138248 | tf_op jit(solution)/shard_map/ppermute | solution.py:55
  14.1 0.8 %shard_map.155 = bf16[3,16,1024]{2,1,0:T(8,128)(2,1)} custom-call(f32[16,4]{1,0:T(8,128)S(1)} %get-tuple-element.54.child_ref, f32[80,288]{1,0:T(8,128)S(1)} %get-tuple-element.43.after_ref.part_ref, bf16[1,24,1024]{2,1,0:T(8,128)(2,1)S(1)} %get-tuple-element.29.after_ref.rest_0_.own_ref, bf16[1,24,1024]{2,1,0:T(8,128)(2,1)S(1)} %collective-permute-done.rest_1_.other_ref, ...), custom_call_target="tpu_custom_call" | custom-call | flops 524288 | bytes 262144 | tf_op jit(solution)/shard_map/pallas_call | solution.py:584
  14.9 0.9 %collective-permute-done.4.rest_4_ = bf16[1,32,1024]{2,1,0:T(8,128)(2,1)S(1)} collective-permute-done((bf16[1,32,1024]{2,1,0:T(8,128)(2,1)S(1)}, bf16[1,32,1024]{2,1,0:T(8,128)(2,1)S(1)}, u32[]{:S(2)}, u32[]{:S(2)}) %collective-permute-start.4) | collective-permute-done | bytes 65568 | tf_op jit(solution)/shard_map/ppermute | solution.py:55
  15.8 0.5 %shard_map.153 = (f32[16,16,1024]{2,1,0:T(8,128)S(1)}, f32[8,8,1024]{2,1,0:T(8,128)S(1)}) custom-call(f32[16,4]{1,0:T(8,128)S(1)} %get-tuple-element.30.pick_ref, f32[1,4]{1,0:T(1,128)S(1)} %get-tuple-element.31.sender_ref, f32[80,288]{1,0:T(8,128)S(1)} %get-tuple-element.43.after_ref.part_ref, ...), custom_call_target="tpu_custom_call" | custom-call | flops 2621440 | bytes 1310720 | tf_op jit(solution)/shard_map/pallas_call | solution.py:592
  16.3 0.5 %collective-permute-done.5.other_ref = bf16[80,288]{1,0:T(8,128)(2,1)S(1)} collective-permute-done((bf16[80,288]{1,0:T(8,128)(2,1)S(1)}, bf16[80,288]{1,0:T(8,128)(2,1)S(1)}, u32[]{:S(2)}, u32[]{:S(2)}) %collective-permute-start.5) | collective-permute-done | bytes 46112 | tf_op jit(solution)/shard_map/ppermute | solution.py:55
  16.8 3.1 %shard_map.154 = (bf16[16,4,1024]{2,1,0:T(4,128)(2,1)}, f32[16,16,1024]{2,1,0:T(8,128)}) custom-call(s32[1]{0:T(128)} %bitcast.owner_hbm, s32[16]{0:T(128)} %child_hbm.3, f32[80,1024]{1,0:T(8,128)S(1)} %get-tuple-element.39.act_ref, f32[4,16,1024]{2,1,0:T(8,128)S(1)} %get-tuple-element.40.gate_ref, f32[16,16,1024]{2,1,0:T(8,128)S(1)} %get-tuple-element.44.own_ref, ...), custom_call_target="tpu_custom_call" | custom-call | flops 10485760 | bytes 1310720 | tf_op jit(solution)/shard_map/pallas_call | solution.py:605
  (2 shorter events, 0.0 us)
Async XLA Ops:
  0.6 6.8 %copy-start = (bf16[16,4,2,1024]{3,2,1,0:T(2,128)(2,1)S(1)}, bf16[16,4,2,1024]{3,2,1,0:T(2,128)(2,1)}, u32[]{:S(2)}) copy-start(bf16[16,4,2,1024]{3,2,1,0:T(2,128)(2,1)} %step_ref.1) | copy-start | bytes 786436
  1.8 8.9 %collective-permute-start = (bf16[1,24,1024]{2,1,0:T(8,128)(2,1)S(1)}, bf16[1,24,1024]{2,1,0:T(8,128)(2,1)S(1)}, u32[]{:S(2)}, u32[]{:S(2)}) collective-permute-start(bf16[1,24,1024]{2,1,0:T(8,128)(2,1)S(1)} %get-tuple-element.36), channel_id=1, source_target_pairs={{0,8},{4,12},{8,4},{12,0},{1,9},{5,13},{9,5},{13,1},{2,10},{6,14},... | collective-permute-start | bytes 147464 | tf_op jit(solution)/shard_map/ppermute | solution.py:498
  5.9 4.6 %collective-permute-start.1 = (bf16[1,8,1024]{2,1,0:T(8,128)(2,1)S(1)}, bf16[1,8,1024]{2,1,0:T(8,128)(2,1)S(1)}, u32[]{:S(2)}, u32[]{:S(2)}) collective-permute-start(bf16[1,8,1024]{2,1,0:T(8,128)(2,1)S(1)} %get-tuple-element.37), channel_id=1, source_target_pairs={{0,12},{4,8},{8,0},{12,4},{1,13},{5,9},{9,1},{13,5},{2,14},{6,10},... | collective-permute-start | bytes 49160 | tf_op jit(solution)/shard_map/ppermute | solution.py:498
  7.0 3.7 %collective-permute-start.2 = (bf16[1,8,1024]{2,1,0:T(8,128)(2,1)S(1)}, bf16[1,8,1024]{2,1,0:T(8,128)(2,1)S(1)}, u32[]{:S(2)}, u32[]{:S(2)}) collective-permute-start(bf16[1,8,1024]{2,1,0:T(8,128)(2,1)S(1)} %get-tuple-element.38), channel_id=1, source_target_pairs={{0,4},{4,0},{8,12},{12,8},{1,5},{5,1},{9,13},{13,9},{2,6},{6,2},{1... | collective-permute-start | bytes 49160 | tf_op jit(solution)/shard_map/ppermute | solution.py:498
  11.2 1.6 %collective-permute-start.3 = (bf16[80,288]{1,0:T(8,128)(2,1)S(1)}, bf16[80,288]{1,0:T(8,128)(2,1)S(1)}, u32[]{:S(2)}, u32[]{:S(2)}) collective-permute-start(bf16[80,288]{1,0:T(8,128)(2,1)S(1)} %get-tuple-element.42), channel_id=1, source_target_pairs={{0,1},{1,0},{2,3},{3,2},{4,5},{5,4},{6,7},{7,6},{8,9},{9,8},{10,11... | collective-permute-start | bytes 138248 | tf_op jit(solution)/shard_map/ppermute | solution.py:55
  11.3 4.5 %collective-permute-start.4 = (bf16[1,32,1024]{2,1,0:T(8,128)(2,1)S(1)}, bf16[1,32,1024]{2,1,0:T(8,128)(2,1)S(1)}, u32[]{:S(2)}, u32[]{:S(2)}) collective-permute-start(bf16[1,32,1024]{2,1,0:T(8,128)(2,1)S(1)} %shard_map.152), channel_id=1, source_target_pairs={{0,4},{4,0},{8,12},{12,8},{1,5},{5,1},{9,13},{13,9},{2,6},{6,2},{1... | collective-permute-start | bytes 196616 | tf_op jit(solution)/shard_map/ppermute | solution.py:55
  12.8 4.0 %collective-permute-start.5 = (bf16[80,288]{1,0:T(8,128)(2,1)S(1)}, bf16[80,288]{1,0:T(8,128)(2,1)S(1)}, u32[]{:S(2)}, u32[]{:S(2)}) collective-permute-start(bf16[80,288]{1,0:T(8,128)(2,1)S(1)} %get-tuple-element.51), channel_id=1, source_target_pairs={{0,3},{1,2},{2,1},{3,0},{4,7},{5,6},{6,5},{7,4},{8,11},{9,10},{10,... | collective-permute-start | bytes 138248 | tf_op jit(solution)/shard_map/ppermute | solution.py:55

commit v10 on v9

--- a/solution.py
+++ b/solution.py
@@ -14,6 +14,8 @@
 VMEM_LIMIT = 48 * 2**20
 WEIGHT_PARTS = 6
 DT_PARTS = 4
+SLOT_UNROLL = 4
+OWN_UNROLL = 2
 DIRECT = 4
 SENDS = ((2, 3, 1, 0), (3, 2, 0, 1), (1, 0, 3, 2))
 
@@ -404,7 +406,7 @@
             slots_s[:, 2 * m + 1, columns] = state[n_slots:, :]
         return carry
 
-    lax.fori_loop(0, chunks, slot_chunk, 0)
+    lax.fori_loop(0, chunks, slot_chunk, 0, unroll=SLOT_UNROLL)
     for copy in scalars:
         copy.wait()
     copies = []
@@ -427,11 +429,13 @@
                 state = jnp.exp2(delta[t] * rate) * state + gain[t] * b_s[n, at[t], :]
                 sums[t] = sums[t] + c_s[n, at[t], :] * state
         for t in range(steps):
-            line_s[pl.ds(t, rb, stride=steps), :] = sums[t] * gate_ref[t, :, columns]
-        dec_ref[:, :, columns] = line_s[...].reshape(rb, steps, LANES).astype(BF16)
+            line_s[chunk, pl.ds(t, rb, stride=steps), :] = sums[t] * gate_ref[t, :, columns]
         return carry
 
-    lax.fori_loop(0, chunks, own_chunk, 0)
+    lax.fori_loop(0, chunks, own_chunk, 0, unroll=OWN_UNROLL)
+    for chunk in range(chunks):
+        columns = slice(chunk * LANES, (chunk + 1) * LANES)
+        dec_ref[:, :, columns] = line_s[chunk].reshape(rb, steps, LANES).astype(BF16)
     for copy in copies:
         copy.wait()
 
@@ -621,7 +625,7 @@
             pltpu.VMEM((n_state, steps * rb, LANES), F32),
             pltpu.VMEM((n_state // 2, steps, 2 * owners, LANES), F32),
             pltpu.VMEM((owners, n_state, channels), F32),
-            pltpu.VMEM((steps * rb, LANES), F32),
+            pltpu.VMEM((channels // LANES, steps * rb, LANES), F32),
             pltpu.SemaphoreType.DMA((2 + rb,)),
         ],
         flops=8 * rows * n_state * channels,

time: 20.2 us -> 20.2 us (level)
  transfers between devices with their start and end apart: 6 -> 6, of which waited for: 4 -> 4; matrix products, arithmetic and copies ran while one was open for 0% -> 0% of each run, Pallas kernels for 15% -> 14%
where the time goes in v10:
time: 20.2 us; the launch traced here: 20 us
  starting transfers between devices  8.52 us (42%)
  Pallas kernels  7.68 us (38%)
  waiting for transfers between devices  3.07 us (15%)
  between operations  0.7 us (3%)
    ppermute x3, starting transfers between devices, on_device(): lax.ppermute(m, 'branch', list(enumerate(to)))  5.67 us
    pallas_call x1, Pallas kernels, on_device(): call(functools.partial(decode_kernel, direct), [shaped((rb, steps, channe...  3.14 us
    ppermute x3, starting transfers between devices, swap(): return lax.ppermute(value, axis, [(i, i ^ distance) for i in range(size)])  2.86 us
    ppermute x3, waiting for transfers between devices, on_device(): lax.ppermute(m, 'branch', list(enumerate(to)))  1.67 us
    pallas_call x1, Pallas kernels, on_device(): call(functools.partial(prepare_kernel, direct), [shaped((steps, rb, chann...  1.56 us
    ppermute x3, waiting for transfers between devices, swap(): return lax.ppermute(value, axis, [(i, i ^ distance) for i in range(size)])  1.4 us
    pallas_call x1, Pallas kernels, on_device(): call(functools.partial(pack_kernel, direct), [shaped(s, BF16) for s in ms...  1.15 us
    pallas_call x1, Pallas kernels, on_device(): call(functools.partial(windows_kernel, n_msgs, steps), shaped((taps - 1,...  0.78 us
  transfers between devices with their start and end apart: 6, of which 4 were waited for; matrix products, arithmetic and copies ran while one was open for 0% of the time, Pallas kernels for 14%

profile of v10, /device:TPU:0, one launch (start us, length us, event | category | flops | bytes accessed | tf_op | source)
XLA Modules:
  0.0 20.0 jit_solution(16633520995247860521)
XLA Ops:
  0.6 0.0 copy-start
  0.6 1.1 %shard_map.148 = (bf16[1,24,1024]{2,1,0:T(8,128)(2,1)S(1)}, bf16[1,24,1024]{2,1,0:T(8,128)(2,1)S(1)}, bf16[1,8,1024]{2,1,0:T(8,128)(2,1)S(1)}, bf16[1,8,1024]{2,1,0:T(8,128)(2,1)S(1)}) custom-call(s32[1]{0:T(128)} %bitcast.owner_hbm, s32[4]{0:T(128)} %bitcast.12, s32[16]{0:T(128)} %prompt_hbm.3, bf16[16,4,2,1024]{3,2,1,0:T(2,128)(2,1)} %step_ref.1, ...), custom_call_target="tpu_custom_call" | custom-call | bytes 196608 | tf_op jit(solution)/shard_map/pallas_call | solution.py:476
  1.8 4.1 %collective-permute-start = (bf16[1,24,1024]{2,1,0:T(8,128)(2,1)S(1)}, bf16[1,24,1024]{2,1,0:T(8,128)(2,1)S(1)}, u32[]{:S(2)}, u32[]{:S(2)}) collective-permute-start(bf16[1,24,1024]{2,1,0:T(8,128)(2,1)S(1)} %get-tuple-element.36), channel_id=1, source_target_pairs={{0,8},{4,12},{8,4},{12,0},{1,9},{5,13},{9,5},{13,1},{2,10},{6,14},... | collective-permute-start | bytes 147464 | tf_op jit(solution)/shard_map/ppermute | solution.py:502
  5.9 1.1 %collective-permute-start.1 = (bf16[1,8,1024]{2,1,0:T(8,128)(2,1)S(1)}, bf16[1,8,1024]{2,1,0:T(8,128)(2,1)S(1)}, u32[]{:S(2)}, u32[]{:S(2)}) collective-permute-start(bf16[1,8,1024]{2,1,0:T(8,128)(2,1)S(1)} %get-tuple-element.37), channel_id=1, source_target_pairs={{0,12},{4,8},{8,0},{12,4},{1,13},{5,9},{9,1},{13,5},{2,14},{6,10},... | collective-permute-start | bytes 49160 | tf_op jit(solution)/shard_map/ppermute | solution.py:502
  7.0 0.5 %collective-permute-start.2 = (bf16[1,8,1024]{2,1,0:T(8,128)(2,1)S(1)}, bf16[1,8,1024]{2,1,0:T(8,128)(2,1)S(1)}, u32[]{:S(2)}, u32[]{:S(2)}) collective-permute-start(bf16[1,8,1024]{2,1,0:T(8,128)(2,1)S(1)} %get-tuple-element.38), channel_id=1, source_target_pairs={{0,4},{4,0},{8,12},{12,8},{1,5},{5,1},{9,13},{13,9},{2,6},{6,2},{1... | collective-permute-start | bytes 49160 | tf_op jit(solution)/shard_map/ppermute | solution.py:502
  7.5 0.0 copy-done
  7.5 1.6 %shard_map.149 = (f32[4,16,1024]{2,1,0:T(8,128)S(1)}, f32[4,16,1024]{2,1,0:T(8,128)S(1)}, f32[16,4]{1,0:T(8,128)S(1)}, f32[16,4]{1,0:T(8,128)S(1)}, f32[1,4]{1,0...) custom-call(s32[1]{0:T(128)} %bitcast.owner_hbm, ...), custom_call_target="tpu_custom_call" | custom-call | flops 655360 | bytes 786432 | tf_op jit(solution)/shard_map/pallas_call | solution.py:516
  9.0 1.5 %collective-permute-done.1.rest_2_ = bf16[1,8,1024]{2,1,0:T(8,128)(2,1)S(1)} collective-permute-done((bf16[1,8,1024]{2,1,0:T(8,128)(2,1)S(1)}, bf16[1,8,1024]{2,1,0:T(8,128)(2,1)S(1)}, u32[]{:S(2)}, u32[]{:S(2)}) %collective-permute-start.1) | collective-permute-done | bytes 16416 | tf_op jit(solution)/shard_map/ppermute | solution.py:502
  10.5 0.2 collective-permute-done.2.rest_3_
  10.7 0.0 collective-permute-done.rest_1_.other_ref
  10.7 0.5 %shard_map.150 = (f32[80,1024]{1,0:T(8,128)S(1)}, f32[80,288]{1,0:T(8,128)S(1)}, bf16[80,288]{1,0:T(8,128)(2,1)S(1)}) custom-call(f32[16,4]{1,0:T(8,128)S(1)} %get-tuple-element.30.pick_ref, f32[1,4]{1,0:T(1,128)S(1)} %get-tuple-element.31.sender_ref, f32[4,16,1024]{2,1,0:T(8,128)S(1)} %get-tuple-element.32.base_ref, ...), custom_call_target="tpu_custom_call" | custom-call | flops 47185920 | bytes 1009664 | tf_op jit(solution)/shard_map/pallas_call | solution.py:561
  11.2 0.1 collective-permute-start.3
  11.3 1.5 %collective-permute-start.4 = (bf16[1,32,1024]{2,1,0:T(8,128)(2,1)S(1)}, bf16[1,32,1024]{2,1,0:T(8,128)(2,1)S(1)}, u32[]{:S(2)}, u32[]{:S(2)}) collective-permute-start(bf16[1,32,1024]{2,1,0:T(8,128)(2,1)S(1)} %shard_map.152), channel_id=1, source_target_pairs={{0,4},{4,0},{8,12},{12,8},{1,5},{5,1},{9,13},{13,9},{2,6},{6,2},{1... | collective-permute-start | bytes 196616 | tf_op jit(solution)/shard_map/ppermute | solution.py:57
  12.8 0.0 collective-permute-done.3.b_ref
  12.8 1.3 %collective-permute-start.5 = (bf16[80,288]{1,0:T(8,128)(2,1)S(1)}, bf16[80,288]{1,0:T(8,128)(2,1)S(1)}, u32[]{:S(2)}, u32[]{:S(2)}) collective-permute-start(bf16[80,288]{1,0:T(8,128)(2,1)S(1)} %get-tuple-element.51), channel_id=1, source_target_pairs={{0,3},{1,2},{2,1},{3,0},{4,7},{5,6},{6,5},{7,4},{8,11},{9,10},{10,... | collective-permute-start | bytes 138248 | tf_op jit(solution)/shard_map/ppermute | solution.py:57
  14.1 0.8 %shard_map.155 = bf16[3,16,1024]{2,1,0:T(8,128)(2,1)} custom-call(f32[16,4]{1,0:T(8,128)S(1)} %get-tuple-element.54.child_ref, f32[80,288]{1,0:T(8,128)S(1)} %get-tuple-element.43.after_ref.part_ref, bf16[1,24,1024]{2,1,0:T(8,128)(2,1)S(1)} %get-tuple-element.29.after_ref.rest_0_.own_ref, bf16[1,24,1024]{2,1,0:T(8,128)(2,1)S(1)} %collective-permute-done.rest_1_.other_ref, ...), custom_call_target="tpu_custom_call" | custom-call | flops 524288 | bytes 262144 | tf_op jit(solution)/shard_map/pallas_call | solution.py:588
  14.9 0.9 %collective-permute-done.4.rest_4_ = bf16[1,32,1024]{2,1,0:T(8,128)(2,1)S(1)} collective-permute-done((bf16[1,32,1024]{2,1,0:T(8,128)(2,1)S(1)}, bf16[1,32,1024]{2,1,0:T(8,128)(2,1)S(1)}, u32[]{:S(2)}, u32[]{:S(2)}) %collective-permute-start.4) | collective-permute-done | bytes 65568 | tf_op jit(solution)/shard_map/ppermute | solution.py:57
  15.8 0.5 %shard_map.153 = (f32[16,16,1024]{2,1,0:T(8,128)S(1)}, f32[8,8,1024]{2,1,0:T(8,128)S(1)}) custom-call(f32[16,4]{1,0:T(8,128)S(1)} %get-tuple-element.30.pick_ref, f32[1,4]{1,0:T(1,128)S(1)} %get-tuple-element.31.sender_ref, f32[80,288]{1,0:T(8,128)S(1)} %get-tuple-element.43.after_ref.part_ref, ...), custom_call_target="tpu_custom_call" | custom-call | flops 2621440 | bytes 1310720 | tf_op jit(solution)/shard_map/pallas_call | solution.py:596
  16.3 0.5 %collective-permute-done.5.other_ref = bf16[80,288]{1,0:T(8,128)(2,1)S(1)} collective-permute-done((bf16[80,288]{1,0:T(8,128)(2,1)S(1)}, bf16[80,288]{1,0:T(8,128)(2,1)S(1)}, u32[]{:S(2)}, u32[]{:S(2)}) %collective-permute-start.5) | collective-permute-done | bytes 46112 | tf_op jit(solution)/shard_map/ppermute | solution.py:57
  16.8 3.1 %shard_map.154 = (bf16[16,4,1024]{2,1,0:T(4,128)(2,1)}, f32[16,16,1024]{2,1,0:T(8,128)}) custom-call(s32[1]{0:T(128)} %bitcast.owner_hbm, s32[16]{0:T(128)} %child_hbm.3, f32[80,1024]{1,0:T(8,128)S(1)} %get-tuple-element.39.act_ref, f32[4,16,1024]{2,1,0:T(8,128)S(1)} %get-tuple-element.40.gate_ref, f32[16,16,1024]{2,1,0:T(8,128)S(1)} %get-tuple-element.44.own_ref, ...), custom_call_target="tpu_custom_call" | custom-call | flops 10485760 | bytes 1310720 | tf_op jit(solution)/shard_map/pallas_call | solution.py:609
  (2 shorter events, 0.0 us)
Async XLA Ops:
  0.6 6.8 %copy-start = (bf16[16,4,2,1024]{3,2,1,0:T(2,128)(2,1)S(1)}, bf16[16,4,2,1024]{3,2,1,0:T(2,128)(2,1)}, u32[]{:S(2)}) copy-start(bf16[16,4,2,1024]{3,2,1,0:T(2,128)(2,1)} %step_ref.1) | copy-start | bytes 786436
  1.8 8.9 %collective-permute-start = (bf16[1,24,1024]{2,1,0:T(8,128)(2,1)S(1)}, bf16[1,24,1024]{2,1,0:T(8,128)(2,1)S(1)}, u32[]{:S(2)}, u32[]{:S(2)}) collective-permute-start(bf16[1,24,1024]{2,1,0:T(8,128)(2,1)S(1)} %get-tuple-element.36), channel_id=1, source_target_pairs={{0,8},{4,12},{8,4},{12,0},{1,9},{5,13},{9,5},{13,1},{2,10},{6,14},... | collective-permute-start | bytes 147464 | tf_op jit(solution)/shard_map/ppermute | solution.py:502
  5.9 4.6 %collective-permute-start.1 = (bf16[1,8,1024]{2,1,0:T(8,128)(2,1)S(1)}, bf16[1,8,1024]{2,1,0:T(8,128)(2,1)S(1)}, u32[]{:S(2)}, u32[]{:S(2)}) collective-permute-start(bf16[1,8,1024]{2,1,0:T(8,128)(2,1)S(1)} %get-tuple-element.37), channel_id=1, source_target_pairs={{0,12},{4,8},{8,0},{12,4},{1,13},{5,9},{9,1},{13,5},{2,14},{6,10},... | collective-permute-start | bytes 49160 | tf_op jit(solution)/shard_map/ppermute | solution.py:502
  7.0 3.7 %collective-permute-start.2 = (bf16[1,8,1024]{2,1,0:T(8,128)(2,1)S(1)}, bf16[1,8,1024]{2,1,0:T(8,128)(2,1)S(1)}, u32[]{:S(2)}, u32[]{:S(2)}) collective-permute-start(bf16[1,8,1024]{2,1,0:T(8,128)(2,1)S(1)} %get-tuple-element.38), channel_id=1, source_target_pairs={{0,4},{4,0},{8,12},{12,8},{1,5},{5,1},{9,13},{13,9},{2,6},{6,2},{1... | collective-permute-start | bytes 49160 | tf_op jit(solution)/shard_map/ppermute | solution.py:502
  11.2 1.6 %collective-permute-start.3 = (bf16[80,288]{1,0:T(8,128)(2,1)S(1)}, bf16[80,288]{1,0:T(8,128)(2,1)S(1)}, u32[]{:S(2)}, u32[]{:S(2)}) collective-permute-start(bf16[80,288]{1,0:T(8,128)(2,1)S(1)} %get-tuple-element.42), channel_id=1, source_target_pairs={{0,1},{1,0},{2,3},{3,2},{4,5},{5,4},{6,7},{7,6},{8,9},{9,8},{10,11... | collective-permute-start | bytes 138248 | tf_op jit(solution)/shard_map/ppermute | solution.py:57
  11.3 4.5 %collective-permute-start.4 = (bf16[1,32,1024]{2,1,0:T(8,128)(2,1)S(1)}, bf16[1,32,1024]{2,1,0:T(8,128)(2,1)S(1)}, u32[]{:S(2)}, u32[]{:S(2)}) collective-permute-start(bf16[1,32,1024]{2,1,0:T(8,128)(2,1)S(1)} %shard_map.152), channel_id=1, source_target_pairs={{0,4},{4,0},{8,12},{12,8},{1,5},{5,1},{9,13},{13,9},{2,6},{6,2},{1... | collective-permute-start | bytes 196616 | tf_op jit(solution)/shard_map/ppermute | solution.py:57
  12.8 4.0 %collective-permute-start.5 = (bf16[80,288]{1,0:T(8,128)(2,1)S(1)}, bf16[80,288]{1,0:T(8,128)(2,1)S(1)}, u32[]{:S(2)}, u32[]{:S(2)}) collective-permute-start(bf16[80,288]{1,0:T(8,128)(2,1)S(1)} %get-tuple-element.51), channel_id=1, source_target_pairs={{0,3},{1,2},{2,1},{3,0},{4,7},{5,6},{6,5},{7,4},{8,11},{9,10},{10,... | collective-permute-start | bytes 138248 | tf_op jit(solution)/shard_map/ppermute | solution.py:57

commit v11 on v9

--- a/solution.py
+++ b/solution.py
@@ -142,9 +142,12 @@
             write(outs[0].at[target], target)
 
 
-def pair_kernel(text, own_ref, other_ref, pair_ref):
-    states = [ref[0].astype(F32)[text:, :] for ref in (own_ref, other_ref)]
-    pair_ref[0] = jnp.concatenate(states, axis=0).astype(BF16)
+def pair_kernel(text, ssm_ref, came_ref, after_ref, pair_ref):
+    del after_ref
+    state = ssm_ref[0]
+    head = state.astype(BF16).astype(F32)
+    came = came_ref[0].astype(F32)[text:, :]
+    pair_ref[0] = jnp.concatenate([head, state - head, came], axis=0).astype(BF16)
 
 
 def silu(v):
@@ -294,18 +297,21 @@
         conv_ref[k] = pick_rows(child_ref[...], rows).astype(BF16)
 
 
-def start_kernel(n_msgs, n_pairs, text, pick_ref, sender_ref, after_ref, *rest):
+def start_kernel(n_msgs, direct, text, pick_ref, sender_ref, after_ref, *rest):
     del after_ref
     msgs, rest = rest[:n_msgs], rest[n_msgs:]
-    pairs, (own_ref, slot_ref, state_s) = rest[:n_pairs], rest[n_pairs:]
+    apart, (own_ref, slot_ref, state_s) = rest[:-3], rest[-3:]
     n_state = own_ref.shape[0]
     held = read_messages(msgs)
     owners = len(held)
     numbers = jnp.concatenate([h[text - 1 : text, :] for h in held], axis=0)
     states = [h[text:, :] for h in held]
-    for ref in pairs:
-        both = ref[0].astype(F32)
-        states[3], states[2] = both[:n_state, :], both[n_state:, :]
+    if direct:
+        ssm_ref, pair_ref = apart
+        head, low, came = [
+            pair_ref[0].astype(F32)[i * n_state : (i + 1) * n_state, :] for i in range(3)
+        ]
+        states[0], states[2], states[3] = ssm_ref[0], came, head + low
     for k, state in enumerate(states):
         state_s[k] = state
     own = pick_ref[...]
@@ -466,7 +472,7 @@
     owner = pinned(lax.axis_index("branch").astype(jnp.int32).reshape(1))
 
     if direct:
-        msg_shapes = [(1, d, channels) for d in (depth, depth, short, short)]
+        msg_shapes = [(1, d, channels) for d in (short, depth, short, short)]
     else:
         msg_shapes = [(owners, depth, channels)]
     msgs = call(
@@ -497,17 +503,10 @@
         msgs = [own] + [
             lax.ppermute(m, "branch", list(enumerate(to))) for m, to in zip(msgs[1:], SENDS)
         ]
-        pair = call(
-            functools.partial(pair_kernel, short),
-            shaped((1, 2 * n_state, channels), BF16),
-            [vmem()] * 2,
-            vmem(),
-            nbytes=8 * n_state * channels,
-        )(own, msgs[1])
-        pairs, after = [swap(pair, "branch", 1)], own
+        after = own
     else:
         msgs = [lax.all_to_all(msgs[0], "branch", split_axis=0, concat_axis=0, tiled=True)]
-        pairs, after = [], msgs[0]
+        after = msgs[0]
     n_msgs = len(msgs)
     near = call(
         functools.partial(prepare_kernel, direct),
@@ -554,6 +553,16 @@
     )
     base, gate, pick, child_pick, sender, taps_near, bias_near, weight_near = near[:8]
     rate, twin, dtw_near, dtb_near, skip_near = near[8:]
+    states = []
+    if direct:
+        pair = call(
+            functools.partial(pair_kernel, short),
+            shaped((1, 3 * n_state, channels), BF16),
+            [vmem()] * 2 + [anywhere()],
+            vmem(),
+            nbytes=12 * n_state * channels,
+        )(prompt_ssm, msgs[1], pick)
+        states = [prompt_ssm, swap(pair, "branch", 1)]
     act, part, brief = call(
         functools.partial(project_kernel, n_msgs),
         [
@@ -590,17 +599,17 @@
         nbytes=4 * taps * rb * channels,
     )(child_pick, part, *msgs)
     own_start, slot_start = call(
-        functools.partial(start_kernel, n_msgs, len(pairs), short),
+        functools.partial(start_kernel, n_msgs, direct, short),
         [
             shaped((n_state, rb, channels), F32),
             shaped((n_state // 2, 2 * owners, channels), F32),
         ],
-        [vmem()] * 2 + [anywhere()] + [vmem()] * (n_msgs + len(pairs)),
+        [vmem()] * 2 + [anywhere()] + [vmem()] * (n_msgs + len(states)),
         [vmem()] * 2,
         [pltpu.VMEM((owners, n_state, channels), F32)],
         flops=2 * owners * n_state * (rb + owners) * channels,
         nbytes=4 * n_state * (rb + owners) * channels,
-    )(pick, sender, part, *msgs, *pairs)
+    )(pick, sender, part, *msgs, *states)
 
     decoded, child_ssm = call(
         functools.partial(decode_kernel, direct),

time: 20.2 us -> 19.9 us (0.985)
  waiting for transfers between devices: 3.07 us -> 2.48 us
  starting transfers between devices: 8.52 us -> 8.81 us
    ppermute x3, waiting for transfers between devices: 1.67 us -> 0.01 us  [on_device(): lax.ppermute(m, 'branch', list(enumerate(to)))]
    ppermute x3, waiting for transfers between devices: 1.4 us -> 2.47 us  [swap(): return lax.ppermute(value, axis, [(i, i ^ distance) for i in range(size)])]
    ppermute x3, starting transfers between devices: 2.86 us -> 3.14 us  [swap(): return lax.ppermute(value, axis, [(i, i ^ distance) for i in range(size)])]
  transfers between devices with their start and end apart: 6 -> 6, of which waited for: 4 -> 2; matrix products, arithmetic and copies ran while one was open for 0% -> 0% of each run, Pallas kernels for 15% -> 17%
where the time goes in v11:
time: 19.9 us; the launch traced here: 19.7 us
  starting transfers between devices  8.81 us (44%)
  Pallas kernels  7.69 us (39%)
  waiting for transfers between devices  2.48 us (12%)
  between operations  0.71 us (4%)
    ppermute x3, starting transfers between devices, on_device(): lax.ppermute(m, 'branch', list(enumerate(to)))  5.67 us
    ppermute x3, starting transfers between devices, swap(): return lax.ppermute(value, axis, [(i, i ^ distance) for i in range(size)])  3.14 us
    pallas_call x1, Pallas kernels, on_device(): call(functools.partial(decode_kernel, direct), [shaped((rb, steps, channe...  3.12 us
    ppermute x3, waiting for transfers between devices, swap(): return lax.ppermute(value, axis, [(i, i ^ distance) for i in range(size)])  2.47 us
    pallas_call x1, Pallas kernels, on_device(): call(functools.partial(prepare_kernel, direct), [shaped((steps, rb, chann...  1.58 us
    pallas_call x1, Pallas kernels, on_device(): call(functools.partial(pack_kernel, direct), [shaped(s, BF16) for s in ms...  1.15 us
    pallas_call x1, Pallas kernels, on_device(): call(functools.partial(windows_kernel, n_msgs, steps), shaped((taps - 1,...  0.78 us
    pallas_call x1, Pallas kernels, on_device(): call(functools.partial(start_kernel, n_msgs, direct, short), [shaped((n_s...  0.53 us
  transfers between devices with their start and end apart: 6, of which 2 were waited for; matrix products, arithmetic and copies ran while one was open for 0% of the time, Pallas kernels for 17%

profile of v11, /device:TPU:0, one launch (start us, length us, event | category | flops | bytes accessed | tf_op | source)
XLA Modules:
  0.0 19.7 jit_solution(14614724370648167199)
XLA Ops:
  0.6 0.0 copy-start
  0.6 1.1 %shard_map.148 = (bf16[1,8,1024]{2,1,0:T(8,128)(2,1)S(1)}, bf16[1,24,1024]{2,1,0:T(8,128)(2,1)S(1)}, bf16[1,8,1024]{2,1,0:T(8,128)(2,1)S(1)}, bf16[1,8,1024]{2,1,0:T(8,128)(2,1)S(1)}) custom-call(s32[1]{0:T(128)} %bitcast.owner_hbm, s32[4]{0:T(128)} %bitcast.12, s32[16]{0:T(128)} %prompt_hbm.3, bf16[16,4,2,1024]{3,2,1,0:T(2,128)(2,1)} %step_ref.1, ...), custom_call_target="tpu_custom_call" | custom-call | bytes 196608 | tf_op jit(solution)/shard_map/pallas_call | solution.py:478
  1.8 4.1 %collective-permute-start = (bf16[1,24,1024]{2,1,0:T(8,128)(2,1)S(1)}, bf16[1,24,1024]{2,1,0:T(8,128)(2,1)S(1)}, u32[]{:S(2)}, u32[]{:S(2)}) collective-permute-start(bf16[1,24,1024]{2,1,0:T(8,128)(2,1)S(1)} %get-tuple-element.36), channel_id=1, source_target_pairs={{0,8},{4,12},{8,4},{12,0},{1,9},{5,13},{9,5},{13,1},{2,10},{6,14},... | collective-permute-start | bytes 147464 | tf_op jit(solution)/shard_map/ppermute | solution.py:504
  5.9 1.1 %collective-permute-start.1 = (bf16[1,8,1024]{2,1,0:T(8,128)(2,1)S(1)}, bf16[1,8,1024]{2,1,0:T(8,128)(2,1)S(1)}, u32[]{:S(2)}, u32[]{:S(2)}) collective-permute-start(bf16[1,8,1024]{2,1,0:T(8,128)(2,1)S(1)} %get-tuple-element.37), channel_id=1, source_target_pairs={{0,12},{4,8},{8,0},{12,4},{1,13},{5,9},{9,1},{13,5},{2,14},{6,10},... | collective-permute-start | bytes 49160 | tf_op jit(solution)/shard_map/ppermute | solution.py:504
  7.0 0.5 %collective-permute-start.2 = (bf16[1,8,1024]{2,1,0:T(8,128)(2,1)S(1)}, bf16[1,8,1024]{2,1,0:T(8,128)(2,1)S(1)}, u32[]{:S(2)}, u32[]{:S(2)}) collective-permute-start(bf16[1,8,1024]{2,1,0:T(8,128)(2,1)S(1)} %get-tuple-element.38), channel_id=1, source_target_pairs={{0,4},{4,0},{8,12},{12,8},{1,5},{5,1},{9,13},{13,9},{2,6},{6,2},{1... | collective-permute-start | bytes 49160 | tf_op jit(solution)/shard_map/ppermute | solution.py:504
  7.5 0.0 copy-done
  7.5 0.0 copy-start.1
  7.5 1.6 %shard_map.149 = (f32[4,16,1024]{2,1,0:T(8,128)S(1)}, f32[4,16,1024]{2,1,0:T(8,128)S(1)}, f32[16,4]{1,0:T(8,128)S(1)}, f32[16,4]{1,0:T(8,128)S(1)}, f32[1,4]{1,0...) custom-call(s32[1]{0:T(128)} %bitcast.owner_hbm, ...), custom_call_target="tpu_custom_call" | custom-call | flops 655360 | bytes 786432 | tf_op jit(solution)/shard_map/pallas_call | solution.py:511
  9.1 0.0 collective-permute-done.rest_1_.came_ref
  9.1 0.0 copy-done.1
  9.1 1.6 %collective-permute-start.4 = (bf16[1,48,1024]{2,1,0:T(8,128)(2,1)S(1)}, bf16[1,48,1024]{2,1,0:T(8,128)(2,1)S(1)}, u32[]{:S(2)}, u32[]{:S(2)}) collective-permute-start(bf16[1,48,1024]{2,1,0:T(8,128)(2,1)S(1)} %shard_map.152), channel_id=1, source_target_pairs={{0,4},{4,0},{8,12},{12,8},{1,5},{5,1},{9,13},{13,9},{2,6},{6,2},{1... | collective-permute-start | bytes 294920 | tf_op jit(solution)/shard_map/ppermute | solution.py:55
  10.7 0.0 collective-permute-done.1.rest_2_
  10.7 0.0 collective-permute-done.2.rest_3_
  10.7 0.5 %shard_map.150 = (f32[80,1024]{1,0:T(8,128)S(1)}, f32[80,288]{1,0:T(8,128)S(1)}, bf16[80,288]{1,0:T(8,128)(2,1)S(1)}) custom-call(f32[16,4]{1,0:T(8,128)S(1)} %get-tuple-element.30.pick_ref.after_ref, f32[1,4]{1,0:T(1,128)S(1)} %get-tuple-element.31.sender_ref, f32[4,16,1024]{2,1,0:T(8,128)S(1)} %get-tuple-element.32.base_ref, ...), custom_call_target="tpu_custom_call" | custom-call | flops 47185920 | bytes 1009664 | tf_op jit(solution)/shard_map/pallas_call | solution.py:566
  11.2 0.1 collective-permute-start.3
  11.3 1.2 %collective-permute-done.3.b_ref = bf16[80,288]{1,0:T(8,128)(2,1)S(1)} collective-permute-done((bf16[80,288]{1,0:T(8,128)(2,1)S(1)}, bf16[80,288]{1,0:T(8,128)(2,1)S(1)}, u32[]{:S(2)}, u32[]{:S(2)}) %collective-permute-start.3) | collective-permute-done | bytes 46112 | tf_op jit(solution)/shard_map/ppermute | solution.py:55
  12.5 1.5 %collective-permute-start.5 = (bf16[80,288]{1,0:T(8,128)(2,1)S(1)}, bf16[80,288]{1,0:T(8,128)(2,1)S(1)}, u32[]{:S(2)}, u32[]{:S(2)}) collective-permute-start(bf16[80,288]{1,0:T(8,128)(2,1)S(1)} %get-tuple-element.51), channel_id=1, source_target_pairs={{0,3},{1,2},{2,1},{3,0},{4,7},{5,6},{6,5},{7,4},{8,11},{9,10},{10,... | collective-permute-start | bytes 138248 | tf_op jit(solution)/shard_map/ppermute | solution.py:55
  14.0 0.8 %shard_map.155 = bf16[3,16,1024]{2,1,0:T(8,128)(2,1)} custom-call(f32[16,4]{1,0:T(8,128)S(1)} %get-tuple-element.54.child_ref, f32[80,288]{1,0:T(8,128)S(1)} %get-tuple-element.43.after_ref.part_ref, bf16[1,8,1024]{2,1,0:T(8,128)(2,1)S(1)} %get-tuple-element.29.after_ref.rest_0_, bf16[1,24,1024]{2,1,0:T(8,128)(2,1)S(1)} %collective-permute-done.rest_1_.came_ref, ...), custom_call_target="tpu_custom_call" | custom-call | flops 524288 | bytes 262144 | tf_op jit(solution)/shard_map/pallas_call | solution.py:593
  14.8 0.0 collective-permute-done.4.rest_5_
  14.8 0.5 %shard_map.153 = (f32[16,16,1024]{2,1,0:T(8,128)S(1)}, f32[8,8,1024]{2,1,0:T(8,128)S(1)}) custom-call(f32[16,4]{1,0:T(8,128)S(1)} %get-tuple-element.30.pick_ref.after_ref, f32[1,4]{1,0:T(1,128)S(1)} %get-tuple-element.31.sender_ref, f32[80,288]{1,0:T(8,128)S(1)} %get-tuple-element.43.after_ref.part_ref, ...), custom_call_target="tpu_custom_call" | custom-call | flops 2621440 | bytes 1310720 | tf_op jit(solution)/shard_map/pallas_call | solution.py:601
  15.3 1.2 %collective-permute-done.5.other_ref = bf16[80,288]{1,0:T(8,128)(2,1)S(1)} collective-permute-done((bf16[80,288]{1,0:T(8,128)(2,1)S(1)}, bf16[80,288]{1,0:T(8,128)(2,1)S(1)}, u32[]{:S(2)}, u32[]{:S(2)}) %collective-permute-start.5) | collective-permute-done | bytes 46112 | tf_op jit(solution)/shard_map/ppermute | solution.py:55
  16.6 3.1 %shard_map.154 = (bf16[16,4,1024]{2,1,0:T(4,128)(2,1)}, f32[16,16,1024]{2,1,0:T(8,128)}) custom-call(s32[1]{0:T(128)} %bitcast.owner_hbm, s32[16]{0:T(128)} %child_hbm.3, f32[80,1024]{1,0:T(8,128)S(1)} %get-tuple-element.39.act_ref, f32[4,16,1024]{2,1,0:T(8,128)S(1)} %get-tuple-element.40.gate_ref, f32[16,16,1024]{2,1,0:T(8,128)S(1)} %get-tuple-element.44.own_ref, ...), custom_call_target="tpu_custom_call" | custom-call | flops 10485760 | bytes 1310720 | tf_op jit(solution)/shard_map/pallas_call | solution.py:614
  (2 shorter events, 0.0 us)
Async XLA Ops:
  0.6 6.8 %copy-start = (bf16[16,4,2,1024]{3,2,1,0:T(2,128)(2,1)S(1)}, bf16[16,4,2,1024]{3,2,1,0:T(2,128)(2,1)}, u32[]{:S(2)}) copy-start(bf16[16,4,2,1024]{3,2,1,0:T(2,128)(2,1)} %step_ref.1) | copy-start | bytes 786436
  1.8 7.3 %collective-permute-start = (bf16[1,24,1024]{2,1,0:T(8,128)(2,1)S(1)}, bf16[1,24,1024]{2,1,0:T(8,128)(2,1)S(1)}, u32[]{:S(2)}, u32[]{:S(2)}) collective-permute-start(bf16[1,24,1024]{2,1,0:T(8,128)(2,1)S(1)} %get-tuple-element.36), channel_id=1, source_target_pairs={{0,8},{4,12},{8,4},{12,0},{1,9},{5,13},{9,5},{13,1},{2,10},{6,14},... | collective-permute-start | bytes 147464 | tf_op jit(solution)/shard_map/ppermute | solution.py:504
  5.9 4.8 %collective-permute-start.1 = (bf16[1,8,1024]{2,1,0:T(8,128)(2,1)S(1)}, bf16[1,8,1024]{2,1,0:T(8,128)(2,1)S(1)}, u32[]{:S(2)}, u32[]{:S(2)}) collective-permute-start(bf16[1,8,1024]{2,1,0:T(8,128)(2,1)S(1)} %get-tuple-element.37), channel_id=1, source_target_pairs={{0,12},{4,8},{8,0},{12,4},{1,13},{5,9},{9,1},{13,5},{2,14},{6,10},... | collective-permute-start | bytes 49160 | tf_op jit(solution)/shard_map/ppermute | solution.py:504
  7.0 3.7 %collective-permute-start.2 = (bf16[1,8,1024]{2,1,0:T(8,128)(2,1)S(1)}, bf16[1,8,1024]{2,1,0:T(8,128)(2,1)S(1)}, u32[]{:S(2)}, u32[]{:S(2)}) collective-permute-start(bf16[1,8,1024]{2,1,0:T(8,128)(2,1)S(1)} %get-tuple-element.38), channel_id=1, source_target_pairs={{0,4},{4,0},{8,12},{12,8},{1,5},{5,1},{9,13},{13,9},{2,6},{6,2},{1... | collective-permute-start | bytes 49160 | tf_op jit(solution)/shard_map/ppermute | solution.py:504
  7.5 1.6 %copy-start.1 = (f32[1,16,1024]{2,1,0:T(8,128)S(1)}, f32[1,16,1024]{2,1,0:T(8,128)}, u32[]{:S(2)}) copy-start(f32[1,16,1024]{2,1,0:T(8,128)} %rest_4_.1) | copy-start | bytes 196612
  9.1 5.7 %collective-permute-start.4 = (bf16[1,48,1024]{2,1,0:T(8,128)(2,1)S(1)}, bf16[1,48,1024]{2,1,0:T(8,128)(2,1)S(1)}, u32[]{:S(2)}, u32[]{:S(2)}) collective-permute-start(bf16[1,48,1024]{2,1,0:T(8,128)(2,1)S(1)} %shard_map.152), channel_id=1, source_target_pairs={{0,4},{4,0},{8,12},{12,8},{1,5},{5,1},{9,13},{13,9},{2,6},{6,2},{1... | collective-permute-start | bytes 294920 | tf_op jit(solution)/shard_map/ppermute | solution.py:55
  11.2 1.3 %collective-permute-start.3 = (bf16[80,288]{1,0:T(8,128)(2,1)S(1)}, bf16[80,288]{1,0:T(8,128)(2,1)S(1)}, u32[]{:S(2)}, u32[]{:S(2)}) collective-permute-start(bf16[80,288]{1,0:T(8,128)(2,1)S(1)} %get-tuple-element.42), channel_id=1, source_target_pairs={{0,1},{1,0},{2,3},{3,2},{4,5},{5,4},{6,7},{7,6},{8,9},{9,8},{10,11... | collective-permute-start | bytes 138248 | tf_op jit(solution)/shard_map/ppermute | solution.py:55
  12.5 4.0 %collective-permute-start.5 = (bf16[80,288]{1,0:T(8,128)(2,1)S(1)}, bf16[80,288]{1,0:T(8,128)(2,1)S(1)}, u32[]{:S(2)}, u32[]{:S(2)}) collective-permute-start(bf16[80,288]{1,0:T(8,128)(2,1)S(1)} %get-tuple-element.51), channel_id=1, source_target_pairs={{0,3},{1,2},{2,1},{3,0},{4,7},{5,6},{6,5},{7,4},{8,11},{9,10},{10,... | collective-permute-start | bytes 138248 | tf_op jit(solution)/shard_map/ppermute | solution.py:55

commit v12 on v11

--- a/solution.py
+++ b/solution.py
@@ -13,7 +13,7 @@
 LANES = 128
 VMEM_LIMIT = 48 * 2**20
 WEIGHT_PARTS = 6
-DT_PARTS = 4
+STEP_PARTS = 4
 DIRECT = 4
 SENDS = ((2, 3, 1, 0), (3, 2, 0, 1), (1, 0, 3, 2))
 
@@ -120,7 +120,7 @@
         pltpu.make_async_copy(conv_hbm, conv, sems.at[2]),
         pltpu.make_async_copy(ssm_hbm, ssm, sems.at[3]),
     ]
-    all_of(copies + in_parts(step_hbm, step, sems, 5, 4))
+    all_of(copies + in_parts(step_hbm, step, sems, 5, STEP_PARTS))
     owner = owner_s[0]
     window = conv[0].astype(F32)
 
@@ -159,12 +159,11 @@
     owner_hbm,
     prompt_hbm,
     child_hbm,
-    step_ref,
+    step_hbm,
     cw_hbm,
     cb_hbm,
     xwt_hbm,
     alog_hbm,
-    dtw_hbm,
     dtb_hbm,
     skip_hbm,
     after_ref,
@@ -178,9 +177,9 @@
     xwt_ref,
     rate_ref,
     twin_ref,
-    dtw_ref,
     dtb_ref,
     skip_ref,
+    step_ref,
     owner_s,
     prompt_s,
     child_s,
@@ -203,10 +202,12 @@
             )
         )
     ]
-    large = in_parts(xwt_hbm, xwt_ref, sems, len(small), WEIGHT_PARTS)
-    large += in_parts(dtw_hbm, dtw_ref, sems, len(small) + WEIGHT_PARTS, DT_PARTS)
-    for copy in small + large:
+    inputs = in_parts(step_hbm, step_ref, sems, len(small), STEP_PARTS)
+    large = in_parts(xwt_hbm, xwt_ref, sems, len(small) + STEP_PARTS, WEIGHT_PARTS)
+    for copy in inputs + small + large:
         copy.start()
+    for copy in inputs:
+        copy.wait()
     steps = step_ref.shape[1]
     taps = cw_hbm.shape[0]
     xs = [step_ref[:, t, 0, :].astype(F32) for t in range(steps)]
@@ -487,7 +488,7 @@
             pltpu.VMEM(step_in.shape, BF16),
             pltpu.VMEM(prompt_conv.shape, BF16),
             pltpu.VMEM(prompt_ssm.shape, F32),
-            pltpu.SemaphoreType.DMA((9,)),
+            pltpu.SemaphoreType.DMA((5 + STEP_PARTS,)),
         ],
         nbytes=owners * depth * channels * 2,
     )(
@@ -521,18 +522,18 @@
             shaped((width, channels), BF16),
             shaped((n_state, channels), F32),
             shaped((n_state // 2, 2 * owners, channels), F32),
-            shaped(dt_weight.shape, BF16),
             shaped((1, channels), F32),
             shaped((1, channels), F32),
         ],
-        [hbm()] * 3 + [vmem()] + [hbm()] * 7 + [anywhere()],
-        [vmem()] * 13,
+        [hbm()] * 10 + [anywhere()],
+        [vmem()] * 12,
         [
+            pltpu.VMEM(step_in.shape, BF16),
             pltpu.SMEM((1,), jnp.int32),
             pltpu.SMEM((rb,), jnp.int32),
             pltpu.SMEM((rb,), jnp.int32),
             pltpu.VMEM((n_state, channels), F32),
-            pltpu.SemaphoreType.DMA((8 + WEIGHT_PARTS + DT_PARTS,)),
+            pltpu.SemaphoreType.DMA((8 + WEIGHT_PARTS + STEP_PARTS,)),
         ],
         flops=10 * steps * rb * channels,
         nbytes=12 * steps * rb * channels,
@@ -541,18 +542,17 @@
         owner,
         pinned(prompt_of),
         pinned(child_slot),
-        step_in,
+        pinned(step_in),
         pinned(conv_weight),
         pinned(conv_bias[None]),
         pinned(x_weight.T),
         pinned(a_log),
-        pinned(dt_weight),
         pinned(dt_bias[None]),
         pinned(skip[None]),
         after,
     )
     base, gate, pick, child_pick, sender, taps_near, bias_near, weight_near = near[:8]
-    rate, twin, dtw_near, dtb_near, skip_near = near[8:]
+    rate, twin, dtb_near, skip_near = near[8:]
     states = []
     if direct:
         pair = call(
@@ -645,7 +645,7 @@
         slot_start,
         rate,
         twin,
-        dtw_near,
+        dt_weight,
         dtb_near,
         skip_near,
         part,

time: 19.9 us -> 19.9 us (level)
  no operation moved by 1% of the time
where the time goes in v12:
time: 19.9 us; the launch traced here: 19.7 us
  starting transfers between devices  8.81 us (44%)
  Pallas kernels  7.65 us (38%)
  waiting for transfers between devices  2.49 us (13%)
  between operations  0.71 us (4%)
    ppermute x3, starting transfers between devices, on_device(): lax.ppermute(m, 'branch', list(enumerate(to)))  5.67 us
    ppermute x3, starting transfers between devices, swap(): return lax.ppermute(value, axis, [(i, i ^ distance) for i in range(size)])  3.14 us
    pallas_call x1, Pallas kernels, on_device(): call(functools.partial(decode_kernel, direct), [shaped((rb, steps, channe...  3.12 us
    ppermute x3, waiting for transfers between devices, swap(): return lax.ppermute(value, axis, [(i, i ^ distance) for i in range(size)])  2.47 us
    pallas_call x1, Pallas kernels, on_device(): call(functools.partial(prepare_kernel, direct), [shaped((steps, rb, chann...  1.58 us
    pallas_call x1, Pallas kernels, on_device(): call(functools.partial(pack_kernel, direct), [shaped(s, BF16) for s in ms...  1.11 us
    pallas_call x1, Pallas kernels, on_device(): call(functools.partial(windows_kernel, n_msgs, steps), shaped((taps - 1,...  0.78 us
    pallas_call x1, Pallas kernels, on_device(): call(functools.partial(start_kernel, n_msgs, direct, short), [shaped((n_s...  0.53 us
  transfers between devices with their start and end apart: 6, of which 2 were waited for; matrix products, arithmetic and copies ran while one was open for 0% of the time, Pallas kernels for 17%

profile of v12, /device:TPU:0, one launch (start us, length us, event | category | flops | bytes accessed | tf_op | source)
XLA Modules:
  0.0 19.7 jit_solution(10725265566945824742)
XLA Ops:
  0.6 1.1 %shard_map.148 = (bf16[1,8,1024]{2,1,0:T(8,128)(2,1)S(1)}, bf16[1,24,1024]{2,1,0:T(8,128)(2,1)S(1)}, bf16[1,8,1024]{2,1,0:T(8,128)(2,1)S(1)}, bf16[1,8,1024]{2,1,0:T(8,128)(2,1)S(1)}) custom-call(s32[1]{0:T(128)} %bitcast.owner_hbm, s32[4]{0:T(128)} %bitcast.12, s32[16]{0:T(128)} %prompt_hbm.3, bf16[16,4,2,1024]{3,2,1,0:T(2,128)(2,1)} %step_hbm.3, ...), custom_call_target="tpu_custom_call" | custom-call | bytes 196608 | tf_op jit(solution)/shard_map/pallas_call | solution.py:479
  1.8 4.1 %collective-permute-start = (bf16[1,24,1024]{2,1,0:T(8,128)(2,1)S(1)}, bf16[1,24,1024]{2,1,0:T(8,128)(2,1)S(1)}, u32[]{:S(2)}, u32[]{:S(2)}) collective-permute-start(bf16[1,24,1024]{2,1,0:T(8,128)(2,1)S(1)} %get-tuple-element.35), channel_id=1, source_target_pairs={{0,8},{4,12},{8,4},{12,0},{1,9},{5,13},{9,5},{13,1},{2,10},{6,14},... | collective-permute-start | bytes 147464 | tf_op jit(solution)/shard_map/ppermute | solution.py:505
  5.8 1.1 %collective-permute-start.1 = (bf16[1,8,1024]{2,1,0:T(8,128)(2,1)S(1)}, bf16[1,8,1024]{2,1,0:T(8,128)(2,1)S(1)}, u32[]{:S(2)}, u32[]{:S(2)}) collective-permute-start(bf16[1,8,1024]{2,1,0:T(8,128)(2,1)S(1)} %get-tuple-element.36), channel_id=1, source_target_pairs={{0,12},{4,8},{8,0},{12,4},{1,13},{5,9},{9,1},{13,5},{2,14},{6,10},... | collective-permute-start | bytes 49160 | tf_op jit(solution)/shard_map/ppermute | solution.py:505
  6.9 0.5 %collective-permute-start.2 = (bf16[1,8,1024]{2,1,0:T(8,128)(2,1)S(1)}, bf16[1,8,1024]{2,1,0:T(8,128)(2,1)S(1)}, u32[]{:S(2)}, u32[]{:S(2)}) collective-permute-start(bf16[1,8,1024]{2,1,0:T(8,128)(2,1)S(1)} %get-tuple-element.37), channel_id=1, source_target_pairs={{0,4},{4,0},{8,12},{12,8},{1,5},{5,1},{9,13},{13,9},{2,6},{6,2},{1... | collective-permute-start | bytes 49160 | tf_op jit(solution)/shard_map/ppermute | solution.py:505
  7.4 0.0 copy-start
  7.4 1.6 %shard_map.149 = (f32[4,16,1024]{2,1,0:T(8,128)S(1)}, f32[4,16,1024]{2,1,0:T(8,128)S(1)}, f32[16,4]{1,0:T(8,128)S(1)}, f32[16,4]{1,0:T(8,128)S(1)}, f32[1,4]{1,0...) custom-call(s32[1]{0:T(128)} %bitcast.owner_hbm, ...), custom_call_target="tpu_custom_call" | custom-call | flops 655360 | bytes 786432 | tf_op jit(solution)/shard_map/pallas_call | solution.py:512
  9.0 0.0 collective-permute-done.rest_1_.came_ref
  9.0 0.0 copy-done
  9.0 1.6 %collective-permute-start.4 = (bf16[1,48,1024]{2,1,0:T(8,128)(2,1)S(1)}, bf16[1,48,1024]{2,1,0:T(8,128)(2,1)S(1)}, u32[]{:S(2)}, u32[]{:S(2)}) collective-permute-start(bf16[1,48,1024]{2,1,0:T(8,128)(2,1)S(1)} %shard_map.152), channel_id=1, source_target_pairs={{0,4},{4,0},{8,12},{12,8},{1,5},{5,1},{9,13},{13,9},{2,6},{6,2},{1... | collective-permute-start | bytes 294920 | tf_op jit(solution)/shard_map/ppermute | solution.py:55
  10.6 0.0 collective-permute-done.1.rest_2_
  10.6 0.0 collective-permute-done.2.rest_3_
  10.7 0.5 %shard_map.150 = (f32[80,1024]{1,0:T(8,128)S(1)}, f32[80,288]{1,0:T(8,128)S(1)}, bf16[80,288]{1,0:T(8,128)(2,1)S(1)}) custom-call(f32[16,4]{1,0:T(8,128)S(1)} %get-tuple-element.29.pick_ref.after_ref, f32[1,4]{1,0:T(1,128)S(1)} %get-tuple-element.30.sender_ref, f32[4,16,1024]{2,1,0:T(8,128)S(1)} %get-tuple-element.31.base_ref, ...), custom_call_target="tpu_custom_call" | custom-call | flops 47185920 | bytes 1009664 | tf_op jit(solution)/shard_map/pallas_call | solution.py:566
  11.2 0.0 copy-start.1
  11.2 0.1 collective-permute-start.3
  11.3 1.2 %collective-permute-done.3.b_ref = bf16[80,288]{1,0:T(8,128)(2,1)S(1)} collective-permute-done((bf16[80,288]{1,0:T(8,128)(2,1)S(1)}, bf16[80,288]{1,0:T(8,128)(2,1)S(1)}, u32[]{:S(2)}, u32[]{:S(2)}) %collective-permute-start.3) | collective-permute-done | bytes 46112 | tf_op jit(solution)/shard_map/ppermute | solution.py:55
  12.5 1.5 %collective-permute-start.5 = (bf16[80,288]{1,0:T(8,128)(2,1)S(1)}, bf16[80,288]{1,0:T(8,128)(2,1)S(1)}, u32[]{:S(2)}, u32[]{:S(2)}) collective-permute-start(bf16[80,288]{1,0:T(8,128)(2,1)S(1)} %get-tuple-element.49), channel_id=1, source_target_pairs={{0,3},{1,2},{2,1},{3,0},{4,7},{5,6},{6,5},{7,4},{8,11},{9,10},{10,... | collective-permute-start | bytes 138248 | tf_op jit(solution)/shard_map/ppermute | solution.py:55
  14.0 0.8 %shard_map.155 = bf16[3,16,1024]{2,1,0:T(8,128)(2,1)} custom-call(f32[16,4]{1,0:T(8,128)S(1)} %get-tuple-element.52.child_ref, f32[80,288]{1,0:T(8,128)S(1)} %get-tuple-element.42.after_ref.part_ref, bf16[1,8,1024]{2,1,0:T(8,128)(2,1)S(1)} %get-tuple-element.28.after_ref.rest_0_, bf16[1,24,1024]{2,1,0:T(8,128)(2,1)S(1)} %collective-permute-done.rest_1_.came_ref, ...), custom_call_target="tpu_custom_call" | custom-call | flops 524288 | bytes 262144 | tf_op jit(solution)/shard_map/pallas_call | solution.py:593
  14.8 0.0 collective-permute-done.4.rest_5_
  14.8 0.5 %shard_map.153 = (f32[16,16,1024]{2,1,0:T(8,128)S(1)}, f32[8,8,1024]{2,1,0:T(8,128)S(1)}) custom-call(f32[16,4]{1,0:T(8,128)S(1)} %get-tuple-element.29.pick_ref.after_ref, f32[1,4]{1,0:T(1,128)S(1)} %get-tuple-element.30.sender_ref, f32[80,288]{1,0:T(8,128)S(1)} %get-tuple-element.42.after_ref.part_ref, ...), custom_call_target="tpu_custom_call" | custom-call | flops 2621440 | bytes 1310720 | tf_op jit(solution)/shard_map/pallas_call | solution.py:601
  15.3 1.2 %collective-permute-done.5.other_ref = bf16[80,288]{1,0:T(8,128)(2,1)S(1)} collective-permute-done((bf16[80,288]{1,0:T(8,128)(2,1)S(1)}, bf16[80,288]{1,0:T(8,128)(2,1)S(1)}, u32[]{:S(2)}, u32[]{:S(2)}) %collective-permute-start.5) | collective-permute-done | bytes 46112 | tf_op jit(solution)/shard_map/ppermute | solution.py:55
  16.5 0.0 copy-done.1
  16.5 3.1 %shard_map.154 = (bf16[16,4,1024]{2,1,0:T(4,128)(2,1)}, f32[16,16,1024]{2,1,0:T(8,128)}) custom-call(s32[1]{0:T(128)} %bitcast.owner_hbm, s32[16]{0:T(128)} %child_hbm.3, f32[80,1024]{1,0:T(8,128)S(1)} %get-tuple-element.38.act_ref, f32[4,16,1024]{2,1,0:T(8,128)S(1)} %get-tuple-element.39.gate_ref, f32[16,16,1024]{2,1,0:T(8,128)S(1)} %get-tuple-element.43.own_ref, ...), custom_call_target="tpu_custom_call" | custom-call | flops 10485760 | bytes 1310720 | tf_op jit(solution)/shard_map/pallas_call | solution.py:614
  (2 shorter events, 0.0 us)
Async XLA Ops:
  1.8 7.3 %collective-permute-start = (bf16[1,24,1024]{2,1,0:T(8,128)(2,1)S(1)}, bf16[1,24,1024]{2,1,0:T(8,128)(2,1)S(1)}, u32[]{:S(2)}, u32[]{:S(2)}) collective-permute-start(bf16[1,24,1024]{2,1,0:T(8,128)(2,1)S(1)} %get-tuple-element.35), channel_id=1, source_target_pairs={{0,8},{4,12},{8,4},{12,0},{1,9},{5,13},{9,5},{13,1},{2,10},{6,14},... | collective-permute-start | bytes 147464 | tf_op jit(solution)/shard_map/ppermute | solution.py:505
  5.8 4.8 %collective-permute-start.1 = (bf16[1,8,1024]{2,1,0:T(8,128)(2,1)S(1)}, bf16[1,8,1024]{2,1,0:T(8,128)(2,1)S(1)}, u32[]{:S(2)}, u32[]{:S(2)}) collective-permute-start(bf16[1,8,1024]{2,1,0:T(8,128)(2,1)S(1)} %get-tuple-element.36), channel_id=1, source_target_pairs={{0,12},{4,8},{8,0},{12,4},{1,13},{5,9},{9,1},{13,5},{2,14},{6,10},... | collective-permute-start | bytes 49160 | tf_op jit(solution)/shard_map/ppermute | solution.py:505
  6.9 3.7 %collective-permute-start.2 = (bf16[1,8,1024]{2,1,0:T(8,128)(2,1)S(1)}, bf16[1,8,1024]{2,1,0:T(8,128)(2,1)S(1)}, u32[]{:S(2)}, u32[]{:S(2)}) collective-permute-start(bf16[1,8,1024]{2,1,0:T(8,128)(2,1)S(1)} %get-tuple-element.37), channel_id=1, source_target_pairs={{0,4},{4,0},{8,12},{12,8},{1,5},{5,1},{9,13},{13,9},{2,6},{6,2},{1... | collective-permute-start | bytes 49160 | tf_op jit(solution)/shard_map/ppermute | solution.py:505
  7.4 1.6 %copy-start = (f32[1,16,1024]{2,1,0:T(8,128)S(1)}, f32[1,16,1024]{2,1,0:T(8,128)}, u32[]{:S(2)}) copy-start(f32[1,16,1024]{2,1,0:T(8,128)} %rest_4_.1) | copy-start | bytes 196612
  9.0 5.7 %collective-permute-start.4 = (bf16[1,48,1024]{2,1,0:T(8,128)(2,1)S(1)}, bf16[1,48,1024]{2,1,0:T(8,128)(2,1)S(1)}, u32[]{:S(2)}, u32[]{:S(2)}) collective-permute-start(bf16[1,48,1024]{2,1,0:T(8,128)(2,1)S(1)} %shard_map.152), channel_id=1, source_target_pairs={{0,4},{4,0},{8,12},{12,8},{1,5},{5,1},{9,13},{13,9},{2,6},{6,2},{1... | collective-permute-start | bytes 294920 | tf_op jit(solution)/shard_map/ppermute | solution.py:55
  11.2 5.4 %copy-start.1 = (bf16[256,1024]{1,0:T(8,128)(2,1)S(1)}, bf16[256,1024]{1,0:T(8,128)(2,1)}, u32[]{:S(2)}) copy-start(bf16[256,1024]{1,0:T(8,128)(2,1)} %dtw_ref.1) | copy-start | bytes 1572868
  11.2 1.3 %collective-permute-start.3 = (bf16[80,288]{1,0:T(8,128)(2,1)S(1)}, bf16[80,288]{1,0:T(8,128)(2,1)S(1)}, u32[]{:S(2)}, u32[]{:S(2)}) collective-permute-start(bf16[80,288]{1,0:T(8,128)(2,1)S(1)} %get-tuple-element.41), channel_id=1, source_target_pairs={{0,1},{1,0},{2,3},{3,2},{4,5},{5,4},{6,7},{7,6},{8,9},{9,8},{10,11... | collective-permute-start | bytes 138248 | tf_op jit(solution)/shard_map/ppermute | solution.py:55
  12.5 4.0 %collective-permute-start.5 = (bf16[80,288]{1,0:T(8,128)(2,1)S(1)}, bf16[80,288]{1,0:T(8,128)(2,1)S(1)}, u32[]{:S(2)}, u32[]{:S(2)}) collective-permute-start(bf16[80,288]{1,0:T(8,128)(2,1)S(1)} %get-tuple-element.49), channel_id=1, source_target_pairs={{0,3},{1,2},{2,1},{3,0},{4,7},{5,6},{6,5},{7,4},{8,11},{9,10},{10,... | collective-permute-start | bytes 138248 | tf_op jit(solution)/shard_map/ppermute | solution.py:55

commit v13 on v12

--- a/solution.py
+++ b/solution.py
@@ -100,6 +100,19 @@
         wanted = jnp.where(row_of == b, senders_s[b], wanted)
     wanted = block_of(wanted, owner, direct)
     return (wanted == lax.broadcasted_iota(jnp.int32, shape, 1)).astype(F32)
+
+
+def each_chunk(body, chunks, straight):
+    if straight:
+        for chunk in range(chunks):
+            body(slice(chunk * LANES, (chunk + 1) * LANES))
+        return
+
+    def step(chunk, carry):
+        body(pl.ds(pl.multiple_of(chunk * LANES, LANES), LANES))
+        return carry
+
+    lax.fori_loop(0, chunks, step, 0)
 
 
 def pick_rows(pick, rows):
@@ -398,8 +411,7 @@
         b_s[n] = column(proj[:own_rows, rank:], n, own_rows)
         c_s[n] = column(proj[:own_rows, rank:], n_state + n, own_rows)
 
-    def slot_chunk(chunk, carry):
-        columns = pl.ds(pl.multiple_of(chunk * LANES, LANES), LANES)
+    def slot_chunk(columns):
         delta = [slot_delta_s[t, :, columns] for t in range(steps)]
         gain = [slot_gain_s[t, :, columns] for t in range(steps)]
         for m in range(n_state // 2):
@@ -409,9 +421,8 @@
                 state = jnp.exp2(delta[t] * rate) * state + gain[t] * twin_b_s[m, t]
             slots_s[:, 2 * m, columns] = state[:n_slots, :]
             slots_s[:, 2 * m + 1, columns] = state[n_slots:, :]
-        return carry
-
-    lax.fori_loop(0, chunks, slot_chunk, 0)
+
+    each_chunk(slot_chunk, chunks, direct)
     for copy in scalars:
         copy.wait()
     copies = []
@@ -421,8 +432,7 @@
         copy.start()
         copies.append(copy)
 
-    def own_chunk(chunk, carry):
-        columns = pl.ds(pl.multiple_of(chunk * LANES, LANES), LANES)
+    def own_chunk(columns):
         at = [pl.ds(t * rb, rb) for t in range(steps)]
         delta = [delta_s[a, columns] for a in at]
         gain = [gain_s[a, columns] for a in at]
@@ -436,9 +446,8 @@
         for t in range(steps):
             line_s[pl.ds(t, rb, stride=steps), :] = sums[t] * gate_ref[t, :, columns]
         dec_ref[:, :, columns] = line_s[...].reshape(rb, steps, LANES).astype(BF16)
-        return carry
-
-    lax.fori_loop(0, chunks, own_chunk, 0)
+
+    each_chunk(own_chunk, chunks, direct)
     for copy in copies:
         copy.wait()
 

time: 19.9 us -> 20 us (level)
  no operation moved by 1% of the time
where the time goes in v13:
time: 20 us; the launch traced here: 19.8 us
  starting transfers between devices  8.81 us (44%)
  Pallas kernels  7.8 us (39%)
  waiting for transfers between devices  2.49 us (12%)
  between operations  0.71 us (4%)
    ppermute x3, starting transfers between devices, on_device(): lax.ppermute(m, 'branch', list(enumerate(to)))  5.67 us
    pallas_call x1, Pallas kernels, on_device(): call(functools.partial(decode_kernel, direct), [shaped((rb, steps, channe...  3.27 us
    ppermute x3, starting transfers between devices, swap(): return lax.ppermute(value, axis, [(i, i ^ distance) for i in range(size)])  3.14 us
    ppermute x3, waiting for transfers between devices, swap(): return lax.ppermute(value, axis, [(i, i ^ distance) for i in range(size)])  2.47 us
    pallas_call x1, Pallas kernels, on_device(): call(functools.partial(prepare_kernel, direct), [shaped((steps, rb, chann...  1.58 us
    pallas_call x1, Pallas kernels, on_device(): call(functools.partial(pack_kernel, direct), [shaped(s, BF16) for s in ms...  1.11 us
    pallas_call x1, Pallas kernels, on_device(): call(functools.partial(windows_kernel, n_msgs, steps), shaped((taps - 1,...  0.78 us
    pallas_call x1, Pallas kernels, on_device(): call(functools.partial(start_kernel, n_msgs, direct, short), [shaped((n_s...  0.53 us
  transfers between devices with their start and end apart: 6, of which 2 were waited for; matrix products, arithmetic and copies ran while one was open for 0% of the time, Pallas kernels for 17%

profile of v13, /device:TPU:0, one launch (start us, length us, event | category | flops | bytes accessed | tf_op | source)
XLA Modules:
  0.0 19.8 jit_solution(4561905366766996431)
XLA Ops:
  0.6 1.1 %shard_map.148 = (bf16[1,8,1024]{2,1,0:T(8,128)(2,1)S(1)}, bf16[1,24,1024]{2,1,0:T(8,128)(2,1)S(1)}, bf16[1,8,1024]{2,1,0:T(8,128)(2,1)S(1)}, bf16[1,8,1024]{2,1,0:T(8,128)(2,1)S(1)}) custom-call(s32[1]{0:T(128)} %bitcast.owner_hbm, s32[4]{0:T(128)} %bitcast.12, s32[16]{0:T(128)} %prompt_hbm.3, bf16[16,4,2,1024]{3,2,1,0:T(2,128)(2,1)} %step_hbm.3, ...), custom_call_target="tpu_custom_call" | custom-call | bytes 196608 | tf_op jit(solution)/shard_map/pallas_call | solution.py:488
  1.8 4.1 %collective-permute-start = (bf16[1,24,1024]{2,1,0:T(8,128)(2,1)S(1)}, bf16[1,24,1024]{2,1,0:T(8,128)(2,1)S(1)}, u32[]{:S(2)}, u32[]{:S(2)}) collective-permute-start(bf16[1,24,1024]{2,1,0:T(8,128)(2,1)S(1)} %get-tuple-element.35), channel_id=1, source_target_pairs={{0,8},{4,12},{8,4},{12,0},{1,9},{5,13},{9,5},{13,1},{2,10},{6,14},... | collective-permute-start | bytes 147464 | tf_op jit(solution)/shard_map/ppermute | solution.py:514
  5.8 1.1 %collective-permute-start.1 = (bf16[1,8,1024]{2,1,0:T(8,128)(2,1)S(1)}, bf16[1,8,1024]{2,1,0:T(8,128)(2,1)S(1)}, u32[]{:S(2)}, u32[]{:S(2)}) collective-permute-start(bf16[1,8,1024]{2,1,0:T(8,128)(2,1)S(1)} %get-tuple-element.36), channel_id=1, source_target_pairs={{0,12},{4,8},{8,0},{12,4},{1,13},{5,9},{9,1},{13,5},{2,14},{6,10},... | collective-permute-start | bytes 49160 | tf_op jit(solution)/shard_map/ppermute | solution.py:514
  6.9 0.5 %collective-permute-start.2 = (bf16[1,8,1024]{2,1,0:T(8,128)(2,1)S(1)}, bf16[1,8,1024]{2,1,0:T(8,128)(2,1)S(1)}, u32[]{:S(2)}, u32[]{:S(2)}) collective-permute-start(bf16[1,8,1024]{2,1,0:T(8,128)(2,1)S(1)} %get-tuple-element.37), channel_id=1, source_target_pairs={{0,4},{4,0},{8,12},{12,8},{1,5},{5,1},{9,13},{13,9},{2,6},{6,2},{1... | collective-permute-start | bytes 49160 | tf_op jit(solution)/shard_map/ppermute | solution.py:514
  7.4 0.0 copy-start
  7.4 1.6 %shard_map.149 = (f32[4,16,1024]{2,1,0:T(8,128)S(1)}, f32[4,16,1024]{2,1,0:T(8,128)S(1)}, f32[16,4]{1,0:T(8,128)S(1)}, f32[16,4]{1,0:T(8,128)S(1)}, f32[1,4]{1,0...) custom-call(s32[1]{0:T(128)} %bitcast.owner_hbm, ...), custom_call_target="tpu_custom_call" | custom-call | flops 655360 | bytes 786432 | tf_op jit(solution)/shard_map/pallas_call | solution.py:521
  9.0 0.0 collective-permute-done.rest_1_.came_ref
  9.0 0.0 copy-done
  9.0 1.6 %collective-permute-start.4 = (bf16[1,48,1024]{2,1,0:T(8,128)(2,1)S(1)}, bf16[1,48,1024]{2,1,0:T(8,128)(2,1)S(1)}, u32[]{:S(2)}, u32[]{:S(2)}) collective-permute-start(bf16[1,48,1024]{2,1,0:T(8,128)(2,1)S(1)} %shard_map.152), channel_id=1, source_target_pairs={{0,4},{4,0},{8,12},{12,8},{1,5},{5,1},{9,13},{13,9},{2,6},{6,2},{1... | collective-permute-start | bytes 294920 | tf_op jit(solution)/shard_map/ppermute | solution.py:55
  10.6 0.0 collective-permute-done.1.rest_2_
  10.6 0.0 collective-permute-done.2.rest_3_
  10.7 0.5 %shard_map.150 = (f32[80,1024]{1,0:T(8,128)S(1)}, f32[80,288]{1,0:T(8,128)S(1)}, bf16[80,288]{1,0:T(8,128)(2,1)S(1)}) custom-call(f32[16,4]{1,0:T(8,128)S(1)} %get-tuple-element.29.pick_ref.after_ref, f32[1,4]{1,0:T(1,128)S(1)} %get-tuple-element.30.sender_ref, f32[4,16,1024]{2,1,0:T(8,128)S(1)} %get-tuple-element.31.base_ref, ...), custom_call_target="tpu_custom_call" | custom-call | flops 47185920 | bytes 1009664 | tf_op jit(solution)/shard_map/pallas_call | solution.py:575
  11.2 0.0 copy-start.1
  11.2 0.1 collective-permute-start.3
  11.3 1.2 %collective-permute-done.3.b_ref = bf16[80,288]{1,0:T(8,128)(2,1)S(1)} collective-permute-done((bf16[80,288]{1,0:T(8,128)(2,1)S(1)}, bf16[80,288]{1,0:T(8,128)(2,1)S(1)}, u32[]{:S(2)}, u32[]{:S(2)}) %collective-permute-start.3) | collective-permute-done | bytes 46112 | tf_op jit(solution)/shard_map/ppermute | solution.py:55
  12.5 1.5 %collective-permute-start.5 = (bf16[80,288]{1,0:T(8,128)(2,1)S(1)}, bf16[80,288]{1,0:T(8,128)(2,1)S(1)}, u32[]{:S(2)}, u32[]{:S(2)}) collective-permute-start(bf16[80,288]{1,0:T(8,128)(2,1)S(1)} %get-tuple-element.49), channel_id=1, source_target_pairs={{0,3},{1,2},{2,1},{3,0},{4,7},{5,6},{6,5},{7,4},{8,11},{9,10},{10,... | collective-permute-start | bytes 138248 | tf_op jit(solution)/shard_map/ppermute | solution.py:55
  14.0 0.8 %shard_map.155 = bf16[3,16,1024]{2,1,0:T(8,128)(2,1)} custom-call(f32[16,4]{1,0:T(8,128)S(1)} %get-tuple-element.52.child_ref, f32[80,288]{1,0:T(8,128)S(1)} %get-tuple-element.42.after_ref.part_ref, bf16[1,8,1024]{2,1,0:T(8,128)(2,1)S(1)} %get-tuple-element.28.after_ref.rest_0_, bf16[1,24,1024]{2,1,0:T(8,128)(2,1)S(1)} %collective-permute-done.rest_1_.came_ref, ...), custom_call_target="tpu_custom_call" | custom-call | flops 524288 | bytes 262144 | tf_op jit(solution)/shard_map/pallas_call | solution.py:602
  14.8 0.0 collective-permute-done.4.rest_5_
  14.8 0.5 %shard_map.153 = (f32[16,16,1024]{2,1,0:T(8,128)S(1)}, f32[8,8,1024]{2,1,0:T(8,128)S(1)}) custom-call(f32[16,4]{1,0:T(8,128)S(1)} %get-tuple-element.29.pick_ref.after_ref, f32[1,4]{1,0:T(1,128)S(1)} %get-tuple-element.30.sender_ref, f32[80,288]{1,0:T(8,128)S(1)} %get-tuple-element.42.after_ref.part_ref, ...), custom_call_target="tpu_custom_call" | custom-call | flops 2621440 | bytes 1310720 | tf_op jit(solution)/shard_map/pallas_call | solution.py:610
  15.3 1.2 %collective-permute-done.5.other_ref = bf16[80,288]{1,0:T(8,128)(2,1)S(1)} collective-permute-done((bf16[80,288]{1,0:T(8,128)(2,1)S(1)}, bf16[80,288]{1,0:T(8,128)(2,1)S(1)}, u32[]{:S(2)}, u32[]{:S(2)}) %collective-permute-start.5) | collective-permute-done | bytes 46112 | tf_op jit(solution)/shard_map/ppermute | solution.py:55
  16.5 0.0 copy-done.1
  16.5 3.3 %shard_map.154 = (bf16[16,4,1024]{2,1,0:T(4,128)(2,1)}, f32[16,16,1024]{2,1,0:T(8,128)}) custom-call(s32[1]{0:T(128)} %bitcast.owner_hbm, s32[16]{0:T(128)} %child_hbm.3, f32[80,1024]{1,0:T(8,128)S(1)} %get-tuple-element.38.act_ref, f32[4,16,1024]{2,1,0:T(8,128)S(1)} %get-tuple-element.39.gate_ref, f32[16,16,1024]{2,1,0:T(8,128)S(1)} %get-tuple-element.43.own_ref, ...), custom_call_target="tpu_custom_call" | custom-call | flops 10485760 | bytes 1310720 | tf_op jit(solution)/shard_map/pallas_call | solution.py:623
  (2 shorter events, 0.0 us)
Async XLA Ops:
  1.8 7.3 %collective-permute-start = (bf16[1,24,1024]{2,1,0:T(8,128)(2,1)S(1)}, bf16[1,24,1024]{2,1,0:T(8,128)(2,1)S(1)}, u32[]{:S(2)}, u32[]{:S(2)}) collective-permute-start(bf16[1,24,1024]{2,1,0:T(8,128)(2,1)S(1)} %get-tuple-element.35), channel_id=1, source_target_pairs={{0,8},{4,12},{8,4},{12,0},{1,9},{5,13},{9,5},{13,1},{2,10},{6,14},... | collective-permute-start | bytes 147464 | tf_op jit(solution)/shard_map/ppermute | solution.py:514
  5.8 4.8 %collective-permute-start.1 = (bf16[1,8,1024]{2,1,0:T(8,128)(2,1)S(1)}, bf16[1,8,1024]{2,1,0:T(8,128)(2,1)S(1)}, u32[]{:S(2)}, u32[]{:S(2)}) collective-permute-start(bf16[1,8,1024]{2,1,0:T(8,128)(2,1)S(1)} %get-tuple-element.36), channel_id=1, source_target_pairs={{0,12},{4,8},{8,0},{12,4},{1,13},{5,9},{9,1},{13,5},{2,14},{6,10},... | collective-permute-start | bytes 49160 | tf_op jit(solution)/shard_map/ppermute | solution.py:514
  6.9 3.7 %collective-permute-start.2 = (bf16[1,8,1024]{2,1,0:T(8,128)(2,1)S(1)}, bf16[1,8,1024]{2,1,0:T(8,128)(2,1)S(1)}, u32[]{:S(2)}, u32[]{:S(2)}) collective-permute-start(bf16[1,8,1024]{2,1,0:T(8,128)(2,1)S(1)} %get-tuple-element.37), channel_id=1, source_target_pairs={{0,4},{4,0},{8,12},{12,8},{1,5},{5,1},{9,13},{13,9},{2,6},{6,2},{1... | collective-permute-start | bytes 49160 | tf_op jit(solution)/shard_map/ppermute | solution.py:514
  7.4 1.6 %copy-start = (f32[1,16,1024]{2,1,0:T(8,128)S(1)}, f32[1,16,1024]{2,1,0:T(8,128)}, u32[]{:S(2)}) copy-start(f32[1,16,1024]{2,1,0:T(8,128)} %rest_4_.1) | copy-start | bytes 196612
  9.0 5.7 %collective-permute-start.4 = (bf16[1,48,1024]{2,1,0:T(8,128)(2,1)S(1)}, bf16[1,48,1024]{2,1,0:T(8,128)(2,1)S(1)}, u32[]{:S(2)}, u32[]{:S(2)}) collective-permute-start(bf16[1,48,1024]{2,1,0:T(8,128)(2,1)S(1)} %shard_map.152), channel_id=1, source_target_pairs={{0,4},{4,0},{8,12},{12,8},{1,5},{5,1},{9,13},{13,9},{2,6},{6,2},{1... | collective-permute-start | bytes 294920 | tf_op jit(solution)/shard_map/ppermute | solution.py:55
  11.2 5.4 %copy-start.1 = (bf16[256,1024]{1,0:T(8,128)(2,1)S(1)}, bf16[256,1024]{1,0:T(8,128)(2,1)}, u32[]{:S(2)}) copy-start(bf16[256,1024]{1,0:T(8,128)(2,1)} %dtw_ref.1) | copy-start | bytes 1572868
  11.2 1.3 %collective-permute-start.3 = (bf16[80,288]{1,0:T(8,128)(2,1)S(1)}, bf16[80,288]{1,0:T(8,128)(2,1)S(1)}, u32[]{:S(2)}, u32[]{:S(2)}) collective-permute-start(bf16[80,288]{1,0:T(8,128)(2,1)S(1)} %get-tuple-element.41), channel_id=1, source_target_pairs={{0,1},{1,0},{2,3},{3,2},{4,5},{5,4},{6,7},{7,6},{8,9},{9,8},{10,11... | collective-permute-start | bytes 138248 | tf_op jit(solution)/shard_map/ppermute | solution.py:55
  12.5 4.0 %collective-permute-start.5 = (bf16[80,288]{1,0:T(8,128)(2,1)S(1)}, bf16[80,288]{1,0:T(8,128)(2,1)S(1)}, u32[]{:S(2)}, u32[]{:S(2)}) collective-permute-start(bf16[80,288]{1,0:T(8,128)(2,1)S(1)} %get-tuple-element.49), channel_id=1, source_target_pairs={{0,3},{1,2},{2,1},{3,0},{4,7},{5,6},{6,5},{7,4},{8,11},{9,10},{10,... | collective-permute-start | bytes 138248 | tf_op jit(solution)/shard_map/ppermute | solution.py:55

commit v14 on v13

--- a/solution.py
+++ b/solution.py
@@ -386,19 +386,19 @@
     own_rows = steps * rb
     chunks = channels // LANES
 
-    proj = part_ref[...] + other_ref[...].astype(F32)
-    delta_in = proj[:, :rank].astype(BF16)
-    delta = jnp.dot(delta_in, dtw_ref[...], preferred_element_type=F32) + dtb_ref[...]
-    delta = jnp.maximum(delta, 0.0) + jnp.log(1.0 + jnp.exp(-jnp.abs(delta)))
-    gain = delta * act_ref[...]
-    delta_s[...] = delta[:own_rows, :]
-    gain_s[...] = gain[:own_rows, :]
+    def sums_of(rows):
+        proj = part_ref[rows, :] + other_ref[rows, :].astype(F32)
+        delta_in = proj[:, :rank].astype(BF16)
+        delta = jnp.dot(delta_in, dtw_ref[...], preferred_element_type=F32) + dtb_ref[...]
+        delta = jnp.maximum(delta, 0.0) + jnp.log(1.0 + jnp.exp(-jnp.abs(delta)))
+        return proj, delta, delta * act_ref[rows, :]
 
     def column(at, n, rows):
         return jnp.broadcast_to(at[:, n : n + 1], (rows, LANES))
 
+    proj, delta, gain = sums_of(slice(own_rows, own_rows + steps * n_slots))
     for t in range(steps):
-        at = slice(own_rows + t * n_slots, own_rows + (t + 1) * n_slots)
+        at = slice(t * n_slots, (t + 1) * n_slots)
         slot_delta_s[t] = jnp.concatenate([delta[at, :]] * 2, axis=0)
         slot_gain_s[t] = jnp.concatenate([gain[at, :]] * 2, axis=0)
         twice = jnp.concatenate([proj[at, rank:]] * 2, axis=0)
@@ -407,9 +407,6 @@
             twin_b_s[m, t] = jnp.where(
                 upper, column(twice, 2 * m, 2 * n_slots), column(twice, 2 * m + 1, 2 * n_slots)
             )
-    for n in range(n_state):
-        b_s[n] = column(proj[:own_rows, rank:], n, own_rows)
-        c_s[n] = column(proj[:own_rows, rank:], n_state + n, own_rows)
 
     def slot_chunk(columns):
         delta = [slot_delta_s[t, :, columns] for t in range(steps)]
@@ -431,6 +428,13 @@
         copy = pltpu.make_async_copy(slots_s.at[at], child_ssm.at[j], sems.at[2 + j])
         copy.start()
         copies.append(copy)
+
+    proj, delta, gain = sums_of(slice(0, own_rows))
+    delta_s[...] = delta
+    gain_s[...] = gain
+    for n in range(n_state):
+        b_s[n] = column(proj[:, rank:], n, own_rows)
+        c_s[n] = column(proj[:, rank:], n_state + n, own_rows)
 
     def own_chunk(columns):
         at = [pl.ds(t * rb, rb) for t in range(steps)]
@@ -447,7 +451,7 @@
             line_s[pl.ds(t, rb, stride=steps), :] = sums[t] * gate_ref[t, :, columns]
         dec_ref[:, :, columns] = line_s[...].reshape(rb, steps, LANES).astype(BF16)
 
-    each_chunk(own_chunk, chunks, direct)
+    each_chunk(own_chunk, chunks, False)
     for copy in copies:
         copy.wait()
 

time: 20 us -> 20 us (level)
  no operation moved by 1% of the time
where the time goes in v14:
time: 20 us; the launch traced here: 19.7 us
  starting transfers between devices  8.81 us (44%)
  Pallas kernels  7.72 us (39%)
  waiting for transfers between devices  2.49 us (12%)
  between operations  0.71 us (4%)
    ppermute x3, starting transfers between devices, on_device(): lax.ppermute(m, 'branch', list(enumerate(to)))  5.67 us
    pallas_call x1, Pallas kernels, on_device(): call(functools.partial(decode_kernel, direct), [shaped((rb, steps, channe...  3.19 us
    ppermute x3, starting transfers between devices, swap(): return lax.ppermute(value, axis, [(i, i ^ distance) for i in range(size)])  3.14 us
    ppermute x3, waiting for transfers between devices, swap(): return lax.ppermute(value, axis, [(i, i ^ distance) for i in range(size)])  2.47 us
    pallas_call x1, Pallas kernels, on_device(): call(functools.partial(prepare_kernel, direct), [shaped((steps, rb, chann...  1.58 us
    pallas_call x1, Pallas kernels, on_device(): call(functools.partial(pack_kernel, direct), [shaped(s, BF16) for s in ms...  1.11 us
    pallas_call x1, Pallas kernels, on_device(): call(functools.partial(windows_kernel, n_msgs, steps), shaped((taps - 1,...  0.78 us
    pallas_call x1, Pallas kernels, on_device(): call(functools.partial(start_kernel, n_msgs, direct, short), [shaped((n_s...  0.53 us
  transfers between devices with their start and end apart: 6, of which 2 were waited for; matrix products, arithmetic and copies ran while one was open for 0% of the time, Pallas kernels for 17%

profile of v14, /device:TPU:0, one launch (start us, length us, event | category | flops | bytes accessed | tf_op | source)
XLA Modules:
  0.0 19.7 jit_solution(13199893273513068195)
XLA Ops:
  0.6 1.1 %shard_map.148 = (bf16[1,8,1024]{2,1,0:T(8,128)(2,1)S(1)}, bf16[1,24,1024]{2,1,0:T(8,128)(2,1)S(1)}, bf16[1,8,1024]{2,1,0:T(8,128)(2,1)S(1)}, bf16[1,8,1024]{2,1,0:T(8,128)(2,1)S(1)}) custom-call(s32[1]{0:T(128)} %bitcast.owner_hbm, s32[4]{0:T(128)} %bitcast.12, s32[16]{0:T(128)} %prompt_hbm.3, bf16[16,4,2,1024]{3,2,1,0:T(2,128)(2,1)} %step_hbm.3, ...), custom_call_target="tpu_custom_call" | custom-call | bytes 196608 | tf_op jit(solution)/shard_map/pallas_call | solution.py:492
  1.8 4.1 %collective-permute-start = (bf16[1,24,1024]{2,1,0:T(8,128)(2,1)S(1)}, bf16[1,24,1024]{2,1,0:T(8,128)(2,1)S(1)}, u32[]{:S(2)}, u32[]{:S(2)}) collective-permute-start(bf16[1,24,1024]{2,1,0:T(8,128)(2,1)S(1)} %get-tuple-element.35), channel_id=1, source_target_pairs={{0,8},{4,12},{8,4},{12,0},{1,9},{5,13},{9,5},{13,1},{2,10},{6,14},... | collective-permute-start | bytes 147464 | tf_op jit(solution)/shard_map/ppermute | solution.py:518
  5.8 1.1 %collective-permute-start.1 = (bf16[1,8,1024]{2,1,0:T(8,128)(2,1)S(1)}, bf16[1,8,1024]{2,1,0:T(8,128)(2,1)S(1)}, u32[]{:S(2)}, u32[]{:S(2)}) collective-permute-start(bf16[1,8,1024]{2,1,0:T(8,128)(2,1)S(1)} %get-tuple-element.36), channel_id=1, source_target_pairs={{0,12},{4,8},{8,0},{12,4},{1,13},{5,9},{9,1},{13,5},{2,14},{6,10},... | collective-permute-start | bytes 49160 | tf_op jit(solution)/shard_map/ppermute | solution.py:518
  6.9 0.5 %collective-permute-start.2 = (bf16[1,8,1024]{2,1,0:T(8,128)(2,1)S(1)}, bf16[1,8,1024]{2,1,0:T(8,128)(2,1)S(1)}, u32[]{:S(2)}, u32[]{:S(2)}) collective-permute-start(bf16[1,8,1024]{2,1,0:T(8,128)(2,1)S(1)} %get-tuple-element.37), channel_id=1, source_target_pairs={{0,4},{4,0},{8,12},{12,8},{1,5},{5,1},{9,13},{13,9},{2,6},{6,2},{1... | collective-permute-start | bytes 49160 | tf_op jit(solution)/shard_map/ppermute | solution.py:518
  7.4 0.0 copy-start
  7.4 1.6 %shard_map.149 = (f32[4,16,1024]{2,1,0:T(8,128)S(1)}, f32[4,16,1024]{2,1,0:T(8,128)S(1)}, f32[16,4]{1,0:T(8,128)S(1)}, f32[16,4]{1,0:T(8,128)S(1)}, f32[1,4]{1,0...) custom-call(s32[1]{0:T(128)} %bitcast.owner_hbm, ...), custom_call_target="tpu_custom_call" | custom-call | flops 655360 | bytes 786432 | tf_op jit(solution)/shard_map/pallas_call | solution.py:525
  9.0 0.0 collective-permute-done.rest_1_.came_ref
  9.0 0.0 copy-done
  9.0 1.6 %collective-permute-start.4 = (bf16[1,48,1024]{2,1,0:T(8,128)(2,1)S(1)}, bf16[1,48,1024]{2,1,0:T(8,128)(2,1)S(1)}, u32[]{:S(2)}, u32[]{:S(2)}) collective-permute-start(bf16[1,48,1024]{2,1,0:T(8,128)(2,1)S(1)} %shard_map.152), channel_id=1, source_target_pairs={{0,4},{4,0},{8,12},{12,8},{1,5},{5,1},{9,13},{13,9},{2,6},{6,2},{1... | collective-permute-start | bytes 294920 | tf_op jit(solution)/shard_map/ppermute | solution.py:55
  10.6 0.0 collective-permute-done.1.rest_2_
  10.6 0.0 collective-permute-done.2.rest_3_
  10.7 0.5 %shard_map.150 = (f32[80,1024]{1,0:T(8,128)S(1)}, f32[80,288]{1,0:T(8,128)S(1)}, bf16[80,288]{1,0:T(8,128)(2,1)S(1)}) custom-call(f32[16,4]{1,0:T(8,128)S(1)} %get-tuple-element.29.pick_ref.after_ref, f32[1,4]{1,0:T(1,128)S(1)} %get-tuple-element.30.sender_ref, f32[4,16,1024]{2,1,0:T(8,128)S(1)} %get-tuple-element.31.base_ref, ...), custom_call_target="tpu_custom_call" | custom-call | flops 47185920 | bytes 1009664 | tf_op jit(solution)/shard_map/pallas_call | solution.py:579
  11.2 0.0 copy-start.1
  11.2 0.1 collective-permute-start.3
  11.3 1.2 %collective-permute-done.3.b_ref = bf16[80,288]{1,0:T(8,128)(2,1)S(1)} collective-permute-done((bf16[80,288]{1,0:T(8,128)(2,1)S(1)}, bf16[80,288]{1,0:T(8,128)(2,1)S(1)}, u32[]{:S(2)}, u32[]{:S(2)}) %collective-permute-start.3) | collective-permute-done | bytes 46112 | tf_op jit(solution)/shard_map/ppermute | solution.py:55
  12.5 1.5 %collective-permute-start.5 = (bf16[80,288]{1,0:T(8,128)(2,1)S(1)}, bf16[80,288]{1,0:T(8,128)(2,1)S(1)}, u32[]{:S(2)}, u32[]{:S(2)}) collective-permute-start(bf16[80,288]{1,0:T(8,128)(2,1)S(1)} %get-tuple-element.49), channel_id=1, source_target_pairs={{0,3},{1,2},{2,1},{3,0},{4,7},{5,6},{6,5},{7,4},{8,11},{9,10},{10,... | collective-permute-start | bytes 138248 | tf_op jit(solution)/shard_map/ppermute | solution.py:55
  14.0 0.8 %shard_map.155 = bf16[3,16,1024]{2,1,0:T(8,128)(2,1)} custom-call(f32[16,4]{1,0:T(8,128)S(1)} %get-tuple-element.52.child_ref, f32[80,288]{1,0:T(8,128)S(1)} %get-tuple-element.42.after_ref.part_ref, bf16[1,8,1024]{2,1,0:T(8,128)(2,1)S(1)} %get-tuple-element.28.after_ref.rest_0_, bf16[1,24,1024]{2,1,0:T(8,128)(2,1)S(1)} %collective-permute-done.rest_1_.came_ref, ...), custom_call_target="tpu_custom_call" | custom-call | flops 524288 | bytes 262144 | tf_op jit(solution)/shard_map/pallas_call | solution.py:606
  14.8 0.0 collective-permute-done.4.rest_5_
  14.8 0.5 %shard_map.153 = (f32[16,16,1024]{2,1,0:T(8,128)S(1)}, f32[8,8,1024]{2,1,0:T(8,128)S(1)}) custom-call(f32[16,4]{1,0:T(8,128)S(1)} %get-tuple-element.29.pick_ref.after_ref, f32[1,4]{1,0:T(1,128)S(1)} %get-tuple-element.30.sender_ref, f32[80,288]{1,0:T(8,128)S(1)} %get-tuple-element.42.after_ref.part_ref, ...), custom_call_target="tpu_custom_call" | custom-call | flops 2621440 | bytes 1310720 | tf_op jit(solution)/shard_map/pallas_call | solution.py:614
  15.3 1.2 %collective-permute-done.5.other_ref = bf16[80,288]{1,0:T(8,128)(2,1)S(1)} collective-permute-done((bf16[80,288]{1,0:T(8,128)(2,1)S(1)}, bf16[80,288]{1,0:T(8,128)(2,1)S(1)}, u32[]{:S(2)}, u32[]{:S(2)}) %collective-permute-start.5) | collective-permute-done | bytes 46112 | tf_op jit(solution)/shard_map/ppermute | solution.py:55
  16.5 0.0 copy-done.1
  16.5 3.2 %shard_map.154 = (bf16[16,4,1024]{2,1,0:T(4,128)(2,1)}, f32[16,16,1024]{2,1,0:T(8,128)}) custom-call(s32[1]{0:T(128)} %bitcast.owner_hbm, s32[16]{0:T(128)} %child_hbm.3, f32[80,1024]{1,0:T(8,128)S(1)} %get-tuple-element.38.act_ref, f32[4,16,1024]{2,1,0:T(8,128)S(1)} %get-tuple-element.39.gate_ref, f32[16,16,1024]{2,1,0:T(8,128)S(1)} %get-tuple-element.43.own_ref, ...), custom_call_target="tpu_custom_call" | custom-call | flops 10485760 | bytes 1310720 | tf_op jit(solution)/shard_map/pallas_call | solution.py:627
  (2 shorter events, 0.0 us)
Async XLA Ops:
  1.8 7.3 %collective-permute-start = (bf16[1,24,1024]{2,1,0:T(8,128)(2,1)S(1)}, bf16[1,24,1024]{2,1,0:T(8,128)(2,1)S(1)}, u32[]{:S(2)}, u32[]{:S(2)}) collective-permute-start(bf16[1,24,1024]{2,1,0:T(8,128)(2,1)S(1)} %get-tuple-element.35), channel_id=1, source_target_pairs={{0,8},{4,12},{8,4},{12,0},{1,9},{5,13},{9,5},{13,1},{2,10},{6,14},... | collective-permute-start | bytes 147464 | tf_op jit(solution)/shard_map/ppermute | solution.py:518
  5.8 4.8 %collective-permute-start.1 = (bf16[1,8,1024]{2,1,0:T(8,128)(2,1)S(1)}, bf16[1,8,1024]{2,1,0:T(8,128)(2,1)S(1)}, u32[]{:S(2)}, u32[]{:S(2)}) collective-permute-start(bf16[1,8,1024]{2,1,0:T(8,128)(2,1)S(1)} %get-tuple-element.36), channel_id=1, source_target_pairs={{0,12},{4,8},{8,0},{12,4},{1,13},{5,9},{9,1},{13,5},{2,14},{6,10},... | collective-permute-start | bytes 49160 | tf_op jit(solution)/shard_map/ppermute | solution.py:518
  6.9 3.7 %collective-permute-start.2 = (bf16[1,8,1024]{2,1,0:T(8,128)(2,1)S(1)}, bf16[1,8,1024]{2,1,0:T(8,128)(2,1)S(1)}, u32[]{:S(2)}, u32[]{:S(2)}) collective-permute-start(bf16[1,8,1024]{2,1,0:T(8,128)(2,1)S(1)} %get-tuple-element.37), channel_id=1, source_target_pairs={{0,4},{4,0},{8,12},{12,8},{1,5},{5,1},{9,13},{13,9},{2,6},{6,2},{1... | collective-permute-start | bytes 49160 | tf_op jit(solution)/shard_map/ppermute | solution.py:518
  7.4 1.6 %copy-start = (f32[1,16,1024]{2,1,0:T(8,128)S(1)}, f32[1,16,1024]{2,1,0:T(8,128)}, u32[]{:S(2)}) copy-start(f32[1,16,1024]{2,1,0:T(8,128)} %rest_4_.1) | copy-start | bytes 196612
  9.0 5.7 %collective-permute-start.4 = (bf16[1,48,1024]{2,1,0:T(8,128)(2,1)S(1)}, bf16[1,48,1024]{2,1,0:T(8,128)(2,1)S(1)}, u32[]{:S(2)}, u32[]{:S(2)}) collective-permute-start(bf16[1,48,1024]{2,1,0:T(8,128)(2,1)S(1)} %shard_map.152), channel_id=1, source_target_pairs={{0,4},{4,0},{8,12},{12,8},{1,5},{5,1},{9,13},{13,9},{2,6},{6,2},{1... | collective-permute-start | bytes 294920 | tf_op jit(solution)/shard_map/ppermute | solution.py:55
  11.2 5.4 %copy-start.1 = (bf16[256,1024]{1,0:T(8,128)(2,1)S(1)}, bf16[256,1024]{1,0:T(8,128)(2,1)}, u32[]{:S(2)}) copy-start(bf16[256,1024]{1,0:T(8,128)(2,1)} %dtw_ref.1) | copy-start | bytes 1572868
  11.2 1.3 %collective-permute-start.3 = (bf16[80,288]{1,0:T(8,128)(2,1)S(1)}, bf16[80,288]{1,0:T(8,128)(2,1)S(1)}, u32[]{:S(2)}, u32[]{:S(2)}) collective-permute-start(bf16[80,288]{1,0:T(8,128)(2,1)S(1)} %get-tuple-element.41), channel_id=1, source_target_pairs={{0,1},{1,0},{2,3},{3,2},{4,5},{5,4},{6,7},{7,6},{8,9},{9,8},{10,11... | collective-permute-start | bytes 138248 | tf_op jit(solution)/shard_map/ppermute | solution.py:55
  12.5 4.0 %collective-permute-start.5 = (bf16[80,288]{1,0:T(8,128)(2,1)S(1)}, bf16[80,288]{1,0:T(8,128)(2,1)S(1)}, u32[]{:S(2)}, u32[]{:S(2)}) collective-permute-start(bf16[80,288]{1,0:T(8,128)(2,1)S(1)} %get-tuple-element.49), channel_id=1, source_target_pairs={{0,3},{1,2},{2,1},{3,0},{4,7},{5,6},{6,5},{7,4},{8,11},{9,10},{10,... | collective-permute-start | bytes 138248 | tf_op jit(solution)/shard_map/ppermute | solution.py:55

commit v15 on v12

--- a/solution.py
+++ b/solution.py
@@ -11,6 +11,8 @@
 F32 = jnp.float32
 BF16 = jnp.bfloat16
 LANES = 128
+ROWS = 8
+WIDE = 2
 VMEM_LIMIT = 48 * 2**20
 WEIGHT_PARTS = 6
 STEP_PARTS = 4
@@ -371,7 +373,7 @@
     n_state = rate_ref.shape[0]
     n_slots = slots_s.shape[0]
     own_rows = steps * rb
-    chunks = channels // LANES
+    chunks = channels // (WIDE * LANES)
 
     proj = part_ref[...] + other_ref[...].astype(F32)
     delta_in = proj[:, :rank].astype(BF16)
@@ -398,15 +400,18 @@
         b_s[n] = column(proj[:own_rows, rank:], n, own_rows)
         c_s[n] = column(proj[:own_rows, rank:], n_state + n, own_rows)
 
+    def wide(part):
+        return jnp.concatenate([part] * WIDE, axis=1)
+
     def slot_chunk(chunk, carry):
-        columns = pl.ds(pl.multiple_of(chunk * LANES, LANES), LANES)
+        columns = pl.ds(pl.multiple_of(chunk * WIDE * LANES, WIDE * LANES), WIDE * LANES)
         delta = [slot_delta_s[t, :, columns] for t in range(steps)]
         gain = [slot_gain_s[t, :, columns] for t in range(steps)]
         for m in range(n_state // 2):
             rate = twin_ref[m, :, columns]
             state = slot_ref[m, :, columns]
             for t in range(steps):
-                state = jnp.exp2(delta[t] * rate) * state + gain[t] * twin_b_s[m, t]
+                state = jnp.exp2(delta[t] * rate) * state + gain[t] * wide(twin_b_s[m, t])
             slots_s[:, 2 * m, columns] = state[:n_slots, :]
             slots_s[:, 2 * m + 1, columns] = state[n_slots:, :]
         return carry
@@ -422,20 +427,27 @@
         copies.append(copy)
 
     def own_chunk(chunk, carry):
-        columns = pl.ds(pl.multiple_of(chunk * LANES, LANES), LANES)
-        at = [pl.ds(t * rb, rb) for t in range(steps)]
-        delta = [delta_s[a, columns] for a in at]
-        gain = [gain_s[a, columns] for a in at]
-        sums = [skip_ref[:, columns] * act_ref[a, columns] for a in at]
-        for n in range(n_state):
-            rate = rate_ref[n : n + 1, columns]
-            state = own_ref[n, :, columns]
+        columns = pl.ds(pl.multiple_of(chunk * WIDE * LANES, WIDE * LANES), WIDE * LANES)
+        for first in range(0, rb, ROWS):
+            at = [pl.ds(t * rb + first, ROWS) for t in range(steps)]
+            delta = [delta_s[a, columns] for a in at]
+            gain = [gain_s[a, columns] for a in at]
+            sums = [skip_ref[:, columns] * act_ref[a, columns] for a in at]
+            for n in range(n_state):
+                rate = rate_ref[n : n + 1, columns]
+                state = own_ref[n, pl.ds(first, ROWS), columns]
+                for t in range(steps):
+                    state = jnp.exp2(delta[t] * rate) * state + gain[t] * wide(b_s[n, at[t], :])
+                    sums[t] = sums[t] + wide(c_s[n, at[t], :]) * state
             for t in range(steps):
-                state = jnp.exp2(delta[t] * rate) * state + gain[t] * b_s[n, at[t], :]
-                sums[t] = sums[t] + c_s[n, at[t], :] * state
-        for t in range(steps):
-            line_s[pl.ds(t, rb, stride=steps), :] = sums[t] * gate_ref[t, :, columns]
-        dec_ref[:, :, columns] = line_s[...].reshape(rb, steps, LANES).astype(BF16)
+                out = sums[t] * gate_ref[t, pl.ds(first, ROWS), columns]
+                for w in range(WIDE):
+                    line_s[w, pl.ds(first * steps + t, ROWS, stride=steps), :] = out[
+                        :, w * LANES : (w + 1) * LANES
+                    ]
+        for w in range(WIDE):
+            some = pl.ds(pl.multiple_of((chunk * WIDE + w) * LANES, LANES), LANES)
+            dec_ref[:, :, some] = line_s[w].reshape(rb, steps, LANES).astype(BF16)
         return carry
 
     lax.fori_loop(0, chunks, own_chunk, 0)
@@ -630,7 +642,7 @@
             pltpu.VMEM((n_state, steps * rb, LANES), F32),
             pltpu.VMEM((n_state // 2, steps, 2 * owners, LANES), F32),
             pltpu.VMEM((owners, n_state, channels), F32),
-            pltpu.VMEM((steps * rb, LANES), F32),
+            pltpu.VMEM((WIDE, steps * rb, LANES), F32),
             pltpu.SemaphoreType.DMA((2 + rb,)),
         ],
         flops=8 * rows * n_state * channels,

time: 19.9 us -> 19.6 us (0.985)
  Pallas kernels: 7.65 us -> 7.42 us
    pallas_call x1, Pallas kernels: 3.12 us -> 2.89 us  [on_device(): call(functools.partial(decode_kernel, direct), [shaped((rb, steps, channe...]
  transfers between devices with their start and end apart: 6 -> 6, of which waited for: 2 -> 2; matrix products, arithmetic and copies ran while one was open for 0% -> 0% of each run, Pallas kernels for 17% -> 18%
where the time goes in v15:
time: 19.6 us; the launch traced here: 19.4 us
  starting transfers between devices  8.81 us (45%)
  Pallas kernels  7.42 us (38%)
  waiting for transfers between devices  2.49 us (13%)
  between operations  0.71 us (4%)
    ppermute x3, starting transfers between devices, on_device(): lax.ppermute(m, 'branch', list(enumerate(to)))  5.67 us
    ppermute x3, starting transfers between devices, swap(): return lax.ppermute(value, axis, [(i, i ^ distance) for i in range(size)])  3.14 us
    pallas_call x1, Pallas kernels, on_device(): call(functools.partial(decode_kernel, direct), [shaped((rb, steps, channe...  2.89 us
    ppermute x3, waiting for transfers between devices, swap(): return lax.ppermute(value, axis, [(i, i ^ distance) for i in range(size)])  2.47 us
    pallas_call x1, Pallas kernels, on_device(): call(functools.partial(prepare_kernel, direct), [shaped((steps, rb, chann...  1.58 us
    pallas_call x1, Pallas kernels, on_device(): call(functools.partial(pack_kernel, direct), [shaped(s, BF16) for s in ms...  1.11 us
    pallas_call x1, Pallas kernels, on_device(): call(functools.partial(windows_kernel, n_msgs, steps), shaped((taps - 1,...  0.78 us
    pallas_call x1, Pallas kernels, on_device(): call(functools.partial(start_kernel, n_msgs, direct, short), [shaped((n_s...  0.53 us
  transfers between devices with their start and end apart: 6, of which 2 were waited for; matrix products, arithmetic and copies ran while one was open for 0% of the time, Pallas kernels for 18%

profile of v15, /device:TPU:0, one launch (start us, length us, event | category | flops | bytes accessed | tf_op | source)
XLA Modules:
  0.0 19.4 jit_solution(3778550109183586950)
XLA Ops:
  0.6 1.1 %shard_map.148 = (bf16[1,8,1024]{2,1,0:T(8,128)(2,1)S(1)}, bf16[1,24,1024]{2,1,0:T(8,128)(2,1)S(1)}, bf16[1,8,1024]{2,1,0:T(8,128)(2,1)S(1)}, bf16[1,8,1024]{2,1,0:T(8,128)(2,1)S(1)}) custom-call(s32[1]{0:T(128)} %bitcast.owner_hbm, s32[4]{0:T(128)} %bitcast.12, s32[16]{0:T(128)} %prompt_hbm.3, bf16[16,4,2,1024]{3,2,1,0:T(2,128)(2,1)} %step_hbm.3, ...), custom_call_target="tpu_custom_call" | custom-call | bytes 196608 | tf_op jit(solution)/shard_map/pallas_call | solution.py:491
  1.8 4.1 %collective-permute-start = (bf16[1,24,1024]{2,1,0:T(8,128)(2,1)S(1)}, bf16[1,24,1024]{2,1,0:T(8,128)(2,1)S(1)}, u32[]{:S(2)}, u32[]{:S(2)}) collective-permute-start(bf16[1,24,1024]{2,1,0:T(8,128)(2,1)S(1)} %get-tuple-element.35), channel_id=1, source_target_pairs={{0,8},{4,12},{8,4},{12,0},{1,9},{5,13},{9,5},{13,1},{2,10},{6,14},... | collective-permute-start | bytes 147464 | tf_op jit(solution)/shard_map/ppermute | solution.py:517
  5.8 1.1 %collective-permute-start.1 = (bf16[1,8,1024]{2,1,0:T(8,128)(2,1)S(1)}, bf16[1,8,1024]{2,1,0:T(8,128)(2,1)S(1)}, u32[]{:S(2)}, u32[]{:S(2)}) collective-permute-start(bf16[1,8,1024]{2,1,0:T(8,128)(2,1)S(1)} %get-tuple-element.36), channel_id=1, source_target_pairs={{0,12},{4,8},{8,0},{12,4},{1,13},{5,9},{9,1},{13,5},{2,14},{6,10},... | collective-permute-start | bytes 49160 | tf_op jit(solution)/shard_map/ppermute | solution.py:517
  6.9 0.5 %collective-permute-start.2 = (bf16[1,8,1024]{2,1,0:T(8,128)(2,1)S(1)}, bf16[1,8,1024]{2,1,0:T(8,128)(2,1)S(1)}, u32[]{:S(2)}, u32[]{:S(2)}) collective-permute-start(bf16[1,8,1024]{2,1,0:T(8,128)(2,1)S(1)} %get-tuple-element.37), channel_id=1, source_target_pairs={{0,4},{4,0},{8,12},{12,8},{1,5},{5,1},{9,13},{13,9},{2,6},{6,2},{1... | collective-permute-start | bytes 49160 | tf_op jit(solution)/shard_map/ppermute | solution.py:517
  7.4 0.0 copy-start
  7.4 1.6 %shard_map.149 = (f32[4,16,1024]{2,1,0:T(8,128)S(1)}, f32[4,16,1024]{2,1,0:T(8,128)S(1)}, f32[16,4]{1,0:T(8,128)S(1)}, f32[16,4]{1,0:T(8,128)S(1)}, f32[1,4]{1,0...) custom-call(s32[1]{0:T(128)} %bitcast.owner_hbm, ...), custom_call_target="tpu_custom_call" | custom-call | flops 655360 | bytes 786432 | tf_op jit(solution)/shard_map/pallas_call | solution.py:524
  9.0 0.0 collective-permute-done.rest_1_.came_ref
  9.0 0.0 copy-done
  9.0 1.6 %collective-permute-start.4 = (bf16[1,48,1024]{2,1,0:T(8,128)(2,1)S(1)}, bf16[1,48,1024]{2,1,0:T(8,128)(2,1)S(1)}, u32[]{:S(2)}, u32[]{:S(2)}) collective-permute-start(bf16[1,48,1024]{2,1,0:T(8,128)(2,1)S(1)} %shard_map.152), channel_id=1, source_target_pairs={{0,4},{4,0},{8,12},{12,8},{1,5},{5,1},{9,13},{13,9},{2,6},{6,2},{1... | collective-permute-start | bytes 294920 | tf_op jit(solution)/shard_map/ppermute | solution.py:57
  10.6 0.0 collective-permute-done.1.rest_2_
  10.6 0.0 collective-permute-done.2.rest_3_
  10.7 0.5 %shard_map.150 = (f32[80,1024]{1,0:T(8,128)S(1)}, f32[80,288]{1,0:T(8,128)S(1)}, bf16[80,288]{1,0:T(8,128)(2,1)S(1)}) custom-call(f32[16,4]{1,0:T(8,128)S(1)} %get-tuple-element.29.pick_ref.after_ref, f32[1,4]{1,0:T(1,128)S(1)} %get-tuple-element.30.sender_ref, f32[4,16,1024]{2,1,0:T(8,128)S(1)} %get-tuple-element.31.base_ref, ...), custom_call_target="tpu_custom_call" | custom-call | flops 47185920 | bytes 1009664 | tf_op jit(solution)/shard_map/pallas_call | solution.py:578
  11.2 0.0 copy-start.1
  11.2 0.1 collective-permute-start.3
  11.3 1.2 %collective-permute-done.3.b_ref = bf16[80,288]{1,0:T(8,128)(2,1)S(1)} collective-permute-done((bf16[80,288]{1,0:T(8,128)(2,1)S(1)}, bf16[80,288]{1,0:T(8,128)(2,1)S(1)}, u32[]{:S(2)}, u32[]{:S(2)}) %collective-permute-start.3) | collective-permute-done | bytes 46112 | tf_op jit(solution)/shard_map/ppermute | solution.py:57
  12.5 1.5 %collective-permute-start.5 = (bf16[80,288]{1,0:T(8,128)(2,1)S(1)}, bf16[80,288]{1,0:T(8,128)(2,1)S(1)}, u32[]{:S(2)}, u32[]{:S(2)}) collective-permute-start(bf16[80,288]{1,0:T(8,128)(2,1)S(1)} %get-tuple-element.49), channel_id=1, source_target_pairs={{0,3},{1,2},{2,1},{3,0},{4,7},{5,6},{6,5},{7,4},{8,11},{9,10},{10,... | collective-permute-start | bytes 138248 | tf_op jit(solution)/shard_map/ppermute | solution.py:57
  14.0 0.8 %shard_map.155 = bf16[3,16,1024]{2,1,0:T(8,128)(2,1)} custom-call(f32[16,4]{1,0:T(8,128)S(1)} %get-tuple-element.52.child_ref, f32[80,288]{1,0:T(8,128)S(1)} %get-tuple-element.42.after_ref.part_ref, bf16[1,8,1024]{2,1,0:T(8,128)(2,1)S(1)} %get-tuple-element.28.after_ref.rest_0_, bf16[1,24,1024]{2,1,0:T(8,128)(2,1)S(1)} %collective-permute-done.rest_1_.came_ref, ...), custom_call_target="tpu_custom_call" | custom-call | flops 524288 | bytes 262144 | tf_op jit(solution)/shard_map/pallas_call | solution.py:605
  14.8 0.0 collective-permute-done.4.rest_5_
  14.8 0.5 %shard_map.153 = (f32[16,16,1024]{2,1,0:T(8,128)S(1)}, f32[8,8,1024]{2,1,0:T(8,128)S(1)}) custom-call(f32[16,4]{1,0:T(8,128)S(1)} %get-tuple-element.29.pick_ref.after_ref, f32[1,4]{1,0:T(1,128)S(1)} %get-tuple-element.30.sender_ref, f32[80,288]{1,0:T(8,128)S(1)} %get-tuple-element.42.after_ref.part_ref, ...), custom_call_target="tpu_custom_call" | custom-call | flops 2621440 | bytes 1310720 | tf_op jit(solution)/shard_map/pallas_call | solution.py:613
  15.3 1.2 %collective-permute-done.5.other_ref = bf16[80,288]{1,0:T(8,128)(2,1)S(1)} collective-permute-done((bf16[80,288]{1,0:T(8,128)(2,1)S(1)}, bf16[80,288]{1,0:T(8,128)(2,1)S(1)}, u32[]{:S(2)}, u32[]{:S(2)}) %collective-permute-start.5) | collective-permute-done | bytes 46112 | tf_op jit(solution)/shard_map/ppermute | solution.py:57
  16.5 0.0 copy-done.1
  16.5 2.9 %shard_map.154 = (bf16[16,4,1024]{2,1,0:T(4,128)(2,1)}, f32[16,16,1024]{2,1,0:T(8,128)}) custom-call(s32[1]{0:T(128)} %bitcast.owner_hbm, s32[16]{0:T(128)} %child_hbm.3, f32[80,1024]{1,0:T(8,128)S(1)} %get-tuple-element.38.act_ref, f32[4,16,1024]{2,1,0:T(8,128)S(1)} %get-tuple-element.39.gate_ref, f32[16,16,1024]{2,1,0:T(8,128)S(1)} %get-tuple-element.43.own_ref, ...), custom_call_target="tpu_custom_call" | custom-call | flops 10485760 | bytes 1310720 | tf_op jit(solution)/shard_map/pallas_call | solution.py:626
  (2 shorter events, 0.0 us)
Async XLA Ops:
  1.8 7.3 %collective-permute-start = (bf16[1,24,1024]{2,1,0:T(8,128)(2,1)S(1)}, bf16[1,24,1024]{2,1,0:T(8,128)(2,1)S(1)}, u32[]{:S(2)}, u32[]{:S(2)}) collective-permute-start(bf16[1,24,1024]{2,1,0:T(8,128)(2,1)S(1)} %get-tuple-element.35), channel_id=1, source_target_pairs={{0,8},{4,12},{8,4},{12,0},{1,9},{5,13},{9,5},{13,1},{2,10},{6,14},... | collective-permute-start | bytes 147464 | tf_op jit(solution)/shard_map/ppermute | solution.py:517
  5.8 4.8 %collective-permute-start.1 = (bf16[1,8,1024]{2,1,0:T(8,128)(2,1)S(1)}, bf16[1,8,1024]{2,1,0:T(8,128)(2,1)S(1)}, u32[]{:S(2)}, u32[]{:S(2)}) collective-permute-start(bf16[1,8,1024]{2,1,0:T(8,128)(2,1)S(1)} %get-tuple-element.36), channel_id=1, source_target_pairs={{0,12},{4,8},{8,0},{12,4},{1,13},{5,9},{9,1},{13,5},{2,14},{6,10},... | collective-permute-start | bytes 49160 | tf_op jit(solution)/shard_map/ppermute | solution.py:517
  6.9 3.7 %collective-permute-start.2 = (bf16[1,8,1024]{2,1,0:T(8,128)(2,1)S(1)}, bf16[1,8,1024]{2,1,0:T(8,128)(2,1)S(1)}, u32[]{:S(2)}, u32[]{:S(2)}) collective-permute-start(bf16[1,8,1024]{2,1,0:T(8,128)(2,1)S(1)} %get-tuple-element.37), channel_id=1, source_target_pairs={{0,4},{4,0},{8,12},{12,8},{1,5},{5,1},{9,13},{13,9},{2,6},{6,2},{1... | collective-permute-start | bytes 49160 | tf_op jit(solution)/shard_map/ppermute | solution.py:517
  7.4 1.6 %copy-start = (f32[1,16,1024]{2,1,0:T(8,128)S(1)}, f32[1,16,1024]{2,1,0:T(8,128)}, u32[]{:S(2)}) copy-start(f32[1,16,1024]{2,1,0:T(8,128)} %rest_4_.1) | copy-start | bytes 196612
  9.0 5.7 %collective-permute-start.4 = (bf16[1,48,1024]{2,1,0:T(8,128)(2,1)S(1)}, bf16[1,48,1024]{2,1,0:T(8,128)(2,1)S(1)}, u32[]{:S(2)}, u32[]{:S(2)}) collective-permute-start(bf16[1,48,1024]{2,1,0:T(8,128)(2,1)S(1)} %shard_map.152), channel_id=1, source_target_pairs={{0,4},{4,0},{8,12},{12,8},{1,5},{5,1},{9,13},{13,9},{2,6},{6,2},{1... | collective-permute-start | bytes 294920 | tf_op jit(solution)/shard_map/ppermute | solution.py:57
  11.2 5.4 %copy-start.1 = (bf16[256,1024]{1,0:T(8,128)(2,1)S(1)}, bf16[256,1024]{1,0:T(8,128)(2,1)}, u32[]{:S(2)}) copy-start(bf16[256,1024]{1,0:T(8,128)(2,1)} %dtw_ref.1) | copy-start | bytes 1572868
  11.2 1.3 %collective-permute-start.3 = (bf16[80,288]{1,0:T(8,128)(2,1)S(1)}, bf16[80,288]{1,0:T(8,128)(2,1)S(1)}, u32[]{:S(2)}, u32[]{:S(2)}) collective-permute-start(bf16[80,288]{1,0:T(8,128)(2,1)S(1)} %get-tuple-element.41), channel_id=1, source_target_pairs={{0,1},{1,0},{2,3},{3,2},{4,5},{5,4},{6,7},{7,6},{8,9},{9,8},{10,11... | collective-permute-start | bytes 138248 | tf_op jit(solution)/shard_map/ppermute | solution.py:57
  12.5 4.0 %collective-permute-start.5 = (bf16[80,288]{1,0:T(8,128)(2,1)S(1)}, bf16[80,288]{1,0:T(8,128)(2,1)S(1)}, u32[]{:S(2)}, u32[]{:S(2)}) collective-permute-start(bf16[80,288]{1,0:T(8,128)(2,1)S(1)} %get-tuple-element.49), channel_id=1, source_target_pairs={{0,3},{1,2},{2,1},{3,0},{4,7},{5,6},{6,5},{7,4},{8,11},{9,10},{10,... | collective-permute-start | bytes 138248 | tf_op jit(solution)/shard_map/ppermute | solution.py:57

commit v16 on v15

--- a/solution.py
+++ b/solution.py
@@ -239,6 +239,10 @@
         copy.wait()
 
 
+def softplus(v):
+    return jnp.maximum(v, 0.0) + jnp.log(1.0 + jnp.exp(-jnp.abs(v)))
+
+
 def slot_onehot(numbers, sender_ref):
     owners = sender_ref.shape[1]
     return (numbers[:, :owners] == sender_ref[...]).astype(F32)
@@ -377,20 +381,19 @@
 
     proj = part_ref[...] + other_ref[...].astype(F32)
     delta_in = proj[:, :rank].astype(BF16)
-    delta = jnp.dot(delta_in, dtw_ref[...], preferred_element_type=F32) + dtb_ref[...]
-    delta = jnp.maximum(delta, 0.0) + jnp.log(1.0 + jnp.exp(-jnp.abs(delta)))
-    gain = delta * act_ref[...]
-    delta_s[...] = delta[:own_rows, :]
-    gain_s[...] = gain[:own_rows, :]
+    raw = jnp.dot(delta_in, dtw_ref[...], preferred_element_type=F32) + dtb_ref[...]
+    delta_s[...] = raw[:own_rows, :]
+    delta = softplus(raw[own_rows:, :])
+    gain = delta * act_ref[own_rows:, :]
 
     def column(at, n, rows):
         return jnp.broadcast_to(at[:, n : n + 1], (rows, LANES))
 
     for t in range(steps):
-        at = slice(own_rows + t * n_slots, own_rows + (t + 1) * n_slots)
+        at = slice(t * n_slots, (t + 1) * n_slots)
         slot_delta_s[t] = jnp.concatenate([delta[at, :]] * 2, axis=0)
         slot_gain_s[t] = jnp.concatenate([gain[at, :]] * 2, axis=0)
-        twice = jnp.concatenate([proj[at, rank:]] * 2, axis=0)
+        twice = jnp.concatenate([proj[own_rows:, rank:][at, :]] * 2, axis=0)
         upper = lax.broadcasted_iota(jnp.int32, (2 * n_slots, LANES), 0) < n_slots
         for m in range(n_state // 2):
             twin_b_s[m, t] = jnp.where(
@@ -414,6 +417,9 @@
                 state = jnp.exp2(delta[t] * rate) * state + gain[t] * wide(twin_b_s[m, t])
             slots_s[:, 2 * m, columns] = state[:n_slots, :]
             slots_s[:, 2 * m + 1, columns] = state[n_slots:, :]
+        own = softplus(delta_s[:, columns])
+        delta_s[:, columns] = own
+        gain_s[:, columns] = own * act_ref[:own_rows, columns]
         return carry
 
     lax.fori_loop(0, chunks, slot_chunk, 0)

time: 19.6 us -> 19.7 us (level)
  no operation moved by 1% of the time
where the time goes in v16:
time: 19.7 us; the launch traced here: 19.5 us
  starting transfers between devices  8.81 us (45%)
  Pallas kernels  7.51 us (38%)
  waiting for transfers between devices  2.49 us (13%)
  between operations  0.71 us (4%)
    ppermute x3, starting transfers between devices, on_device(): lax.ppermute(m, 'branch', list(enumerate(to)))  5.67 us
    ppermute x3, starting transfers between devices, swap(): return lax.ppermute(value, axis, [(i, i ^ distance) for i in range(size)])  3.14 us
    pallas_call x1, Pallas kernels, on_device(): call(functools.partial(decode_kernel, direct), [shaped((rb, steps, channe...  2.98 us
    ppermute x3, waiting for transfers between devices, swap(): return lax.ppermute(value, axis, [(i, i ^ distance) for i in range(size)])  2.47 us
    pallas_call x1, Pallas kernels, on_device(): call(functools.partial(prepare_kernel, direct), [shaped((steps, rb, chann...  1.58 us
    pallas_call x1, Pallas kernels, on_device(): call(functools.partial(pack_kernel, direct), [shaped(s, BF16) for s in ms...  1.11 us
    pallas_call x1, Pallas kernels, on_device(): call(functools.partial(windows_kernel, n_msgs, steps), shaped((taps - 1,...  0.78 us
    pallas_call x1, Pallas kernels, on_device(): call(functools.partial(start_kernel, n_msgs, direct, short), [shaped((n_s...  0.53 us
  transfers between devices with their start and end apart: 6, of which 2 were waited for; matrix products, arithmetic and copies ran while one was open for 0% of the time, Pallas kernels for 18%

profile of v16, /device:TPU:0, one launch (start us, length us, event | category | flops | bytes accessed | tf_op | source)
XLA Modules:
  0.0 19.5 jit_solution(9087552441826477145)
XLA Ops:
  0.6 1.1 %shard_map.148 = (bf16[1,8,1024]{2,1,0:T(8,128)(2,1)S(1)}, bf16[1,24,1024]{2,1,0:T(8,128)(2,1)S(1)}, bf16[1,8,1024]{2,1,0:T(8,128)(2,1)S(1)}, bf16[1,8,1024]{2,1,0:T(8,128)(2,1)S(1)}) custom-call(s32[1]{0:T(128)} %bitcast.owner_hbm, s32[4]{0:T(128)} %bitcast.12, s32[16]{0:T(128)} %prompt_hbm.3, bf16[16,4,2,1024]{3,2,1,0:T(2,128)(2,1)} %step_hbm.3, ...), custom_call_target="tpu_custom_call" | custom-call | bytes 196608 | tf_op jit(solution)/shard_map/pallas_call | solution.py:497
  1.8 4.1 %collective-permute-start = (bf16[1,24,1024]{2,1,0:T(8,128)(2,1)S(1)}, bf16[1,24,1024]{2,1,0:T(8,128)(2,1)S(1)}, u32[]{:S(2)}, u32[]{:S(2)}) collective-permute-start(bf16[1,24,1024]{2,1,0:T(8,128)(2,1)S(1)} %get-tuple-element.35), channel_id=1, source_target_pairs={{0,8},{4,12},{8,4},{12,0},{1,9},{5,13},{9,5},{13,1},{2,10},{6,14},... | collective-permute-start | bytes 147464 | tf_op jit(solution)/shard_map/ppermute | solution.py:523
  5.8 1.1 %collective-permute-start.1 = (bf16[1,8,1024]{2,1,0:T(8,128)(2,1)S(1)}, bf16[1,8,1024]{2,1,0:T(8,128)(2,1)S(1)}, u32[]{:S(2)}, u32[]{:S(2)}) collective-permute-start(bf16[1,8,1024]{2,1,0:T(8,128)(2,1)S(1)} %get-tuple-element.36), channel_id=1, source_target_pairs={{0,12},{4,8},{8,0},{12,4},{1,13},{5,9},{9,1},{13,5},{2,14},{6,10},... | collective-permute-start | bytes 49160 | tf_op jit(solution)/shard_map/ppermute | solution.py:523
  6.9 0.5 %collective-permute-start.2 = (bf16[1,8,1024]{2,1,0:T(8,128)(2,1)S(1)}, bf16[1,8,1024]{2,1,0:T(8,128)(2,1)S(1)}, u32[]{:S(2)}, u32[]{:S(2)}) collective-permute-start(bf16[1,8,1024]{2,1,0:T(8,128)(2,1)S(1)} %get-tuple-element.37), channel_id=1, source_target_pairs={{0,4},{4,0},{8,12},{12,8},{1,5},{5,1},{9,13},{13,9},{2,6},{6,2},{1... | collective-permute-start | bytes 49160 | tf_op jit(solution)/shard_map/ppermute | solution.py:523
  7.4 0.0 copy-start
  7.4 1.6 %shard_map.149 = (f32[4,16,1024]{2,1,0:T(8,128)S(1)}, f32[4,16,1024]{2,1,0:T(8,128)S(1)}, f32[16,4]{1,0:T(8,128)S(1)}, f32[16,4]{1,0:T(8,128)S(1)}, f32[1,4]{1,0...) custom-call(s32[1]{0:T(128)} %bitcast.owner_hbm, ...), custom_call_target="tpu_custom_call" | custom-call | flops 655360 | bytes 786432 | tf_op jit(solution)/shard_map/pallas_call | solution.py:530
  9.0 0.0 collective-permute-done.rest_1_.came_ref
  9.0 0.0 copy-done
  9.0 1.6 %collective-permute-start.4 = (bf16[1,48,1024]{2,1,0:T(8,128)(2,1)S(1)}, bf16[1,48,1024]{2,1,0:T(8,128)(2,1)S(1)}, u32[]{:S(2)}, u32[]{:S(2)}) collective-permute-start(bf16[1,48,1024]{2,1,0:T(8,128)(2,1)S(1)} %shard_map.152), channel_id=1, source_target_pairs={{0,4},{4,0},{8,12},{12,8},{1,5},{5,1},{9,13},{13,9},{2,6},{6,2},{1... | collective-permute-start | bytes 294920 | tf_op jit(solution)/shard_map/ppermute | solution.py:57
  10.6 0.0 collective-permute-done.1.rest_2_
  10.6 0.0 collective-permute-done.2.rest_3_
  10.7 0.5 %shard_map.150 = (f32[80,1024]{1,0:T(8,128)S(1)}, f32[80,288]{1,0:T(8,128)S(1)}, bf16[80,288]{1,0:T(8,128)(2,1)S(1)}) custom-call(f32[16,4]{1,0:T(8,128)S(1)} %get-tuple-element.29.pick_ref.after_ref, f32[1,4]{1,0:T(1,128)S(1)} %get-tuple-element.30.sender_ref, f32[4,16,1024]{2,1,0:T(8,128)S(1)} %get-tuple-element.31.base_ref, ...), custom_call_target="tpu_custom_call" | custom-call | flops 47185920 | bytes 1009664 | tf_op jit(solution)/shard_map/pallas_call | solution.py:584
  11.2 0.0 copy-start.1
  11.2 0.1 collective-permute-start.3
  11.3 1.2 %collective-permute-done.3.b_ref = bf16[80,288]{1,0:T(8,128)(2,1)S(1)} collective-permute-done((bf16[80,288]{1,0:T(8,128)(2,1)S(1)}, bf16[80,288]{1,0:T(8,128)(2,1)S(1)}, u32[]{:S(2)}, u32[]{:S(2)}) %collective-permute-start.3) | collective-permute-done | bytes 46112 | tf_op jit(solution)/shard_map/ppermute | solution.py:57
  12.5 1.5 %collective-permute-start.5 = (bf16[80,288]{1,0:T(8,128)(2,1)S(1)}, bf16[80,288]{1,0:T(8,128)(2,1)S(1)}, u32[]{:S(2)}, u32[]{:S(2)}) collective-permute-start(bf16[80,288]{1,0:T(8,128)(2,1)S(1)} %get-tuple-element.49), channel_id=1, source_target_pairs={{0,3},{1,2},{2,1},{3,0},{4,7},{5,6},{6,5},{7,4},{8,11},{9,10},{10,... | collective-permute-start | bytes 138248 | tf_op jit(solution)/shard_map/ppermute | solution.py:57
  14.0 0.8 %shard_map.155 = bf16[3,16,1024]{2,1,0:T(8,128)(2,1)} custom-call(f32[16,4]{1,0:T(8,128)S(1)} %get-tuple-element.52.child_ref, f32[80,288]{1,0:T(8,128)S(1)} %get-tuple-element.42.after_ref.part_ref, bf16[1,8,1024]{2,1,0:T(8,128)(2,1)S(1)} %get-tuple-element.28.after_ref.rest_0_, bf16[1,24,1024]{2,1,0:T(8,128)(2,1)S(1)} %collective-permute-done.rest_1_.came_ref, ...), custom_call_target="tpu_custom_call" | custom-call | flops 524288 | bytes 262144 | tf_op jit(solution)/shard_map/pallas_call | solution.py:611
  14.8 0.0 collective-permute-done.4.rest_5_
  14.8 0.5 %shard_map.153 = (f32[16,16,1024]{2,1,0:T(8,128)S(1)}, f32[8,8,1024]{2,1,0:T(8,128)S(1)}) custom-call(f32[16,4]{1,0:T(8,128)S(1)} %get-tuple-element.29.pick_ref.after_ref, f32[1,4]{1,0:T(1,128)S(1)} %get-tuple-element.30.sender_ref, f32[80,288]{1,0:T(8,128)S(1)} %get-tuple-element.42.after_ref.part_ref, ...), custom_call_target="tpu_custom_call" | custom-call | flops 2621440 | bytes 1310720 | tf_op jit(solution)/shard_map/pallas_call | solution.py:619
  15.3 1.2 %collective-permute-done.5.other_ref = bf16[80,288]{1,0:T(8,128)(2,1)S(1)} collective-permute-done((bf16[80,288]{1,0:T(8,128)(2,1)S(1)}, bf16[80,288]{1,0:T(8,128)(2,1)S(1)}, u32[]{:S(2)}, u32[]{:S(2)}) %collective-permute-start.5) | collective-permute-done | bytes 46112 | tf_op jit(solution)/shard_map/ppermute | solution.py:57
  16.5 0.0 copy-done.1
  16.5 3.0 %shard_map.154 = (bf16[16,4,1024]{2,1,0:T(4,128)(2,1)}, f32[16,16,1024]{2,1,0:T(8,128)}) custom-call(s32[1]{0:T(128)} %bitcast.owner_hbm, s32[16]{0:T(128)} %child_hbm.3, f32[80,1024]{1,0:T(8,128)S(1)} %get-tuple-element.38.act_ref, f32[4,16,1024]{2,1,0:T(8,128)S(1)} %get-tuple-element.39.gate_ref, f32[16,16,1024]{2,1,0:T(8,128)S(1)} %get-tuple-element.43.own_ref, ...), custom_call_target="tpu_custom_call" | custom-call | flops 10485760 | bytes 1310720 | tf_op jit(solution)/shard_map/pallas_call | solution.py:632
  (2 shorter events, 0.0 us)
Async XLA Ops:
  1.8 7.3 %collective-permute-start = (bf16[1,24,1024]{2,1,0:T(8,128)(2,1)S(1)}, bf16[1,24,1024]{2,1,0:T(8,128)(2,1)S(1)}, u32[]{:S(2)}, u32[]{:S(2)}) collective-permute-start(bf16[1,24,1024]{2,1,0:T(8,128)(2,1)S(1)} %get-tuple-element.35), channel_id=1, source_target_pairs={{0,8},{4,12},{8,4},{12,0},{1,9},{5,13},{9,5},{13,1},{2,10},{6,14},... | collective-permute-start | bytes 147464 | tf_op jit(solution)/shard_map/ppermute | solution.py:523
  5.8 4.8 %collective-permute-start.1 = (bf16[1,8,1024]{2,1,0:T(8,128)(2,1)S(1)}, bf16[1,8,1024]{2,1,0:T(8,128)(2,1)S(1)}, u32[]{:S(2)}, u32[]{:S(2)}) collective-permute-start(bf16[1,8,1024]{2,1,0:T(8,128)(2,1)S(1)} %get-tuple-element.36), channel_id=1, source_target_pairs={{0,12},{4,8},{8,0},{12,4},{1,13},{5,9},{9,1},{13,5},{2,14},{6,10},... | collective-permute-start | bytes 49160 | tf_op jit(solution)/shard_map/ppermute | solution.py:523
  6.9 3.7 %collective-permute-start.2 = (bf16[1,8,1024]{2,1,0:T(8,128)(2,1)S(1)}, bf16[1,8,1024]{2,1,0:T(8,128)(2,1)S(1)}, u32[]{:S(2)}, u32[]{:S(2)}) collective-permute-start(bf16[1,8,1024]{2,1,0:T(8,128)(2,1)S(1)} %get-tuple-element.37), channel_id=1, source_target_pairs={{0,4},{4,0},{8,12},{12,8},{1,5},{5,1},{9,13},{13,9},{2,6},{6,2},{1... | collective-permute-start | bytes 49160 | tf_op jit(solution)/shard_map/ppermute | solution.py:523
  7.4 1.6 %copy-start = (f32[1,16,1024]{2,1,0:T(8,128)S(1)}, f32[1,16,1024]{2,1,0:T(8,128)}, u32[]{:S(2)}) copy-start(f32[1,16,1024]{2,1,0:T(8,128)} %rest_4_.1) | copy-start | bytes 196612
  9.0 5.7 %collective-permute-start.4 = (bf16[1,48,1024]{2,1,0:T(8,128)(2,1)S(1)}, bf16[1,48,1024]{2,1,0:T(8,128)(2,1)S(1)}, u32[]{:S(2)}, u32[]{:S(2)}) collective-permute-start(bf16[1,48,1024]{2,1,0:T(8,128)(2,1)S(1)} %shard_map.152), channel_id=1, source_target_pairs={{0,4},{4,0},{8,12},{12,8},{1,5},{5,1},{9,13},{13,9},{2,6},{6,2},{1... | collective-permute-start | bytes 294920 | tf_op jit(solution)/shard_map/ppermute | solution.py:57
  11.2 5.4 %copy-start.1 = (bf16[256,1024]{1,0:T(8,128)(2,1)S(1)}, bf16[256,1024]{1,0:T(8,128)(2,1)}, u32[]{:S(2)}) copy-start(bf16[256,1024]{1,0:T(8,128)(2,1)} %dtw_ref.1) | copy-start | bytes 1572868
  11.2 1.3 %collective-permute-start.3 = (bf16[80,288]{1,0:T(8,128)(2,1)S(1)}, bf16[80,288]{1,0:T(8,128)(2,1)S(1)}, u32[]{:S(2)}, u32[]{:S(2)}) collective-permute-start(bf16[80,288]{1,0:T(8,128)(2,1)S(1)} %get-tuple-element.41), channel_id=1, source_target_pairs={{0,1},{1,0},{2,3},{3,2},{4,5},{5,4},{6,7},{7,6},{8,9},{9,8},{10,11... | collective-permute-start | bytes 138248 | tf_op jit(solution)/shard_map/ppermute | solution.py:57
  12.5 4.0 %collective-permute-start.5 = (bf16[80,288]{1,0:T(8,128)(2,1)S(1)}, bf16[80,288]{1,0:T(8,128)(2,1)S(1)}, u32[]{:S(2)}, u32[]{:S(2)}) collective-permute-start(bf16[80,288]{1,0:T(8,128)(2,1)S(1)} %get-tuple-element.49), channel_id=1, source_target_pairs={{0,3},{1,2},{2,1},{3,0},{4,7},{5,6},{6,5},{7,4},{8,11},{9,10},{10,... | collective-permute-start | bytes 138248 | tf_op jit(solution)/shard_map/ppermute | solution.py:57

commit v17 on v15

--- a/solution.py
+++ b/solution.py
@@ -64,14 +64,18 @@
     return total
 
 
-def block_of(sender, owner, direct):
-    if not direct:
-        return sender
+def blocks_of(owner):
     table = [
         [0 if s == r else 1 + [to[s] for to in SENDS].index(r) for s in range(DIRECT)]
         for r in range(DIRECT)
     ]
-    places = [chosen(owner, [row[s] for row in table]) for s in range(DIRECT)]
+    return [chosen(owner, [row[s] for row in table]) for s in range(DIRECT)]
+
+
+def block_of(sender, owner, direct):
+    if not direct:
+        return sender
+    places = blocks_of(owner)
     return places[sender] if isinstance(sender, int) else chosen(sender, places)
 
 
@@ -115,14 +119,14 @@
     outs, (owner_s, rows_s, prompt_s, step, conv, ssm, sems) = rest[:-7], rest[-7:]
     owners = rows_hbm.shape[0]
     channels = step_hbm.shape[3]
-    copies = [
+    copies = in_parts(step_hbm, step, sems, 5, STEP_PARTS) + [
         pltpu.make_async_copy(owner_hbm, owner_s, sems.at[4]),
         pltpu.make_async_copy(rows_hbm, rows_s, sems.at[0]),
         pltpu.make_async_copy(prompt_hbm, prompt_s, sems.at[1]),
         pltpu.make_async_copy(conv_hbm, conv, sems.at[2]),
         pltpu.make_async_copy(ssm_hbm, ssm, sems.at[3]),
     ]
-    all_of(copies + in_parts(step_hbm, step, sems, 5, STEP_PARTS))
+    all_of(copies)
     owner = owner_s[0]
     window = conv[0].astype(F32)
 
@@ -419,15 +423,17 @@
     lax.fori_loop(0, chunks, slot_chunk, 0)
     for copy in scalars:
         copy.wait()
-    copies = []
-    for j in range(rb):
-        at = block_of(child_s[j], owner_s[0], direct)
-        copy = pltpu.make_async_copy(slots_s.at[at], child_ssm.at[j], sems.at[2 + j])
-        copy.start()
-        copies.append(copy)
+    places = blocks_of(owner_s[0]) if direct else None
+    batch = rb // chunks
+
+    def child_copy(j):
+        at = chosen(child_s[j], places) if direct else child_s[j]
+        return pltpu.make_async_copy(slots_s.at[at], child_ssm.at[j], sems.at[2 + j])
 
     def own_chunk(chunk, carry):
         columns = pl.ds(pl.multiple_of(chunk * WIDE * LANES, WIDE * LANES), WIDE * LANES)
+        for i in range(batch):
+            child_copy(chunk * batch + i).start()
         for first in range(0, rb, ROWS):
             at = [pl.ds(t * rb + first, ROWS) for t in range(steps)]
             delta = [delta_s[a, columns] for a in at]
@@ -451,8 +457,8 @@
         return carry
 
     lax.fori_loop(0, chunks, own_chunk, 0)
-    for copy in copies:
-        copy.wait()
+    for j in range(rb):
+        child_copy(j).wait()
 
 
 def on_device(

time: 19.6 us -> 20 us (1.020)
  Pallas kernels: 7.42 us -> 7.81 us
    pallas_call x1, Pallas kernels: 2.89 us -> 3.27 us  [on_device(): call(functools.partial(decode_kernel, direct), [shaped((rb, steps, channe...]
  transfers between devices with their start and end apart: 6 -> 6, of which waited for: 2 -> 2; matrix products, arithmetic and copies ran while one was open for 0% -> 0% of each run, Pallas kernels for 18% -> 17%
where the time goes in v17:
time: 20 us; the launch traced here: 19.8 us
  starting transfers between devices  8.81 us (44%)
  Pallas kernels  7.81 us (39%)
  waiting for transfers between devices  2.49 us (12%)
  between operations  0.71 us (4%)
    ppermute x3, starting transfers between devices, on_device(): lax.ppermute(m, 'branch', list(enumerate(to)))  5.67 us
    pallas_call x1, Pallas kernels, on_device(): call(functools.partial(decode_kernel, direct), [shaped((rb, steps, channe...  3.27 us
    ppermute x3, starting transfers between devices, swap(): return lax.ppermute(value, axis, [(i, i ^ distance) for i in range(size)])  3.14 us
    ppermute x3, waiting for transfers between devices, swap(): return lax.ppermute(value, axis, [(i, i ^ distance) for i in range(size)])  2.47 us
    pallas_call x1, Pallas kernels, on_device(): call(functools.partial(prepare_kernel, direct), [shaped((steps, rb, chann...  1.58 us
    pallas_call x1, Pallas kernels, on_device(): call(functools.partial(pack_kernel, direct), [shaped(s, BF16) for s in ms...  1.11 us
    pallas_call x1, Pallas kernels, on_device(): call(functools.partial(windows_kernel, n_msgs, steps), shaped((taps - 1,...  0.78 us
    pallas_call x1, Pallas kernels, on_device(): call(functools.partial(start_kernel, n_msgs, direct, short), [shaped((n_s...  0.53 us
  transfers between devices with their start and end apart: 6, of which 2 were waited for; matrix products, arithmetic and copies ran while one was open for 0% of the time, Pallas kernels for 17%

profile of v17, /device:TPU:0, one launch (start us, length us, event | category | flops | bytes accessed | tf_op | source)
XLA Modules:
  0.0 19.8 jit_solution(15398397357485684639)
XLA Ops:
  0.6 1.1 %shard_map.148 = (bf16[1,8,1024]{2,1,0:T(8,128)(2,1)S(1)}, bf16[1,24,1024]{2,1,0:T(8,128)(2,1)S(1)}, bf16[1,8,1024]{2,1,0:T(8,128)(2,1)S(1)}, bf16[1,8,1024]{2,1,0:T(8,128)(2,1)S(1)}) custom-call(s32[1]{0:T(128)} %bitcast.owner_hbm, s32[4]{0:T(128)} %bitcast.12, s32[16]{0:T(128)} %prompt_hbm.3, bf16[16,4,2,1024]{3,2,1,0:T(2,128)(2,1)} %step_hbm.3, ...), custom_call_target="tpu_custom_call" | custom-call | bytes 196608 | tf_op jit(solution)/shard_map/pallas_call | solution.py:497
  1.8 4.1 %collective-permute-start = (bf16[1,24,1024]{2,1,0:T(8,128)(2,1)S(1)}, bf16[1,24,1024]{2,1,0:T(8,128)(2,1)S(1)}, u32[]{:S(2)}, u32[]{:S(2)}) collective-permute-start(bf16[1,24,1024]{2,1,0:T(8,128)(2,1)S(1)} %get-tuple-element.35), channel_id=1, source_target_pairs={{0,8},{4,12},{8,4},{12,0},{1,9},{5,13},{9,5},{13,1},{2,10},{6,14},... | collective-permute-start | bytes 147464 | tf_op jit(solution)/shard_map/ppermute | solution.py:523
  5.8 1.1 %collective-permute-start.1 = (bf16[1,8,1024]{2,1,0:T(8,128)(2,1)S(1)}, bf16[1,8,1024]{2,1,0:T(8,128)(2,1)S(1)}, u32[]{:S(2)}, u32[]{:S(2)}) collective-permute-start(bf16[1,8,1024]{2,1,0:T(8,128)(2,1)S(1)} %get-tuple-element.36), channel_id=1, source_target_pairs={{0,12},{4,8},{8,0},{12,4},{1,13},{5,9},{9,1},{13,5},{2,14},{6,10},... | collective-permute-start | bytes 49160 | tf_op jit(solution)/shard_map/ppermute | solution.py:523
  6.9 0.5 %collective-permute-start.2 = (bf16[1,8,1024]{2,1,0:T(8,128)(2,1)S(1)}, bf16[1,8,1024]{2,1,0:T(8,128)(2,1)S(1)}, u32[]{:S(2)}, u32[]{:S(2)}) collective-permute-start(bf16[1,8,1024]{2,1,0:T(8,128)(2,1)S(1)} %get-tuple-element.37), channel_id=1, source_target_pairs={{0,4},{4,0},{8,12},{12,8},{1,5},{5,1},{9,13},{13,9},{2,6},{6,2},{1... | collective-permute-start | bytes 49160 | tf_op jit(solution)/shard_map/ppermute | solution.py:523
  7.4 0.0 copy-start
  7.4 1.6 %shard_map.149 = (f32[4,16,1024]{2,1,0:T(8,128)S(1)}, f32[4,16,1024]{2,1,0:T(8,128)S(1)}, f32[16,4]{1,0:T(8,128)S(1)}, f32[16,4]{1,0:T(8,128)S(1)}, f32[1,4]{1,0...) custom-call(s32[1]{0:T(128)} %bitcast.owner_hbm, ...), custom_call_target="tpu_custom_call" | custom-call | flops 655360 | bytes 786432 | tf_op jit(solution)/shard_map/pallas_call | solution.py:530
  9.0 0.0 collective-permute-done.rest_1_.came_ref
  9.0 0.0 copy-done
  9.0 1.6 %collective-permute-start.4 = (bf16[1,48,1024]{2,1,0:T(8,128)(2,1)S(1)}, bf16[1,48,1024]{2,1,0:T(8,128)(2,1)S(1)}, u32[]{:S(2)}, u32[]{:S(2)}) collective-permute-start(bf16[1,48,1024]{2,1,0:T(8,128)(2,1)S(1)} %shard_map.152), channel_id=1, source_target_pairs={{0,4},{4,0},{8,12},{12,8},{1,5},{5,1},{9,13},{13,9},{2,6},{6,2},{1... | collective-permute-start | bytes 294920 | tf_op jit(solution)/shard_map/ppermute | solution.py:57
  10.6 0.0 collective-permute-done.1.rest_2_
  10.6 0.0 collective-permute-done.2.rest_3_
  10.7 0.5 %shard_map.150 = (f32[80,1024]{1,0:T(8,128)S(1)}, f32[80,288]{1,0:T(8,128)S(1)}, bf16[80,288]{1,0:T(8,128)(2,1)S(1)}) custom-call(f32[16,4]{1,0:T(8,128)S(1)} %get-tuple-element.29.pick_ref.after_ref, f32[1,4]{1,0:T(1,128)S(1)} %get-tuple-element.30.sender_ref, f32[4,16,1024]{2,1,0:T(8,128)S(1)} %get-tuple-element.31.base_ref, ...), custom_call_target="tpu_custom_call" | custom-call | flops 47185920 | bytes 1009664 | tf_op jit(solution)/shard_map/pallas_call | solution.py:584
  11.2 0.0 copy-start.1
  11.2 0.1 collective-permute-start.3
  11.3 1.2 %collective-permute-done.3.b_ref = bf16[80,288]{1,0:T(8,128)(2,1)S(1)} collective-permute-done((bf16[80,288]{1,0:T(8,128)(2,1)S(1)}, bf16[80,288]{1,0:T(8,128)(2,1)S(1)}, u32[]{:S(2)}, u32[]{:S(2)}) %collective-permute-start.3) | collective-permute-done | bytes 46112 | tf_op jit(solution)/shard_map/ppermute | solution.py:57
  12.5 1.5 %collective-permute-start.5 = (bf16[80,288]{1,0:T(8,128)(2,1)S(1)}, bf16[80,288]{1,0:T(8,128)(2,1)S(1)}, u32[]{:S(2)}, u32[]{:S(2)}) collective-permute-start(bf16[80,288]{1,0:T(8,128)(2,1)S(1)} %get-tuple-element.49), channel_id=1, source_target_pairs={{0,3},{1,2},{2,1},{3,0},{4,7},{5,6},{6,5},{7,4},{8,11},{9,10},{10,... | collective-permute-start | bytes 138248 | tf_op jit(solution)/shard_map/ppermute | solution.py:57
  14.0 0.8 %shard_map.155 = bf16[3,16,1024]{2,1,0:T(8,128)(2,1)} custom-call(f32[16,4]{1,0:T(8,128)S(1)} %get-tuple-element.52.child_ref, f32[80,288]{1,0:T(8,128)S(1)} %get-tuple-element.42.after_ref.part_ref, bf16[1,8,1024]{2,1,0:T(8,128)(2,1)S(1)} %get-tuple-element.28.after_ref.rest_0_, bf16[1,24,1024]{2,1,0:T(8,128)(2,1)S(1)} %collective-permute-done.rest_1_.came_ref, ...), custom_call_target="tpu_custom_call" | custom-call | flops 524288 | bytes 262144 | tf_op jit(solution)/shard_map/pallas_call | solution.py:611
  14.8 0.0 collective-permute-done.4.rest_5_
  14.8 0.5 %shard_map.153 = (f32[16,16,1024]{2,1,0:T(8,128)S(1)}, f32[8,8,1024]{2,1,0:T(8,128)S(1)}) custom-call(f32[16,4]{1,0:T(8,128)S(1)} %get-tuple-element.29.pick_ref.after_ref, f32[1,4]{1,0:T(1,128)S(1)} %get-tuple-element.30.sender_ref, f32[80,288]{1,0:T(8,128)S(1)} %get-tuple-element.42.after_ref.part_ref, ...), custom_call_target="tpu_custom_call" | custom-call | flops 2621440 | bytes 1310720 | tf_op jit(solution)/shard_map/pallas_call | solution.py:619
  15.3 1.2 %collective-permute-done.5.other_ref = bf16[80,288]{1,0:T(8,128)(2,1)S(1)} collective-permute-done((bf16[80,288]{1,0:T(8,128)(2,1)S(1)}, bf16[80,288]{1,0:T(8,128)(2,1)S(1)}, u32[]{:S(2)}, u32[]{:S(2)}) %collective-permute-start.5) | collective-permute-done | bytes 46112 | tf_op jit(solution)/shard_map/ppermute | solution.py:57
  16.5 0.0 copy-done.1
  16.5 3.3 %shard_map.154 = (bf16[16,4,1024]{2,1,0:T(4,128)(2,1)}, f32[16,16,1024]{2,1,0:T(8,128)}) custom-call(s32[1]{0:T(128)} %bitcast.owner_hbm, s32[16]{0:T(128)} %child_hbm.3, f32[80,1024]{1,0:T(8,128)S(1)} %get-tuple-element.38.act_ref, f32[4,16,1024]{2,1,0:T(8,128)S(1)} %get-tuple-element.39.gate_ref, f32[16,16,1024]{2,1,0:T(8,128)S(1)} %get-tuple-element.43.own_ref, ...), custom_call_target="tpu_custom_call" | custom-call | flops 10485760 | bytes 1310720 | tf_op jit(solution)/shard_map/pallas_call | solution.py:632
  (2 shorter events, 0.0 us)
Async XLA Ops:
  1.8 7.3 %collective-permute-start = (bf16[1,24,1024]{2,1,0:T(8,128)(2,1)S(1)}, bf16[1,24,1024]{2,1,0:T(8,128)(2,1)S(1)}, u32[]{:S(2)}, u32[]{:S(2)}) collective-permute-start(bf16[1,24,1024]{2,1,0:T(8,128)(2,1)S(1)} %get-tuple-element.35), channel_id=1, source_target_pairs={{0,8},{4,12},{8,4},{12,0},{1,9},{5,13},{9,5},{13,1},{2,10},{6,14},... | collective-permute-start | bytes 147464 | tf_op jit(solution)/shard_map/ppermute | solution.py:523
  5.8 4.8 %collective-permute-start.1 = (bf16[1,8,1024]{2,1,0:T(8,128)(2,1)S(1)}, bf16[1,8,1024]{2,1,0:T(8,128)(2,1)S(1)}, u32[]{:S(2)}, u32[]{:S(2)}) collective-permute-start(bf16[1,8,1024]{2,1,0:T(8,128)(2,1)S(1)} %get-tuple-element.36), channel_id=1, source_target_pairs={{0,12},{4,8},{8,0},{12,4},{1,13},{5,9},{9,1},{13,5},{2,14},{6,10},... | collective-permute-start | bytes 49160 | tf_op jit(solution)/shard_map/ppermute | solution.py:523
  6.9 3.7 %collective-permute-start.2 = (bf16[1,8,1024]{2,1,0:T(8,128)(2,1)S(1)}, bf16[1,8,1024]{2,1,0:T(8,128)(2,1)S(1)}, u32[]{:S(2)}, u32[]{:S(2)}) collective-permute-start(bf16[1,8,1024]{2,1,0:T(8,128)(2,1)S(1)} %get-tuple-element.37), channel_id=1, source_target_pairs={{0,4},{4,0},{8,12},{12,8},{1,5},{5,1},{9,13},{13,9},{2,6},{6,2},{1... | collective-permute-start | bytes 49160 | tf_op jit(solution)/shard_map/ppermute | solution.py:523
  7.4 1.6 %copy-start = (f32[1,16,1024]{2,1,0:T(8,128)S(1)}, f32[1,16,1024]{2,1,0:T(8,128)}, u32[]{:S(2)}) copy-start(f32[1,16,1024]{2,1,0:T(8,128)} %rest_4_.1) | copy-start | bytes 196612
  9.0 5.7 %collective-permute-start.4 = (bf16[1,48,1024]{2,1,0:T(8,128)(2,1)S(1)}, bf16[1,48,1024]{2,1,0:T(8,128)(2,1)S(1)}, u32[]{:S(2)}, u32[]{:S(2)}) collective-permute-start(bf16[1,48,1024]{2,1,0:T(8,128)(2,1)S(1)} %shard_map.152), channel_id=1, source_target_pairs={{0,4},{4,0},{8,12},{12,8},{1,5},{5,1},{9,13},{13,9},{2,6},{6,2},{1... | collective-permute-start | bytes 294920 | tf_op jit(solution)/shard_map/ppermute | solution.py:57
  11.2 5.4 %copy-start.1 = (bf16[256,1024]{1,0:T(8,128)(2,1)S(1)}, bf16[256,1024]{1,0:T(8,128)(2,1)}, u32[]{:S(2)}) copy-start(bf16[256,1024]{1,0:T(8,128)(2,1)} %dtw_ref.1) | copy-start | bytes 1572868
  11.2 1.3 %collective-permute-start.3 = (bf16[80,288]{1,0:T(8,128)(2,1)S(1)}, bf16[80,288]{1,0:T(8,128)(2,1)S(1)}, u32[]{:S(2)}, u32[]{:S(2)}) collective-permute-start(bf16[80,288]{1,0:T(8,128)(2,1)S(1)} %get-tuple-element.41), channel_id=1, source_target_pairs={{0,1},{1,0},{2,3},{3,2},{4,5},{5,4},{6,7},{7,6},{8,9},{9,8},{10,11... | collective-permute-start | bytes 138248 | tf_op jit(solution)/shard_map/ppermute | solution.py:57
  12.5 4.0 %collective-permute-start.5 = (bf16[80,288]{1,0:T(8,128)(2,1)S(1)}, bf16[80,288]{1,0:T(8,128)(2,1)S(1)}, u32[]{:S(2)}, u32[]{:S(2)}) collective-permute-start(bf16[80,288]{1,0:T(8,128)(2,1)S(1)} %get-tuple-element.49), channel_id=1, source_target_pairs={{0,3},{1,2},{2,1},{3,0},{4,7},{5,6},{6,5},{7,4},{8,11},{9,10},{10,... | collective-permute-start | bytes 138248 | tf_op jit(solution)/shard_map/ppermute | solution.py:57

commit v18 on v15

--- a/solution.py
+++ b/solution.py
@@ -64,14 +64,18 @@
     return total
 
 
-def block_of(sender, owner, direct):
-    if not direct:
-        return sender
+def blocks_of(owner):
     table = [
         [0 if s == r else 1 + [to[s] for to in SENDS].index(r) for s in range(DIRECT)]
         for r in range(DIRECT)
     ]
-    places = [chosen(owner, [row[s] for row in table]) for s in range(DIRECT)]
+    return [chosen(owner, [row[s] for row in table]) for s in range(DIRECT)]
+
+
+def block_of(sender, owner, direct):
+    if not direct:
+        return sender
+    places = blocks_of(owner)
     return places[sender] if isinstance(sender, int) else chosen(sender, places)
 
 
@@ -375,19 +379,19 @@
     own_rows = steps * rb
     chunks = channels // (WIDE * LANES)
 
-    proj = part_ref[...] + other_ref[...].astype(F32)
-    delta_in = proj[:, :rank].astype(BF16)
-    delta = jnp.dot(delta_in, dtw_ref[...], preferred_element_type=F32) + dtb_ref[...]
-    delta = jnp.maximum(delta, 0.0) + jnp.log(1.0 + jnp.exp(-jnp.abs(delta)))
-    gain = delta * act_ref[...]
-    delta_s[...] = delta[:own_rows, :]
-    gain_s[...] = gain[:own_rows, :]
+    def sums_of(rows):
+        proj = part_ref[rows, :] + other_ref[rows, :].astype(F32)
+        delta_in = proj[:, :rank].astype(BF16)
+        delta = jnp.dot(delta_in, dtw_ref[...], preferred_element_type=F32) + dtb_ref[...]
+        delta = jnp.maximum(delta, 0.0) + jnp.log(1.0 + jnp.exp(-jnp.abs(delta)))
+        return proj, delta, delta * act_ref[rows, :]
 
     def column(at, n, rows):
         return jnp.broadcast_to(at[:, n : n + 1], (rows, LANES))
 
+    proj, delta, gain = sums_of(slice(own_rows, own_rows + steps * n_slots))
     for t in range(steps):
-        at = slice(own_rows + t * n_slots, own_rows + (t + 1) * n_slots)
+        at = slice(t * n_slots, (t + 1) * n_slots)
         slot_delta_s[t] = jnp.concatenate([delta[at, :]] * 2, axis=0)
         slot_gain_s[t] = jnp.concatenate([gain[at, :]] * 2, axis=0)
         twice = jnp.concatenate([proj[at, rank:]] * 2, axis=0)
@@ -396,9 +400,6 @@
             twin_b_s[m, t] = jnp.where(
                 upper, column(twice, 2 * m, 2 * n_slots), column(twice, 2 * m + 1, 2 * n_slots)
             )
-    for n in range(n_state):
-        b_s[n] = column(proj[:own_rows, rank:], n, own_rows)
-        c_s[n] = column(proj[:own_rows, rank:], n_state + n, own_rows)
 
     def wide(part):
         return jnp.concatenate([part] * WIDE, axis=1)
@@ -419,12 +420,20 @@
     lax.fori_loop(0, chunks, slot_chunk, 0)
     for copy in scalars:
         copy.wait()
+    places = blocks_of(owner_s[0]) if direct else None
     copies = []
     for j in range(rb):
-        at = block_of(child_s[j], owner_s[0], direct)
+        at = chosen(child_s[j], places) if direct else child_s[j]
         copy = pltpu.make_async_copy(slots_s.at[at], child_ssm.at[j], sems.at[2 + j])
         copy.start()
         copies.append(copy)
+
+    proj, delta, gain = sums_of(slice(0, own_rows))
+    delta_s[...] = delta
+    gain_s[...] = gain
+    for n in range(n_state):
+        b_s[n] = column(proj[:, rank:], n, own_rows)
+        c_s[n] = column(proj[:, rank:], n_state + n, own_rows)
 
     def own_chunk(chunk, carry):
         columns = pl.ds(pl.multiple_of(chunk * WIDE * LANES, WIDE * LANES), WIDE * LANES)

time: 19.6 us -> 19.8 us (1.010)
  transfers between devices with their start and end apart: 6 -> 6, of which waited for: 2 -> 2; matrix products, arithmetic and copies ran while one was open for 0% -> 0% of each run, Pallas kernels for 18% -> 17%
where the time goes in v18:
time: 19.8 us; the launch traced here: 19.6 us
  starting transfers between devices  8.81 us (44%)
  Pallas kernels  7.61 us (38%)
  waiting for transfers between devices  2.49 us (13%)
  between operations  0.71 us (4%)
    ppermute x3, starting transfers between devices, on_device(): lax.ppermute(m, 'branch', list(enumerate(to)))  5.67 us
    ppermute x3, starting transfers between devices, swap(): return lax.ppermute(value, axis, [(i, i ^ distance) for i in range(size)])  3.14 us
    pallas_call x1, Pallas kernels, on_device(): call(functools.partial(decode_kernel, direct), [shaped((rb, steps, channe...  3.08 us
    ppermute x3, waiting for transfers between devices, swap(): return lax.ppermute(value, axis, [(i, i ^ distance) for i in range(size)])  2.47 us
    pallas_call x1, Pallas kernels, on_device(): call(functools.partial(prepare_kernel, direct), [shaped((steps, rb, chann...  1.58 us
    pallas_call x1, Pallas kernels, on_device(): call(functools.partial(pack_kernel, direct), [shaped(s, BF16) for s in ms...  1.11 us
    pallas_call x1, Pallas kernels, on_device(): call(functools.partial(windows_kernel, n_msgs, steps), shaped((taps - 1,...  0.78 us
    pallas_call x1, Pallas kernels, on_device(): call(functools.partial(start_kernel, n_msgs, direct, short), [shaped((n_s...  0.53 us
  transfers between devices with their start and end apart: 6, of which 2 were waited for; matrix products, arithmetic and copies ran while one was open for 0% of the time, Pallas kernels for 17%

profile of v18, /device:TPU:0, one launch (start us, length us, event | category | flops | bytes accessed | tf_op | source)
XLA Modules:
  0.0 19.6 jit_solution(9797429204420546874)
XLA Ops:
  0.6 1.1 %shard_map.148 = (bf16[1,8,1024]{2,1,0:T(8,128)(2,1)S(1)}, bf16[1,24,1024]{2,1,0:T(8,128)(2,1)S(1)}, bf16[1,8,1024]{2,1,0:T(8,128)(2,1)S(1)}, bf16[1,8,1024]{2,1,0:T(8,128)(2,1)S(1)}) custom-call(s32[1]{0:T(128)} %bitcast.owner_hbm, s32[4]{0:T(128)} %bitcast.12, s32[16]{0:T(128)} %prompt_hbm.3, bf16[16,4,2,1024]{3,2,1,0:T(2,128)(2,1)} %step_hbm.3, ...), custom_call_target="tpu_custom_call" | custom-call | bytes 196608 | tf_op jit(solution)/shard_map/pallas_call | solution.py:500
  1.8 4.1 %collective-permute-start = (bf16[1,24,1024]{2,1,0:T(8,128)(2,1)S(1)}, bf16[1,24,1024]{2,1,0:T(8,128)(2,1)S(1)}, u32[]{:S(2)}, u32[]{:S(2)}) collective-permute-start(bf16[1,24,1024]{2,1,0:T(8,128)(2,1)S(1)} %get-tuple-element.35), channel_id=1, source_target_pairs={{0,8},{4,12},{8,4},{12,0},{1,9},{5,13},{9,5},{13,1},{2,10},{6,14},... | collective-permute-start | bytes 147464 | tf_op jit(solution)/shard_map/ppermute | solution.py:526
  5.8 1.1 %collective-permute-start.1 = (bf16[1,8,1024]{2,1,0:T(8,128)(2,1)S(1)}, bf16[1,8,1024]{2,1,0:T(8,128)(2,1)S(1)}, u32[]{:S(2)}, u32[]{:S(2)}) collective-permute-start(bf16[1,8,1024]{2,1,0:T(8,128)(2,1)S(1)} %get-tuple-element.36), channel_id=1, source_target_pairs={{0,12},{4,8},{8,0},{12,4},{1,13},{5,9},{9,1},{13,5},{2,14},{6,10},... | collective-permute-start | bytes 49160 | tf_op jit(solution)/shard_map/ppermute | solution.py:526
  6.9 0.5 %collective-permute-start.2 = (bf16[1,8,1024]{2,1,0:T(8,128)(2,1)S(1)}, bf16[1,8,1024]{2,1,0:T(8,128)(2,1)S(1)}, u32[]{:S(2)}, u32[]{:S(2)}) collective-permute-start(bf16[1,8,1024]{2,1,0:T(8,128)(2,1)S(1)} %get-tuple-element.37), channel_id=1, source_target_pairs={{0,4},{4,0},{8,12},{12,8},{1,5},{5,1},{9,13},{13,9},{2,6},{6,2},{1... | collective-permute-start | bytes 49160 | tf_op jit(solution)/shard_map/ppermute | solution.py:526
  7.4 0.0 copy-start
  7.4 1.6 %shard_map.149 = (f32[4,16,1024]{2,1,0:T(8,128)S(1)}, f32[4,16,1024]{2,1,0:T(8,128)S(1)}, f32[16,4]{1,0:T(8,128)S(1)}, f32[16,4]{1,0:T(8,128)S(1)}, f32[1,4]{1,0...) custom-call(s32[1]{0:T(128)} %bitcast.owner_hbm, ...), custom_call_target="tpu_custom_call" | custom-call | flops 655360 | bytes 786432 | tf_op jit(solution)/shard_map/pallas_call | solution.py:533
  9.0 0.0 collective-permute-done.rest_1_.came_ref
  9.0 0.0 copy-done
  9.0 1.6 %collective-permute-start.4 = (bf16[1,48,1024]{2,1,0:T(8,128)(2,1)S(1)}, bf16[1,48,1024]{2,1,0:T(8,128)(2,1)S(1)}, u32[]{:S(2)}, u32[]{:S(2)}) collective-permute-start(bf16[1,48,1024]{2,1,0:T(8,128)(2,1)S(1)} %shard_map.152), channel_id=1, source_target_pairs={{0,4},{4,0},{8,12},{12,8},{1,5},{5,1},{9,13},{13,9},{2,6},{6,2},{1... | collective-permute-start | bytes 294920 | tf_op jit(solution)/shard_map/ppermute | solution.py:57
  10.6 0.0 collective-permute-done.1.rest_2_
  10.6 0.0 collective-permute-done.2.rest_3_
  10.7 0.5 %shard_map.150 = (f32[80,1024]{1,0:T(8,128)S(1)}, f32[80,288]{1,0:T(8,128)S(1)}, bf16[80,288]{1,0:T(8,128)(2,1)S(1)}) custom-call(f32[16,4]{1,0:T(8,128)S(1)} %get-tuple-element.29.pick_ref.after_ref, f32[1,4]{1,0:T(1,128)S(1)} %get-tuple-element.30.sender_ref, f32[4,16,1024]{2,1,0:T(8,128)S(1)} %get-tuple-element.31.base_ref, ...), custom_call_target="tpu_custom_call" | custom-call | flops 47185920 | bytes 1009664 | tf_op jit(solution)/shard_map/pallas_call | solution.py:587
  11.2 0.0 copy-start.1
  11.2 0.1 collective-permute-start.3
  11.3 1.2 %collective-permute-done.3.b_ref = bf16[80,288]{1,0:T(8,128)(2,1)S(1)} collective-permute-done((bf16[80,288]{1,0:T(8,128)(2,1)S(1)}, bf16[80,288]{1,0:T(8,128)(2,1)S(1)}, u32[]{:S(2)}, u32[]{:S(2)}) %collective-permute-start.3) | collective-permute-done | bytes 46112 | tf_op jit(solution)/shard_map/ppermute | solution.py:57
  12.5 1.5 %collective-permute-start.5 = (bf16[80,288]{1,0:T(8,128)(2,1)S(1)}, bf16[80,288]{1,0:T(8,128)(2,1)S(1)}, u32[]{:S(2)}, u32[]{:S(2)}) collective-permute-start(bf16[80,288]{1,0:T(8,128)(2,1)S(1)} %get-tuple-element.49), channel_id=1, source_target_pairs={{0,3},{1,2},{2,1},{3,0},{4,7},{5,6},{6,5},{7,4},{8,11},{9,10},{10,... | collective-permute-start | bytes 138248 | tf_op jit(solution)/shard_map/ppermute | solution.py:57
  14.0 0.8 %shard_map.155 = bf16[3,16,1024]{2,1,0:T(8,128)(2,1)} custom-call(f32[16,4]{1,0:T(8,128)S(1)} %get-tuple-element.52.child_ref, f32[80,288]{1,0:T(8,128)S(1)} %get-tuple-element.42.after_ref.part_ref, bf16[1,8,1024]{2,1,0:T(8,128)(2,1)S(1)} %get-tuple-element.28.after_ref.rest_0_, bf16[1,24,1024]{2,1,0:T(8,128)(2,1)S(1)} %collective-permute-done.rest_1_.came_ref, ...), custom_call_target="tpu_custom_call" | custom-call | flops 524288 | bytes 262144 | tf_op jit(solution)/shard_map/pallas_call | solution.py:614
  14.8 0.0 collective-permute-done.4.rest_5_
  14.8 0.5 %shard_map.153 = (f32[16,16,1024]{2,1,0:T(8,128)S(1)}, f32[8,8,1024]{2,1,0:T(8,128)S(1)}) custom-call(f32[16,4]{1,0:T(8,128)S(1)} %get-tuple-element.29.pick_ref.after_ref, f32[1,4]{1,0:T(1,128)S(1)} %get-tuple-element.30.sender_ref, f32[80,288]{1,0:T(8,128)S(1)} %get-tuple-element.42.after_ref.part_ref, ...), custom_call_target="tpu_custom_call" | custom-call | flops 2621440 | bytes 1310720 | tf_op jit(solution)/shard_map/pallas_call | solution.py:622
  15.3 1.2 %collective-permute-done.5.other_ref = bf16[80,288]{1,0:T(8,128)(2,1)S(1)} collective-permute-done((bf16[80,288]{1,0:T(8,128)(2,1)S(1)}, bf16[80,288]{1,0:T(8,128)(2,1)S(1)}, u32[]{:S(2)}, u32[]{:S(2)}) %collective-permute-start.5) | collective-permute-done | bytes 46112 | tf_op jit(solution)/shard_map/ppermute | solution.py:57
  16.5 0.0 copy-done.1
  16.5 3.1 %shard_map.154 = (bf16[16,4,1024]{2,1,0:T(4,128)(2,1)}, f32[16,16,1024]{2,1,0:T(8,128)}) custom-call(s32[1]{0:T(128)} %bitcast.owner_hbm, s32[16]{0:T(128)} %child_hbm.3, f32[80,1024]{1,0:T(8,128)S(1)} %get-tuple-element.38.act_ref, f32[4,16,1024]{2,1,0:T(8,128)S(1)} %get-tuple-element.39.gate_ref, f32[16,16,1024]{2,1,0:T(8,128)S(1)} %get-tuple-element.43.own_ref, ...), custom_call_target="tpu_custom_call" | custom-call | flops 10485760 | bytes 1310720 | tf_op jit(solution)/shard_map/pallas_call | solution.py:635
  (2 shorter events, 0.0 us)
Async XLA Ops:
  1.8 7.3 %collective-permute-start = (bf16[1,24,1024]{2,1,0:T(8,128)(2,1)S(1)}, bf16[1,24,1024]{2,1,0:T(8,128)(2,1)S(1)}, u32[]{:S(2)}, u32[]{:S(2)}) collective-permute-start(bf16[1,24,1024]{2,1,0:T(8,128)(2,1)S(1)} %get-tuple-element.35), channel_id=1, source_target_pairs={{0,8},{4,12},{8,4},{12,0},{1,9},{5,13},{9,5},{13,1},{2,10},{6,14},... | collective-permute-start | bytes 147464 | tf_op jit(solution)/shard_map/ppermute | solution.py:526
  5.8 4.8 %collective-permute-start.1 = (bf16[1,8,1024]{2,1,0:T(8,128)(2,1)S(1)}, bf16[1,8,1024]{2,1,0:T(8,128)(2,1)S(1)}, u32[]{:S(2)}, u32[]{:S(2)}) collective-permute-start(bf16[1,8,1024]{2,1,0:T(8,128)(2,1)S(1)} %get-tuple-element.36), channel_id=1, source_target_pairs={{0,12},{4,8},{8,0},{12,4},{1,13},{5,9},{9,1},{13,5},{2,14},{6,10},... | collective-permute-start | bytes 49160 | tf_op jit(solution)/shard_map/ppermute | solution.py:526
  6.9 3.7 %collective-permute-start.2 = (bf16[1,8,1024]{2,1,0:T(8,128)(2,1)S(1)}, bf16[1,8,1024]{2,1,0:T(8,128)(2,1)S(1)}, u32[]{:S(2)}, u32[]{:S(2)}) collective-permute-start(bf16[1,8,1024]{2,1,0:T(8,128)(2,1)S(1)} %get-tuple-element.37), channel_id=1, source_target_pairs={{0,4},{4,0},{8,12},{12,8},{1,5},{5,1},{9,13},{13,9},{2,6},{6,2},{1... | collective-permute-start | bytes 49160 | tf_op jit(solution)/shard_map/ppermute | solution.py:526
  7.4 1.6 %copy-start = (f32[1,16,1024]{2,1,0:T(8,128)S(1)}, f32[1,16,1024]{2,1,0:T(8,128)}, u32[]{:S(2)}) copy-start(f32[1,16,1024]{2,1,0:T(8,128)} %rest_4_.1) | copy-start | bytes 196612
  9.0 5.7 %collective-permute-start.4 = (bf16[1,48,1024]{2,1,0:T(8,128)(2,1)S(1)}, bf16[1,48,1024]{2,1,0:T(8,128)(2,1)S(1)}, u32[]{:S(2)}, u32[]{:S(2)}) collective-permute-start(bf16[1,48,1024]{2,1,0:T(8,128)(2,1)S(1)} %shard_map.152), channel_id=1, source_target_pairs={{0,4},{4,0},{8,12},{12,8},{1,5},{5,1},{9,13},{13,9},{2,6},{6,2},{1... | collective-permute-start | bytes 294920 | tf_op jit(solution)/shard_map/ppermute | solution.py:57
  11.2 5.4 %copy-start.1 = (bf16[256,1024]{1,0:T(8,128)(2,1)S(1)}, bf16[256,1024]{1,0:T(8,128)(2,1)}, u32[]{:S(2)}) copy-start(bf16[256,1024]{1,0:T(8,128)(2,1)} %dtw_ref.1) | copy-start | bytes 1572868
  11.2 1.3 %collective-permute-start.3 = (bf16[80,288]{1,0:T(8,128)(2,1)S(1)}, bf16[80,288]{1,0:T(8,128)(2,1)S(1)}, u32[]{:S(2)}, u32[]{:S(2)}) collective-permute-start(bf16[80,288]{1,0:T(8,128)(2,1)S(1)} %get-tuple-element.41), channel_id=1, source_target_pairs={{0,1},{1,0},{2,3},{3,2},{4,5},{5,4},{6,7},{7,6},{8,9},{9,8},{10,11... | collective-permute-start | bytes 138248 | tf_op jit(solution)/shard_map/ppermute | solution.py:57
  12.5 4.0 %collective-permute-start.5 = (bf16[80,288]{1,0:T(8,128)(2,1)S(1)}, bf16[80,288]{1,0:T(8,128)(2,1)S(1)}, u32[]{:S(2)}, u32[]{:S(2)}) collective-permute-start(bf16[80,288]{1,0:T(8,128)(2,1)S(1)} %get-tuple-element.49), channel_id=1, source_target_pairs={{0,3},{1,2},{2,1},{3,0},{4,7},{5,6},{6,5},{7,4},{8,11},{9,10},{10,... | collective-permute-start | bytes 138248 | tf_op jit(solution)/shard_map/ppermute | solution.py:57

commit v19 on v15

--- a/solution.py
+++ b/solution.py
@@ -64,14 +64,18 @@
     return total
 
 
-def block_of(sender, owner, direct):
-    if not direct:
-        return sender
+def blocks_of(owner):
     table = [
         [0 if s == r else 1 + [to[s] for to in SENDS].index(r) for s in range(DIRECT)]
         for r in range(DIRECT)
     ]
-    places = [chosen(owner, [row[s] for row in table]) for s in range(DIRECT)]
+    return [chosen(owner, [row[s] for row in table]) for s in range(DIRECT)]
+
+
+def block_of(sender, owner, direct):
+    if not direct:
+        return sender
+    places = blocks_of(owner)
     return places[sender] if isinstance(sender, int) else chosen(sender, places)
 
 
@@ -283,7 +287,8 @@
     short_ref[...] = part.astype(BF16)
 
 
-def add_kernel(a_ref, b_ref, sum_ref, short_ref):
+def add_kernel(a_ref, b_ref, after_ref, sum_ref, short_ref):
+    del after_ref
     total = a_ref[...] + b_ref[...].astype(F32)
     sum_ref[...] = total
     short_ref[...] = total.astype(BF16)
@@ -419,9 +424,10 @@
     lax.fori_loop(0, chunks, slot_chunk, 0)
     for copy in scalars:
         copy.wait()
+    places = blocks_of(owner_s[0]) if direct else None
     copies = []
     for j in range(rb):
-        at = block_of(child_s[j], owner_s[0], direct)
+        at = chosen(child_s[j], places) if direct else child_s[j]
         copy = pltpu.make_async_copy(slots_s.at[at], child_ssm.at[j], sems.at[2 + j])
         copy.start()
         copies.append(copy)
@@ -588,20 +594,7 @@
         nbytes=channels * width * 2 + rows * (channels + width) * 4,
         trans=rows * channels,
     )(pick, sender, base, taps_near, bias_near, weight_near, *msgs)
-    other = swap(brief, "tensor", 1)
-    distance = 2
-    while distance < tensors:
-        part, brief = call(
-            add_kernel,
-            [shaped((rows, width), F32), shaped((rows, width), BF16)],
-            [vmem()] * 2,
-            [vmem()] * 2,
-            flops=rows * width,
-            nbytes=rows * width * 14,
-        )(part, other)
-        other = swap(brief, "tensor", 2 * distance - 1)
-        distance *= 2
-
+    other = swap(brief, "tensor", tensors - 1)
     child_conv = call(
         functools.partial(windows_kernel, n_msgs, steps),
         shaped((taps - 1, rb, channels), BF16),
@@ -610,6 +603,19 @@
         flops=2 * owners * taps * rb * channels,
         nbytes=4 * taps * rb * channels,
     )(child_pick, part, *msgs)
+    total, distance = part, 1
+    while 2 * distance < tensors:
+        total, brief = call(
+            add_kernel,
+            [shaped((rows, width), F32), shaped((rows, width), BF16)],
+            [vmem()] * 2 + [anywhere()],
+            [vmem()] * 2,
+            flops=rows * width,
+            nbytes=rows * width * 14,
+        )(total, other, child_conv)
+        other = swap(brief, "tensor", distance)
+        distance *= 2
+
     own_start, slot_start = call(
         functools.partial(start_kernel, n_msgs, direct, short),
         [
@@ -621,7 +627,7 @@
         [pltpu.VMEM((owners, n_state, channels), F32)],
         flops=2 * owners * n_state * (rb + owners) * channels,
         nbytes=4 * n_state * (rb + owners) * channels,
-    )(pick, sender, part, *msgs, *states)
+    )(pick, sender, total, *msgs, *states)
 
     decoded, child_ssm = call(
         functools.partial(decode_kernel, direct),
@@ -660,7 +666,7 @@
         dt_weight,
         dtb_near,
         skip_near,
-        part,
+        total,
         other,
     )
     return (decoded, child_ssm, jnp.transpose(child_conv, (1, 0, 2)))

time: 19.6 us -> 20.7 us (1.056)
  waiting for transfers between devices: 2.49 us -> 3.85 us
  starting transfers between devices: 8.81 us -> 7.58 us
  local copies, waits for them, and re-layouts: 0.01 us -> 0.9 us
    ppermute x3, waiting for transfers between devices: 2.47 us -> 3.83 us  [swap(): return lax.ppermute(value, axis, [(i, i ^ distance) for i in range(size)])]
    ppermute x3, starting transfers between devices: 3.14 us -> 1.92 us  [swap(): return lax.ppermute(value, axis, [(i, i ^ distance) for i in range(size)])]
    unnamed x4 -> x6, local copies, waits for them, and re-layouts: 0.01 us -> 0.9 us
  transfers between devices with their start and end apart: 6 -> 6, of which waited for: 2 -> 2; matrix products, arithmetic and copies ran while one was open for 0% -> 0% of each run, Pallas kernels for 18% -> 17%
where the time goes in v19:
time: 20.7 us; the launch traced here: 20.4 us
  starting transfers between devices  7.58 us (37%)
  Pallas kernels  7.41 us (36%)
  waiting for transfers between devices  3.85 us (19%)
  local copies, waits for them, and re-layouts  0.9 us (4%)
  between operations  0.7 us (3%)
    ppermute x3, starting transfers between devices, on_device(): lax.ppermute(m, 'branch', list(enumerate(to)))  5.67 us
    ppermute x3, waiting for transfers between devices, swap(): return lax.ppermute(value, axis, [(i, i ^ distance) for i in range(size)])  3.83 us
    pallas_call x1, Pallas kernels, on_device(): call(functools.partial(decode_kernel, direct), [shaped((rb, steps, channe...  2.88 us
    ppermute x3, starting transfers between devices, swap(): return lax.ppermute(value, axis, [(i, i ^ distance) for i in range(size)])  1.92 us
    pallas_call x1, Pallas kernels, on_device(): call(functools.partial(prepare_kernel, direct), [shaped((steps, rb, chann...  1.58 us
    pallas_call x1, Pallas kernels, on_device(): call(functools.partial(pack_kernel, direct), [shaped(s, BF16) for s in ms...  1.11 us
    unnamed x6, local copies, waits for them, and re-layouts  0.9 us
    pallas_call x1, Pallas kernels, on_device(): call(functools.partial(windows_kernel, n_msgs, steps), shaped((taps - 1,...  0.78 us
  transfers between devices with their start and end apart: 6, of which 2 were waited for; matrix products, arithmetic and copies ran while one was open for 0% of the time, Pallas kernels for 17%

profile of v19, /device:TPU:0, one launch (start us, length us, event | category | flops | bytes accessed | tf_op | source)
XLA Modules:
  0.0 20.4 jit_solution(16648442114553565243)
XLA Ops:
  0.6 1.1 %shard_map.148 = (bf16[1,8,1024]{2,1,0:T(8,128)(2,1)S(1)}, bf16[1,24,1024]{2,1,0:T(8,128)(2,1)S(1)}, bf16[1,8,1024]{2,1,0:T(8,128)(2,1)S(1)}, bf16[1,8,1024]{2,1,0:T(8,128)(2,1)S(1)}) custom-call(s32[1]{0:T(128)} %bitcast.owner_hbm, s32[4]{0:T(128)} %bitcast.12, s32[16]{0:T(128)} %prompt_hbm.3, bf16[16,4,2,1024]{3,2,1,0:T(2,128)(2,1)} %step_hbm.3, ...), custom_call_target="tpu_custom_call" | custom-call | bytes 196608 | tf_op jit(solution)/shard_map/pallas_call | solution.py:497
  1.8 4.1 %collective-permute-start = (bf16[1,24,1024]{2,1,0:T(8,128)(2,1)S(1)}, bf16[1,24,1024]{2,1,0:T(8,128)(2,1)S(1)}, u32[]{:S(2)}, u32[]{:S(2)}) collective-permute-start(bf16[1,24,1024]{2,1,0:T(8,128)(2,1)S(1)} %get-tuple-element.35), channel_id=1, source_target_pairs={{0,8},{4,12},{8,4},{12,0},{1,9},{5,13},{9,5},{13,1},{2,10},{6,14},... | collective-permute-start | bytes 147464 | tf_op jit(solution)/shard_map/ppermute | solution.py:523
  5.8 1.1 %collective-permute-start.1 = (bf16[1,8,1024]{2,1,0:T(8,128)(2,1)S(1)}, bf16[1,8,1024]{2,1,0:T(8,128)(2,1)S(1)}, u32[]{:S(2)}, u32[]{:S(2)}) collective-permute-start(bf16[1,8,1024]{2,1,0:T(8,128)(2,1)S(1)} %get-tuple-element.36), channel_id=1, source_target_pairs={{0,12},{4,8},{8,0},{12,4},{1,13},{5,9},{9,1},{13,5},{2,14},{6,10},... | collective-permute-start | bytes 49160 | tf_op jit(solution)/shard_map/ppermute | solution.py:523
  6.9 0.5 %collective-permute-start.2 = (bf16[1,8,1024]{2,1,0:T(8,128)(2,1)S(1)}, bf16[1,8,1024]{2,1,0:T(8,128)(2,1)S(1)}, u32[]{:S(2)}, u32[]{:S(2)}) collective-permute-start(bf16[1,8,1024]{2,1,0:T(8,128)(2,1)S(1)} %get-tuple-element.37), channel_id=1, source_target_pairs={{0,4},{4,0},{8,12},{12,8},{1,5},{5,1},{9,13},{13,9},{2,6},{6,2},{1... | collective-permute-start | bytes 49160 | tf_op jit(solution)/shard_map/ppermute | solution.py:523
  7.4 0.0 copy-start
  7.4 1.6 %shard_map.149 = (f32[4,16,1024]{2,1,0:T(8,128)S(1)}, f32[4,16,1024]{2,1,0:T(8,128)S(1)}, f32[16,4]{1,0:T(8,128)S(1)}, f32[16,4]{1,0:T(8,128)S(1)}, f32[1,4]{1,0...) custom-call(s32[1]{0:T(128)} %bitcast.owner_hbm, ...), custom_call_target="tpu_custom_call" | custom-call | flops 655360 | bytes 786432 | tf_op jit(solution)/shard_map/pallas_call | solution.py:530
  9.0 0.0 collective-permute-done.rest_1_.came_ref
  9.0 0.0 copy-done
  9.1 1.6 %collective-permute-start.4 = (bf16[1,48,1024]{2,1,0:T(8,128)(2,1)S(1)}, bf16[1,48,1024]{2,1,0:T(8,128)(2,1)S(1)}, u32[]{:S(2)}, u32[]{:S(2)}) collective-permute-start(bf16[1,48,1024]{2,1,0:T(8,128)(2,1)S(1)} %shard_map.153), channel_id=1, source_target_pairs={{0,4},{4,0},{8,12},{12,8},{1,5},{5,1},{9,13},{13,9},{2,6},{6,2},{1... | collective-permute-start | bytes 294920 | tf_op jit(solution)/shard_map/ppermute | solution.py:57
  10.6 0.0 collective-permute-done.1.rest_2_
  10.6 0.0 collective-permute-done.2.rest_3_
  10.7 0.5 %shard_map.150 = (f32[80,1024]{1,0:T(8,128)S(1)}, f32[80,288]{1,0:T(8,128)S(1)}, bf16[80,288]{1,0:T(8,128)(2,1)S(1)}) custom-call(f32[16,4]{1,0:T(8,128)S(1)} %get-tuple-element.29.pick_ref.after_ref, f32[1,4]{1,0:T(1,128)S(1)} %get-tuple-element.30.sender_ref, f32[4,16,1024]{2,1,0:T(8,128)S(1)} %get-tuple-element.31.base_ref, ...), custom_call_target="tpu_custom_call" | custom-call | flops 47185920 | bytes 1009664 | tf_op jit(solution)/shard_map/pallas_call | solution.py:584
  11.2 0.0 copy-start.1
  11.2 0.1 collective-permute-start.3
  11.3 0.8 %shard_map.151.after_ref = bf16[3,16,1024]{2,1,0:T(8,128)(2,1)} custom-call(f32[16,4]{1,0:T(8,128)S(1)} %get-tuple-element.42.child_ref, f32[80,288]{1,0:T(8,128)S(1)} %get-tuple-element.40.after_ref.a_ref, bf16[1,8,1024]{2,1,0:T(8,128)(2,1)S(1)} %get-tuple-element.28.after_ref.rest_0_, bf16[1,24,1024]{2,1,0:T(8,128)(2,1)S(1)} %collective-permute-done.rest_1_.came_ref, ...), custom_call_target="tpu_custom_call" | custom-call | flops 524288 | bytes 262144 | tf_op jit(solution)/shard_map/pallas_call | solution.py:598
  12.1 3.2 %collective-permute-done.3.b_ref = bf16[80,288]{1,0:T(8,128)(2,1)S(1)} collective-permute-done((bf16[80,288]{1,0:T(8,128)(2,1)S(1)}, bf16[80,288]{1,0:T(8,128)(2,1)S(1)}, u32[]{:S(2)}, u32[]{:S(2)}) %collective-permute-start.3) | collective-permute-done | bytes 46112 | tf_op jit(solution)/shard_map/ppermute | solution.py:57
  15.3 0.0 copy-start.2
  15.3 0.9 %copy-done.2 = bf16[3,16,1024]{2,1,0:T(8,128)(2,1)S(1)} copy-done((bf16[3,16,1024]{2,1,0:T(8,128)(2,1)S(1)}, bf16[3,16,1024]{2,1,0:T(8,128)(2,1)}, u32[]{:S(2)}) %copy-start.2) | copy-done | bytes 98328
  16.3 0.2 collective-permute-start.5
  16.4 0.0 collective-permute-done.4.rest_5_
  16.4 0.5 %shard_map.154 = (f32[16,16,1024]{2,1,0:T(8,128)S(1)}, f32[8,8,1024]{2,1,0:T(8,128)S(1)}) custom-call(f32[16,4]{1,0:T(8,128)S(1)} %get-tuple-element.29.pick_ref.after_ref, f32[1,4]{1,0:T(1,128)S(1)} %get-tuple-element.30.sender_ref, f32[80,288]{1,0:T(8,128)S(1)} %get-tuple-element.43.after_ref.part_ref, ...), custom_call_target="tpu_custom_call" | custom-call | flops 2621440 | bytes 1310720 | tf_op jit(solution)/shard_map/pallas_call | solution.py:619
  17.0 0.6 %collective-permute-done.5.other_ref = bf16[80,288]{1,0:T(8,128)(2,1)S(1)} collective-permute-done((bf16[80,288]{1,0:T(8,128)(2,1)S(1)}, bf16[80,288]{1,0:T(8,128)(2,1)S(1)}, u32[]{:S(2)}, u32[]{:S(2)}) %collective-permute-start.5) | collective-permute-done | bytes 46112 | tf_op jit(solution)/shard_map/ppermute | solution.py:57
  17.6 0.0 copy-done.1
  17.6 2.9 %shard_map.155 = (bf16[16,4,1024]{2,1,0:T(4,128)(2,1)}, f32[16,16,1024]{2,1,0:T(8,128)}) custom-call(s32[1]{0:T(128)} %bitcast.owner_hbm, s32[16]{0:T(128)} %child_hbm.3, f32[80,1024]{1,0:T(8,128)S(1)} %get-tuple-element.38.act_ref, f32[4,16,1024]{2,1,0:T(8,128)S(1)} %get-tuple-element.39.gate_ref, f32[16,16,1024]{2,1,0:T(8,128)S(1)} %get-tuple-element.44.own_ref, ...), custom_call_target="tpu_custom_call" | custom-call | flops 10485760 | bytes 1310720 | tf_op jit(solution)/shard_map/pallas_call | solution.py:632
  (2 shorter events, 0.0 us)
Async XLA Ops:
  1.8 7.3 %collective-permute-start = (bf16[1,24,1024]{2,1,0:T(8,128)(2,1)S(1)}, bf16[1,24,1024]{2,1,0:T(8,128)(2,1)S(1)}, u32[]{:S(2)}, u32[]{:S(2)}) collective-permute-start(bf16[1,24,1024]{2,1,0:T(8,128)(2,1)S(1)} %get-tuple-element.35), channel_id=1, source_target_pairs={{0,8},{4,12},{8,4},{12,0},{1,9},{5,13},{9,5},{13,1},{2,10},{6,14},... | collective-permute-start | bytes 147464 | tf_op jit(solution)/shard_map/ppermute | solution.py:523
  5.8 4.8 %collective-permute-start.1 = (bf16[1,8,1024]{2,1,0:T(8,128)(2,1)S(1)}, bf16[1,8,1024]{2,1,0:T(8,128)(2,1)S(1)}, u32[]{:S(2)}, u32[]{:S(2)}) collective-permute-start(bf16[1,8,1024]{2,1,0:T(8,128)(2,1)S(1)} %get-tuple-element.36), channel_id=1, source_target_pairs={{0,12},{4,8},{8,0},{12,4},{1,13},{5,9},{9,1},{13,5},{2,14},{6,10},... | collective-permute-start | bytes 49160 | tf_op jit(solution)/shard_map/ppermute | solution.py:523
  6.9 3.7 %collective-permute-start.2 = (bf16[1,8,1024]{2,1,0:T(8,128)(2,1)S(1)}, bf16[1,8,1024]{2,1,0:T(8,128)(2,1)S(1)}, u32[]{:S(2)}, u32[]{:S(2)}) collective-permute-start(bf16[1,8,1024]{2,1,0:T(8,128)(2,1)S(1)} %get-tuple-element.37), channel_id=1, source_target_pairs={{0,4},{4,0},{8,12},{12,8},{1,5},{5,1},{9,13},{13,9},{2,6},{6,2},{1... | collective-permute-start | bytes 49160 | tf_op jit(solution)/shard_map/ppermute | solution.py:523
  7.4 1.6 %copy-start = (f32[1,16,1024]{2,1,0:T(8,128)S(1)}, f32[1,16,1024]{2,1,0:T(8,128)}, u32[]{:S(2)}) copy-start(f32[1,16,1024]{2,1,0:T(8,128)} %rest_4_.1) | copy-start | bytes 196612
  9.1 7.4 %collective-permute-start.4 = (bf16[1,48,1024]{2,1,0:T(8,128)(2,1)S(1)}, bf16[1,48,1024]{2,1,0:T(8,128)(2,1)S(1)}, u32[]{:S(2)}, u32[]{:S(2)}) collective-permute-start(bf16[1,48,1024]{2,1,0:T(8,128)(2,1)S(1)} %shard_map.153), channel_id=1, source_target_pairs={{0,4},{4,0},{8,12},{12,8},{1,5},{5,1},{9,13},{13,9},{2,6},{6,2},{1... | collective-permute-start | bytes 294920 | tf_op jit(solution)/shard_map/ppermute | solution.py:57
  11.2 6.4 %copy-start.1 = (bf16[256,1024]{1,0:T(8,128)(2,1)S(1)}, bf16[256,1024]{1,0:T(8,128)(2,1)}, u32[]{:S(2)}) copy-start(bf16[256,1024]{1,0:T(8,128)(2,1)} %dtw_ref.1) | copy-start | bytes 1572868
  11.2 4.2 %collective-permute-start.3 = (bf16[80,288]{1,0:T(8,128)(2,1)S(1)}, bf16[80,288]{1,0:T(8,128)(2,1)S(1)}, u32[]{:S(2)}, u32[]{:S(2)}) collective-permute-start(bf16[80,288]{1,0:T(8,128)(2,1)S(1)} %get-tuple-element.41), channel_id=1, source_target_pairs={{0,3},{1,2},{2,1},{3,0},{4,7},{5,6},{6,5},{7,4},{8,11},{9,10},{10,... | collective-permute-start | bytes 138248 | tf_op jit(solution)/shard_map/ppermute | solution.py:57
  15.3 0.9 %copy-start.2 = (bf16[3,16,1024]{2,1,0:T(8,128)(2,1)S(1)}, bf16[3,16,1024]{2,1,0:T(8,128)(2,1)}, u32[]{:S(2)}) copy-start(bf16[3,16,1024]{2,1,0:T(8,128)(2,1)} %shard_map.151.after_ref) | copy-start | bytes 294916
  16.3 1.3 %collective-permute-start.5 = (bf16[80,288]{1,0:T(8,128)(2,1)S(1)}, bf16[80,288]{1,0:T(8,128)(2,1)S(1)}, u32[]{:S(2)}, u32[]{:S(2)}) collective-permute-start(bf16[80,288]{1,0:T(8,128)(2,1)S(1)} %get-tuple-element.50), channel_id=1, source_target_pairs={{0,1},{1,0},{2,3},{3,2},{4,5},{5,4},{6,7},{7,6},{8,9},{9,8},{10,11... | collective-permute-start | bytes 138248 | tf_op jit(solution)/shard_map/ppermute | solution.py:57

commit v20 on v15

--- a/solution.py
+++ b/solution.py
@@ -64,15 +64,12 @@
     return total
 
 
-def block_of(sender, owner, direct):
-    if not direct:
-        return sender
+def blocks_of(owner):
     table = [
         [0 if s == r else 1 + [to[s] for to in SENDS].index(r) for s in range(DIRECT)]
         for r in range(DIRECT)
     ]
-    places = [chosen(owner, [row[s] for row in table]) for s in range(DIRECT)]
-    return places[sender] if isinstance(sender, int) else chosen(sender, places)
+    return [chosen(owner, [row[s] for row in table]) for s in range(DIRECT)]
 
 
 def all_of(copies):
@@ -95,12 +92,12 @@
     ]
 
 
-def scalar_onehot(senders_s, owner, shape, direct):
+def scalar_onehot(senders_s, places, shape):
     row_of = lax.broadcasted_iota(jnp.int32, shape, 0)
     wanted = jnp.zeros(shape, jnp.int32)
     for b in range(shape[0]):
         wanted = jnp.where(row_of == b, senders_s[b], wanted)
-    wanted = block_of(wanted, owner, direct)
+    wanted = wanted if places is None else chosen(wanted, places)
     return (wanted == lax.broadcasted_iota(jnp.int32, shape, 1)).astype(F32)
 
 
@@ -222,12 +219,13 @@
         for k in range(max(0, taps - 1 - t), taps - 1):
             total = total + cw_ref[k : k + 1, :] * xs[t + k - taps + 1]
         base_ref[t] = total
-    pick_ref[...] = scalar_onehot(prompt_s, owner_s[0], pick_ref.shape, direct)
-    child_ref[...] = scalar_onehot(child_s, owner_s[0], child_ref.shape, direct)
+    places = blocks_of(owner_s[0]) if direct else None
+    pick_ref[...] = scalar_onehot(prompt_s, places, pick_ref.shape)
+    child_ref[...] = scalar_onehot(child_s, places, child_ref.shape)
     column = lax.broadcasted_iota(jnp.int32, sender_ref.shape, 1)
     sender = column
-    for sent in range(sender_ref.shape[1] if direct else 0):
-        sender = jnp.where(column == block_of(sent, owner_s[0], direct), sent, sender)
+    for sent, place in enumerate(places or []):
+        sender = jnp.where(column == place, sent, sender)
     sender_ref[...] = sender.astype(F32)
     rate = jnp.exp(alog[...]) * (-math.log2(math.e))
     rate_ref[...] = rate
@@ -419,9 +417,10 @@
     lax.fori_loop(0, chunks, slot_chunk, 0)
     for copy in scalars:
         copy.wait()
+    places = blocks_of(owner_s[0]) if direct else None
     copies = []
     for j in range(rb):
-        at = block_of(child_s[j], owner_s[0], direct)
+        at = chosen(child_s[j], places) if direct else child_s[j]
         copy = pltpu.make_async_copy(slots_s.at[at], child_ssm.at[j], sems.at[2 + j])
         copy.start()
         copies.append(copy)

time: 19.6 us -> 19.6 us (level)
  no operation moved by 1% of the time
where the time goes in v20:
time: 19.6 us; the launch traced here: 19.4 us
  starting transfers between devices  8.81 us (45%)
  Pallas kernels  7.42 us (38%)
  waiting for transfers between devices  2.49 us (13%)
  between operations  0.71 us (4%)
    ppermute x3, starting transfers between devices, on_device(): lax.ppermute(m, 'branch', list(enumerate(to)))  5.67 us
    ppermute x3, starting transfers between devices, swap(): return lax.ppermute(value, axis, [(i, i ^ distance) for i in range(size)])  3.14 us
    pallas_call x1, Pallas kernels, on_device(): call(functools.partial(decode_kernel, direct), [shaped((rb, steps, channe...  2.89 us
    ppermute x3, waiting for transfers between devices, swap(): return lax.ppermute(value, axis, [(i, i ^ distance) for i in range(size)])  2.47 us
    pallas_call x1, Pallas kernels, on_device(): call(functools.partial(prepare_kernel, direct), [shaped((steps, rb, chann...  1.58 us
    pallas_call x1, Pallas kernels, on_device(): call(functools.partial(pack_kernel, direct), [shaped(s, BF16) for s in ms...  1.11 us
    pallas_call x1, Pallas kernels, on_device(): call(functools.partial(windows_kernel, n_msgs, steps), shaped((taps - 1,...  0.78 us
    pallas_call x1, Pallas kernels, on_device(): call(functools.partial(start_kernel, n_msgs, direct, short), [shaped((n_s...  0.53 us
  transfers between devices with their start and end apart: 6, of which 2 were waited for; matrix products, arithmetic and copies ran while one was open for 0% of the time, Pallas kernels for 18%

profile of v20, /device:TPU:0, one launch (start us, length us, event | category | flops | bytes accessed | tf_op | source)
XLA Modules:
  0.0 19.4 jit_solution(3669361740983816004)
XLA Ops:
  0.6 1.1 %shard_map.148 = (bf16[1,8,1024]{2,1,0:T(8,128)(2,1)S(1)}, bf16[1,24,1024]{2,1,0:T(8,128)(2,1)S(1)}, bf16[1,8,1024]{2,1,0:T(8,128)(2,1)S(1)}, bf16[1,8,1024]{2,1,0:T(8,128)(2,1)S(1)}) custom-call(s32[1]{0:T(128)} %bitcast.owner_hbm, s32[4]{0:T(128)} %bitcast.12, s32[16]{0:T(128)} %prompt_hbm.3, bf16[16,4,2,1024]{3,2,1,0:T(2,128)(2,1)} %step_hbm.3, ...), custom_call_target="tpu_custom_call" | custom-call | bytes 196608 | tf_op jit(solution)/shard_map/pallas_call | solution.py:490
  1.8 4.1 %collective-permute-start = (bf16[1,24,1024]{2,1,0:T(8,128)(2,1)S(1)}, bf16[1,24,1024]{2,1,0:T(8,128)(2,1)S(1)}, u32[]{:S(2)}, u32[]{:S(2)}) collective-permute-start(bf16[1,24,1024]{2,1,0:T(8,128)(2,1)S(1)} %get-tuple-element.35), channel_id=1, source_target_pairs={{0,8},{4,12},{8,4},{12,0},{1,9},{5,13},{9,5},{13,1},{2,10},{6,14},... | collective-permute-start | bytes 147464 | tf_op jit(solution)/shard_map/ppermute | solution.py:516
  5.8 1.1 %collective-permute-start.1 = (bf16[1,8,1024]{2,1,0:T(8,128)(2,1)S(1)}, bf16[1,8,1024]{2,1,0:T(8,128)(2,1)S(1)}, u32[]{:S(2)}, u32[]{:S(2)}) collective-permute-start(bf16[1,8,1024]{2,1,0:T(8,128)(2,1)S(1)} %get-tuple-element.36), channel_id=1, source_target_pairs={{0,12},{4,8},{8,0},{12,4},{1,13},{5,9},{9,1},{13,5},{2,14},{6,10},... | collective-permute-start | bytes 49160 | tf_op jit(solution)/shard_map/ppermute | solution.py:516
  6.9 0.5 %collective-permute-start.2 = (bf16[1,8,1024]{2,1,0:T(8,128)(2,1)S(1)}, bf16[1,8,1024]{2,1,0:T(8,128)(2,1)S(1)}, u32[]{:S(2)}, u32[]{:S(2)}) collective-permute-start(bf16[1,8,1024]{2,1,0:T(8,128)(2,1)S(1)} %get-tuple-element.37), channel_id=1, source_target_pairs={{0,4},{4,0},{8,12},{12,8},{1,5},{5,1},{9,13},{13,9},{2,6},{6,2},{1... | collective-permute-start | bytes 49160 | tf_op jit(solution)/shard_map/ppermute | solution.py:516
  7.4 0.0 copy-start
  7.4 1.6 %shard_map.149 = (f32[4,16,1024]{2,1,0:T(8,128)S(1)}, f32[4,16,1024]{2,1,0:T(8,128)S(1)}, f32[16,4]{1,0:T(8,128)S(1)}, f32[16,4]{1,0:T(8,128)S(1)}, f32[1,4]{1,0...) custom-call(s32[1]{0:T(128)} %bitcast.owner_hbm, ...), custom_call_target="tpu_custom_call" | custom-call | flops 655360 | bytes 786432 | tf_op jit(solution)/shard_map/pallas_call | solution.py:523
  9.0 0.0 collective-permute-done.rest_1_.came_ref
  9.0 0.0 copy-done
  9.0 1.6 %collective-permute-start.4 = (bf16[1,48,1024]{2,1,0:T(8,128)(2,1)S(1)}, bf16[1,48,1024]{2,1,0:T(8,128)(2,1)S(1)}, u32[]{:S(2)}, u32[]{:S(2)}) collective-permute-start(bf16[1,48,1024]{2,1,0:T(8,128)(2,1)S(1)} %shard_map.152), channel_id=1, source_target_pairs={{0,4},{4,0},{8,12},{12,8},{1,5},{5,1},{9,13},{13,9},{2,6},{6,2},{1... | collective-permute-start | bytes 294920 | tf_op jit(solution)/shard_map/ppermute | solution.py:57
  10.6 0.0 collective-permute-done.1.rest_2_
  10.6 0.0 collective-permute-done.2.rest_3_
  10.7 0.5 %shard_map.150 = (f32[80,1024]{1,0:T(8,128)S(1)}, f32[80,288]{1,0:T(8,128)S(1)}, bf16[80,288]{1,0:T(8,128)(2,1)S(1)}) custom-call(f32[16,4]{1,0:T(8,128)S(1)} %get-tuple-element.29.pick_ref.after_ref, f32[1,4]{1,0:T(1,128)S(1)} %get-tuple-element.30.sender_ref, f32[4,16,1024]{2,1,0:T(8,128)S(1)} %get-tuple-element.31.base_ref, ...), custom_call_target="tpu_custom_call" | custom-call | flops 47185920 | bytes 1009664 | tf_op jit(solution)/shard_map/pallas_call | solution.py:577
  11.2 0.0 copy-start.1
  11.2 0.1 collective-permute-start.3
  11.3 1.2 %collective-permute-done.3.b_ref = bf16[80,288]{1,0:T(8,128)(2,1)S(1)} collective-permute-done((bf16[80,288]{1,0:T(8,128)(2,1)S(1)}, bf16[80,288]{1,0:T(8,128)(2,1)S(1)}, u32[]{:S(2)}, u32[]{:S(2)}) %collective-permute-start.3) | collective-permute-done | bytes 46112 | tf_op jit(solution)/shard_map/ppermute | solution.py:57
  12.5 1.5 %collective-permute-start.5 = (bf16[80,288]{1,0:T(8,128)(2,1)S(1)}, bf16[80,288]{1,0:T(8,128)(2,1)S(1)}, u32[]{:S(2)}, u32[]{:S(2)}) collective-permute-start(bf16[80,288]{1,0:T(8,128)(2,1)S(1)} %get-tuple-element.49), channel_id=1, source_target_pairs={{0,3},{1,2},{2,1},{3,0},{4,7},{5,6},{6,5},{7,4},{8,11},{9,10},{10,... | collective-permute-start | bytes 138248 | tf_op jit(solution)/shard_map/ppermute | solution.py:57
  14.0 0.8 %shard_map.155 = bf16[3,16,1024]{2,1,0:T(8,128)(2,1)} custom-call(f32[16,4]{1,0:T(8,128)S(1)} %get-tuple-element.52.child_ref, f32[80,288]{1,0:T(8,128)S(1)} %get-tuple-element.42.after_ref.part_ref, bf16[1,8,1024]{2,1,0:T(8,128)(2,1)S(1)} %get-tuple-element.28.after_ref.rest_0_, bf16[1,24,1024]{2,1,0:T(8,128)(2,1)S(1)} %collective-permute-done.rest_1_.came_ref, ...), custom_call_target="tpu_custom_call" | custom-call | flops 524288 | bytes 262144 | tf_op jit(solution)/shard_map/pallas_call | solution.py:604
  14.8 0.0 collective-permute-done.4.rest_5_
  14.8 0.5 %shard_map.153 = (f32[16,16,1024]{2,1,0:T(8,128)S(1)}, f32[8,8,1024]{2,1,0:T(8,128)S(1)}) custom-call(f32[16,4]{1,0:T(8,128)S(1)} %get-tuple-element.29.pick_ref.after_ref, f32[1,4]{1,0:T(1,128)S(1)} %get-tuple-element.30.sender_ref, f32[80,288]{1,0:T(8,128)S(1)} %get-tuple-element.42.after_ref.part_ref, ...), custom_call_target="tpu_custom_call" | custom-call | flops 2621440 | bytes 1310720 | tf_op jit(solution)/shard_map/pallas_call | solution.py:612
  15.3 1.2 %collective-permute-done.5.other_ref = bf16[80,288]{1,0:T(8,128)(2,1)S(1)} collective-permute-done((bf16[80,288]{1,0:T(8,128)(2,1)S(1)}, bf16[80,288]{1,0:T(8,128)(2,1)S(1)}, u32[]{:S(2)}, u32[]{:S(2)}) %collective-permute-start.5) | collective-permute-done | bytes 46112 | tf_op jit(solution)/shard_map/ppermute | solution.py:57
  16.5 0.0 copy-done.1
  16.5 2.9 %shard_map.154 = (bf16[16,4,1024]{2,1,0:T(4,128)(2,1)}, f32[16,16,1024]{2,1,0:T(8,128)}) custom-call(s32[1]{0:T(128)} %bitcast.owner_hbm, s32[16]{0:T(128)} %child_hbm.3, f32[80,1024]{1,0:T(8,128)S(1)} %get-tuple-element.38.act_ref, f32[4,16,1024]{2,1,0:T(8,128)S(1)} %get-tuple-element.39.gate_ref, f32[16,16,1024]{2,1,0:T(8,128)S(1)} %get-tuple-element.43.own_ref, ...), custom_call_target="tpu_custom_call" | custom-call | flops 10485760 | bytes 1310720 | tf_op jit(solution)/shard_map/pallas_call | solution.py:625
  (2 shorter events, 0.0 us)
Async XLA Ops:
  1.8 7.3 %collective-permute-start = (bf16[1,24,1024]{2,1,0:T(8,128)(2,1)S(1)}, bf16[1,24,1024]{2,1,0:T(8,128)(2,1)S(1)}, u32[]{:S(2)}, u32[]{:S(2)}) collective-permute-start(bf16[1,24,1024]{2,1,0:T(8,128)(2,1)S(1)} %get-tuple-element.35), channel_id=1, source_target_pairs={{0,8},{4,12},{8,4},{12,0},{1,9},{5,13},{9,5},{13,1},{2,10},{6,14},... | collective-permute-start | bytes 147464 | tf_op jit(solution)/shard_map/ppermute | solution.py:516
  5.8 4.8 %collective-permute-start.1 = (bf16[1,8,1024]{2,1,0:T(8,128)(2,1)S(1)}, bf16[1,8,1024]{2,1,0:T(8,128)(2,1)S(1)}, u32[]{:S(2)}, u32[]{:S(2)}) collective-permute-start(bf16[1,8,1024]{2,1,0:T(8,128)(2,1)S(1)} %get-tuple-element.36), channel_id=1, source_target_pairs={{0,12},{4,8},{8,0},{12,4},{1,13},{5,9},{9,1},{13,5},{2,14},{6,10},... | collective-permute-start | bytes 49160 | tf_op jit(solution)/shard_map/ppermute | solution.py:516
  6.9 3.7 %collective-permute-start.2 = (bf16[1,8,1024]{2,1,0:T(8,128)(2,1)S(1)}, bf16[1,8,1024]{2,1,0:T(8,128)(2,1)S(1)}, u32[]{:S(2)}, u32[]{:S(2)}) collective-permute-start(bf16[1,8,1024]{2,1,0:T(8,128)(2,1)S(1)} %get-tuple-element.37), channel_id=1, source_target_pairs={{0,4},{4,0},{8,12},{12,8},{1,5},{5,1},{9,13},{13,9},{2,6},{6,2},{1... | collective-permute-start | bytes 49160 | tf_op jit(solution)/shard_map/ppermute | solution.py:516
  7.4 1.6 %copy-start = (f32[1,16,1024]{2,1,0:T(8,128)S(1)}, f32[1,16,1024]{2,1,0:T(8,128)}, u32[]{:S(2)}) copy-start(f32[1,16,1024]{2,1,0:T(8,128)} %rest_4_.1) | copy-start | bytes 196612
  9.0 5.7 %collective-permute-start.4 = (bf16[1,48,1024]{2,1,0:T(8,128)(2,1)S(1)}, bf16[1,48,1024]{2,1,0:T(8,128)(2,1)S(1)}, u32[]{:S(2)}, u32[]{:S(2)}) collective-permute-start(bf16[1,48,1024]{2,1,0:T(8,128)(2,1)S(1)} %shard_map.152), channel_id=1, source_target_pairs={{0,4},{4,0},{8,12},{12,8},{1,5},{5,1},{9,13},{13,9},{2,6},{6,2},{1... | collective-permute-start | bytes 294920 | tf_op jit(solution)/shard_map/ppermute | solution.py:57
  11.2 5.4 %copy-start.1 = (bf16[256,1024]{1,0:T(8,128)(2,1)S(1)}, bf16[256,1024]{1,0:T(8,128)(2,1)}, u32[]{:S(2)}) copy-start(bf16[256,1024]{1,0:T(8,128)(2,1)} %dtw_ref.1) | copy-start | bytes 1572868
  11.2 1.3 %collective-permute-start.3 = (bf16[80,288]{1,0:T(8,128)(2,1)S(1)}, bf16[80,288]{1,0:T(8,128)(2,1)S(1)}, u32[]{:S(2)}, u32[]{:S(2)}) collective-permute-start(bf16[80,288]{1,0:T(8,128)(2,1)S(1)} %get-tuple-element.41), channel_id=1, source_target_pairs={{0,1},{1,0},{2,3},{3,2},{4,5},{5,4},{6,7},{7,6},{8,9},{9,8},{10,11... | collective-permute-start | bytes 138248 | tf_op jit(solution)/shard_map/ppermute | solution.py:57
  12.5 4.0 %collective-permute-start.5 = (bf16[80,288]{1,0:T(8,128)(2,1)S(1)}, bf16[80,288]{1,0:T(8,128)(2,1)S(1)}, u32[]{:S(2)}, u32[]{:S(2)}) collective-permute-start(bf16[80,288]{1,0:T(8,128)(2,1)S(1)} %get-tuple-element.49), channel_id=1, source_target_pairs={{0,3},{1,2},{2,1},{3,0},{4,7},{5,6},{6,5},{7,4},{8,11},{9,10},{10,... | collective-permute-start | bytes 138248 | tf_op jit(solution)/shard_map/ppermute | solution.py:57

commit v21 on v20

--- a/solution.py
+++ b/solution.py
@@ -158,7 +158,7 @@
     owner_hbm,
     prompt_hbm,
     child_hbm,
-    step_hbm,
+    step_ref,
     cw_hbm,
     cb_hbm,
     xwt_hbm,
@@ -178,7 +178,6 @@
     twin_ref,
     dtb_ref,
     skip_ref,
-    step_ref,
     owner_s,
     prompt_s,
     child_s,
@@ -201,12 +200,9 @@
             )
         )
     ]
-    inputs = in_parts(step_hbm, step_ref, sems, len(small), STEP_PARTS)
-    large = in_parts(xwt_hbm, xwt_ref, sems, len(small) + STEP_PARTS, WEIGHT_PARTS)
-    for copy in inputs + small + large:
+    large = in_parts(xwt_hbm, xwt_ref, sems, len(small), WEIGHT_PARTS)
+    for copy in small + large:
         copy.start()
-    for copy in inputs:
-        copy.wait()
     steps = step_ref.shape[1]
     taps = cw_hbm.shape[0]
     xs = [step_ref[:, t, 0, :].astype(F32) for t in range(steps)]
@@ -536,15 +532,14 @@
             shaped((1, channels), F32),
             shaped((1, channels), F32),
         ],
-        [hbm()] * 10 + [anywhere()],
+        [hbm()] * 3 + [vmem()] + [hbm()] * 6 + [anywhere()],
         [vmem()] * 12,
         [
-            pltpu.VMEM(step_in.shape, BF16),
             pltpu.SMEM((1,), jnp.int32),
             pltpu.SMEM((rb,), jnp.int32),
             pltpu.SMEM((rb,), jnp.int32),
             pltpu.VMEM((n_state, channels), F32),
-            pltpu.SemaphoreType.DMA((8 + WEIGHT_PARTS + STEP_PARTS,)),
+            pltpu.SemaphoreType.DMA((8 + WEIGHT_PARTS,)),
         ],
         flops=10 * steps * rb * channels,
         nbytes=12 * steps * rb * channels,
@@ -553,7 +548,7 @@
         owner,
         pinned(prompt_of),
         pinned(child_slot),
-        pinned(step_in),
+        step_in,
         pinned(conv_weight),
         pinned(conv_bias[None]),
         pinned(x_weight.T),

time: 19.6 us -> 19.6 us (level)
  waiting for transfers between devices: 2.49 us -> 2.81 us
    ppermute x3, waiting for transfers between devices: 0.02 us -> 0.36 us  [on_device(): lax.ppermute(m, 'branch', list(enumerate(to)))]
  transfers between devices with their start and end apart: 6 -> 6, of which waited for: 2 -> 4; matrix products, arithmetic and copies ran while one was open for 0% -> 0% of each run, Pallas kernels for 18% -> 17%
where the time goes in v21:
time: 19.6 us; the launch traced here: 19.5 us
  starting transfers between devices  8.7 us (44%)
  Pallas kernels  7.24 us (37%)
  waiting for transfers between devices  2.81 us (14%)
  between operations  0.7 us (4%)
    ppermute x3, starting transfers between devices, on_device(): lax.ppermute(m, 'branch', list(enumerate(to)))  5.67 us
    ppermute x3, starting transfers between devices, swap(): return lax.ppermute(value, axis, [(i, i ^ distance) for i in range(size)])  3.03 us
    pallas_call x1, Pallas kernels, on_device(): call(functools.partial(decode_kernel, direct), [shaped((rb, steps, channe...  2.87 us
    ppermute x3, waiting for transfers between devices, swap(): return lax.ppermute(value, axis, [(i, i ^ distance) for i in range(size)])  2.44 us
    pallas_call x1, Pallas kernels, on_device(): call(functools.partial(prepare_kernel, direct), [shaped((steps, rb, chann...  1.38 us
    pallas_call x1, Pallas kernels, on_device(): call(functools.partial(pack_kernel, direct), [shaped(s, BF16) for s in ms...  1.15 us
    pallas_call x1, Pallas kernels, on_device(): call(functools.partial(windows_kernel, n_msgs, steps), shaped((taps - 1,...  0.78 us
    pallas_call x1, Pallas kernels, on_device(): call(functools.partial(start_kernel, n_msgs, direct, short), [shaped((n_s...  0.53 us
  transfers between devices with their start and end apart: 6, of which 4 were waited for; matrix products, arithmetic and copies ran while one was open for 0% of the time, Pallas kernels for 17%

profile of v21, /device:TPU:0, one launch (start us, length us, event | category | flops | bytes accessed | tf_op | source)
XLA Modules:
  0.0 19.5 jit_solution(18239878956129756591)
XLA Ops:
  0.6 0.0 copy-start
  0.6 1.1 %shard_map.148 = (bf16[1,8,1024]{2,1,0:T(8,128)(2,1)S(1)}, bf16[1,24,1024]{2,1,0:T(8,128)(2,1)S(1)}, bf16[1,8,1024]{2,1,0:T(8,128)(2,1)S(1)}, bf16[1,8,1024]{2,1,0:T(8,128)(2,1)S(1)}) custom-call(s32[1]{0:T(128)} %bitcast.owner_hbm, s32[4]{0:T(128)} %bitcast.12, s32[16]{0:T(128)} %prompt_hbm.3, bf16[16,4,2,1024]{3,2,1,0:T(2,128)(2,1)} %step_ref.1, ...), custom_call_target="tpu_custom_call" | custom-call | bytes 196608 | tf_op jit(solution)/shard_map/pallas_call | solution.py:486
  1.8 4.1 %collective-permute-start = (bf16[1,24,1024]{2,1,0:T(8,128)(2,1)S(1)}, bf16[1,24,1024]{2,1,0:T(8,128)(2,1)S(1)}, u32[]{:S(2)}, u32[]{:S(2)}) collective-permute-start(bf16[1,24,1024]{2,1,0:T(8,128)(2,1)S(1)} %get-tuple-element.35), channel_id=1, source_target_pairs={{0,8},{4,12},{8,4},{12,0},{1,9},{5,13},{9,5},{13,1},{2,10},{6,14},... | collective-permute-start | bytes 147464 | tf_op jit(solution)/shard_map/ppermute | solution.py:512
  5.9 1.1 %collective-permute-start.1 = (bf16[1,8,1024]{2,1,0:T(8,128)(2,1)S(1)}, bf16[1,8,1024]{2,1,0:T(8,128)(2,1)S(1)}, u32[]{:S(2)}, u32[]{:S(2)}) collective-permute-start(bf16[1,8,1024]{2,1,0:T(8,128)(2,1)S(1)} %get-tuple-element.36), channel_id=1, source_target_pairs={{0,12},{4,8},{8,0},{12,4},{1,13},{5,9},{9,1},{13,5},{2,14},{6,10},... | collective-permute-start | bytes 49160 | tf_op jit(solution)/shard_map/ppermute | solution.py:512
  7.0 0.5 %collective-permute-start.2 = (bf16[1,8,1024]{2,1,0:T(8,128)(2,1)S(1)}, bf16[1,8,1024]{2,1,0:T(8,128)(2,1)S(1)}, u32[]{:S(2)}, u32[]{:S(2)}) collective-permute-start(bf16[1,8,1024]{2,1,0:T(8,128)(2,1)S(1)} %get-tuple-element.37), channel_id=1, source_target_pairs={{0,4},{4,0},{8,12},{12,8},{1,5},{5,1},{9,13},{13,9},{2,6},{6,2},{1... | collective-permute-start | bytes 49160 | tf_op jit(solution)/shard_map/ppermute | solution.py:512
  7.5 0.0 copy-done
  7.5 0.0 copy-start.1
  7.5 1.4 %shard_map.149 = (f32[4,16,1024]{2,1,0:T(8,128)S(1)}, f32[4,16,1024]{2,1,0:T(8,128)S(1)}, f32[16,4]{1,0:T(8,128)S(1)}, f32[16,4]{1,0:T(8,128)S(1)}, f32[1,4]{1,0...) custom-call(s32[1]{0:T(128)} %bitcast.owner_hbm, ...), custom_call_target="tpu_custom_call" | custom-call | flops 655360 | bytes 786432 | tf_op jit(solution)/shard_map/pallas_call | solution.py:519
  8.9 0.2 collective-permute-done.rest_1_.came_ref
  9.0 0.0 copy-done.1
  9.0 1.5 %collective-permute-start.4 = (bf16[1,48,1024]{2,1,0:T(8,128)(2,1)S(1)}, bf16[1,48,1024]{2,1,0:T(8,128)(2,1)S(1)}, u32[]{:S(2)}, u32[]{:S(2)}) collective-permute-start(bf16[1,48,1024]{2,1,0:T(8,128)(2,1)S(1)} %shard_map.152), channel_id=1, source_target_pairs={{0,4},{4,0},{8,12},{12,8},{1,5},{5,1},{9,13},{13,9},{2,6},{6,2},{1... | collective-permute-start | bytes 294920 | tf_op jit(solution)/shard_map/ppermute | solution.py:57
  10.5 0.0 collective-permute-done.1.rest_2_
  10.5 0.2 collective-permute-done.2.rest_3_
  10.7 0.5 %shard_map.150 = (f32[80,1024]{1,0:T(8,128)S(1)}, f32[80,288]{1,0:T(8,128)S(1)}, bf16[80,288]{1,0:T(8,128)(2,1)S(1)}) custom-call(f32[16,4]{1,0:T(8,128)S(1)} %get-tuple-element.29.pick_ref.after_ref, f32[1,4]{1,0:T(1,128)S(1)} %get-tuple-element.30.sender_ref, f32[4,16,1024]{2,1,0:T(8,128)S(1)} %get-tuple-element.31.base_ref, ...), custom_call_target="tpu_custom_call" | custom-call | flops 47185920 | bytes 1009664 | tf_op jit(solution)/shard_map/pallas_call | solution.py:572
  11.2 0.0 copy-start.2
  11.2 0.1 collective-permute-start.3
  11.3 1.2 %collective-permute-done.3.b_ref = bf16[80,288]{1,0:T(8,128)(2,1)S(1)} collective-permute-done((bf16[80,288]{1,0:T(8,128)(2,1)S(1)}, bf16[80,288]{1,0:T(8,128)(2,1)S(1)}, u32[]{:S(2)}, u32[]{:S(2)}) %collective-permute-start.3) | collective-permute-done | bytes 46112 | tf_op jit(solution)/shard_map/ppermute | solution.py:57
  12.6 1.5 %collective-permute-start.5 = (bf16[80,288]{1,0:T(8,128)(2,1)S(1)}, bf16[80,288]{1,0:T(8,128)(2,1)S(1)}, u32[]{:S(2)}, u32[]{:S(2)}) collective-permute-start(bf16[80,288]{1,0:T(8,128)(2,1)S(1)} %get-tuple-element.49), channel_id=1, source_target_pairs={{0,3},{1,2},{2,1},{3,0},{4,7},{5,6},{6,5},{7,4},{8,11},{9,10},{10,... | collective-permute-start | bytes 138248 | tf_op jit(solution)/shard_map/ppermute | solution.py:57
  14.1 0.8 %shard_map.155 = bf16[3,16,1024]{2,1,0:T(8,128)(2,1)} custom-call(f32[16,4]{1,0:T(8,128)S(1)} %get-tuple-element.52.child_ref, f32[80,288]{1,0:T(8,128)S(1)} %get-tuple-element.42.after_ref.part_ref, bf16[1,8,1024]{2,1,0:T(8,128)(2,1)S(1)} %get-tuple-element.28.after_ref.rest_0_, bf16[1,24,1024]{2,1,0:T(8,128)(2,1)S(1)} %collective-permute-done.rest_1_.came_ref, ...), custom_call_target="tpu_custom_call" | custom-call | flops 524288 | bytes 262144 | tf_op jit(solution)/shard_map/pallas_call | solution.py:599
  14.8 0.0 collective-permute-done.4.rest_5_
  14.8 0.5 %shard_map.153 = (f32[16,16,1024]{2,1,0:T(8,128)S(1)}, f32[8,8,1024]{2,1,0:T(8,128)S(1)}) custom-call(f32[16,4]{1,0:T(8,128)S(1)} %get-tuple-element.29.pick_ref.after_ref, f32[1,4]{1,0:T(1,128)S(1)} %get-tuple-element.30.sender_ref, f32[80,288]{1,0:T(8,128)S(1)} %get-tuple-element.42.after_ref.part_ref, ...), custom_call_target="tpu_custom_call" | custom-call | flops 2621440 | bytes 1310720 | tf_op jit(solution)/shard_map/pallas_call | solution.py:607
  15.4 1.2 %collective-permute-done.5.other_ref = bf16[80,288]{1,0:T(8,128)(2,1)S(1)} collective-permute-done((bf16[80,288]{1,0:T(8,128)(2,1)S(1)}, bf16[80,288]{1,0:T(8,128)(2,1)S(1)}, u32[]{:S(2)}, u32[]{:S(2)}) %collective-permute-start.5) | collective-permute-done | bytes 46112 | tf_op jit(solution)/shard_map/ppermute | solution.py:57
  16.6 0.0 copy-done.2
  16.6 2.9 %shard_map.154 = (bf16[16,4,1024]{2,1,0:T(4,128)(2,1)}, f32[16,16,1024]{2,1,0:T(8,128)}) custom-call(s32[1]{0:T(128)} %bitcast.owner_hbm, s32[16]{0:T(128)} %child_hbm.3, f32[80,1024]{1,0:T(8,128)S(1)} %get-tuple-element.38.act_ref, f32[4,16,1024]{2,1,0:T(8,128)S(1)} %get-tuple-element.39.gate_ref, f32[16,16,1024]{2,1,0:T(8,128)S(1)} %get-tuple-element.43.own_ref, ...), custom_call_target="tpu_custom_call" | custom-call | flops 10485760 | bytes 1310720 | tf_op jit(solution)/shard_map/pallas_call | solution.py:620
  (2 shorter events, 0.0 us)
Async XLA Ops:
  0.6 6.8 %copy-start = (bf16[16,4,2,1024]{3,2,1,0:T(2,128)(2,1)S(1)}, bf16[16,4,2,1024]{3,2,1,0:T(2,128)(2,1)}, u32[]{:S(2)}) copy-start(bf16[16,4,2,1024]{3,2,1,0:T(2,128)(2,1)} %step_ref.1) | copy-start | bytes 786436
  1.8 7.2 %collective-permute-start = (bf16[1,24,1024]{2,1,0:T(8,128)(2,1)S(1)}, bf16[1,24,1024]{2,1,0:T(8,128)(2,1)S(1)}, u32[]{:S(2)}, u32[]{:S(2)}) collective-permute-start(bf16[1,24,1024]{2,1,0:T(8,128)(2,1)S(1)} %get-tuple-element.35), channel_id=1, source_target_pairs={{0,8},{4,12},{8,4},{12,0},{1,9},{5,13},{9,5},{13,1},{2,10},{6,14},... | collective-permute-start | bytes 147464 | tf_op jit(solution)/shard_map/ppermute | solution.py:512
  5.9 4.6 %collective-permute-start.1 = (bf16[1,8,1024]{2,1,0:T(8,128)(2,1)S(1)}, bf16[1,8,1024]{2,1,0:T(8,128)(2,1)S(1)}, u32[]{:S(2)}, u32[]{:S(2)}) collective-permute-start(bf16[1,8,1024]{2,1,0:T(8,128)(2,1)S(1)} %get-tuple-element.36), channel_id=1, source_target_pairs={{0,12},{4,8},{8,0},{12,4},{1,13},{5,9},{9,1},{13,5},{2,14},{6,10},... | collective-permute-start | bytes 49160 | tf_op jit(solution)/shard_map/ppermute | solution.py:512
  7.0 3.7 %collective-permute-start.2 = (bf16[1,8,1024]{2,1,0:T(8,128)(2,1)S(1)}, bf16[1,8,1024]{2,1,0:T(8,128)(2,1)S(1)}, u32[]{:S(2)}, u32[]{:S(2)}) collective-permute-start(bf16[1,8,1024]{2,1,0:T(8,128)(2,1)S(1)} %get-tuple-element.37), channel_id=1, source_target_pairs={{0,4},{4,0},{8,12},{12,8},{1,5},{5,1},{9,13},{13,9},{2,6},{6,2},{1... | collective-permute-start | bytes 49160 | tf_op jit(solution)/shard_map/ppermute | solution.py:512
  7.5 1.6 %copy-start.1 = (f32[1,16,1024]{2,1,0:T(8,128)S(1)}, f32[1,16,1024]{2,1,0:T(8,128)}, u32[]{:S(2)}) copy-start(f32[1,16,1024]{2,1,0:T(8,128)} %rest_4_.1) | copy-start | bytes 196612
  9.0 5.8 %collective-permute-start.4 = (bf16[1,48,1024]{2,1,0:T(8,128)(2,1)S(1)}, bf16[1,48,1024]{2,1,0:T(8,128)(2,1)S(1)}, u32[]{:S(2)}, u32[]{:S(2)}) collective-permute-start(bf16[1,48,1024]{2,1,0:T(8,128)(2,1)S(1)} %shard_map.152), channel_id=1, source_target_pairs={{0,4},{4,0},{8,12},{12,8},{1,5},{5,1},{9,13},{13,9},{2,6},{6,2},{1... | collective-permute-start | bytes 294920 | tf_op jit(solution)/shard_map/ppermute | solution.py:57
  11.2 5.4 %copy-start.2 = (bf16[256,1024]{1,0:T(8,128)(2,1)S(1)}, bf16[256,1024]{1,0:T(8,128)(2,1)}, u32[]{:S(2)}) copy-start(bf16[256,1024]{1,0:T(8,128)(2,1)} %dtw_ref.1) | copy-start | bytes 1572868
  11.2 1.3 %collective-permute-start.3 = (bf16[80,288]{1,0:T(8,128)(2,1)S(1)}, bf16[80,288]{1,0:T(8,128)(2,1)S(1)}, u32[]{:S(2)}, u32[]{:S(2)}) collective-permute-start(bf16[80,288]{1,0:T(8,128)(2,1)S(1)} %get-tuple-element.41), channel_id=1, source_target_pairs={{0,1},{1,0},{2,3},{3,2},{4,5},{5,4},{6,7},{7,6},{8,9},{9,8},{10,11... | collective-permute-start | bytes 138248 | tf_op jit(solution)/shard_map/ppermute | solution.py:57
  12.6 4.0 %collective-permute-start.5 = (bf16[80,288]{1,0:T(8,128)(2,1)S(1)}, bf16[80,288]{1,0:T(8,128)(2,1)S(1)}, u32[]{:S(2)}, u32[]{:S(2)}) collective-permute-start(bf16[80,288]{1,0:T(8,128)(2,1)S(1)} %get-tuple-element.49), channel_id=1, source_target_pairs={{0,3},{1,2},{2,1},{3,0},{4,7},{5,6},{6,5},{7,4},{8,11},{9,10},{10,... | collective-permute-start | bytes 138248 | tf_op jit(solution)/shard_map/ppermute | solution.py:57

commit v22 on v20

--- a/solution.py
+++ b/solution.py
@@ -157,63 +157,38 @@
     direct,
     owner_hbm,
     prompt_hbm,
-    child_hbm,
     step_hbm,
     cw_hbm,
     cb_hbm,
     xwt_hbm,
-    alog_hbm,
-    dtb_hbm,
-    skip_hbm,
     after_ref,
     base_ref,
-    gate_ref,
     pick_ref,
-    child_ref,
     sender_ref,
     cw_ref,
     cb_ref,
     xwt_ref,
-    rate_ref,
-    twin_ref,
-    dtb_ref,
-    skip_ref,
     step_ref,
     owner_s,
     prompt_s,
-    child_s,
-    alog,
     sems,
 ):
     del after_ref
     small = [
         pltpu.make_async_copy(source, target, sems.at[i])
         for i, (source, target) in enumerate(
-            (
-                (cw_hbm, cw_ref),
-                (cb_hbm, cb_ref),
-                (owner_hbm, owner_s),
-                (prompt_hbm, prompt_s),
-                (child_hbm, child_s),
-                (alog_hbm, alog),
-                (dtb_hbm, dtb_ref),
-                (skip_hbm, skip_ref),
-            )
+            ((cw_hbm, cw_ref), (cb_hbm, cb_ref), (owner_hbm, owner_s), (prompt_hbm, prompt_s))
         )
     ]
     inputs = in_parts(step_hbm, step_ref, sems, len(small), STEP_PARTS)
     large = in_parts(xwt_hbm, xwt_ref, sems, len(small) + STEP_PARTS, WEIGHT_PARTS)
     for copy in inputs + small + large:
         copy.start()
-    for copy in inputs:
+    for copy in inputs + small:
         copy.wait()
     steps = step_ref.shape[1]
     taps = cw_hbm.shape[0]
     xs = [step_ref[:, t, 0, :].astype(F32) for t in range(steps)]
-    for t in range(steps):
-        gate_ref[t] = silu(step_ref[:, t, 1, :].astype(F32))
-    for copy in small:
-        copy.wait()
     for t in range(steps):
         total = cw_ref[taps - 1 : taps, :] * xs[t] + cb_ref[...]
         for k in range(max(0, taps - 1 - t), taps - 1):
@@ -221,18 +196,11 @@
         base_ref[t] = total
     places = blocks_of(owner_s[0]) if direct else None
     pick_ref[...] = scalar_onehot(prompt_s, places, pick_ref.shape)
-    child_ref[...] = scalar_onehot(child_s, places, child_ref.shape)
     column = lax.broadcasted_iota(jnp.int32, sender_ref.shape, 1)
     sender = column
     for sent, place in enumerate(places or []):
         sender = jnp.where(column == place, sent, sender)
     sender_ref[...] = sender.astype(F32)
-    rate = jnp.exp(alog[...]) * (-math.log2(math.e))
-    rate_ref[...] = rate
-    half = (twin_ref.shape[1] // 2, rate.shape[1])
-    for m in range(rate.shape[0] // 2):
-        two = [jnp.broadcast_to(rate[n : n + 1, :], half) for n in (2 * m, 2 * m + 1)]
-        twin_ref[m] = jnp.concatenate(two, axis=0)
     for copy in large:
         copy.wait()
 
@@ -287,15 +255,50 @@
     short_ref[...] = total.astype(BF16)
 
 
-def windows_kernel(n_msgs, steps, child_ref, after_ref, *rest):
-    del after_ref
-    msgs, (conv_ref,) = rest[:n_msgs], rest[n_msgs:]
+def late_kernel(n_msgs, direct, *refs):
+    sources, refs = refs[:6], refs[7:]
+    owner_hbm, child_hbm, step_hbm, alog_hbm, dtb_hbm, skip_hbm = sources
+    msgs, refs = refs[:n_msgs], refs[n_msgs:]
+    conv_hbm, gate_ref, rate_ref, twin_ref, dtb_ref, skip_ref = refs[:6]
+    owner_s, child_s, step_ref, alog, conv_s, sems = refs[6:]
+    small = [
+        pltpu.make_async_copy(source, target, sems.at[i])
+        for i, (source, target) in enumerate(
+            (
+                (owner_hbm, owner_s),
+                (child_hbm, child_s),
+                (alog_hbm, alog),
+                (dtb_hbm, dtb_ref),
+                (skip_hbm, skip_ref),
+            )
+        )
+    ]
+    inputs = in_parts(step_hbm, step_ref, sems, len(small), STEP_PARTS)
+    for copy in small + inputs:
+        copy.start()
     held = read_messages(msgs)
-    past = conv_ref.shape[0]
+    past, rb, _ = conv_s.shape
+    steps = step_ref.shape[1]
+    for copy in small:
+        copy.wait()
+    places = blocks_of(owner_s[0]) if direct else None
+    child = scalar_onehot(child_s, places, (rb, len(held)))
     for k in range(past):
         at = steps - past + k
-        rows = [h[at : at + 1, :] for h in held]
-        conv_ref[k] = pick_rows(child_ref[...], rows).astype(BF16)
+        conv_s[k] = pick_rows(child, [h[at : at + 1, :] for h in held]).astype(BF16)
+    out = pltpu.make_async_copy(conv_s, conv_hbm, sems.at[len(small) + STEP_PARTS])
+    out.start()
+    rate = jnp.exp(alog[...]) * (-math.log2(math.e))
+    rate_ref[...] = rate
+    half = (twin_ref.shape[1] // 2, rate.shape[1])
+    for m in range(rate.shape[0] // 2):
+        two = [jnp.broadcast_to(rate[n : n + 1, :], half) for n in (2 * m, 2 * m + 1)]
+        twin_ref[m] = jnp.concatenate(two, axis=0)
+    for copy in inputs:
+        copy.wait()
+    for t in range(steps):
+        gate_ref[t] = silu(step_ref[:, t, 1, :].astype(F32))
+    out.wait()
 
 
 def start_kernel(n_msgs, direct, text, pick_ref, sender_ref, after_ref, *rest):
@@ -520,50 +523,35 @@
         msgs = [lax.all_to_all(msgs[0], "branch", split_axis=0, concat_axis=0, tiled=True)]
         after = msgs[0]
     n_msgs = len(msgs)
-    near = call(
+    base, pick, sender, taps_near, bias_near, weight_near = call(
         functools.partial(prepare_kernel, direct),
         [
             shaped((steps, rb, channels), F32),
-            shaped((steps, rb, channels), F32),
-            shaped((rb, owners), F32),
             shaped((rb, owners), F32),
             shaped((1, owners), F32),
             shaped((taps, channels), F32),
             shaped((1, channels), F32),
             shaped((width, channels), BF16),
-            shaped((n_state, channels), F32),
-            shaped((n_state // 2, 2 * owners, channels), F32),
-            shaped((1, channels), F32),
-            shaped((1, channels), F32),
-        ],
-        [hbm()] * 10 + [anywhere()],
-        [vmem()] * 12,
+        ],
+        [hbm()] * 6 + [anywhere()],
+        [vmem()] * 6,
         [
             pltpu.VMEM(step_in.shape, BF16),
             pltpu.SMEM((1,), jnp.int32),
             pltpu.SMEM((rb,), jnp.int32),
-            pltpu.SMEM((rb,), jnp.int32),
-            pltpu.VMEM((n_state, channels), F32),
-            pltpu.SemaphoreType.DMA((8 + WEIGHT_PARTS + STEP_PARTS,)),
+            pltpu.SemaphoreType.DMA((4 + WEIGHT_PARTS + STEP_PARTS,)),
         ],
         flops=10 * steps * rb * channels,
         nbytes=12 * steps * rb * channels,
-        trans=steps * rb * channels,
     )(
         owner,
         pinned(prompt_of),
-        pinned(child_slot),
         pinned(step_in),
         pinned(conv_weight),
         pinned(conv_bias[None]),
         pinned(x_weight.T),
-        pinned(a_log),
-        pinned(dt_bias[None]),
-        pinned(skip[None]),
         after,
     )
-    base, gate, pick, child_pick, sender, taps_near, bias_near, weight_near = near[:8]
-    rate, twin, dtb_near, skip_near = near[8:]
     states = []
     if direct:
         pair = call(
@@ -601,14 +589,39 @@
         other = swap(brief, "tensor", 2 * distance - 1)
         distance *= 2
 
-    child_conv = call(
-        functools.partial(windows_kernel, n_msgs, steps),
-        shaped((taps - 1, rb, channels), BF16),
-        [vmem(), anywhere()] + [vmem()] * n_msgs,
-        vmem(),
-        flops=2 * owners * taps * rb * channels,
-        nbytes=4 * taps * rb * channels,
-    )(child_pick, part, *msgs)
+    child_conv, gate, rate, twin, dtb_near, skip_near = call(
+        functools.partial(late_kernel, n_msgs, direct),
+        [
+            shaped((taps - 1, rb, channels), BF16),
+            shaped((steps, rb, channels), F32),
+            shaped((n_state, channels), F32),
+            shaped((n_state // 2, 2 * owners, channels), F32),
+            shaped((1, channels), F32),
+            shaped((1, channels), F32),
+        ],
+        [hbm()] * 6 + [anywhere()] + [vmem()] * n_msgs,
+        [anywhere()] + [vmem()] * 5,
+        [
+            pltpu.SMEM((1,), jnp.int32),
+            pltpu.SMEM((rb,), jnp.int32),
+            pltpu.VMEM(step_in.shape, BF16),
+            pltpu.VMEM((n_state, channels), F32),
+            pltpu.VMEM((taps - 1, rb, channels), BF16),
+            pltpu.SemaphoreType.DMA((6 + STEP_PARTS,)),
+        ],
+        flops=10 * steps * rb * channels,
+        nbytes=12 * steps * rb * channels,
+        trans=steps * rb * channels,
+    )(
+        owner,
+        pinned(child_slot),
+        pinned(step_in),
+        pinned(a_log),
+        pinned(dt_bias[None]),
+        pinned(skip[None]),
+        part,
+        *msgs,
+    )
     own_start, slot_start = call(
         functools.partial(start_kernel, n_msgs, direct, short),
         [

time: 19.6 us -> 19.7 us (level)
  Pallas kernels: 7.42 us -> 8.24 us
  waiting for transfers between devices: 2.49 us -> 1.76 us
    ppermute x3, waiting for transfers between devices: 2.47 us -> 1.45 us  [swap(): return lax.ppermute(value, axis, [(i, i ^ distance) for i in range(size)])]
    pallas_call x1, Pallas kernels: 0.78 us -> 1.78 us  [on_device(): call(functools.partial(late_kernel, n_msgs, direct), [shaped((taps - 1, r...]
    ppermute x3, waiting for transfers between devices: 0.02 us -> 0.31 us  [on_device(): lax.ppermute(m, 'branch', list(enumerate(to)))]
  transfers between devices with their start and end apart: 6 -> 6, of which waited for: 2 -> 4; matrix products, arithmetic and copies ran while one was open for 0% -> 0% of each run, Pallas kernels for 18% -> 22%
where the time goes in v22:
time: 19.7 us; the launch traced here: 19.4 us
  starting transfers between devices  8.7 us (44%)
  Pallas kernels  8.24 us (42%)
  waiting for transfers between devices  1.76 us (9%)
  between operations  0.71 us (4%)
    ppermute x3, starting transfers between devices, on_device(): lax.ppermute(m, 'branch', list(enumerate(to)))  5.67 us
    ppermute x3, starting transfers between devices, swap(): return lax.ppermute(value, axis, [(i, i ^ distance) for i in range(size)])  3.03 us
    pallas_call x1, Pallas kernels, on_device(): call(functools.partial(decode_kernel, direct), [shaped((rb, steps, channe...  2.88 us
    pallas_call x1, Pallas kernels, on_device(): call(functools.partial(late_kernel, n_msgs, direct), [shaped((taps - 1, r...  1.78 us
    ppermute x3, waiting for transfers between devices, swap(): return lax.ppermute(value, axis, [(i, i ^ distance) for i in range(size)])  1.45 us
    pallas_call x1, Pallas kernels, on_device(): call(functools.partial(prepare_kernel, direct), [shaped((steps, rb, chann...  1.41 us
    pallas_call x1, Pallas kernels, on_device(): call(functools.partial(pack_kernel, direct), [shaped(s, BF16) for s in ms...  1.11 us
    pallas_call x1, Pallas kernels, on_device(): call(functools.partial(start_kernel, n_msgs, direct, short), [shaped((n_s...  0.53 us
  transfers between devices with their start and end apart: 6, of which 4 were waited for; matrix products, arithmetic and copies ran while one was open for 0% of the time, Pallas kernels for 22%

profile of v22, /device:TPU:0, one launch (start us, length us, event | category | flops | bytes accessed | tf_op | source)
XLA Modules:
  0.0 19.4 jit_solution(6891789886772620496)
XLA Ops:
  0.6 1.1 %shard_map.148 = (bf16[1,8,1024]{2,1,0:T(8,128)(2,1)S(1)}, bf16[1,24,1024]{2,1,0:T(8,128)(2,1)S(1)}, bf16[1,8,1024]{2,1,0:T(8,128)(2,1)S(1)}, bf16[1,8,1024]{2,1,0:T(8,128)(2,1)S(1)}) custom-call(s32[1]{0:T(128)} %bitcast.owner_hbm.refs_0_, s32[4]{0:T(128)} %bitcast.11, s32[16]{0:T(128)} %prompt_hbm.3, bf16[16,4,2,1024]{3,2,1,0:T(2,128)(2,1)} %refs_2_.1, ...), custom_call_target="tpu_custom_call" | custom-call | bytes 196608 | tf_op jit(solution)/shard_map/pallas_call | solution.py:493
  1.8 4.1 %collective-permute-start = (bf16[1,24,1024]{2,1,0:T(8,128)(2,1)S(1)}, bf16[1,24,1024]{2,1,0:T(8,128)(2,1)S(1)}, u32[]{:S(2)}, u32[]{:S(2)}) collective-permute-start(bf16[1,24,1024]{2,1,0:T(8,128)(2,1)S(1)} %get-tuple-element.35), channel_id=1, source_target_pairs={{0,8},{4,12},{8,4},{12,0},{1,9},{5,13},{9,5},{13,1},{2,10},{6,14},... | collective-permute-start | bytes 147464 | tf_op jit(solution)/shard_map/ppermute | solution.py:519
  5.8 1.1 %collective-permute-start.1 = (bf16[1,8,1024]{2,1,0:T(8,128)(2,1)S(1)}, bf16[1,8,1024]{2,1,0:T(8,128)(2,1)S(1)}, u32[]{:S(2)}, u32[]{:S(2)}) collective-permute-start(bf16[1,8,1024]{2,1,0:T(8,128)(2,1)S(1)} %get-tuple-element.36), channel_id=1, source_target_pairs={{0,12},{4,8},{8,0},{12,4},{1,13},{5,9},{9,1},{13,5},{2,14},{6,10},... | collective-permute-start | bytes 49160 | tf_op jit(solution)/shard_map/ppermute | solution.py:519
  6.9 0.5 %collective-permute-start.2 = (bf16[1,8,1024]{2,1,0:T(8,128)(2,1)S(1)}, bf16[1,8,1024]{2,1,0:T(8,128)(2,1)S(1)}, u32[]{:S(2)}, u32[]{:S(2)}) collective-permute-start(bf16[1,8,1024]{2,1,0:T(8,128)(2,1)S(1)} %get-tuple-element.37), channel_id=1, source_target_pairs={{0,4},{4,0},{8,12},{12,8},{1,5},{5,1},{9,13},{13,9},{2,6},{6,2},{1... | collective-permute-start | bytes 49160 | tf_op jit(solution)/shard_map/ppermute | solution.py:519
  7.4 0.0 copy-start
  7.4 1.4 %shard_map.149 = (f32[4,16,1024]{2,1,0:T(8,128)S(1)}, f32[16,4]{1,0:T(8,128)S(1)}, f32[1,4]{1,0:T(1,128)S(1)}, f32[4,1024]{1,0:T(4,128)S(1)}, f32[1,1024]{1,0:T(1,128)S(1)}, /*index=5*/bf16[288,1024]{1,0:T(8,128)(2,1)S(1)}) custom-call(s32[1]{0:T(128)} %bitcast.owner_hbm.refs_0_, s32[16]{0:T(128)} %prompt_hbm.3, bf16[16,4,2,1024]{3,2,1,0:T(2,128)(2,1)} %refs_2_.1, ...), custom_call_target="tpu_custom_call" | custom-call | flops 655360 | bytes 786432 | tf_op jit(solution)/shard_map/pallas_call | solution.py:526
  8.8 0.1 collective-permute-done.rest_1_.refs_8_.came_ref
  9.0 0.0 copy-done
  9.0 1.5 %collective-permute-start.4 = (bf16[1,48,1024]{2,1,0:T(8,128)(2,1)S(1)}, bf16[1,48,1024]{2,1,0:T(8,128)(2,1)S(1)}, u32[]{:S(2)}, u32[]{:S(2)}) collective-permute-start(bf16[1,48,1024]{2,1,0:T(8,128)(2,1)S(1)} %shard_map.153), channel_id=1, source_target_pairs={{0,4},{4,0},{8,12},{12,8},{1,5},{5,1},{9,13},{13,9},{2,6},{6,2},{1... | collective-permute-start | bytes 294920 | tf_op jit(solution)/shard_map/ppermute | solution.py:57
  10.5 0.0 collective-permute-done.1.rest_2_.refs_9_
  10.5 0.2 collective-permute-done.2.rest_3_.refs_10_
  10.7 0.5 %shard_map.150 = (f32[80,1024]{1,0:T(8,128)S(1)}, f32[80,288]{1,0:T(8,128)S(1)}, bf16[80,288]{1,0:T(8,128)(2,1)S(1)}) custom-call(f32[16,4]{1,0:T(8,128)S(1)} %get-tuple-element.29.pick_ref.after_ref, f32[1,4]{1,0:T(1,128)S(1)} %get-tuple-element.30.sender_ref, f32[4,16,1024]{2,1,0:T(8,128)S(1)} %get-tuple-element.31.base_ref, ...), custom_call_target="tpu_custom_call" | custom-call | flops 47185920 | bytes 1009664 | tf_op jit(solution)/shard_map/pallas_call | solution.py:565
  11.2 0.1 collective-permute-start.3
  11.2 1.2 %collective-permute-done.3.b_ref = bf16[80,288]{1,0:T(8,128)(2,1)S(1)} collective-permute-done((bf16[80,288]{1,0:T(8,128)(2,1)S(1)}, bf16[80,288]{1,0:T(8,128)(2,1)S(1)}, u32[]{:S(2)}, u32[]{:S(2)}) %collective-permute-start.3) | collective-permute-done | bytes 46112 | tf_op jit(solution)/shard_map/ppermute | solution.py:57
  12.5 0.0 copy-start.1
  12.5 1.5 %collective-permute-start.5 = (bf16[80,288]{1,0:T(8,128)(2,1)S(1)}, bf16[80,288]{1,0:T(8,128)(2,1)S(1)}, u32[]{:S(2)}, u32[]{:S(2)}) collective-permute-start(bf16[80,288]{1,0:T(8,128)(2,1)S(1)} %get-tuple-element.49), channel_id=1, source_target_pairs={{0,3},{1,2},{2,1},{3,0},{4,7},{5,6},{6,5},{7,4},{8,11},{9,10},{10,... | collective-permute-start | bytes 138248 | tf_op jit(solution)/shard_map/ppermute | solution.py:57
  14.0 1.8 %shard_map.152 = (bf16[3,16,1024]{2,1,0:T(8,128)(2,1)}, f32[4,16,1024]{2,1,0:T(8,128)S(1)}, f32[16,1024]{1,0:T(8,128)S(1)}, f32[8,8,1024]{2,1,0:T(8,128)S(1)}, f...) custom-call(s32[1]{0:T(128)} %bitcast.owner_hbm.refs_0_, s32[16]{0:T(128)} %child_hbm.1, bf16[16,4,2,1024]{3,2,1,0:T(2,128)(2,1)} %refs_2_.1, ...), custom_call_target="tpu_custom_call" | custom-call | flops 655360 | bytes 786432 | tf_op jit(solution)/shard_map/pallas_call | solution.py:592
  15.8 0.0 collective-permute-done.4.rest_5_
  15.8 0.5 %shard_map.154 = (f32[16,16,1024]{2,1,0:T(8,128)S(1)}, f32[8,8,1024]{2,1,0:T(8,128)S(1)}) custom-call(f32[16,4]{1,0:T(8,128)S(1)} %get-tuple-element.29.pick_ref.after_ref, f32[1,4]{1,0:T(1,128)S(1)} %get-tuple-element.30.sender_ref, f32[80,288]{1,0:T(8,128)S(1)} %get-tuple-element.41.refs_6_.after_ref.part_ref, ...), custom_call_target="tpu_custom_call" | custom-call | flops 2621440 | bytes 1310720 | tf_op jit(solution)/shard_map/pallas_call | solution.py:625
  16.3 0.2 %collective-permute-done.5.other_ref = bf16[80,288]{1,0:T(8,128)(2,1)S(1)} collective-permute-done((bf16[80,288]{1,0:T(8,128)(2,1)S(1)}, bf16[80,288]{1,0:T(8,128)(2,1)S(1)}, u32[]{:S(2)}, u32[]{:S(2)}) %collective-permute-start.5) | collective-permute-done | bytes 46112 | tf_op jit(solution)/shard_map/ppermute | solution.py:57
  16.5 0.0 copy-done.1
  16.5 2.9 %shard_map.155 = (bf16[16,4,1024]{2,1,0:T(4,128)(2,1)}, f32[16,16,1024]{2,1,0:T(8,128)}) custom-call(s32[1]{0:T(128)} %bitcast.owner_hbm.refs_0_, s32[16]{0:T(128)} %child_hbm.1, f32[80,1024]{1,0:T(8,128)S(1)} %get-tuple-element.38.act_ref, f32[4,16,1024]{2,1,0:T(8,128)S(1)} %get-tuple-element.42.gate_ref, f32[16,16,1024]{2,1,0:T(8,128)S(1)} %get-tuple-element.43.own_ref, ...), custom_call_target="tpu_custom_call" | custom-call | flops 10485760 | bytes 1310720 | tf_op jit(solution)/shard_map/pallas_call | solution.py:638
  (2 shorter events, 0.0 us)
Async XLA Ops:
  1.8 7.2 %collective-permute-start = (bf16[1,24,1024]{2,1,0:T(8,128)(2,1)S(1)}, bf16[1,24,1024]{2,1,0:T(8,128)(2,1)S(1)}, u32[]{:S(2)}, u32[]{:S(2)}) collective-permute-start(bf16[1,24,1024]{2,1,0:T(8,128)(2,1)S(1)} %get-tuple-element.35), channel_id=1, source_target_pairs={{0,8},{4,12},{8,4},{12,0},{1,9},{5,13},{9,5},{13,1},{2,10},{6,14},... | collective-permute-start | bytes 147464 | tf_op jit(solution)/shard_map/ppermute | solution.py:519
  5.8 4.6 %collective-permute-start.1 = (bf16[1,8,1024]{2,1,0:T(8,128)(2,1)S(1)}, bf16[1,8,1024]{2,1,0:T(8,128)(2,1)S(1)}, u32[]{:S(2)}, u32[]{:S(2)}) collective-permute-start(bf16[1,8,1024]{2,1,0:T(8,128)(2,1)S(1)} %get-tuple-element.36), channel_id=1, source_target_pairs={{0,12},{4,8},{8,0},{12,4},{1,13},{5,9},{9,1},{13,5},{2,14},{6,10},... | collective-permute-start | bytes 49160 | tf_op jit(solution)/shard_map/ppermute | solution.py:519
  6.9 3.7 %collective-permute-start.2 = (bf16[1,8,1024]{2,1,0:T(8,128)(2,1)S(1)}, bf16[1,8,1024]{2,1,0:T(8,128)(2,1)S(1)}, u32[]{:S(2)}, u32[]{:S(2)}) collective-permute-start(bf16[1,8,1024]{2,1,0:T(8,128)(2,1)S(1)} %get-tuple-element.37), channel_id=1, source_target_pairs={{0,4},{4,0},{8,12},{12,8},{1,5},{5,1},{9,13},{13,9},{2,6},{6,2},{1... | collective-permute-start | bytes 49160 | tf_op jit(solution)/shard_map/ppermute | solution.py:519
  7.4 1.6 %copy-start = (f32[1,16,1024]{2,1,0:T(8,128)S(1)}, f32[1,16,1024]{2,1,0:T(8,128)}, u32[]{:S(2)}) copy-start(f32[1,16,1024]{2,1,0:T(8,128)} %rest_4_.1) | copy-start | bytes 196612
  9.0 6.8 %collective-permute-start.4 = (bf16[1,48,1024]{2,1,0:T(8,128)(2,1)S(1)}, bf16[1,48,1024]{2,1,0:T(8,128)(2,1)S(1)}, u32[]{:S(2)}, u32[]{:S(2)}) collective-permute-start(bf16[1,48,1024]{2,1,0:T(8,128)(2,1)S(1)} %shard_map.153), channel_id=1, source_target_pairs={{0,4},{4,0},{8,12},{12,8},{1,5},{5,1},{9,13},{13,9},{2,6},{6,2},{1... | collective-permute-start | bytes 294920 | tf_op jit(solution)/shard_map/ppermute | solution.py:57
  11.2 1.3 %collective-permute-start.3 = (bf16[80,288]{1,0:T(8,128)(2,1)S(1)}, bf16[80,288]{1,0:T(8,128)(2,1)S(1)}, u32[]{:S(2)}, u32[]{:S(2)}) collective-permute-start(bf16[80,288]{1,0:T(8,128)(2,1)S(1)} %get-tuple-element.40), channel_id=1, source_target_pairs={{0,1},{1,0},{2,3},{3,2},{4,5},{5,4},{6,7},{7,6},{8,9},{9,8},{10,11... | collective-permute-start | bytes 138248 | tf_op jit(solution)/shard_map/ppermute | solution.py:57
  12.5 4.0 %copy-start.1 = (bf16[256,1024]{1,0:T(8,128)(2,1)S(1)}, bf16[256,1024]{1,0:T(8,128)(2,1)}, u32[]{:S(2)}) copy-start(bf16[256,1024]{1,0:T(8,128)(2,1)} %dtw_ref.1) | copy-start | bytes 1572868
  12.5 4.0 %collective-permute-start.5 = (bf16[80,288]{1,0:T(8,128)(2,1)S(1)}, bf16[80,288]{1,0:T(8,128)(2,1)S(1)}, u32[]{:S(2)}, u32[]{:S(2)}) collective-permute-start(bf16[80,288]{1,0:T(8,128)(2,1)S(1)} %get-tuple-element.49), channel_id=1, source_target_pairs={{0,3},{1,2},{2,1},{3,0},{4,7},{5,6},{6,5},{7,4},{8,11},{9,10},{10,... | collective-permute-start | bytes 138248 | tf_op jit(solution)/shard_map/ppermute | solution.py:57

commit v23 on v22

--- a/solution.py
+++ b/solution.py
@@ -205,6 +205,10 @@
         copy.wait()
 
 
+def softplus(v):
+    return jnp.maximum(v, 0.0) + jnp.log(1.0 + jnp.exp(-jnp.abs(v)))
+
+
 def slot_onehot(numbers, sender_ref):
     owners = sender_ref.shape[1]
     return (numbers[:, :owners] == sender_ref[...]).astype(F32)
@@ -378,28 +382,24 @@
 
     proj = part_ref[...] + other_ref[...].astype(F32)
     delta_in = proj[:, :rank].astype(BF16)
-    delta = jnp.dot(delta_in, dtw_ref[...], preferred_element_type=F32) + dtb_ref[...]
-    delta = jnp.maximum(delta, 0.0) + jnp.log(1.0 + jnp.exp(-jnp.abs(delta)))
-    gain = delta * act_ref[...]
-    delta_s[...] = delta[:own_rows, :]
-    gain_s[...] = gain[:own_rows, :]
+    raw = jnp.dot(delta_in, dtw_ref[...], preferred_element_type=F32) + dtb_ref[...]
+    delta_s[...] = raw[:own_rows, :]
+    delta = softplus(raw[own_rows:, :])
+    gain = delta * act_ref[own_rows:, :]
 
     def column(at, n, rows):
         return jnp.broadcast_to(at[:, n : n + 1], (rows, LANES))
 
     for t in range(steps):
-        at = slice(own_rows + t * n_slots, own_rows + (t + 1) * n_slots)
+        at = slice(t * n_slots, (t + 1) * n_slots)
         slot_delta_s[t] = jnp.concatenate([delta[at, :]] * 2, axis=0)
         slot_gain_s[t] = jnp.concatenate([gain[at, :]] * 2, axis=0)
-        twice = jnp.concatenate([proj[at, rank:]] * 2, axis=0)
+        twice = jnp.concatenate([proj[own_rows:, rank:][at, :]] * 2, axis=0)
         upper = lax.broadcasted_iota(jnp.int32, (2 * n_slots, LANES), 0) < n_slots
         for m in range(n_state // 2):
             twin_b_s[m, t] = jnp.where(
                 upper, column(twice, 2 * m, 2 * n_slots), column(twice, 2 * m + 1, 2 * n_slots)
             )
-    for n in range(n_state):
-        b_s[n] = column(proj[:own_rows, rank:], n, own_rows)
-        c_s[n] = column(proj[:own_rows, rank:], n_state + n, own_rows)
 
     def wide(part):
         return jnp.concatenate([part] * WIDE, axis=1)
@@ -427,6 +427,14 @@
         copy = pltpu.make_async_copy(slots_s.at[at], child_ssm.at[j], sems.at[2 + j])
         copy.start()
         copies.append(copy)
+
+    delta = softplus(delta_s[...])
+    delta_s[...] = delta
+    gain_s[...] = delta * act_ref[:own_rows, :]
+    proj = part_ref[:own_rows, rank:] + other_ref[:own_rows, rank:].astype(F32)
+    for n in range(n_state):
+        b_s[n] = column(proj, n, own_rows)
+        c_s[n] = column(proj, n_state + n, own_rows)
 
     def own_chunk(chunk, carry):
         columns = pl.ds(pl.multiple_of(chunk * WIDE * LANES, WIDE * LANES), WIDE * LANES)

time: 19.7 us -> 19.9 us (1.010)
  Pallas kernels: 8.24 us -> 8.46 us
    pallas_call x1, Pallas kernels: 2.88 us -> 3.1 us  [on_device(): call(functools.partial(decode_kernel, direct), [shaped((rb, steps, channe...]
where the time goes in v23:
time: 19.9 us; the launch traced here: 19.6 us
  starting transfers between devices  8.7 us (44%)
  Pallas kernels  8.46 us (43%)
  waiting for transfers between devices  1.76 us (9%)
  between operations  0.71 us (4%)
    ppermute x3, starting transfers between devices, on_device(): lax.ppermute(m, 'branch', list(enumerate(to)))  5.67 us
    pallas_call x1, Pallas kernels, on_device(): call(functools.partial(decode_kernel, direct), [shaped((rb, steps, channe...  3.1 us
    ppermute x3, starting transfers between devices, swap(): return lax.ppermute(value, axis, [(i, i ^ distance) for i in range(size)])  3.03 us
    pallas_call x1, Pallas kernels, on_device(): call(functools.partial(late_kernel, n_msgs, direct), [shaped((taps - 1, r...  1.78 us
    ppermute x3, waiting for transfers between devices, swap(): return lax.ppermute(value, axis, [(i, i ^ distance) for i in range(size)])  1.45 us
    pallas_call x1, Pallas kernels, on_device(): call(functools.partial(prepare_kernel, direct), [shaped((steps, rb, chann...  1.41 us
    pallas_call x1, Pallas kernels, on_device(): call(functools.partial(pack_kernel, direct), [shaped(s, BF16) for s in ms...  1.11 us
    pallas_call x1, Pallas kernels, on_device(): call(functools.partial(start_kernel, n_msgs, direct, short), [shaped((n_s...  0.53 us
  transfers between devices with their start and end apart: 6, of which 4 were waited for; matrix products, arithmetic and copies ran while one was open for 0% of the time, Pallas kernels for 22%

profile of v23, /device:TPU:0, one launch (start us, length us, event | category | flops | bytes accessed | tf_op | source)
XLA Modules:
  0.0 19.6 jit_solution(1029875344045245050)
XLA Ops:
  0.6 1.1 %shard_map.148 = (bf16[1,8,1024]{2,1,0:T(8,128)(2,1)S(1)}, bf16[1,24,1024]{2,1,0:T(8,128)(2,1)S(1)}, bf16[1,8,1024]{2,1,0:T(8,128)(2,1)S(1)}, bf16[1,8,1024]{2,1,0:T(8,128)(2,1)S(1)}) custom-call(s32[1]{0:T(128)} %bitcast.owner_hbm.refs_0_, s32[4]{0:T(128)} %bitcast.11, s32[16]{0:T(128)} %prompt_hbm.3, bf16[16,4,2,1024]{3,2,1,0:T(2,128)(2,1)} %refs_2_.1, ...), custom_call_target="tpu_custom_call" | custom-call | bytes 196608 | tf_op jit(solution)/shard_map/pallas_call | solution.py:501
  1.8 4.1 %collective-permute-start = (bf16[1,24,1024]{2,1,0:T(8,128)(2,1)S(1)}, bf16[1,24,1024]{2,1,0:T(8,128)(2,1)S(1)}, u32[]{:S(2)}, u32[]{:S(2)}) collective-permute-start(bf16[1,24,1024]{2,1,0:T(8,128)(2,1)S(1)} %get-tuple-element.35), channel_id=1, source_target_pairs={{0,8},{4,12},{8,4},{12,0},{1,9},{5,13},{9,5},{13,1},{2,10},{6,14},... | collective-permute-start | bytes 147464 | tf_op jit(solution)/shard_map/ppermute | solution.py:527
  5.8 1.1 %collective-permute-start.1 = (bf16[1,8,1024]{2,1,0:T(8,128)(2,1)S(1)}, bf16[1,8,1024]{2,1,0:T(8,128)(2,1)S(1)}, u32[]{:S(2)}, u32[]{:S(2)}) collective-permute-start(bf16[1,8,1024]{2,1,0:T(8,128)(2,1)S(1)} %get-tuple-element.36), channel_id=1, source_target_pairs={{0,12},{4,8},{8,0},{12,4},{1,13},{5,9},{9,1},{13,5},{2,14},{6,10},... | collective-permute-start | bytes 49160 | tf_op jit(solution)/shard_map/ppermute | solution.py:527
  6.9 0.5 %collective-permute-start.2 = (bf16[1,8,1024]{2,1,0:T(8,128)(2,1)S(1)}, bf16[1,8,1024]{2,1,0:T(8,128)(2,1)S(1)}, u32[]{:S(2)}, u32[]{:S(2)}) collective-permute-start(bf16[1,8,1024]{2,1,0:T(8,128)(2,1)S(1)} %get-tuple-element.37), channel_id=1, source_target_pairs={{0,4},{4,0},{8,12},{12,8},{1,5},{5,1},{9,13},{13,9},{2,6},{6,2},{1... | collective-permute-start | bytes 49160 | tf_op jit(solution)/shard_map/ppermute | solution.py:527
  7.4 0.0 copy-start
  7.4 1.4 %shard_map.149 = (f32[4,16,1024]{2,1,0:T(8,128)S(1)}, f32[16,4]{1,0:T(8,128)S(1)}, f32[1,4]{1,0:T(1,128)S(1)}, f32[4,1024]{1,0:T(4,128)S(1)}, f32[1,1024]{1,0:T(1,128)S(1)}, /*index=5*/bf16[288,1024]{1,0:T(8,128)(2,1)S(1)}) custom-call(s32[1]{0:T(128)} %bitcast.owner_hbm.refs_0_, s32[16]{0:T(128)} %prompt_hbm.3, bf16[16,4,2,1024]{3,2,1,0:T(2,128)(2,1)} %refs_2_.1, ...), custom_call_target="tpu_custom_call" | custom-call | flops 655360 | bytes 786432 | tf_op jit(solution)/shard_map/pallas_call | solution.py:534
  8.8 0.1 collective-permute-done.rest_1_.refs_8_.came_ref
  9.0 0.0 copy-done
  9.0 1.5 %collective-permute-start.4 = (bf16[1,48,1024]{2,1,0:T(8,128)(2,1)S(1)}, bf16[1,48,1024]{2,1,0:T(8,128)(2,1)S(1)}, u32[]{:S(2)}, u32[]{:S(2)}) collective-permute-start(bf16[1,48,1024]{2,1,0:T(8,128)(2,1)S(1)} %shard_map.153), channel_id=1, source_target_pairs={{0,4},{4,0},{8,12},{12,8},{1,5},{5,1},{9,13},{13,9},{2,6},{6,2},{1... | collective-permute-start | bytes 294920 | tf_op jit(solution)/shard_map/ppermute | solution.py:57
  10.5 0.0 collective-permute-done.1.rest_2_.refs_9_
  10.5 0.2 collective-permute-done.2.rest_3_.refs_10_
  10.7 0.5 %shard_map.150 = (f32[80,1024]{1,0:T(8,128)S(1)}, f32[80,288]{1,0:T(8,128)S(1)}, bf16[80,288]{1,0:T(8,128)(2,1)S(1)}) custom-call(f32[16,4]{1,0:T(8,128)S(1)} %get-tuple-element.29.pick_ref.after_ref, f32[1,4]{1,0:T(1,128)S(1)} %get-tuple-element.30.sender_ref, f32[4,16,1024]{2,1,0:T(8,128)S(1)} %get-tuple-element.31.base_ref, ...), custom_call_target="tpu_custom_call" | custom-call | flops 47185920 | bytes 1009664 | tf_op jit(solution)/shard_map/pallas_call | solution.py:573
  11.2 0.1 collective-permute-start.3
  11.2 1.2 %collective-permute-done.3.b_ref = bf16[80,288]{1,0:T(8,128)(2,1)S(1)} collective-permute-done((bf16[80,288]{1,0:T(8,128)(2,1)S(1)}, bf16[80,288]{1,0:T(8,128)(2,1)S(1)}, u32[]{:S(2)}, u32[]{:S(2)}) %collective-permute-start.3) | collective-permute-done | bytes 46112 | tf_op jit(solution)/shard_map/ppermute | solution.py:57
  12.5 0.0 copy-start.1
  12.5 1.5 %collective-permute-start.5 = (bf16[80,288]{1,0:T(8,128)(2,1)S(1)}, bf16[80,288]{1,0:T(8,128)(2,1)S(1)}, u32[]{:S(2)}, u32[]{:S(2)}) collective-permute-start(bf16[80,288]{1,0:T(8,128)(2,1)S(1)} %get-tuple-element.49), channel_id=1, source_target_pairs={{0,3},{1,2},{2,1},{3,0},{4,7},{5,6},{6,5},{7,4},{8,11},{9,10},{10,... | collective-permute-start | bytes 138248 | tf_op jit(solution)/shard_map/ppermute | solution.py:57
  14.0 1.8 %shard_map.152 = (bf16[3,16,1024]{2,1,0:T(8,128)(2,1)}, f32[4,16,1024]{2,1,0:T(8,128)S(1)}, f32[16,1024]{1,0:T(8,128)S(1)}, f32[8,8,1024]{2,1,0:T(8,128)S(1)}, f...) custom-call(s32[1]{0:T(128)} %bitcast.owner_hbm.refs_0_, s32[16]{0:T(128)} %child_hbm.1, bf16[16,4,2,1024]{3,2,1,0:T(2,128)(2,1)} %refs_2_.1, ...), custom_call_target="tpu_custom_call" | custom-call | flops 655360 | bytes 786432 | tf_op jit(solution)/shard_map/pallas_call | solution.py:600
  15.8 0.0 collective-permute-done.4.rest_5_
  15.8 0.5 %shard_map.154 = (f32[16,16,1024]{2,1,0:T(8,128)S(1)}, f32[8,8,1024]{2,1,0:T(8,128)S(1)}) custom-call(f32[16,4]{1,0:T(8,128)S(1)} %get-tuple-element.29.pick_ref.after_ref, f32[1,4]{1,0:T(1,128)S(1)} %get-tuple-element.30.sender_ref, f32[80,288]{1,0:T(8,128)S(1)} %get-tuple-element.41.refs_6_.after_ref.part_ref, ...), custom_call_target="tpu_custom_call" | custom-call | flops 2621440 | bytes 1310720 | tf_op jit(solution)/shard_map/pallas_call | solution.py:633
  16.3 0.2 %collective-permute-done.5.other_ref = bf16[80,288]{1,0:T(8,128)(2,1)S(1)} collective-permute-done((bf16[80,288]{1,0:T(8,128)(2,1)S(1)}, bf16[80,288]{1,0:T(8,128)(2,1)S(1)}, u32[]{:S(2)}, u32[]{:S(2)}) %collective-permute-start.5) | collective-permute-done | bytes 46112 | tf_op jit(solution)/shard_map/ppermute | solution.py:57
  16.5 0.0 copy-done.1
  16.5 3.1 %shard_map.155 = (bf16[16,4,1024]{2,1,0:T(4,128)(2,1)}, f32[16,16,1024]{2,1,0:T(8,128)}) custom-call(s32[1]{0:T(128)} %bitcast.owner_hbm.refs_0_, s32[16]{0:T(128)} %child_hbm.1, f32[80,1024]{1,0:T(8,128)S(1)} %get-tuple-element.38.act_ref, f32[4,16,1024]{2,1,0:T(8,128)S(1)} %get-tuple-element.42.gate_ref, f32[16,16,1024]{2,1,0:T(8,128)S(1)} %get-tuple-element.43.own_ref, ...), custom_call_target="tpu_custom_call" | custom-call | flops 10485760 | bytes 1310720 | tf_op jit(solution)/shard_map/pallas_call | solution.py:646
  (2 shorter events, 0.0 us)
Async XLA Ops:
  1.8 7.2 %collective-permute-start = (bf16[1,24,1024]{2,1,0:T(8,128)(2,1)S(1)}, bf16[1,24,1024]{2,1,0:T(8,128)(2,1)S(1)}, u32[]{:S(2)}, u32[]{:S(2)}) collective-permute-start(bf16[1,24,1024]{2,1,0:T(8,128)(2,1)S(1)} %get-tuple-element.35), channel_id=1, source_target_pairs={{0,8},{4,12},{8,4},{12,0},{1,9},{5,13},{9,5},{13,1},{2,10},{6,14},... | collective-permute-start | bytes 147464 | tf_op jit(solution)/shard_map/ppermute | solution.py:527
  5.8 4.6 %collective-permute-start.1 = (bf16[1,8,1024]{2,1,0:T(8,128)(2,1)S(1)}, bf16[1,8,1024]{2,1,0:T(8,128)(2,1)S(1)}, u32[]{:S(2)}, u32[]{:S(2)}) collective-permute-start(bf16[1,8,1024]{2,1,0:T(8,128)(2,1)S(1)} %get-tuple-element.36), channel_id=1, source_target_pairs={{0,12},{4,8},{8,0},{12,4},{1,13},{5,9},{9,1},{13,5},{2,14},{6,10},... | collective-permute-start | bytes 49160 | tf_op jit(solution)/shard_map/ppermute | solution.py:527
  6.9 3.7 %collective-permute-start.2 = (bf16[1,8,1024]{2,1,0:T(8,128)(2,1)S(1)}, bf16[1,8,1024]{2,1,0:T(8,128)(2,1)S(1)}, u32[]{:S(2)}, u32[]{:S(2)}) collective-permute-start(bf16[1,8,1024]{2,1,0:T(8,128)(2,1)S(1)} %get-tuple-element.37), channel_id=1, source_target_pairs={{0,4},{4,0},{8,12},{12,8},{1,5},{5,1},{9,13},{13,9},{2,6},{6,2},{1... | collective-permute-start | bytes 49160 | tf_op jit(solution)/shard_map/ppermute | solution.py:527
  7.4 1.6 %copy-start = (f32[1,16,1024]{2,1,0:T(8,128)S(1)}, f32[1,16,1024]{2,1,0:T(8,128)}, u32[]{:S(2)}) copy-start(f32[1,16,1024]{2,1,0:T(8,128)} %rest_4_.1) | copy-start | bytes 196612
  9.0 6.8 %collective-permute-start.4 = (bf16[1,48,1024]{2,1,0:T(8,128)(2,1)S(1)}, bf16[1,48,1024]{2,1,0:T(8,128)(2,1)S(1)}, u32[]{:S(2)}, u32[]{:S(2)}) collective-permute-start(bf16[1,48,1024]{2,1,0:T(8,128)(2,1)S(1)} %shard_map.153), channel_id=1, source_target_pairs={{0,4},{4,0},{8,12},{12,8},{1,5},{5,1},{9,13},{13,9},{2,6},{6,2},{1... | collective-permute-start | bytes 294920 | tf_op jit(solution)/shard_map/ppermute | solution.py:57
  11.2 1.3 %collective-permute-start.3 = (bf16[80,288]{1,0:T(8,128)(2,1)S(1)}, bf16[80,288]{1,0:T(8,128)(2,1)S(1)}, u32[]{:S(2)}, u32[]{:S(2)}) collective-permute-start(bf16[80,288]{1,0:T(8,128)(2,1)S(1)} %get-tuple-element.40), channel_id=1, source_target_pairs={{0,1},{1,0},{2,3},{3,2},{4,5},{5,4},{6,7},{7,6},{8,9},{9,8},{10,11... | collective-permute-start | bytes 138248 | tf_op jit(solution)/shard_map/ppermute | solution.py:57
  12.5 4.0 %copy-start.1 = (bf16[256,1024]{1,0:T(8,128)(2,1)S(1)}, bf16[256,1024]{1,0:T(8,128)(2,1)}, u32[]{:S(2)}) copy-start(bf16[256,1024]{1,0:T(8,128)(2,1)} %dtw_ref.1) | copy-start | bytes 1572868
  12.5 4.0 %collective-permute-start.5 = (bf16[80,288]{1,0:T(8,128)(2,1)S(1)}, bf16[80,288]{1,0:T(8,128)(2,1)S(1)}, u32[]{:S(2)}, u32[]{:S(2)}) collective-permute-start(bf16[80,288]{1,0:T(8,128)(2,1)S(1)} %get-tuple-element.49), channel_id=1, source_target_pairs={{0,3},{1,2},{2,1},{3,0},{4,7},{5,6},{6,5},{7,4},{8,11},{9,10},{10,... | collective-permute-start | bytes 138248 | tf_op jit(solution)/shard_map/ppermute | solution.py:57

commit v24 on v22

--- a/solution.py
+++ b/solution.py
@@ -13,6 +13,7 @@
 LANES = 128
 ROWS = 8
 WIDE = 2
+SLOT_WIDE = 4
 VMEM_LIMIT = 48 * 2**20
 WEIGHT_PARTS = 6
 STEP_PARTS = 4
@@ -108,10 +109,17 @@
     return total
 
 
+def message(target, rows_s, prompt_s, step, conv, state):
+    row = jnp.maximum(rows_s[target], 0)
+    xs = step[row, :, 0, :].astype(F32)
+    number = jnp.full((1, xs.shape[1]), prompt_s[row].astype(F32), F32)
+    pieces = [xs, conv[0].astype(F32), number] + ([] if state is None else [state])
+    return jnp.concatenate(pieces, axis=0).astype(BF16)
+
+
 def pack_kernel(direct, owner_hbm, rows_hbm, prompt_hbm, step_hbm, conv_hbm, ssm_hbm, *rest):
     outs, (owner_s, rows_s, prompt_s, step, conv, ssm, sems) = rest[:-7], rest[-7:]
     owners = rows_hbm.shape[0]
-    channels = step_hbm.shape[3]
     copies = [
         pltpu.make_async_copy(owner_hbm, owner_s, sems.at[4]),
         pltpu.make_async_copy(rows_hbm, rows_s, sems.at[0]),
@@ -121,24 +129,11 @@
     ]
     all_of(copies + in_parts(step_hbm, step, sems, 5, STEP_PARTS))
     owner = owner_s[0]
-    window = conv[0].astype(F32)
-
-    def write(ref, target):
-        row = jnp.maximum(rows_s[target], 0)
-        xs = step[row, :, 0, :].astype(F32)
-        number = prompt_s[row].astype(F32)
-        pieces = [xs, window, jnp.full((1, channels), number, F32)]
-        if ref.shape[0] > sum(p.shape[0] for p in pieces):
-            pieces.append(ssm[0])
-        ref[...] = jnp.concatenate(pieces, axis=0).astype(BF16)
-
-    if direct:
-        write(outs[0].at[0], owner)
-        for ref, to in zip(outs[1:], SENDS):
-            write(ref.at[0], chosen(owner, to))
-    else:
-        for target in range(owners):
-            write(outs[0].at[target], target)
+    targets = [chosen(owner, to) for to in SENDS] if direct else range(owners)
+    for i, target in enumerate(targets):
+        ref = outs[i].at[0] if direct else outs[0].at[i]
+        state = ssm[0] if ref.shape[0] > conv.shape[1] + step.shape[1] + 1 else None
+        ref[...] = message(target, rows_s, prompt_s, step, conv, state)
 
 
 def pair_kernel(text, ssm_ref, came_ref, after_ref, pair_ref):
@@ -157,11 +152,14 @@
     direct,
     owner_hbm,
     prompt_hbm,
+    rows_hbm,
+    conv_hbm,
     step_hbm,
     cw_hbm,
     cb_hbm,
     xwt_hbm,
     after_ref,
+    own_ref,
     base_ref,
     pick_ref,
     sender_ref,
@@ -171,13 +169,22 @@
     step_ref,
     owner_s,
     prompt_s,
+    rows_s,
+    conv,
     sems,
 ):
     del after_ref
     small = [
         pltpu.make_async_copy(source, target, sems.at[i])
         for i, (source, target) in enumerate(
-            ((cw_hbm, cw_ref), (cb_hbm, cb_ref), (owner_hbm, owner_s), (prompt_hbm, prompt_s))
+            (
+                (cw_hbm, cw_ref),
+                (cb_hbm, cb_ref),
+                (owner_hbm, owner_s),
+                (prompt_hbm, prompt_s),
+                (rows_hbm, rows_s),
+                (conv_hbm, conv),
+            )
         )
     ]
     inputs = in_parts(step_hbm, step_ref, sems, len(small), STEP_PARTS)
@@ -186,6 +193,7 @@
         copy.start()
     for copy in inputs + small:
         copy.wait()
+    own_ref[0] = message(owner_s[0], rows_s, prompt_s, step_ref, conv, None)
     steps = step_ref.shape[1]
     taps = cw_hbm.shape[0]
     xs = [step_ref[:, t, 0, :].astype(F32) for t in range(steps)]
@@ -401,23 +409,24 @@
         b_s[n] = column(proj[:own_rows, rank:], n, own_rows)
         c_s[n] = column(proj[:own_rows, rank:], n_state + n, own_rows)
 
-    def wide(part):
-        return jnp.concatenate([part] * WIDE, axis=1)
+    def wide(part, times=WIDE):
+        return jnp.concatenate([part] * times, axis=1)
 
     def slot_chunk(chunk, carry):
-        columns = pl.ds(pl.multiple_of(chunk * WIDE * LANES, WIDE * LANES), WIDE * LANES)
+        breadth = SLOT_WIDE * LANES
+        columns = pl.ds(pl.multiple_of(chunk * breadth, breadth), breadth)
         delta = [slot_delta_s[t, :, columns] for t in range(steps)]
         gain = [slot_gain_s[t, :, columns] for t in range(steps)]
         for m in range(n_state // 2):
             rate = twin_ref[m, :, columns]
             state = slot_ref[m, :, columns]
             for t in range(steps):
-                state = jnp.exp2(delta[t] * rate) * state + gain[t] * wide(twin_b_s[m, t])
+                state = jnp.exp2(delta[t] * rate) * state + gain[t] * wide(twin_b_s[m, t], SLOT_WIDE)
             slots_s[:, 2 * m, columns] = state[:n_slots, :]
             slots_s[:, 2 * m + 1, columns] = state[n_slots:, :]
         return carry
 
-    lax.fori_loop(0, chunks, slot_chunk, 0)
+    lax.fori_loop(0, channels // (SLOT_WIDE * LANES), slot_chunk, 0)
     for copy in scalars:
         copy.wait()
     places = blocks_of(owner_s[0]) if direct else None
@@ -487,7 +496,7 @@
     owner = pinned(lax.axis_index("branch").astype(jnp.int32).reshape(1))
 
     if direct:
-        msg_shapes = [(1, d, channels) for d in (short, depth, short, short)]
+        msg_shapes = [(1, d, channels) for d in (depth, short, short)]
     else:
         msg_shapes = [(owners, depth, channels)]
     msgs = call(
@@ -513,19 +522,15 @@
         pinned(prompt_conv),
         pinned(prompt_ssm),
     )
+    after = msgs[0]
     if direct:
-        own = msgs[0]
-        msgs = [own] + [
-            lax.ppermute(m, "branch", list(enumerate(to))) for m, to in zip(msgs[1:], SENDS)
-        ]
-        after = own
+        msgs = [lax.ppermute(m, "branch", list(enumerate(to))) for m, to in zip(msgs, SENDS)]
     else:
         msgs = [lax.all_to_all(msgs[0], "branch", split_axis=0, concat_axis=0, tiled=True)]
-        after = msgs[0]
-    n_msgs = len(msgs)
-    base, pick, sender, taps_near, bias_near, weight_near = call(
+    own, base, pick, sender, taps_near, bias_near, weight_near = call(
         functools.partial(prepare_kernel, direct),
         [
+            shaped((1, short, channels), BF16),
             shaped((steps, rb, channels), F32),
             shaped((rb, owners), F32),
             shaped((1, owners), F32),
@@ -533,19 +538,23 @@
             shaped((1, channels), F32),
             shaped((width, channels), BF16),
         ],
-        [hbm()] * 6 + [anywhere()],
-        [vmem()] * 6,
+        [hbm()] * 8 + [anywhere()],
+        [vmem()] * 7,
         [
             pltpu.VMEM(step_in.shape, BF16),
             pltpu.SMEM((1,), jnp.int32),
             pltpu.SMEM((rb,), jnp.int32),
-            pltpu.SemaphoreType.DMA((4 + WEIGHT_PARTS + STEP_PARTS,)),
+            pltpu.SMEM((owners,), jnp.int32),
+            pltpu.VMEM(prompt_conv.shape, BF16),
+            pltpu.SemaphoreType.DMA((6 + WEIGHT_PARTS + STEP_PARTS,)),
         ],
         flops=10 * steps * rb * channels,
         nbytes=12 * steps * rb * channels,
     )(
         owner,
         pinned(prompt_of),
+        pinned(send_rows.reshape(owners)),
+        pinned(prompt_conv),
         pinned(step_in),
         pinned(conv_weight),
         pinned(conv_bias[None]),
@@ -554,6 +563,7 @@
     )
     states = []
     if direct:
+        msgs = [own] + msgs
         pair = call(
             functools.partial(pair_kernel, short),
             shaped((1, 3 * n_state, channels), BF16),
@@ -562,6 +572,7 @@
             nbytes=12 * n_state * channels,
         )(prompt_ssm, msgs[1], pick)
         states = [prompt_ssm, swap(pair, "branch", 1)]
+    n_msgs = len(msgs)
     act, part, brief = call(
         functools.partial(project_kernel, n_msgs),
         [

time: 19.7 us -> 19.6 us (level)
  no operation moved by 1% of the time
where the time goes in v24:
time: 19.6 us; the launch traced here: 19.4 us
  starting transfers between devices  8.73 us (45%)
  Pallas kernels  8.22 us (42%)
  waiting for transfers between devices  1.69 us (9%)
  between operations  0.71 us (4%)
    ppermute x3, starting transfers between devices, on_device(): lax.ppermute(m, 'branch', list(enumerate(to)))  5.67 us
    ppermute x3, starting transfers between devices, swap(): return lax.ppermute(value, axis, [(i, i ^ distance) for i in range(size)])  3.07 us
    pallas_call x1, Pallas kernels, on_device(): call(functools.partial(decode_kernel, direct), [shaped((rb, steps, channe...  2.83 us
    pallas_call x1, Pallas kernels, on_device(): call(functools.partial(late_kernel, n_msgs, direct), [shaped((taps - 1, r...  1.78 us
    ppermute x3, waiting for transfers between devices, swap(): return lax.ppermute(value, axis, [(i, i ^ distance) for i in range(size)])  1.45 us
    pallas_call x1, Pallas kernels, on_device(): call(functools.partial(prepare_kernel, direct), [shaped((1, short, channe...  1.45 us
    pallas_call x1, Pallas kernels, on_device(): call(functools.partial(pack_kernel, direct), [shaped(s, BF16) for s in ms...  1.1 us
    pallas_call x1, Pallas kernels, on_device(): call(functools.partial(start_kernel, n_msgs, direct, short), [shaped((n_s...  0.53 us
  transfers between devices with their start and end apart: 6, of which 4 were waited for; matrix products, arithmetic and copies ran while one was open for 0% of the time, Pallas kernels for 22%

profile of v24, /device:TPU:0, one launch (start us, length us, event | category | flops | bytes accessed | tf_op | source)
XLA Modules:
  0.0 19.4 jit_solution(15006869956897295325)
XLA Ops:
  0.6 1.1 %shard_map.148 = (bf16[1,24,1024]{2,1,0:T(8,128)(2,1)S(1)}, bf16[1,8,1024]{2,1,0:T(8,128)(2,1)S(1)}, bf16[1,8,1024]{2,1,0:T(8,128)(2,1)S(1)}) custom-call(s32[1]{0:T(128)} %bitcast.owner_hbm.refs_0_, s32[4]{0:T(128)} %bitcast.11, s32[16]{0:T(128)} %prompt_hbm.3, bf16[16,4,2,1024]{3,2,1,0:T(2,128)(2,1)} %refs_2_.1, bf16[1,3,1024]{2,1,0:T(4,128)(2,1)} %conv_hbm.3, ...), custom_call_target="tpu_custom_call" | custom-call | bytes 196608 | tf_op jit(solution)/shard_map/pallas_call | solution.py:502
  1.7 4.1 %collective-permute-start = (bf16[1,24,1024]{2,1,0:T(8,128)(2,1)S(1)}, bf16[1,24,1024]{2,1,0:T(8,128)(2,1)S(1)}, u32[]{:S(2)}, u32[]{:S(2)}) collective-permute-start(bf16[1,24,1024]{2,1,0:T(8,128)(2,1)S(1)} %get-tuple-element.28.after_ref), channel_id=1, source_target_pairs={{0,8},{4,12},{8,4},{12,0},{1,9},{5,13},{9,5},{13,1},{2,10},{6,14},... | collective-permute-start | bytes 147464 | tf_op jit(solution)/shard_map/ppermute | solution.py:527
  5.8 1.1 %collective-permute-start.1 = (bf16[1,8,1024]{2,1,0:T(8,128)(2,1)S(1)}, bf16[1,8,1024]{2,1,0:T(8,128)(2,1)S(1)}, u32[]{:S(2)}, u32[]{:S(2)}) collective-permute-start(bf16[1,8,1024]{2,1,0:T(8,128)(2,1)S(1)} %get-tuple-element.36), channel_id=1, source_target_pairs={{0,12},{4,8},{8,0},{12,4},{1,13},{5,9},{9,1},{13,5},{2,14},{6,10},... | collective-permute-start | bytes 49160 | tf_op jit(solution)/shard_map/ppermute | solution.py:527
  6.9 0.5 %collective-permute-start.2 = (bf16[1,8,1024]{2,1,0:T(8,128)(2,1)S(1)}, bf16[1,8,1024]{2,1,0:T(8,128)(2,1)S(1)}, u32[]{:S(2)}, u32[]{:S(2)}) collective-permute-start(bf16[1,8,1024]{2,1,0:T(8,128)(2,1)S(1)} %get-tuple-element.37), channel_id=1, source_target_pairs={{0,4},{4,0},{8,12},{12,8},{1,5},{5,1},{9,13},{13,9},{2,6},{6,2},{1... | collective-permute-start | bytes 49160 | tf_op jit(solution)/shard_map/ppermute | solution.py:527
  7.4 0.0 copy-start
  7.4 1.4 %shard_map.149 = (bf16[1,8,1024]{2,1,0:T(8,128)(2,1)S(1)}, f32[4,16,1024]{2,1,0:T(8,128)S(1)}, f32[16,4]{1,0:T(8,128)S(1)}, f32[1,4]{1,0:T(1,128)S(1)}, f32[4,10...) custom-call(s32[1]{0:T(128)} %bitcast.owner_hbm.refs_0_, s32[16]{0:T(128)} %prompt_hbm.3, ...), custom_call_target="tpu_custom_call" | custom-call | flops 655360 | bytes 786432 | tf_op jit(solution)/shard_map/pallas_call | solution.py:530
  8.9 0.1 collective-permute-done.rest_1_.refs_8_.came_ref
  9.0 0.0 copy-done
  9.0 1.5 %collective-permute-start.4 = (bf16[1,48,1024]{2,1,0:T(8,128)(2,1)S(1)}, bf16[1,48,1024]{2,1,0:T(8,128)(2,1)S(1)}, u32[]{:S(2)}, u32[]{:S(2)}) collective-permute-start(bf16[1,48,1024]{2,1,0:T(8,128)(2,1)S(1)} %shard_map.153), channel_id=1, source_target_pairs={{0,4},{4,0},{8,12},{12,8},{1,5},{5,1},{9,13},{13,9},{2,6},{6,2},{1... | collective-permute-start | bytes 294920 | tf_op jit(solution)/shard_map/ppermute | solution.py:58
  10.5 0.0 collective-permute-done.1.rest_2_.refs_9_
  10.5 0.1 collective-permute-done.2.rest_3_.refs_10_
  10.6 0.5 %shard_map.150 = (f32[80,1024]{1,0:T(8,128)S(1)}, f32[80,288]{1,0:T(8,128)S(1)}, bf16[80,288]{1,0:T(8,128)(2,1)S(1)}) custom-call(f32[16,4]{1,0:T(8,128)S(1)} %get-tuple-element.29.pick_ref.after_ref, f32[1,4]{1,0:T(1,128)S(1)} %get-tuple-element.30.sender_ref, f32[4,16,1024]{2,1,0:T(8,128)S(1)} %get-tuple-element.31.base_ref, ...), custom_call_target="tpu_custom_call" | custom-call | flops 47185920 | bytes 1009664 | tf_op jit(solution)/shard_map/pallas_call | solution.py:576
  11.2 0.1 collective-permute-start.3
  11.2 1.2 %collective-permute-done.3.b_ref = bf16[80,288]{1,0:T(8,128)(2,1)S(1)} collective-permute-done((bf16[80,288]{1,0:T(8,128)(2,1)S(1)}, bf16[80,288]{1,0:T(8,128)(2,1)S(1)}, u32[]{:S(2)}, u32[]{:S(2)}) %collective-permute-start.3) | collective-permute-done | bytes 46112 | tf_op jit(solution)/shard_map/ppermute | solution.py:58
  12.5 0.0 copy-start.1
  12.5 1.5 %collective-permute-start.5 = (bf16[80,288]{1,0:T(8,128)(2,1)S(1)}, bf16[80,288]{1,0:T(8,128)(2,1)S(1)}, u32[]{:S(2)}, u32[]{:S(2)}) collective-permute-start(bf16[80,288]{1,0:T(8,128)(2,1)S(1)} %get-tuple-element.49), channel_id=1, source_target_pairs={{0,3},{1,2},{2,1},{3,0},{4,7},{5,6},{6,5},{7,4},{8,11},{9,10},{10,... | collective-permute-start | bytes 138248 | tf_op jit(solution)/shard_map/ppermute | solution.py:58
  14.0 1.8 %shard_map.152 = (bf16[3,16,1024]{2,1,0:T(8,128)(2,1)}, f32[4,16,1024]{2,1,0:T(8,128)S(1)}, f32[16,1024]{1,0:T(8,128)S(1)}, f32[8,8,1024]{2,1,0:T(8,128)S(1)}, f...) custom-call(s32[1]{0:T(128)} %bitcast.owner_hbm.refs_0_, s32[16]{0:T(128)} %child_hbm.1, bf16[16,4,2,1024]{3,2,1,0:T(2,128)(2,1)} %refs_2_.1, ...), custom_call_target="tpu_custom_call" | custom-call | flops 655360 | bytes 786432 | tf_op jit(solution)/shard_map/pallas_call | solution.py:603
  15.8 0.0 collective-permute-done.4.rest_5_
  15.8 0.5 %shard_map.154 = (f32[16,16,1024]{2,1,0:T(8,128)S(1)}, f32[8,8,1024]{2,1,0:T(8,128)S(1)}) custom-call(f32[16,4]{1,0:T(8,128)S(1)} %get-tuple-element.29.pick_ref.after_ref, f32[1,4]{1,0:T(1,128)S(1)} %get-tuple-element.30.sender_ref, f32[80,288]{1,0:T(8,128)S(1)} %get-tuple-element.41.refs_6_.after_ref.part_ref, ...), custom_call_target="tpu_custom_call" | custom-call | flops 2621440 | bytes 1310720 | tf_op jit(solution)/shard_map/pallas_call | solution.py:636
  16.3 0.2 %collective-permute-done.5.other_ref = bf16[80,288]{1,0:T(8,128)(2,1)S(1)} collective-permute-done((bf16[80,288]{1,0:T(8,128)(2,1)S(1)}, bf16[80,288]{1,0:T(8,128)(2,1)S(1)}, u32[]{:S(2)}, u32[]{:S(2)}) %collective-permute-start.5) | collective-permute-done | bytes 46112 | tf_op jit(solution)/shard_map/ppermute | solution.py:58
  16.5 0.0 copy-done.1
  16.5 2.8 %shard_map.155 = (bf16[16,4,1024]{2,1,0:T(4,128)(2,1)}, f32[16,16,1024]{2,1,0:T(8,128)}) custom-call(s32[1]{0:T(128)} %bitcast.owner_hbm.refs_0_, s32[16]{0:T(128)} %child_hbm.1, f32[80,1024]{1,0:T(8,128)S(1)} %get-tuple-element.38.act_ref, f32[4,16,1024]{2,1,0:T(8,128)S(1)} %get-tuple-element.42.gate_ref, f32[16,16,1024]{2,1,0:T(8,128)S(1)} %get-tuple-element.43.own_ref, ...), custom_call_target="tpu_custom_call" | custom-call | flops 10485760 | bytes 1310720 | tf_op jit(solution)/shard_map/pallas_call | solution.py:649
  (2 shorter events, 0.0 us)
Async XLA Ops:
  1.7 7.2 %collective-permute-start = (bf16[1,24,1024]{2,1,0:T(8,128)(2,1)S(1)}, bf16[1,24,1024]{2,1,0:T(8,128)(2,1)S(1)}, u32[]{:S(2)}, u32[]{:S(2)}) collective-permute-start(bf16[1,24,1024]{2,1,0:T(8,128)(2,1)S(1)} %get-tuple-element.28.after_ref), channel_id=1, source_target_pairs={{0,8},{4,12},{8,4},{12,0},{1,9},{5,13},{9,5},{13,1},{2,10},{6,14},... | collective-permute-start | bytes 147464 | tf_op jit(solution)/shard_map/ppermute | solution.py:527
  5.8 4.7 %collective-permute-start.1 = (bf16[1,8,1024]{2,1,0:T(8,128)(2,1)S(1)}, bf16[1,8,1024]{2,1,0:T(8,128)(2,1)S(1)}, u32[]{:S(2)}, u32[]{:S(2)}) collective-permute-start(bf16[1,8,1024]{2,1,0:T(8,128)(2,1)S(1)} %get-tuple-element.36), channel_id=1, source_target_pairs={{0,12},{4,8},{8,0},{12,4},{1,13},{5,9},{9,1},{13,5},{2,14},{6,10},... | collective-permute-start | bytes 49160 | tf_op jit(solution)/shard_map/ppermute | solution.py:527
  6.9 3.7 %collective-permute-start.2 = (bf16[1,8,1024]{2,1,0:T(8,128)(2,1)S(1)}, bf16[1,8,1024]{2,1,0:T(8,128)(2,1)S(1)}, u32[]{:S(2)}, u32[]{:S(2)}) collective-permute-start(bf16[1,8,1024]{2,1,0:T(8,128)(2,1)S(1)} %get-tuple-element.37), channel_id=1, source_target_pairs={{0,4},{4,0},{8,12},{12,8},{1,5},{5,1},{9,13},{13,9},{2,6},{6,2},{1... | collective-permute-start | bytes 49160 | tf_op jit(solution)/shard_map/ppermute | solution.py:527
  7.4 1.6 %copy-start = (f32[1,16,1024]{2,1,0:T(8,128)S(1)}, f32[1,16,1024]{2,1,0:T(8,128)}, u32[]{:S(2)}) copy-start(f32[1,16,1024]{2,1,0:T(8,128)} %rest_4_.1) | copy-start | bytes 196612
  9.0 6.8 %collective-permute-start.4 = (bf16[1,48,1024]{2,1,0:T(8,128)(2,1)S(1)}, bf16[1,48,1024]{2,1,0:T(8,128)(2,1)S(1)}, u32[]{:S(2)}, u32[]{:S(2)}) collective-permute-start(bf16[1,48,1024]{2,1,0:T(8,128)(2,1)S(1)} %shard_map.153), channel_id=1, source_target_pairs={{0,4},{4,0},{8,12},{12,8},{1,5},{5,1},{9,13},{13,9},{2,6},{6,2},{1... | collective-permute-start | bytes 294920 | tf_op jit(solution)/shard_map/ppermute | solution.py:58
  11.2 1.3 %collective-permute-start.3 = (bf16[80,288]{1,0:T(8,128)(2,1)S(1)}, bf16[80,288]{1,0:T(8,128)(2,1)S(1)}, u32[]{:S(2)}, u32[]{:S(2)}) collective-permute-start(bf16[80,288]{1,0:T(8,128)(2,1)S(1)} %get-tuple-element.40), channel_id=1, source_target_pairs={{0,1},{1,0},{2,3},{3,2},{4,5},{5,4},{6,7},{7,6},{8,9},{9,8},{10,11... | collective-permute-start | bytes 138248 | tf_op jit(solution)/shard_map/ppermute | solution.py:58
  12.5 4.0 %copy-start.1 = (bf16[256,1024]{1,0:T(8,128)(2,1)S(1)}, bf16[256,1024]{1,0:T(8,128)(2,1)}, u32[]{:S(2)}) copy-start(bf16[256,1024]{1,0:T(8,128)(2,1)} %dtw_ref.1) | copy-start | bytes 1572868
  12.5 4.0 %collective-permute-start.5 = (bf16[80,288]{1,0:T(8,128)(2,1)S(1)}, bf16[80,288]{1,0:T(8,128)(2,1)S(1)}, u32[]{:S(2)}, u32[]{:S(2)}) collective-permute-start(bf16[80,288]{1,0:T(8,128)(2,1)S(1)} %get-tuple-element.49), channel_id=1, source_target_pairs={{0,3},{1,2},{2,1},{3,0},{4,7},{5,6},{6,5},{7,4},{8,11},{9,10},{10,... | collective-permute-start | bytes 138248 | tf_op jit(solution)/shard_map/ppermute | solution.py:58

commit v25 on v24

--- a/solution.py
+++ b/solution.py
@@ -12,7 +12,7 @@
 BF16 = jnp.bfloat16
 LANES = 128
 ROWS = 8
-WIDE = 2
+WIDE = 4
 SLOT_WIDE = 4
 VMEM_LIMIT = 48 * 2**20
 WEIGHT_PARTS = 6

time: 19.6 us -> 19.6 us (level)
  no operation moved by 1% of the time
where the time goes in v25:
time: 19.6 us; the launch traced here: 19.3 us
  starting transfers between devices  8.73 us (45%)
  Pallas kernels  8.19 us (42%)
  waiting for transfers between devices  1.69 us (9%)
  between operations  0.71 us (4%)
    ppermute x3, starting transfers between devices, on_device(): lax.ppermute(m, 'branch', list(enumerate(to)))  5.67 us
    ppermute x3, starting transfers between devices, swap(): return lax.ppermute(value, axis, [(i, i ^ distance) for i in range(size)])  3.07 us
    pallas_call x1, Pallas kernels, on_device(): call(functools.partial(decode_kernel, direct), [shaped((rb, steps, channe...  2.8 us
    pallas_call x1, Pallas kernels, on_device(): call(functools.partial(late_kernel, n_msgs, direct), [shaped((taps - 1, r...  1.78 us
    ppermute x3, waiting for transfers between devices, swap(): return lax.ppermute(value, axis, [(i, i ^ distance) for i in range(size)])  1.45 us
    pallas_call x1, Pallas kernels, on_device(): call(functools.partial(prepare_kernel, direct), [shaped((1, short, channe...  1.45 us
    pallas_call x1, Pallas kernels, on_device(): call(functools.partial(pack_kernel, direct), [shaped(s, BF16) for s in ms...  1.1 us
    pallas_call x1, Pallas kernels, on_device(): call(functools.partial(start_kernel, n_msgs, direct, short), [shaped((n_s...  0.53 us
  transfers between devices with their start and end apart: 6, of which 4 were waited for; matrix products, arithmetic and copies ran while one was open for 0% of the time, Pallas kernels for 22%

profile of v25, /device:TPU:0, one launch (start us, length us, event | category | flops | bytes accessed | tf_op | source)
XLA Modules:
  0.0 19.3 jit_solution(17057970783533112747)
XLA Ops:
  0.6 1.1 %shard_map.148 = (bf16[1,24,1024]{2,1,0:T(8,128)(2,1)S(1)}, bf16[1,8,1024]{2,1,0:T(8,128)(2,1)S(1)}, bf16[1,8,1024]{2,1,0:T(8,128)(2,1)S(1)}) custom-call(s32[1]{0:T(128)} %bitcast.owner_hbm.refs_0_, s32[4]{0:T(128)} %bitcast.11, s32[16]{0:T(128)} %prompt_hbm.3, bf16[16,4,2,1024]{3,2,1,0:T(2,128)(2,1)} %refs_2_.1, bf16[1,3,1024]{2,1,0:T(4,128)(2,1)} %conv_hbm.3, ...), custom_call_target="tpu_custom_call" | custom-call | bytes 196608 | tf_op jit(solution)/shard_map/pallas_call | solution.py:502
  1.7 4.1 %collective-permute-start = (bf16[1,24,1024]{2,1,0:T(8,128)(2,1)S(1)}, bf16[1,24,1024]{2,1,0:T(8,128)(2,1)S(1)}, u32[]{:S(2)}, u32[]{:S(2)}) collective-permute-start(bf16[1,24,1024]{2,1,0:T(8,128)(2,1)S(1)} %get-tuple-element.28.after_ref), channel_id=1, source_target_pairs={{0,8},{4,12},{8,4},{12,0},{1,9},{5,13},{9,5},{13,1},{2,10},{6,14},... | collective-permute-start | bytes 147464 | tf_op jit(solution)/shard_map/ppermute | solution.py:527
  5.8 1.1 %collective-permute-start.1 = (bf16[1,8,1024]{2,1,0:T(8,128)(2,1)S(1)}, bf16[1,8,1024]{2,1,0:T(8,128)(2,1)S(1)}, u32[]{:S(2)}, u32[]{:S(2)}) collective-permute-start(bf16[1,8,1024]{2,1,0:T(8,128)(2,1)S(1)} %get-tuple-element.36), channel_id=1, source_target_pairs={{0,12},{4,8},{8,0},{12,4},{1,13},{5,9},{9,1},{13,5},{2,14},{6,10},... | collective-permute-start | bytes 49160 | tf_op jit(solution)/shard_map/ppermute | solution.py:527
  6.9 0.5 %collective-permute-start.2 = (bf16[1,8,1024]{2,1,0:T(8,128)(2,1)S(1)}, bf16[1,8,1024]{2,1,0:T(8,128)(2,1)S(1)}, u32[]{:S(2)}, u32[]{:S(2)}) collective-permute-start(bf16[1,8,1024]{2,1,0:T(8,128)(2,1)S(1)} %get-tuple-element.37), channel_id=1, source_target_pairs={{0,4},{4,0},{8,12},{12,8},{1,5},{5,1},{9,13},{13,9},{2,6},{6,2},{1... | collective-permute-start | bytes 49160 | tf_op jit(solution)/shard_map/ppermute | solution.py:527
  7.4 0.0 copy-start
  7.4 1.4 %shard_map.149 = (bf16[1,8,1024]{2,1,0:T(8,128)(2,1)S(1)}, f32[4,16,1024]{2,1,0:T(8,128)S(1)}, f32[16,4]{1,0:T(8,128)S(1)}, f32[1,4]{1,0:T(1,128)S(1)}, f32[4,10...) custom-call(s32[1]{0:T(128)} %bitcast.owner_hbm.refs_0_, s32[16]{0:T(128)} %prompt_hbm.3, ...), custom_call_target="tpu_custom_call" | custom-call | flops 655360 | bytes 786432 | tf_op jit(solution)/shard_map/pallas_call | solution.py:530
  8.9 0.1 collective-permute-done.rest_1_.refs_8_.came_ref
  9.0 0.0 copy-done
  9.0 1.5 %collective-permute-start.4 = (bf16[1,48,1024]{2,1,0:T(8,128)(2,1)S(1)}, bf16[1,48,1024]{2,1,0:T(8,128)(2,1)S(1)}, u32[]{:S(2)}, u32[]{:S(2)}) collective-permute-start(bf16[1,48,1024]{2,1,0:T(8,128)(2,1)S(1)} %shard_map.153), channel_id=1, source_target_pairs={{0,4},{4,0},{8,12},{12,8},{1,5},{5,1},{9,13},{13,9},{2,6},{6,2},{1... | collective-permute-start | bytes 294920 | tf_op jit(solution)/shard_map/ppermute | solution.py:58
  10.5 0.0 collective-permute-done.1.rest_2_.refs_9_
  10.5 0.1 collective-permute-done.2.rest_3_.refs_10_
  10.6 0.5 %shard_map.150 = (f32[80,1024]{1,0:T(8,128)S(1)}, f32[80,288]{1,0:T(8,128)S(1)}, bf16[80,288]{1,0:T(8,128)(2,1)S(1)}) custom-call(f32[16,4]{1,0:T(8,128)S(1)} %get-tuple-element.29.pick_ref.after_ref, f32[1,4]{1,0:T(1,128)S(1)} %get-tuple-element.30.sender_ref, f32[4,16,1024]{2,1,0:T(8,128)S(1)} %get-tuple-element.31.base_ref, ...), custom_call_target="tpu_custom_call" | custom-call | flops 47185920 | bytes 1009664 | tf_op jit(solution)/shard_map/pallas_call | solution.py:576
  11.2 0.1 collective-permute-start.3
  11.2 1.2 %collective-permute-done.3.b_ref = bf16[80,288]{1,0:T(8,128)(2,1)S(1)} collective-permute-done((bf16[80,288]{1,0:T(8,128)(2,1)S(1)}, bf16[80,288]{1,0:T(8,128)(2,1)S(1)}, u32[]{:S(2)}, u32[]{:S(2)}) %collective-permute-start.3) | collective-permute-done | bytes 46112 | tf_op jit(solution)/shard_map/ppermute | solution.py:58
  12.5 0.0 copy-start.1
  12.5 1.5 %collective-permute-start.5 = (bf16[80,288]{1,0:T(8,128)(2,1)S(1)}, bf16[80,288]{1,0:T(8,128)(2,1)S(1)}, u32[]{:S(2)}, u32[]{:S(2)}) collective-permute-start(bf16[80,288]{1,0:T(8,128)(2,1)S(1)} %get-tuple-element.49), channel_id=1, source_target_pairs={{0,3},{1,2},{2,1},{3,0},{4,7},{5,6},{6,5},{7,4},{8,11},{9,10},{10,... | collective-permute-start | bytes 138248 | tf_op jit(solution)/shard_map/ppermute | solution.py:58
  14.0 1.8 %shard_map.152 = (bf16[3,16,1024]{2,1,0:T(8,128)(2,1)}, f32[4,16,1024]{2,1,0:T(8,128)S(1)}, f32[16,1024]{1,0:T(8,128)S(1)}, f32[8,8,1024]{2,1,0:T(8,128)S(1)}, f...) custom-call(s32[1]{0:T(128)} %bitcast.owner_hbm.refs_0_, s32[16]{0:T(128)} %child_hbm.1, bf16[16,4,2,1024]{3,2,1,0:T(2,128)(2,1)} %refs_2_.1, ...), custom_call_target="tpu_custom_call" | custom-call | flops 655360 | bytes 786432 | tf_op jit(solution)/shard_map/pallas_call | solution.py:603
  15.8 0.0 collective-permute-done.4.rest_5_
  15.8 0.5 %shard_map.154 = (f32[16,16,1024]{2,1,0:T(8,128)S(1)}, f32[8,8,1024]{2,1,0:T(8,128)S(1)}) custom-call(f32[16,4]{1,0:T(8,128)S(1)} %get-tuple-element.29.pick_ref.after_ref, f32[1,4]{1,0:T(1,128)S(1)} %get-tuple-element.30.sender_ref, f32[80,288]{1,0:T(8,128)S(1)} %get-tuple-element.41.refs_6_.after_ref.part_ref, ...), custom_call_target="tpu_custom_call" | custom-call | flops 2621440 | bytes 1310720 | tf_op jit(solution)/shard_map/pallas_call | solution.py:636
  16.3 0.2 %collective-permute-done.5.other_ref = bf16[80,288]{1,0:T(8,128)(2,1)S(1)} collective-permute-done((bf16[80,288]{1,0:T(8,128)(2,1)S(1)}, bf16[80,288]{1,0:T(8,128)(2,1)S(1)}, u32[]{:S(2)}, u32[]{:S(2)}) %collective-permute-start.5) | collective-permute-done | bytes 46112 | tf_op jit(solution)/shard_map/ppermute | solution.py:58
  16.5 0.0 copy-done.1
  16.5 2.8 %shard_map.155 = (bf16[16,4,1024]{2,1,0:T(4,128)(2,1)}, f32[16,16,1024]{2,1,0:T(8,128)}) custom-call(s32[1]{0:T(128)} %bitcast.owner_hbm.refs_0_, s32[16]{0:T(128)} %child_hbm.1, f32[80,1024]{1,0:T(8,128)S(1)} %get-tuple-element.38.act_ref, f32[4,16,1024]{2,1,0:T(8,128)S(1)} %get-tuple-element.42.gate_ref, f32[16,16,1024]{2,1,0:T(8,128)S(1)} %get-tuple-element.43.own_ref, ...), custom_call_target="tpu_custom_call" | custom-call | flops 10485760 | bytes 1310720 | tf_op jit(solution)/shard_map/pallas_call | solution.py:649
  (2 shorter events, 0.0 us)
Async XLA Ops:
  1.7 7.2 %collective-permute-start = (bf16[1,24,1024]{2,1,0:T(8,128)(2,1)S(1)}, bf16[1,24,1024]{2,1,0:T(8,128)(2,1)S(1)}, u32[]{:S(2)}, u32[]{:S(2)}) collective-permute-start(bf16[1,24,1024]{2,1,0:T(8,128)(2,1)S(1)} %get-tuple-element.28.after_ref), channel_id=1, source_target_pairs={{0,8},{4,12},{8,4},{12,0},{1,9},{5,13},{9,5},{13,1},{2,10},{6,14},... | collective-permute-start | bytes 147464 | tf_op jit(solution)/shard_map/ppermute | solution.py:527
  5.8 4.7 %collective-permute-start.1 = (bf16[1,8,1024]{2,1,0:T(8,128)(2,1)S(1)}, bf16[1,8,1024]{2,1,0:T(8,128)(2,1)S(1)}, u32[]{:S(2)}, u32[]{:S(2)}) collective-permute-start(bf16[1,8,1024]{2,1,0:T(8,128)(2,1)S(1)} %get-tuple-element.36), channel_id=1, source_target_pairs={{0,12},{4,8},{8,0},{12,4},{1,13},{5,9},{9,1},{13,5},{2,14},{6,10},... | collective-permute-start | bytes 49160 | tf_op jit(solution)/shard_map/ppermute | solution.py:527
  6.9 3.7 %collective-permute-start.2 = (bf16[1,8,1024]{2,1,0:T(8,128)(2,1)S(1)}, bf16[1,8,1024]{2,1,0:T(8,128)(2,1)S(1)}, u32[]{:S(2)}, u32[]{:S(2)}) collective-permute-start(bf16[1,8,1024]{2,1,0:T(8,128)(2,1)S(1)} %get-tuple-element.37), channel_id=1, source_target_pairs={{0,4},{4,0},{8,12},{12,8},{1,5},{5,1},{9,13},{13,9},{2,6},{6,2},{1... | collective-permute-start | bytes 49160 | tf_op jit(solution)/shard_map/ppermute | solution.py:527
  7.4 1.6 %copy-start = (f32[1,16,1024]{2,1,0:T(8,128)S(1)}, f32[1,16,1024]{2,1,0:T(8,128)}, u32[]{:S(2)}) copy-start(f32[1,16,1024]{2,1,0:T(8,128)} %rest_4_.1) | copy-start | bytes 196612
  9.0 6.8 %collective-permute-start.4 = (bf16[1,48,1024]{2,1,0:T(8,128)(2,1)S(1)}, bf16[1,48,1024]{2,1,0:T(8,128)(2,1)S(1)}, u32[]{:S(2)}, u32[]{:S(2)}) collective-permute-start(bf16[1,48,1024]{2,1,0:T(8,128)(2,1)S(1)} %shard_map.153), channel_id=1, source_target_pairs={{0,4},{4,0},{8,12},{12,8},{1,5},{5,1},{9,13},{13,9},{2,6},{6,2},{1... | collective-permute-start | bytes 294920 | tf_op jit(solution)/shard_map/ppermute | solution.py:58
  11.2 1.3 %collective-permute-start.3 = (bf16[80,288]{1,0:T(8,128)(2,1)S(1)}, bf16[80,288]{1,0:T(8,128)(2,1)S(1)}, u32[]{:S(2)}, u32[]{:S(2)}) collective-permute-start(bf16[80,288]{1,0:T(8,128)(2,1)S(1)} %get-tuple-element.40), channel_id=1, source_target_pairs={{0,1},{1,0},{2,3},{3,2},{4,5},{5,4},{6,7},{7,6},{8,9},{9,8},{10,11... | collective-permute-start | bytes 138248 | tf_op jit(solution)/shard_map/ppermute | solution.py:58
  12.5 4.0 %copy-start.1 = (bf16[256,1024]{1,0:T(8,128)(2,1)S(1)}, bf16[256,1024]{1,0:T(8,128)(2,1)}, u32[]{:S(2)}) copy-start(bf16[256,1024]{1,0:T(8,128)(2,1)} %dtw_ref.1) | copy-start | bytes 1572868
  12.5 4.0 %collective-permute-start.5 = (bf16[80,288]{1,0:T(8,128)(2,1)S(1)}, bf16[80,288]{1,0:T(8,128)(2,1)S(1)}, u32[]{:S(2)}, u32[]{:S(2)}) collective-permute-start(bf16[80,288]{1,0:T(8,128)(2,1)S(1)} %get-tuple-element.49), channel_id=1, source_target_pairs={{0,3},{1,2},{2,1},{3,0},{4,7},{5,6},{6,5},{7,4},{8,11},{9,10},{10,... | collective-permute-start | bytes 138248 | tf_op jit(solution)/shard_map/ppermute | solution.py:58

commit v26 on v25

--- a/solution.py
+++ b/solution.py
@@ -368,6 +368,7 @@
     c_s,
     twin_b_s,
     slots_s,
+    rows_s,
     line_s,
     sems,
 ):
@@ -422,11 +423,17 @@
             state = slot_ref[m, :, columns]
             for t in range(steps):
                 state = jnp.exp2(delta[t] * rate) * state + gain[t] * wide(twin_b_s[m, t], SLOT_WIDE)
-            slots_s[:, 2 * m, columns] = state[:n_slots, :]
-            slots_s[:, 2 * m + 1, columns] = state[n_slots:, :]
+            for w in range(SLOT_WIDE):
+                rows = pl.ds(2 * m * n_slots, 2 * n_slots)
+                lanes = slice(w * LANES, (w + 1) * LANES)
+                rows_s[chunk * SLOT_WIDE + w, rows, :] = state[:, lanes]
         return carry
 
     lax.fori_loop(0, channels // (SLOT_WIDE * LANES), slot_chunk, 0)
+    for slot in range(n_slots):
+        for i in range(channels // LANES):
+            rows = rows_s[i, pl.ds(slot, n_state, stride=n_slots), :]
+            slots_s[slot, :, i * LANES : (i + 1) * LANES] = rows
     for copy in scalars:
         copy.wait()
     places = blocks_of(owner_s[0]) if direct else None
@@ -665,6 +672,7 @@
             pltpu.VMEM((n_state, steps * rb, LANES), F32),
             pltpu.VMEM((n_state // 2, steps, 2 * owners, LANES), F32),
             pltpu.VMEM((owners, n_state, channels), F32),
+            pltpu.VMEM((channels // LANES, n_state * owners, LANES), F32),
             pltpu.VMEM((WIDE, steps * rb, LANES), F32),
             pltpu.SemaphoreType.DMA((2 + rb,)),
         ],

time: 19.6 us -> 19.6 us (level)
  no operation moved by 1% of the time
where the time goes in v26:
time: 19.6 us; the launch traced here: 19.3 us
  starting transfers between devices  8.73 us (45%)
  Pallas kernels  8.17 us (42%)
  waiting for transfers between devices  1.69 us (9%)
  between operations  0.71 us (4%)
    ppermute x3, starting transfers between devices, on_device(): lax.ppermute(m, 'branch', list(enumerate(to)))  5.67 us
    ppermute x3, starting transfers between devices, swap(): return lax.ppermute(value, axis, [(i, i ^ distance) for i in range(size)])  3.07 us
    pallas_call x1, Pallas kernels, on_device(): call(functools.partial(decode_kernel, direct), [shaped((rb, steps, channe...  2.78 us
    pallas_call x1, Pallas kernels, on_device(): call(functools.partial(late_kernel, n_msgs, direct), [shaped((taps - 1, r...  1.78 us
    ppermute x3, waiting for transfers between devices, swap(): return lax.ppermute(value, axis, [(i, i ^ distance) for i in range(size)])  1.45 us
    pallas_call x1, Pallas kernels, on_device(): call(functools.partial(prepare_kernel, direct), [shaped((1, short, channe...  1.45 us
    pallas_call x1, Pallas kernels, on_device(): call(functools.partial(pack_kernel, direct), [shaped(s, BF16) for s in ms...  1.1 us
    pallas_call x1, Pallas kernels, on_device(): call(functools.partial(start_kernel, n_msgs, direct, short), [shaped((n_s...  0.53 us
  transfers between devices with their start and end apart: 6, of which 4 were waited for; matrix products, arithmetic and copies ran while one was open for 0% of the time, Pallas kernels for 22%

profile of v26, /device:TPU:0, one launch (start us, length us, event | category | flops | bytes accessed | tf_op | source)
XLA Modules:
  0.0 19.3 jit_solution(10932281738423661686)
XLA Ops:
  0.6 1.1 %shard_map.148 = (bf16[1,24,1024]{2,1,0:T(8,128)(2,1)S(1)}, bf16[1,8,1024]{2,1,0:T(8,128)(2,1)S(1)}, bf16[1,8,1024]{2,1,0:T(8,128)(2,1)S(1)}) custom-call(s32[1]{0:T(128)} %bitcast.owner_hbm.refs_0_, s32[4]{0:T(128)} %bitcast.11, s32[16]{0:T(128)} %prompt_hbm.3, bf16[16,4,2,1024]{3,2,1,0:T(2,128)(2,1)} %refs_2_.1, bf16[1,3,1024]{2,1,0:T(4,128)(2,1)} %conv_hbm.3, ...), custom_call_target="tpu_custom_call" | custom-call | bytes 196608 | tf_op jit(solution)/shard_map/pallas_call | solution.py:509
  1.7 4.1 %collective-permute-start = (bf16[1,24,1024]{2,1,0:T(8,128)(2,1)S(1)}, bf16[1,24,1024]{2,1,0:T(8,128)(2,1)S(1)}, u32[]{:S(2)}, u32[]{:S(2)}) collective-permute-start(bf16[1,24,1024]{2,1,0:T(8,128)(2,1)S(1)} %get-tuple-element.28.after_ref), channel_id=1, source_target_pairs={{0,8},{4,12},{8,4},{12,0},{1,9},{5,13},{9,5},{13,1},{2,10},{6,14},... | collective-permute-start | bytes 147464 | tf_op jit(solution)/shard_map/ppermute | solution.py:534
  5.8 1.1 %collective-permute-start.1 = (bf16[1,8,1024]{2,1,0:T(8,128)(2,1)S(1)}, bf16[1,8,1024]{2,1,0:T(8,128)(2,1)S(1)}, u32[]{:S(2)}, u32[]{:S(2)}) collective-permute-start(bf16[1,8,1024]{2,1,0:T(8,128)(2,1)S(1)} %get-tuple-element.36), channel_id=1, source_target_pairs={{0,12},{4,8},{8,0},{12,4},{1,13},{5,9},{9,1},{13,5},{2,14},{6,10},... | collective-permute-start | bytes 49160 | tf_op jit(solution)/shard_map/ppermute | solution.py:534
  6.9 0.5 %collective-permute-start.2 = (bf16[1,8,1024]{2,1,0:T(8,128)(2,1)S(1)}, bf16[1,8,1024]{2,1,0:T(8,128)(2,1)S(1)}, u32[]{:S(2)}, u32[]{:S(2)}) collective-permute-start(bf16[1,8,1024]{2,1,0:T(8,128)(2,1)S(1)} %get-tuple-element.37), channel_id=1, source_target_pairs={{0,4},{4,0},{8,12},{12,8},{1,5},{5,1},{9,13},{13,9},{2,6},{6,2},{1... | collective-permute-start | bytes 49160 | tf_op jit(solution)/shard_map/ppermute | solution.py:534
  7.4 0.0 copy-start
  7.4 1.4 %shard_map.149 = (bf16[1,8,1024]{2,1,0:T(8,128)(2,1)S(1)}, f32[4,16,1024]{2,1,0:T(8,128)S(1)}, f32[16,4]{1,0:T(8,128)S(1)}, f32[1,4]{1,0:T(1,128)S(1)}, f32[4,10...) custom-call(s32[1]{0:T(128)} %bitcast.owner_hbm.refs_0_, s32[16]{0:T(128)} %prompt_hbm.3, ...), custom_call_target="tpu_custom_call" | custom-call | flops 655360 | bytes 786432 | tf_op jit(solution)/shard_map/pallas_call | solution.py:537
  8.9 0.1 collective-permute-done.rest_1_.refs_8_.came_ref
  9.0 0.0 copy-done
  9.0 1.5 %collective-permute-start.4 = (bf16[1,48,1024]{2,1,0:T(8,128)(2,1)S(1)}, bf16[1,48,1024]{2,1,0:T(8,128)(2,1)S(1)}, u32[]{:S(2)}, u32[]{:S(2)}) collective-permute-start(bf16[1,48,1024]{2,1,0:T(8,128)(2,1)S(1)} %shard_map.153), channel_id=1, source_target_pairs={{0,4},{4,0},{8,12},{12,8},{1,5},{5,1},{9,13},{13,9},{2,6},{6,2},{1... | collective-permute-start | bytes 294920 | tf_op jit(solution)/shard_map/ppermute | solution.py:58
  10.5 0.0 collective-permute-done.1.rest_2_.refs_9_
  10.5 0.1 collective-permute-done.2.rest_3_.refs_10_
  10.6 0.5 %shard_map.150 = (f32[80,1024]{1,0:T(8,128)S(1)}, f32[80,288]{1,0:T(8,128)S(1)}, bf16[80,288]{1,0:T(8,128)(2,1)S(1)}) custom-call(f32[16,4]{1,0:T(8,128)S(1)} %get-tuple-element.29.pick_ref.after_ref, f32[1,4]{1,0:T(1,128)S(1)} %get-tuple-element.30.sender_ref, f32[4,16,1024]{2,1,0:T(8,128)S(1)} %get-tuple-element.31.base_ref, ...), custom_call_target="tpu_custom_call" | custom-call | flops 47185920 | bytes 1009664 | tf_op jit(solution)/shard_map/pallas_call | solution.py:583
  11.2 0.1 collective-permute-start.3
  11.2 1.2 %collective-permute-done.3.b_ref = bf16[80,288]{1,0:T(8,128)(2,1)S(1)} collective-permute-done((bf16[80,288]{1,0:T(8,128)(2,1)S(1)}, bf16[80,288]{1,0:T(8,128)(2,1)S(1)}, u32[]{:S(2)}, u32[]{:S(2)}) %collective-permute-start.3) | collective-permute-done | bytes 46112 | tf_op jit(solution)/shard_map/ppermute | solution.py:58
  12.5 0.0 copy-start.1
  12.5 1.5 %collective-permute-start.5 = (bf16[80,288]{1,0:T(8,128)(2,1)S(1)}, bf16[80,288]{1,0:T(8,128)(2,1)S(1)}, u32[]{:S(2)}, u32[]{:S(2)}) collective-permute-start(bf16[80,288]{1,0:T(8,128)(2,1)S(1)} %get-tuple-element.49), channel_id=1, source_target_pairs={{0,3},{1,2},{2,1},{3,0},{4,7},{5,6},{6,5},{7,4},{8,11},{9,10},{10,... | collective-permute-start | bytes 138248 | tf_op jit(solution)/shard_map/ppermute | solution.py:58
  14.0 1.8 %shard_map.152 = (bf16[3,16,1024]{2,1,0:T(8,128)(2,1)}, f32[4,16,1024]{2,1,0:T(8,128)S(1)}, f32[16,1024]{1,0:T(8,128)S(1)}, f32[8,8,1024]{2,1,0:T(8,128)S(1)}, f...) custom-call(s32[1]{0:T(128)} %bitcast.owner_hbm.refs_0_, s32[16]{0:T(128)} %child_hbm.1, bf16[16,4,2,1024]{3,2,1,0:T(2,128)(2,1)} %refs_2_.1, ...), custom_call_target="tpu_custom_call" | custom-call | flops 655360 | bytes 786432 | tf_op jit(solution)/shard_map/pallas_call | solution.py:610
  15.8 0.0 collective-permute-done.4.rest_5_
  15.8 0.5 %shard_map.154 = (f32[16,16,1024]{2,1,0:T(8,128)S(1)}, f32[8,8,1024]{2,1,0:T(8,128)S(1)}) custom-call(f32[16,4]{1,0:T(8,128)S(1)} %get-tuple-element.29.pick_ref.after_ref, f32[1,4]{1,0:T(1,128)S(1)} %get-tuple-element.30.sender_ref, f32[80,288]{1,0:T(8,128)S(1)} %get-tuple-element.41.refs_6_.after_ref.part_ref, ...), custom_call_target="tpu_custom_call" | custom-call | flops 2621440 | bytes 1310720 | tf_op jit(solution)/shard_map/pallas_call | solution.py:643
  16.3 0.2 %collective-permute-done.5.other_ref = bf16[80,288]{1,0:T(8,128)(2,1)S(1)} collective-permute-done((bf16[80,288]{1,0:T(8,128)(2,1)S(1)}, bf16[80,288]{1,0:T(8,128)(2,1)S(1)}, u32[]{:S(2)}, u32[]{:S(2)}) %collective-permute-start.5) | collective-permute-done | bytes 46112 | tf_op jit(solution)/shard_map/ppermute | solution.py:58
  16.5 0.0 copy-done.1
  16.5 2.8 %shard_map.155 = (bf16[16,4,1024]{2,1,0:T(4,128)(2,1)}, f32[16,16,1024]{2,1,0:T(8,128)}) custom-call(s32[1]{0:T(128)} %bitcast.owner_hbm.refs_0_, s32[16]{0:T(128)} %child_hbm.1, f32[80,1024]{1,0:T(8,128)S(1)} %get-tuple-element.38.act_ref, f32[4,16,1024]{2,1,0:T(8,128)S(1)} %get-tuple-element.42.gate_ref, f32[16,16,1024]{2,1,0:T(8,128)S(1)} %get-tuple-element.43.own_ref, ...), custom_call_target="tpu_custom_call" | custom-call | flops 10485760 | bytes 1310720 | tf_op jit(solution)/shard_map/pallas_call | solution.py:656
  (2 shorter events, 0.0 us)
Async XLA Ops:
  1.7 7.2 %collective-permute-start = (bf16[1,24,1024]{2,1,0:T(8,128)(2,1)S(1)}, bf16[1,24,1024]{2,1,0:T(8,128)(2,1)S(1)}, u32[]{:S(2)}, u32[]{:S(2)}) collective-permute-start(bf16[1,24,1024]{2,1,0:T(8,128)(2,1)S(1)} %get-tuple-element.28.after_ref), channel_id=1, source_target_pairs={{0,8},{4,12},{8,4},{12,0},{1,9},{5,13},{9,5},{13,1},{2,10},{6,14},... | collective-permute-start | bytes 147464 | tf_op jit(solution)/shard_map/ppermute | solution.py:534
  5.8 4.7 %collective-permute-start.1 = (bf16[1,8,1024]{2,1,0:T(8,128)(2,1)S(1)}, bf16[1,8,1024]{2,1,0:T(8,128)(2,1)S(1)}, u32[]{:S(2)}, u32[]{:S(2)}) collective-permute-start(bf16[1,8,1024]{2,1,0:T(8,128)(2,1)S(1)} %get-tuple-element.36), channel_id=1, source_target_pairs={{0,12},{4,8},{8,0},{12,4},{1,13},{5,9},{9,1},{13,5},{2,14},{6,10},... | collective-permute-start | bytes 49160 | tf_op jit(solution)/shard_map/ppermute | solution.py:534
  6.9 3.7 %collective-permute-start.2 = (bf16[1,8,1024]{2,1,0:T(8,128)(2,1)S(1)}, bf16[1,8,1024]{2,1,0:T(8,128)(2,1)S(1)}, u32[]{:S(2)}, u32[]{:S(2)}) collective-permute-start(bf16[1,8,1024]{2,1,0:T(8,128)(2,1)S(1)} %get-tuple-element.37), channel_id=1, source_target_pairs={{0,4},{4,0},{8,12},{12,8},{1,5},{5,1},{9,13},{13,9},{2,6},{6,2},{1... | collective-permute-start | bytes 49160 | tf_op jit(solution)/shard_map/ppermute | solution.py:534
  7.4 1.6 %copy-start = (f32[1,16,1024]{2,1,0:T(8,128)S(1)}, f32[1,16,1024]{2,1,0:T(8,128)}, u32[]{:S(2)}) copy-start(f32[1,16,1024]{2,1,0:T(8,128)} %rest_4_.1) | copy-start | bytes 196612
  9.0 6.8 %collective-permute-start.4 = (bf16[1,48,1024]{2,1,0:T(8,128)(2,1)S(1)}, bf16[1,48,1024]{2,1,0:T(8,128)(2,1)S(1)}, u32[]{:S(2)}, u32[]{:S(2)}) collective-permute-start(bf16[1,48,1024]{2,1,0:T(8,128)(2,1)S(1)} %shard_map.153), channel_id=1, source_target_pairs={{0,4},{4,0},{8,12},{12,8},{1,5},{5,1},{9,13},{13,9},{2,6},{6,2},{1... | collective-permute-start | bytes 294920 | tf_op jit(solution)/shard_map/ppermute | solution.py:58
  11.2 1.3 %collective-permute-start.3 = (bf16[80,288]{1,0:T(8,128)(2,1)S(1)}, bf16[80,288]{1,0:T(8,128)(2,1)S(1)}, u32[]{:S(2)}, u32[]{:S(2)}) collective-permute-start(bf16[80,288]{1,0:T(8,128)(2,1)S(1)} %get-tuple-element.40), channel_id=1, source_target_pairs={{0,1},{1,0},{2,3},{3,2},{4,5},{5,4},{6,7},{7,6},{8,9},{9,8},{10,11... | collective-permute-start | bytes 138248 | tf_op jit(solution)/shard_map/ppermute | solution.py:58
  12.5 4.0 %copy-start.1 = (bf16[256,1024]{1,0:T(8,128)(2,1)S(1)}, bf16[256,1024]{1,0:T(8,128)(2,1)}, u32[]{:S(2)}) copy-start(bf16[256,1024]{1,0:T(8,128)(2,1)} %dtw_ref.1) | copy-start | bytes 1572868
  12.5 4.0 %collective-permute-start.5 = (bf16[80,288]{1,0:T(8,128)(2,1)S(1)}, bf16[80,288]{1,0:T(8,128)(2,1)S(1)}, u32[]{:S(2)}, u32[]{:S(2)}) collective-permute-start(bf16[80,288]{1,0:T(8,128)(2,1)S(1)} %get-tuple-element.49), channel_id=1, source_target_pairs={{0,3},{1,2},{2,1},{3,0},{4,7},{5,6},{6,5},{7,4},{8,11},{9,10},{10,... | collective-permute-start | bytes 138248 | tf_op jit(solution)/shard_map/ppermute | solution.py:58

commit v27 on v26

--- a/solution.py
+++ b/solution.py
@@ -465,7 +465,7 @@
                     ]
         for w in range(WIDE):
             some = pl.ds(pl.multiple_of((chunk * WIDE + w) * LANES, LANES), LANES)
-            dec_ref[:, :, some] = line_s[w].reshape(rb, steps, LANES).astype(BF16)
+            dec_ref[:, :, some] = line_s[w, : steps * rb, :].reshape(rb, steps, LANES).astype(BF16)
         return carry
 
     lax.fori_loop(0, chunks, own_chunk, 0)
@@ -672,8 +672,8 @@
             pltpu.VMEM((n_state, steps * rb, LANES), F32),
             pltpu.VMEM((n_state // 2, steps, 2 * owners, LANES), F32),
             pltpu.VMEM((owners, n_state, channels), F32),
-            pltpu.VMEM((channels // LANES, n_state * owners, LANES), F32),
-            pltpu.VMEM((WIDE, steps * rb, LANES), F32),
+            pltpu.VMEM((channels // LANES, (n_state + 1) * owners + 4, LANES), F32),
+            pltpu.VMEM((WIDE, steps * rb + 8, LANES), F32),
             pltpu.SemaphoreType.DMA((2 + rb,)),
         ],
         flops=8 * rows * n_state * channels,

time: 19.6 us -> 19.6 us (level)
  no operation moved by 1% of the time
where the time goes in v27:
time: 19.6 us; the launch traced here: 19.3 us
  starting transfers between devices  8.73 us (45%)
  Pallas kernels  8.17 us (42%)
  waiting for transfers between devices  1.69 us (9%)
  between operations  0.71 us (4%)
    ppermute x3, starting transfers between devices, on_device(): lax.ppermute(m, 'branch', list(enumerate(to)))  5.67 us
    ppermute x3, starting transfers between devices, swap(): return lax.ppermute(value, axis, [(i, i ^ distance) for i in range(size)])  3.07 us
    pallas_call x1, Pallas kernels, on_device(): call(functools.partial(decode_kernel, direct), [shaped((rb, steps, channe...  2.78 us
    pallas_call x1, Pallas kernels, on_device(): call(functools.partial(late_kernel, n_msgs, direct), [shaped((taps - 1, r...  1.78 us
    ppermute x3, waiting for transfers between devices, swap(): return lax.ppermute(value, axis, [(i, i ^ distance) for i in range(size)])  1.45 us
    pallas_call x1, Pallas kernels, on_device(): call(functools.partial(prepare_kernel, direct), [shaped((1, short, channe...  1.45 us
    pallas_call x1, Pallas kernels, on_device(): call(functools.partial(pack_kernel, direct), [shaped(s, BF16) for s in ms...  1.1 us
    pallas_call x1, Pallas kernels, on_device(): call(functools.partial(start_kernel, n_msgs, direct, short), [shaped((n_s...  0.53 us
  transfers between devices with their start and end apart: 6, of which 4 were waited for; matrix products, arithmetic and copies ran while one was open for 0% of the time, Pallas kernels for 22%

profile of v27, /device:TPU:0, one launch (start us, length us, event | category | flops | bytes accessed | tf_op | source)
XLA Modules:
  0.0 19.3 jit_solution(15739616948870721379)
XLA Ops:
  0.6 1.1 %shard_map.148 = (bf16[1,24,1024]{2,1,0:T(8,128)(2,1)S(1)}, bf16[1,8,1024]{2,1,0:T(8,128)(2,1)S(1)}, bf16[1,8,1024]{2,1,0:T(8,128)(2,1)S(1)}) custom-call(s32[1]{0:T(128)} %bitcast.owner_hbm.refs_0_, s32[4]{0:T(128)} %bitcast.11, s32[16]{0:T(128)} %prompt_hbm.3, bf16[16,4,2,1024]{3,2,1,0:T(2,128)(2,1)} %refs_2_.1, bf16[1,3,1024]{2,1,0:T(4,128)(2,1)} %conv_hbm.3, ...), custom_call_target="tpu_custom_call" | custom-call | bytes 196608 | tf_op jit(solution)/shard_map/pallas_call | solution.py:509
  1.7 4.1 %collective-permute-start = (bf16[1,24,1024]{2,1,0:T(8,128)(2,1)S(1)}, bf16[1,24,1024]{2,1,0:T(8,128)(2,1)S(1)}, u32[]{:S(2)}, u32[]{:S(2)}) collective-permute-start(bf16[1,24,1024]{2,1,0:T(8,128)(2,1)S(1)} %get-tuple-element.28.after_ref), channel_id=1, source_target_pairs={{0,8},{4,12},{8,4},{12,0},{1,9},{5,13},{9,5},{13,1},{2,10},{6,14},... | collective-permute-start | bytes 147464 | tf_op jit(solution)/shard_map/ppermute | solution.py:534
  5.8 1.1 %collective-permute-start.1 = (bf16[1,8,1024]{2,1,0:T(8,128)(2,1)S(1)}, bf16[1,8,1024]{2,1,0:T(8,128)(2,1)S(1)}, u32[]{:S(2)}, u32[]{:S(2)}) collective-permute-start(bf16[1,8,1024]{2,1,0:T(8,128)(2,1)S(1)} %get-tuple-element.36), channel_id=1, source_target_pairs={{0,12},{4,8},{8,0},{12,4},{1,13},{5,9},{9,1},{13,5},{2,14},{6,10},... | collective-permute-start | bytes 49160 | tf_op jit(solution)/shard_map/ppermute | solution.py:534
  6.9 0.5 %collective-permute-start.2 = (bf16[1,8,1024]{2,1,0:T(8,128)(2,1)S(1)}, bf16[1,8,1024]{2,1,0:T(8,128)(2,1)S(1)}, u32[]{:S(2)}, u32[]{:S(2)}) collective-permute-start(bf16[1,8,1024]{2,1,0:T(8,128)(2,1)S(1)} %get-tuple-element.37), channel_id=1, source_target_pairs={{0,4},{4,0},{8,12},{12,8},{1,5},{5,1},{9,13},{13,9},{2,6},{6,2},{1... | collective-permute-start | bytes 49160 | tf_op jit(solution)/shard_map/ppermute | solution.py:534
  7.4 0.0 copy-start
  7.4 1.4 %shard_map.149 = (bf16[1,8,1024]{2,1,0:T(8,128)(2,1)S(1)}, f32[4,16,1024]{2,1,0:T(8,128)S(1)}, f32[16,4]{1,0:T(8,128)S(1)}, f32[1,4]{1,0:T(1,128)S(1)}, f32[4,10...) custom-call(s32[1]{0:T(128)} %bitcast.owner_hbm.refs_0_, s32[16]{0:T(128)} %prompt_hbm.3, ...), custom_call_target="tpu_custom_call" | custom-call | flops 655360 | bytes 786432 | tf_op jit(solution)/shard_map/pallas_call | solution.py:537
  8.9 0.1 collective-permute-done.rest_1_.refs_8_.came_ref
  9.0 0.0 copy-done
  9.0 1.5 %collective-permute-start.4 = (bf16[1,48,1024]{2,1,0:T(8,128)(2,1)S(1)}, bf16[1,48,1024]{2,1,0:T(8,128)(2,1)S(1)}, u32[]{:S(2)}, u32[]{:S(2)}) collective-permute-start(bf16[1,48,1024]{2,1,0:T(8,128)(2,1)S(1)} %shard_map.153), channel_id=1, source_target_pairs={{0,4},{4,0},{8,12},{12,8},{1,5},{5,1},{9,13},{13,9},{2,6},{6,2},{1... | collective-permute-start | bytes 294920 | tf_op jit(solution)/shard_map/ppermute | solution.py:58
  10.5 0.0 collective-permute-done.1.rest_2_.refs_9_
  10.5 0.1 collective-permute-done.2.rest_3_.refs_10_
  10.6 0.5 %shard_map.150 = (f32[80,1024]{1,0:T(8,128)S(1)}, f32[80,288]{1,0:T(8,128)S(1)}, bf16[80,288]{1,0:T(8,128)(2,1)S(1)}) custom-call(f32[16,4]{1,0:T(8,128)S(1)} %get-tuple-element.29.pick_ref.after_ref, f32[1,4]{1,0:T(1,128)S(1)} %get-tuple-element.30.sender_ref, f32[4,16,1024]{2,1,0:T(8,128)S(1)} %get-tuple-element.31.base_ref, ...), custom_call_target="tpu_custom_call" | custom-call | flops 47185920 | bytes 1009664 | tf_op jit(solution)/shard_map/pallas_call | solution.py:583
  11.2 0.1 collective-permute-start.3
  11.2 1.2 %collective-permute-done.3.b_ref = bf16[80,288]{1,0:T(8,128)(2,1)S(1)} collective-permute-done((bf16[80,288]{1,0:T(8,128)(2,1)S(1)}, bf16[80,288]{1,0:T(8,128)(2,1)S(1)}, u32[]{:S(2)}, u32[]{:S(2)}) %collective-permute-start.3) | collective-permute-done | bytes 46112 | tf_op jit(solution)/shard_map/ppermute | solution.py:58
  12.5 0.0 copy-start.1
  12.5 1.5 %collective-permute-start.5 = (bf16[80,288]{1,0:T(8,128)(2,1)S(1)}, bf16[80,288]{1,0:T(8,128)(2,1)S(1)}, u32[]{:S(2)}, u32[]{:S(2)}) collective-permute-start(bf16[80,288]{1,0:T(8,128)(2,1)S(1)} %get-tuple-element.49), channel_id=1, source_target_pairs={{0,3},{1,2},{2,1},{3,0},{4,7},{5,6},{6,5},{7,4},{8,11},{9,10},{10,... | collective-permute-start | bytes 138248 | tf_op jit(solution)/shard_map/ppermute | solution.py:58
  14.0 1.8 %shard_map.152 = (bf16[3,16,1024]{2,1,0:T(8,128)(2,1)}, f32[4,16,1024]{2,1,0:T(8,128)S(1)}, f32[16,1024]{1,0:T(8,128)S(1)}, f32[8,8,1024]{2,1,0:T(8,128)S(1)}, f...) custom-call(s32[1]{0:T(128)} %bitcast.owner_hbm.refs_0_, s32[16]{0:T(128)} %child_hbm.1, bf16[16,4,2,1024]{3,2,1,0:T(2,128)(2,1)} %refs_2_.1, ...), custom_call_target="tpu_custom_call" | custom-call | flops 655360 | bytes 786432 | tf_op jit(solution)/shard_map/pallas_call | solution.py:610
  15.8 0.0 collective-permute-done.4.rest_5_
  15.8 0.5 %shard_map.154 = (f32[16,16,1024]{2,1,0:T(8,128)S(1)}, f32[8,8,1024]{2,1,0:T(8,128)S(1)}) custom-call(f32[16,4]{1,0:T(8,128)S(1)} %get-tuple-element.29.pick_ref.after_ref, f32[1,4]{1,0:T(1,128)S(1)} %get-tuple-element.30.sender_ref, f32[80,288]{1,0:T(8,128)S(1)} %get-tuple-element.41.refs_6_.after_ref.part_ref, ...), custom_call_target="tpu_custom_call" | custom-call | flops 2621440 | bytes 1310720 | tf_op jit(solution)/shard_map/pallas_call | solution.py:643
  16.3 0.2 %collective-permute-done.5.other_ref = bf16[80,288]{1,0:T(8,128)(2,1)S(1)} collective-permute-done((bf16[80,288]{1,0:T(8,128)(2,1)S(1)}, bf16[80,288]{1,0:T(8,128)(2,1)S(1)}, u32[]{:S(2)}, u32[]{:S(2)}) %collective-permute-start.5) | collective-permute-done | bytes 46112 | tf_op jit(solution)/shard_map/ppermute | solution.py:58
  16.5 0.0 copy-done.1
  16.5 2.8 %shard_map.155 = (bf16[16,4,1024]{2,1,0:T(4,128)(2,1)}, f32[16,16,1024]{2,1,0:T(8,128)}) custom-call(s32[1]{0:T(128)} %bitcast.owner_hbm.refs_0_, s32[16]{0:T(128)} %child_hbm.1, f32[80,1024]{1,0:T(8,128)S(1)} %get-tuple-element.38.act_ref, f32[4,16,1024]{2,1,0:T(8,128)S(1)} %get-tuple-element.42.gate_ref, f32[16,16,1024]{2,1,0:T(8,128)S(1)} %get-tuple-element.43.own_ref, ...), custom_call_target="tpu_custom_call" | custom-call | flops 10485760 | bytes 1310720 | tf_op jit(solution)/shard_map/pallas_call | solution.py:656
  (2 shorter events, 0.0 us)
Async XLA Ops:
  1.7 7.2 %collective-permute-start = (bf16[1,24,1024]{2,1,0:T(8,128)(2,1)S(1)}, bf16[1,24,1024]{2,1,0:T(8,128)(2,1)S(1)}, u32[]{:S(2)}, u32[]{:S(2)}) collective-permute-start(bf16[1,24,1024]{2,1,0:T(8,128)(2,1)S(1)} %get-tuple-element.28.after_ref), channel_id=1, source_target_pairs={{0,8},{4,12},{8,4},{12,0},{1,9},{5,13},{9,5},{13,1},{2,10},{6,14},... | collective-permute-start | bytes 147464 | tf_op jit(solution)/shard_map/ppermute | solution.py:534
  5.8 4.7 %collective-permute-start.1 = (bf16[1,8,1024]{2,1,0:T(8,128)(2,1)S(1)}, bf16[1,8,1024]{2,1,0:T(8,128)(2,1)S(1)}, u32[]{:S(2)}, u32[]{:S(2)}) collective-permute-start(bf16[1,8,1024]{2,1,0:T(8,128)(2,1)S(1)} %get-tuple-element.36), channel_id=1, source_target_pairs={{0,12},{4,8},{8,0},{12,4},{1,13},{5,9},{9,1},{13,5},{2,14},{6,10},... | collective-permute-start | bytes 49160 | tf_op jit(solution)/shard_map/ppermute | solution.py:534
  6.9 3.7 %collective-permute-start.2 = (bf16[1,8,1024]{2,1,0:T(8,128)(2,1)S(1)}, bf16[1,8,1024]{2,1,0:T(8,128)(2,1)S(1)}, u32[]{:S(2)}, u32[]{:S(2)}) collective-permute-start(bf16[1,8,1024]{2,1,0:T(8,128)(2,1)S(1)} %get-tuple-element.37), channel_id=1, source_target_pairs={{0,4},{4,0},{8,12},{12,8},{1,5},{5,1},{9,13},{13,9},{2,6},{6,2},{1... | collective-permute-start | bytes 49160 | tf_op jit(solution)/shard_map/ppermute | solution.py:534
  7.4 1.6 %copy-start = (f32[1,16,1024]{2,1,0:T(8,128)S(1)}, f32[1,16,1024]{2,1,0:T(8,128)}, u32[]{:S(2)}) copy-start(f32[1,16,1024]{2,1,0:T(8,128)} %rest_4_.1) | copy-start | bytes 196612
  9.0 6.8 %collective-permute-start.4 = (bf16[1,48,1024]{2,1,0:T(8,128)(2,1)S(1)}, bf16[1,48,1024]{2,1,0:T(8,128)(2,1)S(1)}, u32[]{:S(2)}, u32[]{:S(2)}) collective-permute-start(bf16[1,48,1024]{2,1,0:T(8,128)(2,1)S(1)} %shard_map.153), channel_id=1, source_target_pairs={{0,4},{4,0},{8,12},{12,8},{1,5},{5,1},{9,13},{13,9},{2,6},{6,2},{1... | collective-permute-start | bytes 294920 | tf_op jit(solution)/shard_map/ppermute | solution.py:58
  11.2 1.3 %collective-permute-start.3 = (bf16[80,288]{1,0:T(8,128)(2,1)S(1)}, bf16[80,288]{1,0:T(8,128)(2,1)S(1)}, u32[]{:S(2)}, u32[]{:S(2)}) collective-permute-start(bf16[80,288]{1,0:T(8,128)(2,1)S(1)} %get-tuple-element.40), channel_id=1, source_target_pairs={{0,1},{1,0},{2,3},{3,2},{4,5},{5,4},{6,7},{7,6},{8,9},{9,8},{10,11... | collective-permute-start | bytes 138248 | tf_op jit(solution)/shard_map/ppermute | solution.py:58
  12.5 4.0 %copy-start.1 = (bf16[256,1024]{1,0:T(8,128)(2,1)S(1)}, bf16[256,1024]{1,0:T(8,128)(2,1)}, u32[]{:S(2)}) copy-start(bf16[256,1024]{1,0:T(8,128)(2,1)} %dtw_ref.1) | copy-start | bytes 1572868
  12.5 4.0 %collective-permute-start.5 = (bf16[80,288]{1,0:T(8,128)(2,1)S(1)}, bf16[80,288]{1,0:T(8,128)(2,1)S(1)}, u32[]{:S(2)}, u32[]{:S(2)}) collective-permute-start(bf16[80,288]{1,0:T(8,128)(2,1)S(1)} %get-tuple-element.49), channel_id=1, source_target_pairs={{0,3},{1,2},{2,1},{3,0},{4,7},{5,6},{6,5},{7,4},{8,11},{9,10},{10,... | collective-permute-start | bytes 138248 | tf_op jit(solution)/shard_map/ppermute | solution.py:58

commit v28 on v27

--- a/solution.py
+++ b/solution.py
@@ -145,7 +145,9 @@
 
 
 def silu(v):
-    return v / (1.0 + jnp.exp(-v))
+    below = 1.0 + jnp.exp(-v)
+    estimate = pl.reciprocal(below, approx=True)
+    return v * (estimate * (2.0 - below * estimate))
 
 
 def prepare_kernel(

time: 19.6 us -> 19.6 us (level)
  no operation moved by 1% of the time
where the time goes in v28:
time: 19.6 us; the launch traced here: 19.4 us
  starting transfers between devices  8.73 us (45%)
  Pallas kernels  8.22 us (42%)
  waiting for transfers between devices  1.69 us (9%)
  between operations  0.71 us (4%)
    ppermute x3, starting transfers between devices, on_device(): lax.ppermute(m, 'branch', list(enumerate(to)))  5.67 us
    ppermute x3, starting transfers between devices, swap(): return lax.ppermute(value, axis, [(i, i ^ distance) for i in range(size)])  3.07 us
    pallas_call x1, Pallas kernels, on_device(): call(functools.partial(decode_kernel, direct), [shaped((rb, steps, channe...  2.78 us
    pallas_call x1, Pallas kernels, on_device(): call(functools.partial(late_kernel, n_msgs, direct), [shaped((taps - 1, r...  1.78 us
    ppermute x3, waiting for transfers between devices, swap(): return lax.ppermute(value, axis, [(i, i ^ distance) for i in range(size)])  1.45 us
    pallas_call x1, Pallas kernels, on_device(): call(functools.partial(prepare_kernel, direct), [shaped((1, short, channe...  1.45 us
    pallas_call x1, Pallas kernels, on_device(): call(functools.partial(pack_kernel, direct), [shaped(s, BF16) for s in ms...  1.1 us
    pallas_call x1, Pallas kernels, on_device(): call(functools.partial(project_kernel, n_msgs), [shaped((rows, channels),...  0.55 us
  transfers between devices with their start and end apart: 6, of which 4 were waited for; matrix products, arithmetic and copies ran while one was open for 0% of the time, Pallas kernels for 22%

profile of v28, /device:TPU:0, one launch (start us, length us, event | category | flops | bytes accessed | tf_op | source)
XLA Modules:
  0.0 19.4 jit_solution(9339999502282230722)
XLA Ops:
  0.6 1.1 %shard_map.148 = (bf16[1,24,1024]{2,1,0:T(8,128)(2,1)S(1)}, bf16[1,8,1024]{2,1,0:T(8,128)(2,1)S(1)}, bf16[1,8,1024]{2,1,0:T(8,128)(2,1)S(1)}) custom-call(s32[1]{0:T(128)} %bitcast.owner_hbm.refs_0_, s32[4]{0:T(128)} %bitcast.11, s32[16]{0:T(128)} %prompt_hbm.3, bf16[16,4,2,1024]{3,2,1,0:T(2,128)(2,1)} %refs_2_.1, bf16[1,3,1024]{2,1,0:T(4,128)(2,1)} %conv_hbm.3, ...), custom_call_target="tpu_custom_call" | custom-call | bytes 196608 | tf_op jit(solution)/shard_map/pallas_call | solution.py:511
  1.7 4.1 %collective-permute-start = (bf16[1,24,1024]{2,1,0:T(8,128)(2,1)S(1)}, bf16[1,24,1024]{2,1,0:T(8,128)(2,1)S(1)}, u32[]{:S(2)}, u32[]{:S(2)}) collective-permute-start(bf16[1,24,1024]{2,1,0:T(8,128)(2,1)S(1)} %get-tuple-element.28.after_ref), channel_id=1, source_target_pairs={{0,8},{4,12},{8,4},{12,0},{1,9},{5,13},{9,5},{13,1},{2,10},{6,14},... | collective-permute-start | bytes 147464 | tf_op jit(solution)/shard_map/ppermute | solution.py:536
  5.8 1.1 %collective-permute-start.1 = (bf16[1,8,1024]{2,1,0:T(8,128)(2,1)S(1)}, bf16[1,8,1024]{2,1,0:T(8,128)(2,1)S(1)}, u32[]{:S(2)}, u32[]{:S(2)}) collective-permute-start(bf16[1,8,1024]{2,1,0:T(8,128)(2,1)S(1)} %get-tuple-element.36), channel_id=1, source_target_pairs={{0,12},{4,8},{8,0},{12,4},{1,13},{5,9},{9,1},{13,5},{2,14},{6,10},... | collective-permute-start | bytes 49160 | tf_op jit(solution)/shard_map/ppermute | solution.py:536
  6.9 0.5 %collective-permute-start.2 = (bf16[1,8,1024]{2,1,0:T(8,128)(2,1)S(1)}, bf16[1,8,1024]{2,1,0:T(8,128)(2,1)S(1)}, u32[]{:S(2)}, u32[]{:S(2)}) collective-permute-start(bf16[1,8,1024]{2,1,0:T(8,128)(2,1)S(1)} %get-tuple-element.37), channel_id=1, source_target_pairs={{0,4},{4,0},{8,12},{12,8},{1,5},{5,1},{9,13},{13,9},{2,6},{6,2},{1... | collective-permute-start | bytes 49160 | tf_op jit(solution)/shard_map/ppermute | solution.py:536
  7.4 0.0 copy-start
  7.4 1.4 %shard_map.149 = (bf16[1,8,1024]{2,1,0:T(8,128)(2,1)S(1)}, f32[4,16,1024]{2,1,0:T(8,128)S(1)}, f32[16,4]{1,0:T(8,128)S(1)}, f32[1,4]{1,0:T(1,128)S(1)}, f32[4,10...) custom-call(s32[1]{0:T(128)} %bitcast.owner_hbm.refs_0_, s32[16]{0:T(128)} %prompt_hbm.3, ...), custom_call_target="tpu_custom_call" | custom-call | flops 655360 | bytes 786432 | tf_op jit(solution)/shard_map/pallas_call | solution.py:539
  8.9 0.1 collective-permute-done.rest_1_.refs_8_.came_ref
  9.0 0.0 copy-done
  9.0 1.5 %collective-permute-start.4 = (bf16[1,48,1024]{2,1,0:T(8,128)(2,1)S(1)}, bf16[1,48,1024]{2,1,0:T(8,128)(2,1)S(1)}, u32[]{:S(2)}, u32[]{:S(2)}) collective-permute-start(bf16[1,48,1024]{2,1,0:T(8,128)(2,1)S(1)} %shard_map.153), channel_id=1, source_target_pairs={{0,4},{4,0},{8,12},{12,8},{1,5},{5,1},{9,13},{13,9},{2,6},{6,2},{1... | collective-permute-start | bytes 294920 | tf_op jit(solution)/shard_map/ppermute | solution.py:58
  10.5 0.0 collective-permute-done.1.rest_2_.refs_9_
  10.5 0.1 collective-permute-done.2.rest_3_.refs_10_
  10.6 0.5 %shard_map.150 = (f32[80,1024]{1,0:T(8,128)S(1)}, f32[80,288]{1,0:T(8,128)S(1)}, bf16[80,288]{1,0:T(8,128)(2,1)S(1)}) custom-call(f32[16,4]{1,0:T(8,128)S(1)} %get-tuple-element.29.pick_ref.after_ref, f32[1,4]{1,0:T(1,128)S(1)} %get-tuple-element.30.sender_ref, f32[4,16,1024]{2,1,0:T(8,128)S(1)} %get-tuple-element.31.base_ref, ...), custom_call_target="tpu_custom_call" | custom-call | flops 47185920 | bytes 1009664 | tf_op jit(solution)/shard_map/pallas_call | solution.py:585
  11.2 0.1 collective-permute-start.3
  11.3 1.2 %collective-permute-done.3.b_ref = bf16[80,288]{1,0:T(8,128)(2,1)S(1)} collective-permute-done((bf16[80,288]{1,0:T(8,128)(2,1)S(1)}, bf16[80,288]{1,0:T(8,128)(2,1)S(1)}, u32[]{:S(2)}, u32[]{:S(2)}) %collective-permute-start.3) | collective-permute-done | bytes 46112 | tf_op jit(solution)/shard_map/ppermute | solution.py:58
  12.5 0.0 copy-start.1
  12.6 1.5 %collective-permute-start.5 = (bf16[80,288]{1,0:T(8,128)(2,1)S(1)}, bf16[80,288]{1,0:T(8,128)(2,1)S(1)}, u32[]{:S(2)}, u32[]{:S(2)}) collective-permute-start(bf16[80,288]{1,0:T(8,128)(2,1)S(1)} %get-tuple-element.49), channel_id=1, source_target_pairs={{0,3},{1,2},{2,1},{3,0},{4,7},{5,6},{6,5},{7,4},{8,11},{9,10},{10,... | collective-permute-start | bytes 138248 | tf_op jit(solution)/shard_map/ppermute | solution.py:58
  14.0 1.8 %shard_map.152 = (bf16[3,16,1024]{2,1,0:T(8,128)(2,1)}, f32[4,16,1024]{2,1,0:T(8,128)S(1)}, f32[16,1024]{1,0:T(8,128)S(1)}, f32[8,8,1024]{2,1,0:T(8,128)S(1)}, f...) custom-call(s32[1]{0:T(128)} %bitcast.owner_hbm.refs_0_, s32[16]{0:T(128)} %child_hbm.1, bf16[16,4,2,1024]{3,2,1,0:T(2,128)(2,1)} %refs_2_.1, ...), custom_call_target="tpu_custom_call" | custom-call | flops 655360 | bytes 786432 | tf_op jit(solution)/shard_map/pallas_call | solution.py:612
  15.8 0.0 collective-permute-done.4.rest_5_
  15.8 0.5 %shard_map.154 = (f32[16,16,1024]{2,1,0:T(8,128)S(1)}, f32[8,8,1024]{2,1,0:T(8,128)S(1)}) custom-call(f32[16,4]{1,0:T(8,128)S(1)} %get-tuple-element.29.pick_ref.after_ref, f32[1,4]{1,0:T(1,128)S(1)} %get-tuple-element.30.sender_ref, f32[80,288]{1,0:T(8,128)S(1)} %get-tuple-element.41.refs_6_.after_ref.part_ref, ...), custom_call_target="tpu_custom_call" | custom-call | flops 2621440 | bytes 1310720 | tf_op jit(solution)/shard_map/pallas_call | solution.py:645
  16.4 0.2 %collective-permute-done.5.other_ref = bf16[80,288]{1,0:T(8,128)(2,1)S(1)} collective-permute-done((bf16[80,288]{1,0:T(8,128)(2,1)S(1)}, bf16[80,288]{1,0:T(8,128)(2,1)S(1)}, u32[]{:S(2)}, u32[]{:S(2)}) %collective-permute-start.5) | collective-permute-done | bytes 46112 | tf_op jit(solution)/shard_map/ppermute | solution.py:58
  16.6 0.0 copy-done.1
  16.6 2.8 %shard_map.155 = (bf16[16,4,1024]{2,1,0:T(4,128)(2,1)}, f32[16,16,1024]{2,1,0:T(8,128)}) custom-call(s32[1]{0:T(128)} %bitcast.owner_hbm.refs_0_, s32[16]{0:T(128)} %child_hbm.1, f32[80,1024]{1,0:T(8,128)S(1)} %get-tuple-element.38.act_ref, f32[4,16,1024]{2,1,0:T(8,128)S(1)} %get-tuple-element.42.gate_ref, f32[16,16,1024]{2,1,0:T(8,128)S(1)} %get-tuple-element.43.own_ref, ...), custom_call_target="tpu_custom_call" | custom-call | flops 10485760 | bytes 1310720 | tf_op jit(solution)/shard_map/pallas_call | solution.py:658
  (2 shorter events, 0.0 us)
Async XLA Ops:
  1.7 7.2 %collective-permute-start = (bf16[1,24,1024]{2,1,0:T(8,128)(2,1)S(1)}, bf16[1,24,1024]{2,1,0:T(8,128)(2,1)S(1)}, u32[]{:S(2)}, u32[]{:S(2)}) collective-permute-start(bf16[1,24,1024]{2,1,0:T(8,128)(2,1)S(1)} %get-tuple-element.28.after_ref), channel_id=1, source_target_pairs={{0,8},{4,12},{8,4},{12,0},{1,9},{5,13},{9,5},{13,1},{2,10},{6,14},... | collective-permute-start | bytes 147464 | tf_op jit(solution)/shard_map/ppermute | solution.py:536
  5.8 4.7 %collective-permute-start.1 = (bf16[1,8,1024]{2,1,0:T(8,128)(2,1)S(1)}, bf16[1,8,1024]{2,1,0:T(8,128)(2,1)S(1)}, u32[]{:S(2)}, u32[]{:S(2)}) collective-permute-start(bf16[1,8,1024]{2,1,0:T(8,128)(2,1)S(1)} %get-tuple-element.36), channel_id=1, source_target_pairs={{0,12},{4,8},{8,0},{12,4},{1,13},{5,9},{9,1},{13,5},{2,14},{6,10},... | collective-permute-start | bytes 49160 | tf_op jit(solution)/shard_map/ppermute | solution.py:536
  6.9 3.7 %collective-permute-start.2 = (bf16[1,8,1024]{2,1,0:T(8,128)(2,1)S(1)}, bf16[1,8,1024]{2,1,0:T(8,128)(2,1)S(1)}, u32[]{:S(2)}, u32[]{:S(2)}) collective-permute-start(bf16[1,8,1024]{2,1,0:T(8,128)(2,1)S(1)} %get-tuple-element.37), channel_id=1, source_target_pairs={{0,4},{4,0},{8,12},{12,8},{1,5},{5,1},{9,13},{13,9},{2,6},{6,2},{1... | collective-permute-start | bytes 49160 | tf_op jit(solution)/shard_map/ppermute | solution.py:536
  7.4 1.6 %copy-start = (f32[1,16,1024]{2,1,0:T(8,128)S(1)}, f32[1,16,1024]{2,1,0:T(8,128)}, u32[]{:S(2)}) copy-start(f32[1,16,1024]{2,1,0:T(8,128)} %rest_4_.1) | copy-start | bytes 196612
  9.0 6.8 %collective-permute-start.4 = (bf16[1,48,1024]{2,1,0:T(8,128)(2,1)S(1)}, bf16[1,48,1024]{2,1,0:T(8,128)(2,1)S(1)}, u32[]{:S(2)}, u32[]{:S(2)}) collective-permute-start(bf16[1,48,1024]{2,1,0:T(8,128)(2,1)S(1)} %shard_map.153), channel_id=1, source_target_pairs={{0,4},{4,0},{8,12},{12,8},{1,5},{5,1},{9,13},{13,9},{2,6},{6,2},{1... | collective-permute-start | bytes 294920 | tf_op jit(solution)/shard_map/ppermute | solution.py:58
  11.2 1.3 %collective-permute-start.3 = (bf16[80,288]{1,0:T(8,128)(2,1)S(1)}, bf16[80,288]{1,0:T(8,128)(2,1)S(1)}, u32[]{:S(2)}, u32[]{:S(2)}) collective-permute-start(bf16[80,288]{1,0:T(8,128)(2,1)S(1)} %get-tuple-element.40), channel_id=1, source_target_pairs={{0,1},{1,0},{2,3},{3,2},{4,5},{5,4},{6,7},{7,6},{8,9},{9,8},{10,11... | collective-permute-start | bytes 138248 | tf_op jit(solution)/shard_map/ppermute | solution.py:58
  12.5 4.0 %copy-start.1 = (bf16[256,1024]{1,0:T(8,128)(2,1)S(1)}, bf16[256,1024]{1,0:T(8,128)(2,1)}, u32[]{:S(2)}) copy-start(bf16[256,1024]{1,0:T(8,128)(2,1)} %dtw_ref.1) | copy-start | bytes 1572868
  12.6 4.0 %collective-permute-start.5 = (bf16[80,288]{1,0:T(8,128)(2,1)S(1)}, bf16[80,288]{1,0:T(8,128)(2,1)S(1)}, u32[]{:S(2)}, u32[]{:S(2)}) collective-permute-start(bf16[80,288]{1,0:T(8,128)(2,1)S(1)} %get-tuple-element.49), channel_id=1, source_target_pairs={{0,3},{1,2},{2,1},{3,0},{4,7},{5,6},{6,5},{7,4},{8,11},{9,10},{10,... | collective-permute-start | bytes 138248 | tf_op jit(solution)/shard_map/ppermute | solution.py:58
